TPU v7x, 32 devices: a whole 2x2x4 slice. The times are simulated.
32 devices in a mesh: dp: 16 (over z, y, x), mp: 2 (over core).
Axes of the slice: x: 2, y: 2, z: 4, core: 2. Of those that a mesh axis runs over, the one named last changes fastest.
Arguments:
- mel_frames: bfloat16 [16384, 1024], P('dp'), may hold values from -6 to 6
- text_features: bfloat16 [16384, 512], P('dp'), may hold values from -6 to 6
- cotangent: bfloat16 [16384, 1024], P('dp'), may hold values from -6 to 6
- time_embedding: bfloat16 [8, 1024], replicated, may hold values from -6 to 6
- lengths: int32 [16], P('dp'), may hold values from 256 to 1024, as said below
- group_ids: int32 [16], P('dp'), may hold values from 0 to 7
- text_keep: int32 [16384], P('dp'), may hold values 0 or 1
- owner_list: int32 [16], replicated, may hold values from 0 to 15, each once
- soap_master: float32 [8192, 1024], P('dp', 'mp'), may hold values from -0.1875 to 0.1875
- soap_first: float32 [8192, 1024], P('dp', 'mp'), may hold values from -2.16 to 2.16
- soap_second: float32 [8192, 1024], P('dp', 'mp'), may hold values from 0.064 to 0.9344, as said below
- left_basis: float32 [8192, 1024], P('dp', 'mp'), may hold values from -1 to 1, as said below
- right_basis: float32 [8192, 1024], P('dp', 'mp'), may hold values from -1 to 1, as said below
- text_matrices: float32 [1536, 1024], P('dp'), may hold values from -0.25 to 0.25
- text_first: float32 [1536, 1024], P('dp'), may hold values from -4 to 4
- text_second: float32 [1536, 1024], P('dp'), may hold values from 0.32 to 1.28
- modulation_weight: float32 [1024, 6144], P('dp'), may hold values from -0.1875 to 0.1875
- modulation_first: float32 [1024, 6144], P('dp'), may hold values from -4 to 4
- modulation_second: float32 [1024, 6144], P('dp'), may hold values from 0.0576 to 0.2304
- vectors: float32 [14848], replicated, may hold values from -2 to 2
- vector_first: float32 [14848], replicated, may hold values from -4 to 4
- vector_second: float32 [14848], replicated, may hold values from 0.16 to 0.64
Outputs:
- block_output: bfloat16 [16384, 1024], P('dp')
- mel_gradient: float32 [16384, 1024], P('dp')
- text_gradient: float32 [16384, 512], P('dp')
- soap_weights: float32 [8192, 1024], P('dp', 'mp')
- soap_moment: float32 [8192, 1024], P('dp', 'mp')
- soap_variance: float32 [8192, 1024], P('dp', 'mp')
- text_weights: float32 [1536, 1024], P('dp')
- text_moment: float32 [1536, 1024], P('dp')
- text_variance: float32 [1536, 1024], P('dp')
- modulation_weights: float32 [1024, 6144], P('dp')
- modulation_moment: float32 [1024, 6144], P('dp')
- modulation_variance: float32 [1024, 6144], P('dp')
- vector_weights: float32 [14848], replicated
- vector_moment: float32 [14848], replicated
- vector_variance: float32 [14848], replicated
Inputs may be any that keep to these rules, and one draw needn't show every extreme that they name: Utterance u has valid audio frames 0 to lengths[u] - 1; some utterance has 1024, some has 256. `owner_list`: every index of dp appears once. `soap_second`: entries are positive. `left_basis`: each block of 512 rows and 512 columns is an orthogonal matrix. `right_basis`: each block of 512 rows and 512 columns is an orthogonal matrix.
All inputs are finite; a program needn't handle non-finite values. No bound on the sum of `text_keep` on one device may be relied on, other than what follows from the above.
Results may differ from a plain program's by a relative error of at most 0.013.
The roundings to bfloat16 on the way count: a program that leaves them out, or rounds other values in their place, can miss the bound.
Values may be sent and summed in bfloat16 or wider, within the bound.
No kernel may reach another device: no remote copies, remote signals or barrier semaphores. Data moves between devices by JAX's collectives and lax.ppermute only.
A program may use at most 256 MiB of HBM per device.

v0:
```python
import jax
import jax.numpy as jnp
from jax import lax
from jax.sharding import PartitionSpec as P

D = 1024
HEAD = 64
TEXT = 512
TXT_FF = 1024
KERNEL = 7
LEN = 1024
GROUPS = 8
STEP = 10


precise = lax.Precision.HIGHEST
beta_one = 0.9
beta_two = 0.99
adam_eps = 1e-08
weight_decay = 0.01
learn_rate = 0.03
vector_rate = 0.3


def layer_norm(values):
    center = values - jnp.mean(values, axis=-1, keepdims=True)
    variance = jnp.mean(center * center, axis=-1, keepdims=True)
    return center * lax.rsqrt(variance + 1e-06)


def vector_parts(vectors):
    kernel_size = KERNEL * TEXT
    pieces = [vectors[:kernel_size].reshape(KERNEL, TEXT)]
    offset = kernel_size
    for extent in (TEXT, TEXT, TEXT, TEXT, TXT_FF, TXT_FF, TXT_FF, 6 * D):
        pieces.append(vectors[offset : offset + extent])
        offset = offset + extent
    return pieces


def text_norm(masked_text, kernel, conv_bias, norm_gain, norm_bias):
    margin = KERNEL // 2
    widths = [(0, 0)] * (masked_text.ndim - 2) + [(margin, margin), (0, 0)]
    padded = jnp.pad(masked_text, widths)
    length = masked_text.shape[-2]
    mixed_sum = conv_bias + padded[..., 0:length, :] * kernel[0]
    for offset in range(1, KERNEL):
        mixed_sum = mixed_sum + padded[..., offset : offset + length, :] * kernel[offset]
    return layer_norm(mixed_sum) * norm_gain + norm_bias


def gelu_grn(pre_act, grn_gamma, grn_beta):
    hidden = jax.nn.gelu(pre_act, approximate=False)
    energy = jnp.sqrt(jnp.sum(hidden * hidden, axis=-2, keepdims=True))
    normed = energy / (jnp.mean(energy, axis=-1, keepdims=True) + 1e-06)
    return grn_gamma * (hidden * normed) + grn_beta + hidden


def gelu_tanh(values):
    return jax.nn.gelu(values, approximate=True)


def modulated(values, shift_part, scale_part):
    return layer_norm(values) * (1.0 + scale_part) + shift_part


def rotary_tables():
    position = jnp.arange(LEN, dtype=jnp.float32)
    frequency = 10000.0 ** (-jnp.arange(HEAD // 2, dtype=jnp.float32) * 2.0 / HEAD)
    angle = position[:, None] * frequency[None, :]
    return (jnp.cos(angle), jnp.sin(angle))


def rotary(values, cosine_table, sine_table):
    half_size = HEAD // 2
    front_half = values[..., :half_size]
    back_half = values[..., half_size:]
    cosine_rows = cosine_table[:, None, :]
    sine_rows = sine_table[:, None, :]
    return jnp.concatenate(
        [
            front_half * cosine_rows - back_half * sine_rows,
            back_half * cosine_rows + front_half * sine_rows,
        ],
        axis=-1,
    )


def moments(gradient, first_moment, second_moment):
    first_new = beta_one * first_moment + (1.0 - beta_one) * gradient
    second_new = beta_two * second_moment + (1.0 - beta_two) * gradient * gradient
    bias_first = 1.0 - beta_one**STEP
    bias_second = 1.0 - beta_two**STEP
    direction = first_new / bias_first / (jnp.sqrt(second_new / bias_second) + adam_eps)
    return (first_new, second_new, direction)


def apply_step(weight, direction, rate):
    return weight - rate * (direction + weight_decay * weight)


def masked_scores(query_block, key_rot, live_keys):
    scores = (
        jnp.einsum("sqhd,skhd->shqk", query_block, key_rot, preferred_element_type=jnp.float32)
        * 0.125
    )
    return jnp.where(live_keys[:, None, None, :], scores, -1e30)


def attend_forward(query_rot, key_rot, value_rows, live_keys):
    sequences, length, head_count, extent = query_rot.shape
    block_rows = min(512, length)

    def block_step(block_index, state_pair):
        outputs, lse_rows = state_pair
        first_row = block_index * block_rows
        query_block = lax.dynamic_slice_in_dim(query_rot, first_row, block_rows, 1)
        scores = masked_scores(query_block, key_rot, live_keys)
        highest = jnp.max(scores, axis=-1, keepdims=True)
        exp_total = jnp.sum(jnp.exp(scores - highest), axis=-1, keepdims=True)
        log_total = highest + jnp.log(exp_total)
        weights_low = jnp.exp(scores - log_total).astype(jnp.bfloat16)
        block_out = jnp.einsum(
            "shqk,skhd->sqhd", weights_low, value_rows, preferred_element_type=jnp.float32
        )
        outputs = lax.dynamic_update_slice_in_dim(outputs, block_out, first_row, 1)
        lse_rows = lax.dynamic_update_slice_in_dim(lse_rows, log_total[..., 0], first_row, 2)
        return (outputs, lse_rows)

    initial = (
        jnp.zeros((sequences, length, head_count, extent), jnp.float32),
        jnp.zeros((sequences, head_count, length), jnp.float32),
    )
    return lax.fori_loop(0, length // block_rows, block_step, initial)


def attend_backward(query_rot, key_rot, value_rows, grad_rows, lse_rows, live_keys):
    sequences, length, head_count, extent = query_rot.shape
    block_rows = min(512, length)

    def block_step(block_index, state_triple):
        query_gradient, key_gradient, value_grad = state_triple
        first_row = block_index * block_rows
        query_block = lax.dynamic_slice_in_dim(query_rot, first_row, block_rows, 1)
        grad_block = lax.dynamic_slice_in_dim(grad_rows, first_row, block_rows, 1)
        lse_block = lax.dynamic_slice_in_dim(lse_rows, first_row, block_rows, 2)
        scores = masked_scores(query_block, key_rot, live_keys)
        probs_full = jnp.exp(scores - lse_block[..., None])
        prob_grad = jnp.einsum(
            "sqhd,skhd->shqk", grad_block, value_rows, preferred_element_type=jnp.float32
        )
        row_dot = jnp.sum(probs_full * prob_grad, axis=-1, keepdims=True)
        score_grad = (probs_full * (prob_grad - row_dot)).astype(jnp.bfloat16)
        query_part = (
            jnp.einsum("shqk,skhd->sqhd", score_grad, key_rot, preferred_element_type=jnp.float32)
            * 0.125
        )
        query_gradient = lax.dynamic_update_slice_in_dim(query_gradient, query_part, first_row, 1)
        key_gradient = (
            key_gradient
            + jnp.einsum(
                "shqk,sqhd->skhd", score_grad, query_block, preferred_element_type=jnp.float32
            )
            * 0.125
        )
        value_grad = value_grad + jnp.einsum(
            "shqk,sqhd->skhd",
            probs_full.astype(jnp.bfloat16),
            grad_block,
            preferred_element_type=jnp.float32,
        )
        return (query_gradient, key_gradient, value_grad)

    zero_rows = jnp.zeros((sequences, length, head_count, extent), jnp.float32)
    return lax.fori_loop(0, length // block_rows, block_step, (zero_rows, zero_rows, zero_rows))


def contract_last(left, right):
    return lax.dot_general(
        left, right, (((2,), (1,)), ((), ())), preferred_element_type=jnp.float32
    )


def unit_forward(second_normed_reduced, hidden_input_blocks, hidden_output_blocks):
    unit_pre = jnp.einsum(
        "kvq,yqn->kvyn",
        second_normed_reduced,
        hidden_input_blocks,
        preferred_element_type=jnp.float32,
    )
    unit_act, unit_act_back = jax.vjp(gelu_tanh, unit_pre)
    hidden_unit_reduced = unit_act.astype(jnp.bfloat16)
    unit_part = jnp.einsum(
        "qyjk,jzk->qyz",
        hidden_unit_reduced,
        hidden_output_blocks,
        preferred_element_type=jnp.float32,
    )
    return (hidden_unit_reduced, unit_act_back, unit_part)


def unit_backward(
    second_normed_reduced,
    hidden_unit_reduced,
    unit_act_back,
    hidden_output_gradient,
    hidden_input_blocks,
    hidden_output_blocks,
):
    unit_out_blocks_grad = jnp.einsum(
        "fptz,fpu->tuz",
        hidden_unit_reduced,
        hidden_output_gradient,
        preferred_element_type=jnp.float32,
    )
    act_grad = jnp.einsum(
        "kvq,yqn->kvyn",
        hidden_output_gradient,
        hidden_output_blocks,
        preferred_element_type=jnp.float32,
    )
    (pre_grad_full,) = unit_act_back(act_grad)
    hidden_preactivation_gradient = pre_grad_full.astype(jnp.bfloat16)
    unit_in_blocks_grad = jnp.einsum(
        "gmt,gmox->otx",
        second_normed_reduced,
        hidden_preactivation_gradient,
        preferred_element_type=jnp.float32,
    )
    normed_two_part = jnp.einsum(
        "qyjk,jzk->qyz",
        hidden_preactivation_gradient,
        hidden_input_blocks,
        preferred_element_type=jnp.float32,
    )
    return (unit_in_blocks_grad, unit_out_blocks_grad, normed_two_part)


def body(
    mel_frames,
    text_features,
    cotangent,
    time_embedding,
    lengths,
    group_ids,
    text_keep,
    owner_list,
    soap_master,
    soap_first,
    soap_second,
    left_basis,
    right_basis,
    text_matrices,
    text_first,
    text_second,
    modulation_weight,
    modulation_first,
    modulation_second,
    vectors,
    vector_first,
    vector_second,
):
    sequences = lengths.shape[0]
    dp_count = lax.axis_size("dp")
    utterance_count = sequences * dp_count
    panel_rows = soap_master.shape[0]
    local_width = soap_master.shape[1]
    local_heads = local_width // HEAD
    share_rows = modulation_weight.shape[0]
    silu_time = jax.nn.silu(time_embedding.astype(jnp.float32)).astype(jnp.bfloat16)
    time_rows = lax.dynamic_slice_in_dim(
        silu_time, lax.axis_index("dp") * share_rows, share_rows, 1
    )
    modulation_low = modulation_weight.astype(jnp.bfloat16)
    panels_all, texts_all, modulation_all = (
        lax.all_gather(soap_master.astype(jnp.bfloat16), "dp", axis=0, tiled=True),
        lax.all_gather(text_matrices.astype(jnp.bfloat16), "dp", axis=0, tiled=True),
        lax.all_gather(modulation_low, "dp", axis=0, tiled=True),
    )
    modulation_pre = jnp.dot(silu_time, modulation_all, preferred_element_type=jnp.float32)
    (
        kernel,
        conv_bias,
        norm_gain,
        norm_bias,
        out_bias,
        in_bias,
        grn_gamma,
        grn_beta,
        modulation_bias,
    ) = vector_parts(vectors)
    group_table = (group_ids[:, None] == jnp.arange(GROUPS)[None, :]).astype(jnp.float32)
    modulation_rows = jnp.dot(group_table, modulation_pre + modulation_bias, precision=precise)
    modulation_parts = [
        modulation_rows[:, None, part_index * D : (part_index + 1) * D] for part_index in range(6)
    ]
    shift_one, scale_one, gate_one, shift_two, scale_two, gate_two = modulation_parts
    slot_blocks = panels_all.reshape(dp_count, panel_rows, local_width)
    stacked = jnp.take(slot_blocks, owner_list, axis=0).reshape(8, D, local_width)
    expand_weight = texts_all[0:TEXT]
    shrink_rows = texts_all[TEXT : 2 * TEXT]
    text_to_model = texts_all[2 * TEXT : 3 * TEXT]
    keep_rows = text_keep.reshape(sequences, LEN, 1).astype(jnp.float32)
    masked_text = text_features.astype(jnp.float32).reshape(sequences, LEN, TEXT) * keep_rows
    normed_text, text_norm_back = jax.vjp(
        text_norm, masked_text, kernel, conv_bias, norm_gain, norm_bias
    )
    normed_low = normed_text.astype(jnp.bfloat16)
    expand_pre = jnp.dot(normed_low, expand_weight, preferred_element_type=jnp.float32) + in_bias
    grn_out, grn_back = jax.vjp(gelu_grn, expand_pre, grn_gamma, grn_beta)
    grn_low = grn_out.astype(jnp.bfloat16)
    shrink_out = contract_last(grn_low, shrink_rows) + out_bias
    text_out = (masked_text + shrink_out) * keep_rows
    text_reduced = text_out.astype(jnp.bfloat16)
    stream = mel_frames.astype(jnp.float32).reshape(sequences, LEN, D) + jnp.dot(
        text_reduced, text_to_model, preferred_element_type=jnp.float32
    )
    normed_one, norm_one_back = jax.vjp(modulated, stream, shift_one, scale_one)
    first_normed_reduced = normed_one.astype(jnp.bfloat16)
    query_weight = stacked[0]
    key_weight = stacked[1]
    value_weight = stacked[2]
    out_weight = stacked[3]
    hidden_input_blocks = stacked[4:6]
    hidden_output_blocks = stacked[6:8]
    head_shape = (sequences, LEN, local_heads, HEAD)
    cosine_table, sine_table = rotary_tables()
    queries = jnp.dot(
        first_normed_reduced, query_weight, preferred_element_type=jnp.float32
    ).reshape(head_shape)
    key_rows = jnp.dot(
        first_normed_reduced, key_weight, preferred_element_type=jnp.float32
    ).reshape(head_shape)
    query_rot = rotary(queries, cosine_table, sine_table).astype(jnp.bfloat16)
    key_rot = rotary(key_rows, cosine_table, sine_table).astype(jnp.bfloat16)
    value_rows = (
        jnp.dot(first_normed_reduced, value_weight, preferred_element_type=jnp.float32)
        .astype(jnp.bfloat16)
        .reshape(head_shape)
    )
    live_keys = jnp.arange(LEN)[None, :] < lengths[:, None]
    attended, lse_rows = attend_forward(query_rot, key_rot, value_rows, live_keys)
    attended_reduced = attended.astype(jnp.bfloat16).reshape(sequences, LEN, local_width)
    head_part = contract_last(attended_reduced, out_weight)
    out_grad = cotangent.astype(jnp.float32).reshape(sequences, LEN, D)
    hidden_output_gradient = (gate_two * out_grad).astype(jnp.bfloat16)
    attention_out = lax.psum(head_part, "mp")
    stream_one = stream + gate_one * attention_out
    normed_two, norm_two_back = jax.vjp(modulated, stream_one, shift_two, scale_two)
    second_normed_reduced = normed_two.astype(jnp.bfloat16)
    hidden_unit_reduced, unit_act_back, unit_part = unit_forward(
        second_normed_reduced, hidden_input_blocks, hidden_output_blocks
    )
    unit_out = lax.psum(unit_part, "mp")
    final_stream = stream_one + gate_two * unit_out
    block_output = final_stream.astype(jnp.bfloat16).reshape(-1, D)
    gate_two_grad = jnp.sum(out_grad * unit_out, axis=1, keepdims=True)
    unit_in_blocks_grad, unit_out_blocks_grad, normed_two_part = unit_backward(
        second_normed_reduced,
        hidden_unit_reduced,
        unit_act_back,
        hidden_output_gradient,
        hidden_input_blocks,
        hidden_output_blocks,
    )
    normed_two_grad = lax.psum(normed_two_part, "mp")
    stream_one_norm, shift_two_grad, scale_two_grad = norm_two_back(normed_two_grad)
    stream_one_grad = out_grad + stream_one_norm
    gate_one_grad = jnp.sum(stream_one_grad * attention_out, axis=1, keepdims=True)
    attention_gradient = (gate_one * stream_one_grad).astype(jnp.bfloat16)
    out_weight_grad = jnp.einsum(
        "kfo,kfv->ov", attention_gradient, attended_reduced, preferred_element_type=jnp.float32
    )
    attended_grad = (
        jnp.dot(attention_gradient, out_weight, preferred_element_type=jnp.float32)
        .astype(jnp.bfloat16)
        .reshape(head_shape)
    )
    query_rot_grad, key_rot_grad, value_grad = attend_backward(
        query_rot, key_rot, value_rows, attended_grad, lse_rows, live_keys
    )
    query_gradient = (
        rotary(query_rot_grad, cosine_table, -sine_table)
        .astype(jnp.bfloat16)
        .reshape(sequences, LEN, local_width)
    )
    key_gradient = (
        rotary(key_rot_grad, cosine_table, -sine_table)
        .astype(jnp.bfloat16)
        .reshape(sequences, LEN, local_width)
    )
    value_reduced_gradient = value_grad.astype(jnp.bfloat16).reshape(sequences, LEN, local_width)
    query_weight_grad = jnp.einsum(
        "kfo,kfv->ov", first_normed_reduced, query_gradient, preferred_element_type=jnp.float32
    )
    key_weight_grad = jnp.einsum(
        "kfo,kfv->ov", first_normed_reduced, key_gradient, preferred_element_type=jnp.float32
    )
    value_weight_grad = jnp.einsum(
        "kfo,kfv->ov",
        first_normed_reduced,
        value_reduced_gradient,
        preferred_element_type=jnp.float32,
    )
    normed_one_part = (
        contract_last(query_gradient, query_weight)
        + contract_last(key_gradient, key_weight)
        + contract_last(value_reduced_gradient, value_weight)
    )
    head_grads, normed_one_part = (
        (query_weight_grad, key_weight_grad, value_weight_grad, out_weight_grad),
        normed_one_part,
    )
    normed_one_grad = lax.psum(normed_one_part, "mp")
    stream_norm_grad, shift_one_grad, scale_one_grad = norm_one_back(normed_one_grad)
    mel_gradient = (stream_one_grad + stream_norm_grad).reshape(-1, D)
    share_factor = 0.5
    query_weight_grad, key_weight_grad, value_weight_grad, out_weight_grad = head_grads
    residual_reduced_gradient = mel_gradient.reshape(sequences, LEN, D).astype(jnp.bfloat16)
    text_to_model_grad = jnp.einsum(
        "ecm,ecy->my", text_reduced, residual_reduced_gradient, preferred_element_type=jnp.float32
    )
    text_out_grad = contract_last(residual_reduced_gradient, text_to_model)
    shrink_grad = text_out_grad * keep_rows
    out_bias_grad = jnp.sum(shrink_grad, axis=(0, 1))
    shrink_low_grad = shrink_grad.astype(jnp.bfloat16)
    shrink_rows_grad = jnp.einsum(
        "slt,slc->tc", shrink_low_grad, grn_low, preferred_element_type=jnp.float32
    )
    grn_grad = jnp.dot(shrink_low_grad, shrink_rows, preferred_element_type=jnp.float32)
    expand_pre_grad, gamma_grad, beta_grad = grn_back(grn_grad)
    in_bias_grad = jnp.sum(expand_pre_grad, axis=(0, 1))
    expand_low_grad = expand_pre_grad.astype(jnp.bfloat16)
    expand_weight_grad = jnp.einsum(
        "slt,slc->tc", normed_low, expand_low_grad, preferred_element_type=jnp.float32
    )
    normed_text_grad = contract_last(expand_low_grad, expand_weight)
    masked_grad, kernel_grad, conv_bias_grad, gain_grad, norm_bias_grad = text_norm_back(
        normed_text_grad
    )
    text_gradient = ((masked_grad + shrink_grad) * keep_rows).reshape(-1, TEXT)
    modulation_token = jnp.concatenate(
        [
            shift_one_grad,
            scale_one_grad,
            gate_one_grad,
            shift_two_grad,
            scale_two_grad,
            gate_two_grad,
        ],
        axis=2,
    )[:, 0, :]
    modulation_local = jnp.dot(group_table.T, modulation_token, precision=precise) * share_factor
    text_vector_grad = (
        jnp.concatenate(
            [
                kernel_grad.reshape(-1),
                conv_bias_grad,
                gain_grad,
                norm_bias_grad,
                out_bias_grad,
                in_bias_grad,
                gamma_grad,
                beta_grad,
            ]
        )
        * 0.5
    )
    vector_sum, modulation_grad = lax.psum((text_vector_grad, modulation_local), ("dp", "mp"))
    vector_gradient = (
        jnp.concatenate([vector_sum, jnp.sum(modulation_grad, axis=0)]) / utterance_count
    )
    share_grad = (
        jnp.dot(
            time_rows.T, modulation_grad.astype(jnp.bfloat16), preferred_element_type=jnp.float32
        )
        / utterance_count
    )
    panel_grad = jnp.stack(
        [
            query_weight_grad,
            key_weight_grad,
            value_weight_grad,
            out_weight_grad,
            unit_in_blocks_grad[0],
            unit_in_blocks_grad[1],
            unit_out_blocks_grad[0],
            unit_out_blocks_grad[1],
        ]
    )
    panel_grad = panel_grad.reshape(dp_count, panel_rows, local_width)
    slot_index = jnp.arange(dp_count)
    inverse = jnp.sum(
        jnp.where(owner_list[None, :] == slot_index[:, None], slot_index[None, :], 0), axis=1
    )
    slot_grad = jnp.take(panel_grad, inverse, axis=0).reshape(-1, local_width)
    text_grad_rows = jnp.concatenate(
        [expand_weight_grad, shrink_rows_grad, text_to_model_grad], axis=0
    )
    own_panel, own_text = (
        lax.psum_scatter(slot_grad, "dp", scatter_dimension=0, tiled=True),
        lax.psum_scatter(text_grad_rows, "dp", scatter_dimension=0, tiled=True),
    )
    own_panel = own_panel / utterance_count
    own_text = own_text / utterance_count
    rotated = jnp.dot(
        jnp.dot(left_basis.T, own_panel, precision=precise), right_basis, precision=precise
    )
    soap_moment, soap_variance, soap_direction = moments(rotated, soap_first, soap_second)
    turned_back = jnp.dot(
        jnp.dot(left_basis, soap_direction, precision=precise), right_basis.T, precision=precise
    )
    soap_weights = apply_step(soap_master, turned_back, learn_rate)
    text_moment, text_variance, text_direction = moments(own_text, text_first, text_second)
    text_weights = apply_step(text_matrices, text_direction, learn_rate)
    modulation_moment, modulation_variance, modulation_direction = moments(
        share_grad, modulation_first, modulation_second
    )
    modulation_weights = apply_step(modulation_weight, modulation_direction, learn_rate)
    vector_moment, vector_variance, vector_direction = moments(
        vector_gradient, vector_first, vector_second
    )
    vector_weights = apply_step(vectors, vector_direction, vector_rate)
    return (
        block_output,
        mel_gradient,
        text_gradient,
        soap_weights,
        soap_moment,
        soap_variance,
        text_weights,
        text_moment,
        text_variance,
        modulation_weights,
        modulation_moment,
        modulation_variance,
        vector_weights,
        vector_moment,
        vector_variance,
    )


def solution(mesh):
    return jax.shard_map(
        body,
        mesh=mesh,
        in_specs=(
            P("dp", None),
            P("dp", None),
            P("dp", None),
            P(),
            P("dp"),
            P("dp"),
            P("dp"),
            P(),
            P("dp", "mp"),
            P("dp", "mp"),
            P("dp", "mp"),
            P("dp", "mp"),
            P("dp", "mp"),
            P("dp", None),
            P("dp", None),
            P("dp", None),
            P("dp", None),
            P("dp", None),
            P("dp", None),
            P(),
            P(),
            P(),
        ),
        out_specs=(
            P("dp", None),
            P("dp", None),
            P("dp", None),
            P("dp", "mp"),
            P("dp", "mp"),
            P("dp", "mp"),
            P("dp", None),
            P("dp", None),
            P("dp", None),
            P("dp", None),
            P("dp", None),
            P("dp", None),
            P(),
            P(),
            P(),
        ),
        check_vma=False,
    )
```

profile of v0, /device:TPU:0, one launch (start us, length us, event | category | flops | bytes accessed | tf_op | source)
XLA Modules:
  0.0 1304.4 jit_solution(1284611934506183921)
XLA Ops:
  13.8 3.9 copy.84
  21.2 3.6 fusion.159
  26.7 55.6 %all-gather.4.cloned.1.call-done = bf16[1536,1024]{1,0:T(8,128)(2,1)} async-done(((bf16[96,1024]{1,0:T(8,128)(2,1)}), bf16[1536,1024]{1,0:T(8,128)(2,1)}) %all-gather.4.cloned.1.call-update) | async-done | bytes 3145744 | tf_op jit(solution)/shard_map/all_gather | solution.py:277
  82.3 13.6 %multiply_reduce_fusion.8 = (f32[1024]{0:T(1024)S(1)}, f32[1024,1024]{1,0:T(8,128)}, f32[1024,1024]{1,0:T(8,128)}, f32[1024,1024]{1,0:T(8,128)}) fusion(f32[1024]{0:T(1024)S(1)} %get-tuple-element.532, bf16[1536,1024]{1,0:T(8,128)(2,1)} %all-gather.4.cloned.1.call-done, f32[1,1024,512]{2,1,0:T(8,128)S(1)} %get-tuple-element.494, ...), kind=kOutput, calls=%fused_computation.98 | convolution fusion | flops 1146616832 | bytes 15749120 | tf_op jit(solution)/shard_map/dot_general | solution.py:309
  97.2 4.4 multiply_convert_fusion.3
  101.7 5.0 fusion.166
  109.4 87.6 %all-gather.8.cloned.1.call-done = bf16[8192,512]{1,0:T(8,128)(2,1)} async-done(((bf16[512,512]{1,0:T(8,128)(2,1)}), bf16[8192,512]{1,0:T(8,128)(2,1)}) %all-gather.8.cloned.1.call-update) | async-done | bytes 8388624 | tf_op jit(solution)/shard_map/all_gather | solution.py:276
  197.0 8.2 gather_fusion
  205.2 8.3 broadcast_select_fusion
  213.5 3.9 fusion.162
  220.5 130.0 %all-gather.6.cloned.1.call-done = bf16[1024,6144]{1,0:T(8,128)(2,1)} async-done(((bf16[64,6144]{1,0:T(8,128)(2,1)}), bf16[1024,6144]{1,0:T(8,128)(2,1)}) %all-gather.6.cloned.1.call-update) | async-done | bytes 12582928 | tf_op jit(solution)/shard_map/all_gather | solution.py:278
  350.6 6.3 convolution_add_fusion
  366.8 27.0 %while.34 = (s32[]{:T(128)}, bf16[1,1024,8,64]{1,3,2,0:T(8,128)(2,1)}, f32[1,8,1024]{2,1,0:T(8,128)S(1)}, bf16[1,1024,8,64]{1,3,2,0:T(8,128)(2,1)}, bf16[1,1024,...) while((s32[]{:T(128)}, ...), condition=%wide.region_9.10_spmd.clone, body=%wide.region_6.9_spmd.clone.sunk | while | flops 1119876096 | bytes 66720000 | solution.py:134
  367.4 3.6 fusion.223
  371.0 4.0 exponential_reduce_fusion.2
  375.0 4.1 fusion.224
  380.7 3.6 fusion.223
  384.3 4.0 exponential_reduce_fusion.2
  388.4 4.1 fusion.224
  393.8 4.8 convolution_bitcast_fusion
  398.6 4.0 copy.92
  402.6 4.7 fusion.161
  407.3 18.0 %all-reduce.21.cloned.1.call-done = f32[1,1024,1024]{1,2,0:T(8,128)} async-done(((f32[1,1024,1024]{1,2,0:T(8,128)}), f32[1,1024,1024]{1,2,0:T(8,128)}) %all-reduce.21.cloned.1.call-update) | async-done | bytes 4194320 | tf_op jit(solution)/shard_map/psum | solution.py:347
  425.3 4.0 fusion.157
  435.3 5.0 fusion.49
  441.7 4.4 convolution_bitcast_fusion.1
  446.3 7.4 convolution_bitcast_fusion.2
  453.7 22.1 %all-reduce.23.cloned.1.call-done = f32[1,1024,1024]{1,2,0:T(8,128)} async-done(((f32[1,1024,1024]{1,2,0:T(8,128)}), f32[1,1024,1024]{1,2,0:T(8,128)}) %all-reduce.23.cloned.1.call-update) | async-done | bytes 4194320 | tf_op jit(solution)/shard_map/psum | solution.py:366
  475.8 4.2 multiply_reduce_fusion.5
  491.7 85.3 %while.35 = (s32[]{:T(128)}, f32[1,1024,8,64]{1,3,2,0:T(8,128)}, f32[1,1024,8,64]{1,3,2,0:T(8,128)}, f32[1,1024,8,64]{1,3,2,0:T(8,128)}, bf16[1,1024,8,64]{1,3,2...) while((s32[]{:T(128)}, f32[1,1024,8,64]{1,3,2,0:T(8,128)}, ...), condition=%wide.region_19.20_spmd.clone, body=%wide.region_17.19_spmd.clone.sunk | while | flops 2724983808 | bytes 211896608 | solution.py:175
  491.9 3.8 fusion.233
  496.3 9.8 multiply_reduce_fusion.20
  506.2 9.5 multiply_convert_fusion.10
  515.6 6.6 bitcast_add_fusion.7
  522.2 7.8 fusion.234
  533.1 3.8 fusion.233
  537.6 9.8 multiply_reduce_fusion.20
  547.4 9.5 multiply_convert_fusion.10
  556.9 7.2 bitcast_add_fusion.7
  564.1 7.8 fusion.234
  571.9 4.7 bitcast_add_fusion.8
  588.0 40.1 %all-reduce.27.cloned.1.call-done = (f32[1,1024,1024]{1,2,0:T(8,128)}, f32[1,1024,1024]{1,2,0:T(8,128)}) async-done(((f32[1,1024,1024]{1,2,0:T(8,128)}, f32[1,1024,1024]{1,2,0:T(8,128)}), (f32[1,1024,1024]{1,2,0:T(8,128)}, f32[1,1024,1024]{1,2,0:T(8,128)})) %all-reduce.27.cloned.1.call-update) | async-done | bytes 8388624 | tf_op jit(solution)/shard_map/psum | solution.py:354
  628.2 4.4 fusion.51
  647.1 3.6 multiply_reduce_fusion.1
  652.0 5.6 fusion.41
  658.5 7.6 fusion.153
  673.2 4.6 bitcast_dynamic-update-slice_fusion.6
  687.4 4.9 bitcast_dynamic-update-slice_fusion.2
  692.4 4.8 bitcast_dynamic-update-slice_fusion.1
  697.2 16.7 %copy.105 = f32[8,1024,512]{2,1,0:T(8,128)} copy(f32[8,1024,512]{1,2,0:T(8,128)} %bitcast_dynamic-update-slice_fusion.1) | data formatting | bytes 33554432 | tf_op jit(solution)/shard_map/stack | solution.py:479
  713.9 14.0 %gather_fusion.1 = f32[16,512,512]{2,1,0:T(8,128)} fusion(f32[16,512,512]{2,1,0:T(8,128)} %bitcast.323, s32[1024]{0:T(1024)S(1)} %pad_clamp_fusion), kind=kCustom, calls=%fused_computation.1 | custom fusion | bytes 33554496 | tf_op jit(solution)/shard_map/jit(_take)/gather | solution.py:496
  727.9 11.5 bitcast_select_fusion
  740.1 4.7 fusion.65
  750.1 6.8 multiply_reduce_fusion.15
  756.9 5.4 copy.107
  762.3 4.1 copy.106
  766.5 40.8 %psum.47 = f32[8704]{0:T(1024)S(1)} all-reduce(f32[8704]{0:T(1024)S(1)} %broadcast_multiply_fusion.7), channel_id=1, replica_groups=mesh['dp'=16,'mp'=2] {'dp','mp'}, use_global_device_ids=true, to_apply=%region_51.52 | all-reduce | flops 8704 | bytes 69632 | tf_op jit(solution)/shard_map/psum | solution.py:469
  807.3 8.0 fusion.64
  817.1 6.3 multiply_subtract_fusion
  823.4 111.2 %reduce-scatter.5.cloned.1.call-done = f32[96,1024]{1,0:T(8,128)} async-done(((f32[1536,1024]{1,0:T(8,128)}), f32[96,1024]{1,0:T(8,128)}) %reduce-scatter.5.cloned.1.call-update) | async-done | bytes 393232 | tf_op jit(solution)/shard_map/reduce_scatter | solution.py:502
  937.0 345.5 %reduce-scatter.3.cloned.1.call-done = f32[512,512]{1,0:T(8,128)} async-done(((f32[8192,512]{1,0:T(8,128)}), f32[512,512]{1,0:T(8,128)}) %reduce-scatter.3.cloned.1.call-update) | async-done | bytes 1048592 | tf_op jit(solution)/shard_map/reduce_scatter | solution.py:501
  1285.6 3.4 multiply_add_fusion.3
  1289.1 3.9 fusion.93
  1293.0 4.5 fusion.88
  (411 shorter events, 110.3 us)
Async XLA Ops:
  7.2 1278.4 %copy-start = (f32[512,512]{1,0:T(8,128)S(1)}, f32[512,512]{1,0:T(8,128)}, u32[]{:S(2)}) copy-start(f32[512,512]{1,0:T(8,128)} %param.38) | copy-start | bytes 3145732
  7.2 6.6 copy-start.127
  7.2 75.1 %all-gather.4.cloned.1.call-start = ((), (), s32[]{:S(2)}) async-start(), calls=%async_computation.2 | async-start | bytes 3342336 | tf_op jit(solution)/shard_map/all_gather | solution.py:277
  9.1 187.9 %all-gather.8.cloned.1.call-start = ((), (), s32[]{:S(2)}) async-start(), calls=%async_computation.4 | async-start | bytes 8912896 | tf_op jit(solution)/shard_map/all_gather | solution.py:276
  11.2 7.2 copy-start.66
  11.2 7.3 copy-start.130
  11.2 8.4 copy-start.24
  11.2 339.3 %all-gather.6.cloned.1.call-start = ((), (), s32[]{:S(2)}) async-start(), calls=%async_computation.3 | async-start | bytes 13369344 | tf_op jit(solution)/shard_map/all_gather | solution.py:278
  13.7 411.6 %all-reduce.21.cloned.1.call-start = ((), (), s32[]{:S(2)}) async-start(), calls=%async_computation.5 | async-start | bytes 8388608 | tf_op jit(solution)/shard_map/psum | solution.py:347
  13.8 83.4 %copy-start.63 = (f32[1024]{0:T(1024)}, f32[1024]{0:T(1024)S(1)}, u32[]{:S(2)}) copy-start(f32[1024]{0:T(1024)S(1)} %convert_element_type.189) | copy-start | bytes 12292
  19.7 62.6 %copy-start.123 = (f32[512]{0:T(512)}, f32[512]{0:T(512)S(1)}, u32[]{:S(2)}) copy-start(f32[512]{0:T(512)S(1)} %get-tuple-element.533) | copy-start | bytes 6148
  19.7 62.6 %copy-start.128 = (f32[512]{0:T(512)}, f32[512]{0:T(512)S(1)}, u32[]{:S(2)}) copy-start(f32[512]{0:T(512)S(1)} %get-tuple-element.535) | copy-start | bytes 6148
  24.9 70.9 %copy-start.11 = (f32[1,1024,512]{2,1,0:T(8,128)}, f32[1,1024,512]{2,1,0:T(8,128)S(1)}, u32[]{:S(2)}) copy-start(f32[1,1024,512]{2,1,0:T(8,128)S(1)} %get-tuple-element.494) | copy-start | bytes 6291460
  25.0 70.9 %copy-start.92 = (f32[1024]{0:T(1024)}, f32[1024]{0:T(1024)S(1)}, u32[]{:S(2)}) copy-start(f32[1024]{0:T(1024)S(1)} %broadcast_multiply_fusion.10) | copy-start | bytes 12292
  25.4 70.5 %copy-start.90 = (f32[1024]{0:T(1024)}, f32[1024]{0:T(1024)S(1)}, u32[]{:S(2)}) copy-start(f32[1024]{0:T(1024)S(1)} %multiply_reduce_fusion.16) | copy-start | bytes 12292
  25.4 70.5 %copy-start.117 = (f32[1024]{0:T(1024)}, f32[1024]{0:T(1024)S(1)}, u32[]{:S(2)}) copy-start(f32[1024]{0:T(1024)S(1)} %get-tuple-element.532) | copy-start | bytes 12292
  25.4 70.5 %copy-start.121 = (f32[1024]{0:T(1024)}, f32[1024]{0:T(1024)S(1)}, u32[]{:S(2)}) copy-start(f32[1024]{0:T(1024)S(1)} %get-tuple-element.560) | copy-start | bytes 12292
  25.4 71.8 %copy-start.88 = (f32[1024]{0:T(1024)}, f32[1024]{0:T(1024)S(1)}, u32[]{:S(2)}) copy-start(f32[1024]{0:T(1024)S(1)} %get-tuple-element.530) | copy-start | bytes 12292
  25.5 71.8 %copy-start.119 = (f32[1024]{0:T(1024)}, f32[1024]{0:T(1024)S(1)}, u32[]{:S(2)}) copy-start(f32[1024]{0:T(1024)S(1)} %get-tuple-element.531) | copy-start | bytes 12292
  26.7 338.3 %copy-start.45 = (f32[1024,32]{0,1:T(8,128)}, f32[1024,32]{0,1:T(8,128)S(1)}, u32[]{:S(2)}) copy-start(f32[1024,32]{0,1:T(8,128)S(1)} %get-tuple-element.552) | copy-start | bytes 393220
  106.7 250.5 %copy-start.68 = (f32[1024]{0:T(1024)}, f32[1024]{0:T(1024)S(1)}, u32[]{:S(2)}) copy-start(f32[1024]{0:T(1024)S(1)} %broadcast_multiply_fusion.9) | copy-start | bytes 12292
  109.4 95.8 %copy-start.94 = (f32[1024]{0:T(1024)}, f32[1024]{0:T(1024)S(1)}, u32[]{:S(2)}) copy-start(f32[1024]{0:T(1024)S(1)} %multiply_reduce_fusion.7) | copy-start | bytes 12292
  109.4 247.8 %copy-start.76 = (f32[1024]{0:T(1024)}, f32[1024]{0:T(1024)S(1)}, u32[]{:S(2)}) copy-start(f32[1024]{0:T(1024)S(1)} %fusion.128) | copy-start | bytes 12292
  217.4 139.5 %copy-start.26 = (bf16[2,512,512]{2,1,0:T(8,128)(2,1)}, bf16[2,512,512]{2,1,0:T(8,128)(2,1)S(1)}, u32[]{:S(2)}) copy-start(bf16[2,512,512]{2,1,0:T(8,128)(2,1)S(1)} %get-tuple-element.505) | copy-start | bytes 3145732
  217.4 139.5 %copy-start.34 = (bf16[2,512,512]{2,1,0:T(8,128)(2,1)}, bf16[2,512,512]{2,1,0:T(8,128)(2,1)S(1)}, u32[]{:S(2)}) copy-start(bf16[2,512,512]{2,1,0:T(8,128)(2,1)S(1)} %get-tuple-element.506) | copy-start | bytes 3145732
  217.4 133.2 %copy-start.72 = (bf16[8,1024]{1,0:T(8,128)(2,1)S(1)}, bf16[8,1024]{1,0:T(8,128)(2,1)}, u32[]{:S(2)}) copy-start(bf16[8,1024]{1,0:T(8,128)(2,1)} %param.29) | copy-start | bytes 49156
  357.1 72.8 %copy-start.125 = (f32[1,1024]{1,0:T(1,128)}, f32[1,1024]{1,0:T(1,128)S(1)}, u32[]{:S(2)}) copy-start(f32[1,1024]{1,0:T(1,128)S(1)} %get-tuple-element.549) | copy-start | bytes 12292
  357.2 78.1 %copy-start.110 = (f32[1,1024]{1,0:T(1,128)}, f32[1,1024]{1,0:T(1,128)S(1)}, u32[]{:S(2)}) copy-start(f32[1,1024]{1,0:T(1,128)S(1)} %get-tuple-element.544) | copy-start | bytes 12292
  357.2 127.5 %copy-start.78 = (f32[1,1024]{1,0:T(1,128)}, f32[1,1024]{1,0:T(1,128)S(1)}, u32[]{:S(2)}) copy-start(f32[1,1024]{1,0:T(1,128)S(1)} %get-tuple-element.545) | copy-start | bytes 12292
  357.2 130.6 %copy-start.112 = (f32[1,1024]{1,0:T(1,128)}, f32[1,1024]{1,0:T(1,128)S(1)}, u32[]{:S(2)}) copy-start(f32[1,1024]{1,0:T(1,128)S(1)} %get-tuple-element.548) | copy-start | bytes 12292
  398.6 77.2 %all-reduce.23.cloned.1.call-start = ((), (), s32[]{:S(2)}) async-start(), calls=%async_computation.6 | async-start | bytes 8388608 | tf_op jit(solution)/shard_map/psum | solution.py:366
  429.4 5.9 copy-start.2
  429.4 55.2 %copy-start.70 = (f32[1024]{0:T(1024)}, f32[1024]{0:T(1024)S(1)}, u32[]{:S(2)}) copy-start(f32[1024]{0:T(1024)S(1)} %broadcast_multiply_fusion.8) | copy-start | bytes 12292
  429.9 54.8 %copy-start.86 = (f32[1024]{0:T(1024)}, f32[1024]{0:T(1024)S(1)}, u32[]{:S(2)}) copy-start(f32[1024]{0:T(1024)S(1)} %fusion.129) | copy-start | bytes 12292
  446.1 182.1 %all-reduce.27.cloned.1.call-start = ((), (), s32[]{:S(2)}) async-start(), calls=%async_computation.10 | async-start | bytes 16777216 | tf_op jit(solution)/shard_map/psum | solution.py:354
  491.7 85.3 %copy-start.46 = (f32[1024,32]{0,1:T(8,128)S(1)}, f32[1024,32]{0,1:T(8,128)}, u32[]{:S(2)}) copy-start(f32[1024,32]{0,1:T(8,128)} %copy-done.45) | copy-start | bytes 393220
  491.7 85.3 %copy-start.62 = (f32[1024,32]{0,1:T(8,128)S(1)}, f32[1024,32]{0,1:T(8,128)}, u32[]{:S(2)}) copy-start(f32[1024,32]{0,1:T(8,128)} %get-tuple-element.550) | copy-start | bytes 393220
  515.6 14.4 %copy-start.1 = (f32[8,512,1024]{2,1,0:T(8,128)S(1)}, f32[8,512,1024]{2,1,0:T(8,128)}, u32[]{:S(2)}) copy-start(f32[8,512,1024]{2,1,0:T(8,128)} %get-tuple-element.677) | copy-start | bytes 50331652 | tf_op jit(solution)/shard_map/while
  522.2 7.8 copy-start.8
  556.9 15.0 %copy-start.1 = (f32[8,512,1024]{2,1,0:T(8,128)S(1)}, f32[8,512,1024]{2,1,0:T(8,128)}, u32[]{:S(2)}) copy-start(f32[8,512,1024]{2,1,0:T(8,128)} %get-tuple-element.677) | copy-start | bytes 50331652 | tf_op jit(solution)/shard_map/while
  564.1 7.8 copy-start.8
  587.9 40.3 %copy-start.69 = (f32[1024]{0:T(1024)S(1)}, f32[1024]{0:T(1024)}, u32[]{:S(2)}) copy-start(f32[1024]{0:T(1024)} %copy-done.68) | copy-start | bytes 12292
  587.9 40.3 %copy-start.75 = (f32[1,1024]{1,0:T(1,128)S(1)}, f32[1,1024]{1,0:T(1,128)}, u32[]{:S(2)}) copy-start(f32[1,1024]{1,0:T(1,128)} %copy-done.74) | copy-start | bytes 12292
  587.9 40.3 %copy-start.77 = (f32[1024]{0:T(1024)S(1)}, f32[1024]{0:T(1024)}, u32[]{:S(2)}) copy-start(f32[1024]{0:T(1024)} %copy-done.76) | copy-start | bytes 12292
  587.9 227.4 %all-reduce.25.cloned.1.call-start = ((), (), s32[]{:S(2)}) async-start(), calls=%async_computation.9 | async-start | bytes 393216 | tf_op jit(solution)/shard_map/psum | solution.py:469
  652.0 6.5 copy-start.118
  658.4 276.1 %reduce-scatter.5.cloned.1.call-start = ((), (), s32[]{:S(2)}) async-start(), calls=%async_computation.8 | async-start | bytes 6684672 | tf_op jit(solution)/shard_map/reduce_scatter | solution.py:502
  658.5 7.6 copy-start.12
  658.5 7.6 copy-start.93
  658.5 7.6 copy-start.122
  658.5 7.6 copy-start.124
  658.5 7.6 copy-start.129
  672.3 610.1 %reduce-scatter.3.cloned.1.call-start = ((), (), s32[]{:S(2)}) async-start(), calls=%async_computation.7 | async-start | bytes 17825792 | tf_op jit(solution)/shard_map/reduce_scatter | solution.py:501
  740.1 6.7 copy-start.91
  762.3 45.0 %copy-start.29 = (f32[1024,512]{1,0:T(8,128)S(1)}, f32[1024,512]{1,0:T(8,128)}, u32[]{:S(2)}) copy-start(f32[1024,512]{1,0:T(8,128)} %copy-done.28) | copy-start | bytes 6291460
  807.2 9.1 copy-start.67
  807.3 9.1 copy-start.82
  807.3 9.1 copy-start.83
  817.1 117.5 %copy-start.44 = (f32[96,1024]{1,0:T(8,128)S(1)}, f32[96,1024]{1,0:T(8,128)}, u32[]{:S(2)}) copy-start(f32[96,1024]{1,0:T(8,128)} %param.39) | copy-start | bytes 1179652
  817.1 465.4 %copy-start.47 = (f32[512,512]{1,0:T(8,128)S(1)}, f32[512,512]{1,0:T(8,128)}, u32[]{:S(2)}) copy-start(f32[512,512]{1,0:T(8,128)} %param.37) | copy-start | bytes 3145732
  823.4 462.2 %copy-start.56 = (f32[512,512]{1,0:T(8,128)S(1)}, f32[512,512]{1,0:T(8,128)}, u32[]{:S(2)}) copy-start(f32[512,512]{1,0:T(8,128)} %param.35) | copy-start | bytes 3145732
  1285.6 7.4 copy-start.33
  1289.0 8.4 copy-start.57
  1289.0 8.4 copy-start.58
  (86 other events, 306.9 us)
Sparse Core Ops, SparseCore 0:
  11.4 70.8 all-gather.3
  85.6 111.3 all-gather.7
  200.3 150.1 all-gather.5
  398.7 26.5 all-reduce.20
  446.2 29.5 all-reduce.22
  588.1 40.0 all-reduce.26
  658.6 124.2 all-reduce.24
  788.1 146.4 reduce-scatter.4
  936.8 345.5 reduce-scatter.2
where the time goes:
time: 1320 us; the launch traced here: 1300 us
  waiting for transfers between devices  810 us (61%)
  matrix products  207 us (16%)
  other arithmetic  141 us (11%)
  local copies, waits for them, and re-layouts  86.1 us (7%)
  blocking collectives  40.8 us (3%)
  between operations  18.1 us (1%)
    reduce_scatter x1, waiting for transfers between devices, body(): lax.psum_scatter(slot_grad, 'dp', scatter_dimension=0, tiled=True)  345 us
    all_gather x1, waiting for transfers between devices, body(): lax.all_gather(modulation_low, 'dp', axis=0, tiled=True)  130 us
    reduce_scatter x1, waiting for transfers between devices, body(): lax.psum_scatter(text_grad_rows, 'dp', scatter_dimension=0, tiled=True)  111 us
    all_gather x1, waiting for transfers between devices, body(): lax.all_gather(soap_master.astype(jnp.bfloat16), 'dp', axis=0, tiled=True)  87.6 us
    all_gather x1, waiting for transfers between devices, body(): lax.all_gather(text_matrices.astype(jnp.bfloat16), 'dp', axis=0, tiled=True)  55.6 us
    psum x1, blocking collectives, body(): lax.psum((text_vector_grad, modulation_local), ('dp', 'mp'))  40.8 us
    psum x1, waiting for transfers between devices, body(): unit_out = lax.psum(unit_part, 'mp')  40.1 us
    unnamed x280, local copies, waits for them, and re-layouts  31.8 us
  transfers between devices with their start and end apart: 9, of which 8 were waited for; matrix products, arithmetic and copies ran while one was open for 16% of the time, Pallas kernels for 0%

commit v1 on v0

v1 whole, which is shorter than its diff:
```python
import jax
import jax.numpy as jnp
from jax import lax
from jax.experimental import pallas as pl
from jax.experimental.pallas import tpu as pltpu
from jax.sharding import PartitionSpec as P

D = 1024
HEAD = 64
TEXT = 512
TXT_FF = 1024
KERNEL = 7
LEN = 1024
GROUPS = 8
STEP = 10

f32 = jnp.float32
bf16 = jnp.bfloat16
beta_one = 0.9
beta_two = 0.99
adam_eps = 1e-08
weight_decay = 0.01
learn_rate = 0.03
vector_rate = 0.3
norm_eps = 1e-06
solver = lax.Precision.HIGH


def swap_core(array):
    return lax.ppermute(array, "mp", [(0, 1), (1, 0)])


def swap_bit(array, bit):
    count = lax.axis_size("dp")
    return lax.ppermute(array, "dp", [(i, i ^ (1 << bit)) for i in range(count)])


def by_core(core, mine, other, axis=0):
    return jnp.where(
        core == 0,
        jnp.concatenate([mine, other], axis=axis),
        jnp.concatenate([other, mine], axis=axis),
    )


def bit_count(count):
    return count.bit_length() - 1


def third_cuts(rows):
    step = rows // 3
    if rows >= 48:
        step = (rows + 24) // 48 * 16
    return (0, step, 2 * step, rows)


axis_orders = ((0, 1, 2), (1, 2, 0), (2, 0, 1))


def tie(*values):
    return lax.optimization_barrier(values)


def spread_step(parts, phase):
    return [
        jnp.stack([part, swap_bit(part, axis_orders[index][phase])])
        for index, part in enumerate(parts)
    ]


def spread_close(parts):
    pieces = []
    for index, part in enumerate(parts):
        order = axis_orders[index]
        held = [order[2], order[1], order[0]]
        axes = [3] + [held.index(bit) for bit in (2, 1, 0)] + [4, 5]
        pieces.append(part.transpose(axes))
    return jnp.concatenate(pieces, axis=4)


def gather_relative(block):
    count = lax.axis_size("dp")
    rows, columns = block.shape
    held = block[None]
    for bit in range(4, bit_count(count)):
        held = jnp.concatenate([held, swap_bit(held, bit)], axis=0)
    cuts = third_cuts(rows)
    split = lambda array: [array[:, cuts[i] : cuts[i + 1]] for i in range(3)]
    far = swap_bit(held, 3)
    near_parts = spread_step(split(held), 0)
    near_parts = spread_step(list(tie(*near_parts)), 1)
    tied = tie(far, *near_parts)
    far, near_parts = tied[0], list(tied[1:])
    near_parts = spread_step(near_parts, 2)
    far_parts = spread_step(split(far), 0)
    tied = tie(*near_parts, *far_parts)
    near_parts, far_parts = list(tied[:3]), list(tied[3:])
    far_parts = spread_step(far_parts, 1)
    far_parts = spread_step(list(tie(*far_parts)), 2)
    near, far = spread_close(near_parts), spread_close(far_parts)
    return jnp.stack([near, far], axis=1).reshape(count, rows, columns)


def add_low(left, right):
    return (left.astype(f32) + right.astype(f32)).astype(bf16)


def fold_step(parts, held, phase):
    folded = []
    for index, part in enumerate(parts):
        bit = axis_orders[index][phase]
        axis = 1 + held[index].index(bit)
        keep = lax.index_in_dim(part, 0, axis, keepdims=False)
        send = lax.index_in_dim(part, 1, axis, keepdims=False)
        folded.append(add_low(keep, swap_bit(send, bit)))
        held[index].remove(bit)
    return folded


def scatter_relative(full):
    count, rows, columns = full.shape
    bits = bit_count(count)
    near, far = [
        full.reshape(count // 16, 2, 2, 2, 2, rows, columns)[:, i] for i in range(2)
    ]
    cuts = third_cuts(rows)
    split = lambda array: [array[..., cuts[i] : cuts[i + 1], :] for i in range(3)]
    near_parts, far_parts = split(near), split(far)
    near_held = [[2, 1, 0] for _ in range(3)]
    far_held = [[2, 1, 0] for _ in range(3)]
    far_parts = fold_step(far_parts, far_held, 2)
    far_parts = fold_step(list(tie(*far_parts)), far_held, 1)
    far_parts = fold_step(list(tie(*far_parts)), far_held, 0)
    near_parts = fold_step(near_parts, near_held, 2)
    tied = tie(*near_parts, *far_parts)
    near_parts, far_parts = list(tied[:3]), list(tied[3:])
    far_sum = swap_bit(jnp.concatenate(far_parts, axis=-2), 3)
    near_parts = fold_step(near_parts, near_held, 1)
    near_parts = fold_step(list(tie(*near_parts)), near_held, 0)
    near_sum = jnp.concatenate(near_parts, axis=-2)
    if bits == 4:
        return near_sum[0].astype(f32) + far_sum[0].astype(f32)
    total = add_low(near_sum, far_sum)
    for bit in range(bits - 1, 3, -1):
        half = 1 << (bit - 4)
        total = total[:half].astype(f32) + swap_bit(total[half:], bit).astype(f32)
        if bit > 4:
            total = total.astype(bf16)
    return total[0]


def sum_dp(array):
    for bit in range(bit_count(lax.axis_size("dp"))):
        array = array + swap_bit(array, bit)
    return array


NT = (((1,), (1,)), ((), ()))
NN = (((1,), (0,)), ((), ()))
ROWS = 256
PAIR = 2 * HEAD
vmem_bytes = 48 * 1024 * 1024


def dot32(left, right, dims=NN):
    return lax.dot_general(left, right, dims, preferred_element_type=f32)


def three_terms(values):
    high = values.astype(bf16).astype(f32)
    rest = values - high
    middle = rest.astype(bf16).astype(f32)
    return high, middle, rest - middle


def rotate(values, cosine, sine, lane):
    partner = jnp.where(
        lane % HEAD < HEAD // 2,
        pltpu.roll(values, PAIR - HEAD // 2, 1),
        pltpu.roll(values, HEAD // 2, 1),
    )
    return values * cosine + partner * sine


def attend_kernel(q_ref, k_ref, v_ref, cos_ref, sin_ref, bias_ref, o_ref, qa_ref, kr_ref):
    lane = lax.broadcasted_iota(jnp.int32, (LEN, PAIR), 1)
    lane_rows = lax.broadcasted_iota(jnp.int32, (ROWS, PAIR), 1)
    row_index = lax.broadcasted_iota(jnp.int32, (PAIR, ROWS), 0)
    cosine, sine = cos_ref[...], sin_ref[...]
    q_turned = (rotate(q_ref[...], cosine, sine, lane).astype(bf16).astype(f32) * 0.125)
    k_turned = rotate(k_ref[...], cosine, sine, lane).astype(bf16)
    kr_ref[...] = k_turned
    k_wide = k_turned.astype(f32)
    values_t = v_ref[...].T
    bias = bias_ref[...].astype(f32)
    keys = []
    for head in range(2):
        own = lane // HEAD == head
        spare = (1 - head) * HEAD
        keys.append(
            jnp.where(
                own, k_wide, jnp.where(lane == spare, bias, 0.0)
            ).astype(bf16)
        )
        qa_ref[:, head * PAIR : (head + 1) * PAIR] = jnp.where(
            own, q_turned, jnp.where(lane == spare, 1.0, 0.0)
        ).astype(bf16)
    for block in range(LEN // ROWS):
        rows = slice(block * ROWS, (block + 1) * ROWS)
        outs = []
        extra = jnp.zeros((PAIR, ROWS), f32)
        for head in range(2):
            spare = (1 - head) * HEAD
            q_block = qa_ref[rows, head * PAIR : (head + 1) * PAIR]
            scores = dot32(keys[head], q_block, NT)
            highest = jnp.max(scores, axis=0, keepdims=True)
            weights = jnp.exp(scores - highest)
            total = jnp.sum(weights, axis=0, keepdims=True)
            out_t = dot32(values_t[head * HEAD : (head + 1) * HEAD], weights.astype(bf16))
            outs.append(out_t / total)
            for place, term in enumerate(three_terms(highest + jnp.log(total))):
                extra = jnp.where(row_index == spare + 1 + place, -term, extra)
        o_ref[rows, :] = jnp.concatenate(outs, axis=0).T.astype(bf16)
        extra_t = extra.T
        for head in range(2):
            spare = (1 - head) * HEAD
            columns = slice(head * PAIR, (head + 1) * PAIR)
            is_extra = (lane_rows > spare) & (lane_rows < spare + 4)
            qa_ref[rows, columns] = jnp.where(
                is_extra, extra_t, qa_ref[rows, columns].astype(f32)
            ).astype(bf16)


def attend_forward(queries, keys, values, cosine, sine, bias):
    width = values.shape[1]
    pairs = width // PAIR
    tall = lambda columns: pl.BlockSpec((LEN, columns), lambda pair: (0, pair))
    whole = pl.BlockSpec((LEN, PAIR), lambda pair: (0, 0))
    return pl.pallas_call(
        attend_kernel,
        grid=(pairs,),
        in_specs=[tall(PAIR), tall(PAIR), tall(PAIR), whole, whole, whole],
        out_specs=[tall(PAIR), tall(2 * PAIR), tall(PAIR)],
        out_shape=[
            jax.ShapeDtypeStruct((LEN, width), bf16),
            jax.ShapeDtypeStruct((LEN, 2 * width), bf16),
            jax.ShapeDtypeStruct((LEN, width), bf16),
        ],
        compiler_params=pltpu.CompilerParams(vmem_limit_bytes=vmem_bytes),
        cost_estimate=pl.CostEstimate(
            flops=2 * 4 * LEN * LEN * width * 4,
            bytes_accessed=10 * LEN * width * 2,
            transcendentals=LEN * LEN * width // HEAD,
        ),
        name="attend",
    )(queries, keys, values, cosine, sine, bias)


def attend_back_kernel(
    qa_ref, kr_ref, v_ref, do_ref, o_ref, cos_ref, sin_ref, bias_ref,
    dq_ref, dk_ref, dv_ref, doa_ref, dka_ref, dva_ref,
):
    lane = lax.broadcasted_iota(jnp.int32, (LEN, PAIR), 1)
    lane_rows = lax.broadcasted_iota(jnp.int32, (ROWS, PAIR), 1)
    cosine, sine = cos_ref[...], sin_ref[...]
    k_wide = kr_ref[...].astype(f32)
    keys_t = kr_ref[...].T
    v_wide = v_ref[...].astype(f32)
    do_wide = do_ref[...].astype(f32)
    bias = bias_ref[...].astype(f32)
    product = do_wide * o_ref[...].astype(f32)
    keys, values = [], []
    for head in range(2):
        own = lane // HEAD == head
        spare = (1 - head) * HEAD
        is_extra = (lane > spare) & (lane < spare + 4)
        ones = jnp.where(is_extra, 1.0, 0.0)
        keys.append(
            jnp.where(own, k_wide, jnp.where(lane == spare, bias, ones)).astype(bf16)
        )
        values.append(jnp.where(own, v_wide, ones).astype(bf16))
        row_dot = jnp.sum(jnp.where(own, product, 0.0), axis=1, keepdims=True)
        grad = jnp.where(own, do_wide, 0.0)
        for place, term in enumerate(three_terms(row_dot)):
            grad = jnp.where(lane == spare + 1 + place, -term, grad)
        doa_ref[:, head * PAIR : (head + 1) * PAIR] = grad.astype(bf16)
    for block in range(LEN // ROWS):
        rows = slice(block * ROWS, (block + 1) * ROWS)
        turned = []
        for head in range(2):
            columns = slice(head * PAIR, (head + 1) * PAIR)
            q_block = qa_ref[rows, columns]
            do_block = doa_ref[rows, columns]
            probs = jnp.exp(dot32(keys[head], q_block, NT))
            prob_grad = dot32(values[head], do_block, NT)
            score_grad = (probs * prob_grad).astype(bf16)
            dv_part = dot32(probs.astype(bf16), do_block)
            dk_part = dot32(score_grad, q_block)
            if block == 0:
                dva_ref[:, columns] = dv_part
                dka_ref[:, columns] = dk_part
            else:
                dva_ref[:, columns] += dv_part
                dka_ref[:, columns] += dk_part
            turned.append(dot32(keys_t[head * HEAD : (head + 1) * HEAD], score_grad))
        dq = jnp.concatenate(turned, axis=0).T * 0.125
        dq_ref[rows, :] = rotate(dq, cosine[rows], -sine[rows], lane_rows).astype(bf16)
    first = lane < HEAD
    dk = jnp.where(first, dka_ref[:, :PAIR], dka_ref[:, PAIR:])
    dk_ref[...] = rotate(dk, cosine, -sine, lane).astype(bf16)
    dv_ref[...] = jnp.where(first, dva_ref[:, :PAIR], dva_ref[:, PAIR:]).astype(bf16)


def attend_backward(queries, keys, values, grads, outputs, cosine, sine, bias):
    width = values.shape[1]
    pairs = width // PAIR
    tall = lambda columns: pl.BlockSpec((LEN, columns), lambda pair: (0, pair))
    whole = pl.BlockSpec((LEN, PAIR), lambda pair: (0, 0))
    return pl.pallas_call(
        attend_back_kernel,
        grid=(pairs,),
        in_specs=[tall(2 * PAIR)] + [tall(PAIR)] * 4 + [whole] * 3,
        out_specs=[tall(PAIR)] * 3,
        out_shape=[jax.ShapeDtypeStruct((LEN, width), bf16)] * 3,
        scratch_shapes=[
            pltpu.VMEM((LEN, 2 * PAIR), bf16),
            pltpu.VMEM((LEN, 2 * PAIR), f32),
            pltpu.VMEM((LEN, 2 * PAIR), f32),
        ],
        compiler_params=pltpu.CompilerParams(vmem_limit_bytes=vmem_bytes),
        cost_estimate=pl.CostEstimate(
            flops=2 * 10 * LEN * LEN * width * 4,
            bytes_accessed=12 * LEN * width * 2,
            transcendentals=LEN * LEN * width // HEAD,
        ),
        name="attend_back",
    )(queries, keys, values, grads, outputs, cosine, sine, bias)


def vector_parts(vectors):
    kernel_size = KERNEL * TEXT
    pieces = [vectors[:kernel_size].reshape(KERNEL, TEXT)]
    offset = kernel_size
    for extent in (TEXT, TEXT, TEXT, TEXT, TXT_FF, TXT_FF, TXT_FF, 6 * D):
        pieces.append(vectors[offset : offset + extent])
        offset = offset + extent
    return pieces


def normalise(values):
    center = values - jnp.mean(values, axis=-1, keepdims=True)
    variance = jnp.mean(center * center, axis=-1, keepdims=True)
    scale = lax.rsqrt(variance + norm_eps)
    return center * scale, scale


def normalise_back(grad, normed, scale):
    mean_grad = jnp.mean(grad, axis=-1, keepdims=True)
    mean_dot = jnp.mean(grad * normed, axis=-1, keepdims=True)
    return scale * (grad - mean_grad - normed * mean_dot)


def gelu_parts(values):
    share = 0.5 * (1.0 + lax.erf(values * 0.7071067811865476))
    density = 0.3989422804014327 * jnp.exp(-0.5 * values * values)
    return share, density


def gelu_tanh(values):
    return jax.nn.gelu(values, approximate=True)


def moments(gradient, first_moment, second_moment):
    first_new = beta_one * first_moment + (1.0 - beta_one) * gradient
    second_new = beta_two * second_moment + (1.0 - beta_two) * gradient * gradient
    bias_first = 1.0 - beta_one**STEP
    bias_second = 1.0 - beta_two**STEP
    direction = first_new / bias_first / (jnp.sqrt(second_new / bias_second) + adam_eps)
    return (first_new, second_new, direction)


def apply_step(weight, direction, rate):
    return weight - rate * (direction + weight_decay * weight)


def rotary_tables(core, half):
    position = ((jnp.arange(LEN) + core * half) % LEN).astype(f32)
    frequency = 10000.0 ** (-jnp.arange(HEAD // 2, dtype=f32) * 2.0 / HEAD)
    angle = position[:, None] * frequency[None, :]
    cosine, sine = jnp.cos(angle), jnp.sin(angle)
    return (
        jnp.concatenate([cosine] * 4, axis=1),
        jnp.concatenate([-sine, sine, -sine, sine], axis=1),
    )


def take_blocks(blocks, index):
    return jnp.take(blocks, index, axis=0, mode="clip")


def both_halves(mine):
    return jnp.concatenate([mine, swap_core(mine)], axis=0)


def sum_halves(multiply, rows, half):
    theirs = multiply(rows[half:]).astype(bf16)
    received = swap_core(theirs)
    return multiply(rows[:half]) + received.astype(f32)


def body(
    mel_frames,
    text_features,
    cotangent,
    time_embedding,
    lengths,
    group_ids,
    text_keep,
    owner_list,
    soap_master,
    soap_first,
    soap_second,
    left_basis,
    right_basis,
    text_matrices,
    text_first,
    text_second,
    modulation_weight,
    modulation_first,
    modulation_second,
    vectors,
    vector_first,
    vector_second,
):
    count = lax.axis_size("dp")
    me, core = lax.axis_index("dp"), lax.axis_index("mp")
    half = LEN // 2
    utterances = lengths.shape[0] * count
    panel_rows, width = soap_master.shape
    share_rows = modulation_weight.shape[0]
    text_rows = text_matrices.shape[0]
    text_half = text_rows // 2
    relative = jnp.arange(count) ^ me

    own_rows = lax.dynamic_slice_in_dim(text_matrices, core * text_half, text_half, 0)
    text_half_all = gather_relative(own_rows.astype(bf16))
    text_other = swap_core(text_half_all)
    slots = gather_relative(soap_master.astype(bf16))
    texts = take_blocks(by_core(core, text_half_all, text_other, axis=1), relative)
    texts = texts.reshape(3 * TEXT, D)
    expand_weight, shrink_rows, text_to_model = texts[:TEXT], texts[TEXT : 2 * TEXT], texts[2 * TEXT :]
    stacked = take_blocks(slots, owner_list ^ me).reshape(8, D, width)
    query_weight, key_weight, value_weight, out_weight = (stacked[i] for i in range(4))
    hidden_in, hidden_out = stacked[4:6], stacked[6:8]

    silu_time = jax.nn.silu(time_embedding.astype(f32)).astype(bf16)
    time_rows = lax.dynamic_slice_in_dim(silu_time, me * share_rows, share_rows, 1)
    weight_half = lax.dynamic_slice_in_dim(modulation_weight, core * 3 * D, 3 * D, 1).astype(bf16)
    modulation_half = sum_dp(dot32(time_rows, weight_half))
    modulation = by_core(core, modulation_half, swap_core(modulation_half), axis=1)
    (
        kernel,
        conv_bias,
        norm_gain,
        norm_bias,
        out_bias,
        in_bias,
        grn_gamma,
        grn_beta,
        modulation_bias,
    ) = vector_parts(vectors)
    group = group_ids[0]
    modulation_row = lax.dynamic_slice_in_dim(modulation, group, 1, 0) + modulation_bias
    shift_one, scale_one, gate_one, shift_two, scale_two, gate_two = (
        modulation_row[:, i * D : (i + 1) * D] for i in range(6)
    )

    first = core * half
    margin = KERNEL // 2
    edge = 8
    keep_all = jnp.pad(text_keep.astype(f32), (edge, edge))[:, None]
    text_all = jnp.pad(text_features, ((edge, edge), (0, 0)))
    window = lax.dynamic_slice_in_dim(text_all, first, half + 2 * edge, 0).astype(f32)
    window = window * lax.dynamic_slice_in_dim(keep_all, first, half + 2 * edge, 0)
    keep = lax.dynamic_slice_in_dim(keep_all, first + edge, half, 0)
    masked_text = window[edge : edge + half]
    taps = [window[edge - margin + j : edge - margin + j + half] for j in range(KERNEL)]
    mixed = conv_bias[None, :]
    for j in range(KERNEL):
        mixed = mixed + taps[j] * kernel[j][None, :]
    conv_normed, conv_scale = normalise(mixed)
    normed_low = (conv_normed * norm_gain + norm_bias).astype(bf16)
    expand_pre = dot32(normed_low, expand_weight) + in_bias
    share, density = gelu_parts(expand_pre)
    hidden = expand_pre * share
    energy_sum = jnp.sum(hidden * hidden, axis=0, keepdims=True)
    energy = jnp.sqrt(energy_sum + swap_core(energy_sum))
    energy_mean = jnp.mean(energy, axis=-1, keepdims=True) + norm_eps
    ratio = energy / energy_mean
    grn_low = (grn_gamma * (hidden * ratio) + grn_beta + hidden).astype(bf16)
    text_out = (masked_text + dot32(grn_low, shrink_rows, NT) + out_bias) * keep
    text_low = text_out.astype(bf16)
    mel_mine = lax.dynamic_slice_in_dim(mel_frames, first, half, 0).astype(f32)
    stream = mel_mine + dot32(text_low, text_to_model)

    normed_one, scale_norm_one = normalise(stream)
    first_normed = both_halves((normed_one * (1.0 + scale_one) + shift_one).astype(bf16))
    cosine, sine = rotary_tables(core, half)
    position = (jnp.arange(LEN) + first) % LEN
    bias = jnp.where(position < lengths[0], 0.0, -1e30).astype(bf16)
    bias = jnp.broadcast_to(bias[:, None], (LEN, PAIR))
    queries = dot32(first_normed, query_weight)
    keys = dot32(first_normed, key_weight)
    value_rows = dot32(first_normed, value_weight).astype(bf16)
    attended, query_aug, key_rot = attend_forward(queries, keys, value_rows, cosine, sine, bias)
    attention_out = sum_halves(lambda rows: dot32(rows, out_weight, NT), attended, half)
    stream_one = stream + gate_one * attention_out

    normed_two, scale_norm_two = normalise(stream_one)
    second_normed = both_halves((normed_two * (1.0 + scale_two) + shift_two).astype(bf16))
    unit_pre = [dot32(second_normed, hidden_in[i]) for i in range(2)]
    unit_act, unit_back = zip(*[jax.vjp(gelu_tanh, pre) for pre in unit_pre])
    unit_low = jnp.concatenate([act.astype(bf16) for act in unit_act], axis=1)
    unit_out = sum_halves(
        lambda rows: dot32(rows[:, :width], hidden_out[0], NT) + dot32(rows[:, width:], hidden_out[1], NT),
        unit_low,
        half,
    )
    output_mine = (stream_one + gate_two * unit_out).astype(bf16)
    block_output = by_core(core, output_mine, swap_core(output_mine))

    cot_mine = lax.dynamic_slice_in_dim(cotangent, first, half, 0)
    cot_other = lax.dynamic_slice_in_dim(cotangent, half - first, half, 0)
    out_grad = cot_mine.astype(f32)
    gate_two_grad = jnp.sum(out_grad * unit_out, axis=0)
    hidden_out_grad = jnp.concatenate(
        [(gate_two * out_grad).astype(bf16), (gate_two * cot_other.astype(f32)).astype(bf16)], axis=0
    )
    TN = (((0,), (0,)), ((), ()))
    out_blocks_grad = [dot32(hidden_out_grad, unit_low[:, i * width : (i + 1) * width], TN) for i in range(2)]
    pre_grad = [
        unit_back[i](dot32(hidden_out_grad, hidden_out[i]))[0].astype(bf16) for i in range(2)
    ]
    in_blocks_grad = [dot32(second_normed, pre_grad[i], TN) for i in range(2)]
    normed_two_grad = sum_halves(
        lambda rows: dot32(rows[:, :width], hidden_in[0], NT) + dot32(rows[:, width:], hidden_in[1], NT),
        jnp.concatenate(pre_grad, axis=1),
        half,
    )
    shift_two_grad = jnp.sum(normed_two_grad, axis=0)
    scale_two_grad = jnp.sum(normed_two_grad * normed_two, axis=0)
    stream_one_grad = out_grad + normalise_back(
        normed_two_grad * (1.0 + scale_two), normed_two, scale_norm_two
    )

    gate_one_grad = jnp.sum(stream_one_grad * attention_out, axis=0)
    attention_grad = both_halves((gate_one * stream_one_grad).astype(bf16))
    out_weight_grad = dot32(attention_grad, attended, TN)
    attended_grad = dot32(attention_grad, out_weight).astype(bf16)
    query_grad, key_grad, value_grad = attend_backward(
        query_aug, key_rot, value_rows, attended_grad, attended, cosine, sine, bias
    )
    head_grads = [dot32(first_normed, grad, TN) for grad in (query_grad, key_grad, value_grad)]
    normed_one_grad = sum_halves(
        lambda rows: dot32(rows[:, :width], query_weight, NT)
        + dot32(rows[:, width : 2 * width], key_weight, NT)
        + dot32(rows[:, 2 * width :], value_weight, NT),
        jnp.concatenate([query_grad, key_grad, value_grad], axis=1),
        half,
    )
    panel_grad = jnp.concatenate(
        [grad.astype(bf16) for grad in head_grads + [out_weight_grad] + in_blocks_grad + out_blocks_grad],
        axis=0,
    ).reshape(count, panel_rows, width)
    slot_index = jnp.arange(count)
    inverse = jnp.sum(jnp.where(owner_list[None, :] == slot_index[:, None], slot_index[None, :], 0), axis=1)
    own_panel = scatter_relative(take_blocks(panel_grad, jnp.take(inverse, relative, mode="clip")))

    shift_one_grad = jnp.sum(normed_one_grad, axis=0)
    scale_one_grad = jnp.sum(normed_one_grad * normed_one, axis=0)
    mel_grad_mine = stream_one_grad + normalise_back(
        normed_one_grad * (1.0 + scale_one), normed_one, scale_norm_one
    )
    mel_gradient = by_core(core, mel_grad_mine, swap_core(mel_grad_mine))

    stream_grad = mel_grad_mine.astype(bf16)
    text_to_model_grad = dot32(text_low, stream_grad, TN)
    shrink_grad = dot32(stream_grad, text_to_model, NT) * keep
    out_bias_grad = jnp.sum(shrink_grad, axis=0)
    shrink_low = shrink_grad.astype(bf16)
    shrink_rows_grad = dot32(shrink_low, grn_low, TN)
    grn_grad = dot32(shrink_low, shrink_rows)
    hidden_dot = jnp.sum(grn_grad * hidden, axis=0, keepdims=True)
    hidden_dot_all = hidden_dot + swap_core(hidden_dot)
    ratio_grad = grn_gamma * hidden_dot_all
    energy_grad = ratio_grad / energy_mean - jnp.mean(ratio_grad * ratio, axis=-1, keepdims=True) / energy_mean
    gamma_grad = (ratio * hidden_dot)[0]
    beta_grad = jnp.sum(grn_grad, axis=0)
    hidden_grad = grn_grad * (grn_gamma * ratio + 1.0) + hidden * (energy_grad / energy)
    expand_grad = hidden_grad * (share + expand_pre * density)
    in_bias_grad = jnp.sum(expand_grad, axis=0)
    expand_low = expand_grad.astype(bf16)
    expand_weight_grad = dot32(normed_low, expand_low, TN)
    text_grads = jnp.concatenate(
        [grad.astype(bf16) for grad in (expand_weight_grad, shrink_rows_grad, text_to_model_grad)], axis=0
    ).reshape(count, 2, text_half, D)
    text_keep_half = lax.dynamic_index_in_dim(text_grads, core, 1, keepdims=False)
    text_send_half = lax.dynamic_index_in_dim(text_grads, 1 - core, 1, keepdims=False)
    text_sum = add_low(text_keep_half, swap_core(text_send_half))
    own_text = scatter_relative(take_blocks(text_sum, relative))
    own_text = by_core(core, own_text, swap_core(own_text))

    normed_text_grad = dot32(expand_low, expand_weight, NT)
    gain_grad = jnp.sum(normed_text_grad * conv_normed, axis=0)
    norm_bias_grad = jnp.sum(normed_text_grad, axis=0)
    mixed_grad = normalise_back(normed_text_grad * norm_gain, conv_normed, conv_scale)
    conv_bias_grad = jnp.sum(mixed_grad, axis=0)
    kernel_grad = jnp.stack([jnp.sum(mixed_grad * taps[j], axis=0) for j in range(KERNEL)])
    border = lax.dynamic_slice_in_dim(mixed_grad, (1 - core) * (half - edge), edge, 0)
    border = swap_core(border)
    before = jnp.where(core == 1, border, 0.0)
    after = jnp.where(core == 0, border, 0.0)
    wide_grad = jnp.concatenate([before, mixed_grad, after], axis=0)
    masked_grad = shrink_grad
    for j in range(KERNEL):
        start = edge + margin - j
        masked_grad = masked_grad + wide_grad[start : start + half] * kernel[j][None, :]
    text_grad_mine = masked_grad * keep
    text_gradient = by_core(core, text_grad_mine, swap_core(text_grad_mine))

    vector_mine = jnp.concatenate(
        [
            kernel_grad.reshape(-1),
            conv_bias_grad,
            gain_grad,
            norm_bias_grad,
            out_bias_grad,
            in_bias_grad,
            gamma_grad,
            beta_grad,
        ]
    )
    token = jnp.concatenate(
        [shift_one_grad, scale_one_grad, gate_one_grad, shift_two_grad, scale_two_grad, gate_two_grad]
    )
    vector_half = vector_mine.shape[0] // 2
    token_half = 3 * D

    def half_of(which):
        return jnp.concatenate(
            [
                lax.dynamic_slice_in_dim(vector_mine, which * vector_half, vector_half, 0),
                lax.dynamic_slice_in_dim(token, which * token_half, token_half, 0),
            ]
        )

    small = half_of(core) + swap_core(half_of(1 - core))
    in_group = (jnp.arange(GROUPS) == group).astype(f32)
    table = in_group[:, None] * small[None, vector_half:]
    small = sum_dp(jnp.concatenate([small[:vector_half], table.reshape(-1)]).reshape(-1, 128))
    small = by_core(core, small[None], swap_core(small)[None]).reshape(2, -1)
    vector_sum = small[:, :vector_half].reshape(-1)
    tables = small[:, vector_half:].reshape(2, GROUPS, token_half)
    modulation_grad = jnp.concatenate([tables[0], tables[1]], axis=1)
    vector_gradient = jnp.concatenate([vector_sum, jnp.sum(modulation_grad, axis=0)]) / utterances
    share_grad = (
        lax.dot_general(
            time_rows, modulation_grad.astype(bf16), TN, preferred_element_type=f32
        )
        / utterances
    )

    own_panel = own_panel / utterances
    own_text = own_text / utterances
    rotated = jnp.dot(jnp.dot(left_basis.T, own_panel, precision=solver), right_basis, precision=solver)
    soap_moment, soap_variance, soap_direction = moments(rotated, soap_first, soap_second)
    turned_back = jnp.dot(
        jnp.dot(left_basis, soap_direction, precision=solver), right_basis.T, precision=solver
    )
    soap_weights = apply_step(soap_master, turned_back, learn_rate)
    text_moment, text_variance, text_direction = moments(own_text, text_first, text_second)
    text_weights = apply_step(text_matrices, text_direction, learn_rate)
    modulation_moment, modulation_variance, modulation_direction = moments(
        share_grad, modulation_first, modulation_second
    )
    modulation_weights = apply_step(modulation_weight, modulation_direction, learn_rate)
    vector_moment, vector_variance, vector_direction = moments(
        vector_gradient, vector_first, vector_second
    )
    vector_weights = apply_step(vectors, vector_direction, vector_rate)
    return (
        block_output,
        mel_gradient,
        text_gradient,
        soap_weights,
        soap_moment,
        soap_variance,
        text_weights,
        text_moment,
        text_variance,
        modulation_weights,
        modulation_moment,
        modulation_variance,
        vector_weights,
        vector_moment,
        vector_variance,
    )


def solution(mesh):
    rows, quarter, same = P("dp", None), P("dp", "mp"), P()
    return jax.shard_map(
        body,
        mesh=mesh,
        in_specs=(
            (rows,) * 3 + (same,) + (P("dp"),) * 3 + (same,) + (quarter,) * 5 + (rows,) * 6 + (same,) * 3
        ),
        out_specs=(rows,) * 3 + (quarter,) * 3 + (rows,) * 6 + (same,) * 3,
        check_vma=False,
    )
```

time: 1320 us -> 599 us (0.45)
  waiting for transfers between devices: 810 us -> 153 us
  matrix products: 207 us -> 114 us
  starting transfers between devices: 0.55 us -> 89.4 us
  Pallas kernels: 0 us -> 51.8 us
  other arithmetic: 141 us -> 96.5 us
  blocking collectives: 40.8 us -> 0 us
    reduce_scatter x2 -> x0, waiting for transfers between devices: 457 us -> none  [the longest x1 345 us: body(): lax.psum_scatter(slot_grad, 'dp', scatter_dimension=0, tiled=True)]
    all_gather x3 -> x0, waiting for transfers between devices: 273 us -> none  [the longest x1 130 us: body(): lax.all_gather(modulation_low, 'dp', axis=0, tiled=True)]
    ppermute x0 -> x103, waiting for transfers between devices: none -> 153 us  [the longest x84 147 us: swap_bit(): return lax.ppermute(array, 'dp', [(i, i ^ 1 << bit) for i in range(count)])]
    dot_general x48 -> x47, matrix products: 207 us -> 114 us  [the longest x42 99.3 us: dot32(): return lax.dot_general(left, right, dims, preferred_element_type=f32)]
    ppermute x0 -> x103, starting transfers between devices: none -> 89.4 us  [the longest x84 86.1 us: swap_bit(): return lax.ppermute(array, 'dp', [(i, i ^ 1 << bit) for i in range(count)])]
    psum x4 -> x0, waiting for transfers between devices: 80.2 us -> none  [the longest x1 40.1 us: body(): unit_out = lax.psum(unit_part, 'mp')]
    pallas_call x0 -> x2, Pallas kernels: none -> 51.8 us  [the longest x1 26.7 us: attend_forward(): pl.pallas_call(attend_kernel, grid=(pairs,), in_specs=[tall(PAIR), tall(P...]
    reduce_sum x19 -> x8, other arithmetic: 63.4 us -> 12.1 us  [the longest x1 3.95 us: body(): in_bias_grad = jnp.sum(expand_grad, axis=0)]
  transfers between devices with their start and end apart: 9 -> 103, of which waited for: 8 -> 49; matrix products, arithmetic and copies ran while one was open for 16% -> 40% of each run, Pallas kernels for 0% -> 4%
where the time goes in v1:
time: 599 us; the launch traced here: 589 us
  waiting for transfers between devices  153 us (26%)
  matrix products  114 us (19%)
  other arithmetic  96.5 us (16%)
  starting transfers between devices  89.4 us (15%)
  local copies, waits for them, and re-layouts  78 us (13%)
  Pallas kernels  51.8 us (9%)
  between operations  6.45 us (1%)
    ppermute x84, waiting for transfers between devices, swap_bit(): return lax.ppermute(array, 'dp', [(i, i ^ 1 << bit) for i in range(count)])  147 us
    dot_general x42, matrix products, dot32(): return lax.dot_general(left, right, dims, preferred_element_type=f32)  99.3 us
    ppermute x84, starting transfers between devices, swap_bit(): return lax.ppermute(array, 'dp', [(i, i ^ 1 << bit) for i in range(count)])  86.1 us
    pallas_call x1, Pallas kernels, attend_forward(): pl.pallas_call(attend_kernel, grid=(pairs,), in_specs=[tall(PAIR), tall(P...  26.7 us
    pallas_call x1, Pallas kernels, attend_backward(): pl.pallas_call(attend_back_kernel, grid=(pairs,), in_specs=[tall(2 * PAIR...  25.1 us
    gather x4, local copies, waits for them, and re-layouts, take_blocks(): return jnp.take(blocks, index, axis=0, mode='clip')  24.6 us
    another operation x30, other arithmetic, spread_step(): jnp.stack([part, swap_bit(part, axis_orders[index][phase])])  18.3 us
    select_n x5, other arithmetic, by_core(): jnp.where(core == 0, jnp.concatenate([mine, other], axis=axis), jnp.conca...  16.7 us
  transfers between devices with their start and end apart: 103, of which 49 were waited for; matrix products, arithmetic and copies ran while one was open for 40% of the time, Pallas kernels for 4%

profile of v1, /device:TPU:0, one launch (start us, length us, event | category | flops | bytes accessed | tf_op | source)
XLA Modules:
  0.0 589.2 jit_solution(730948628850900516)
XLA Ops:
  3.6 2.9 collective-permute-start.21
  8.1 2.6 collective-permute-start
  35.8 3.2 collective-permute-done.4
  40.0 7.0 %collective-permute-done.5 = bf16[2,1,16,1024]{3,2,0,1:T(8,128)(2,1)S(1)} collective-permute-done((bf16[2,1,16,1024]{3,2,0,1:T(8,128)(2,1)S(1)}, bf16[2,1,16,1024]{3,2,0,1:T(8,128)(2,1)S(1)}, u32[]{:S(2)}, u32[]{:S(2)}) %collective-permute-start.5) | collective-permute-done | bytes 65568 | tf_op jit(solution)/shard_map/ppermute | solution.py:35
  48.3 3.1 collective-permute-done.6
  78.5 2.6 collective-permute-start.14
  81.1 2.9 collective-permute-done.14
  85.3 3.8 collective-permute-done.15
  94.4 3.7 collective-permute-done.24
  100.8 3.6 collective-permute-done.17
  104.6 4.5 collective-permute-done.31
  109.1 3.0 collective-permute-done.32
  120.7 5.1 collective-permute-done.38
  125.8 5.8 collective-permute-done.37
  137.9 7.4 %collective-permute-done.42 = bf16[2,1,160,512]{3,2,0,1:T(8,128)(2,1)S(1)} collective-permute-done((bf16[2,1,160,512]{3,2,0,1:T(8,128)(2,1)S(1)}, bf16[2,1,160,512]{3,2,0,1:T(8,128)(2,1)S(1)}, u32[]{:S(2)}, u32[]{:S(2)}) %collective-permute-start.42) | collective-permute-done | bytes 327712 | tf_op jit(solution)/shard_map/ppermute | solution.py:35
  147.6 3.0 maximum_select_fusion.1
  150.6 4.5 gather_fusion
  155.0 4.6 multiply_reduce_fusion.8
  165.7 2.9 add_convert_fusion.6
  173.6 5.4 collective-permute-done.45
  184.9 3.7 pad_maximum_fusion
  188.7 8.5 %gather_fusion.1 = bf16[16,512,512]{2,1,0:T(8,128)(2,1)} fusion(bf16[16,512,512]{2,1,0:T(8,128)(2,1)} %bitcast.510, s32[1024]{0:T(1024)} %pad_clamp_fusion.1), kind=kCustom, calls=%fused_computation.1 | custom fusion | bytes 16777280 | tf_op jit(solution)/shard_map/jit(_take)/gather | solution.py:398
  197.1 5.2 fusion.185
  202.4 4.3 convolution_convert_fusion.9.v_ref
  206.7 4.5 fusion.177.k_ref
  211.2 4.1 fusion.178.q_ref
  215.5 26.7 %attend.1 = (bf16[1024,512]{1,0:T(8,128)(2,1)S(1)}, bf16[1024,1024]{1,0:T(8,128)(2,1)}, bf16[1024,512]{1,0:T(8,128)(2,1)S(1)}) custom-call(f32[1024,512]{1,0:T(8,128)} %fusion.178.q_ref, f32[1024,512]{1,0:T(8,128)} %fusion.177.k_ref, bf16[1024,512]{1,0:T(8,128)(2,1)S(1)} %convolution_convert_fusion.9.v_ref, f32[1024,128]{1,0:T(8,128)S(1)} %get-tuple-element.294.cos_ref, ...), custom_call_target="tpu_custom_call" | custom-call | flops 17179869184 | bytes 10485760 | tf_op jit(solution)/shard_map/attend/pallas_call | solution.py:239
  243.1 2.6 collective-permute-done.46
  253.0 3.2 multiply_convert_fusion.3
  256.3 3.9 fusion.7
  261.8 3.3 multiply_convert_fusion.2
  265.1 3.7 fusion.14
  275.7 2.9 multiply_reduce_fusion.1
  284.2 3.8 convolution_convert_fusion.8.do_ref
  288.0 25.1 %attend_back.1 = (bf16[1024,512]{1,0:T(8,128)(2,1)S(1)}, bf16[1024,512]{1,0:T(8,128)(2,1)S(1)}, bf16[1024,512]{1,0:T(8,128)(2,1)S(1)}) custom-call(bf16[1024,1024]{1,0:T(8,128)(2,1)} %get-tuple-element.116.qa_ref, bf16[1024,512]{1,0:T(8,128)(2,1)S(1)} %copy-done.9, bf16[1024,512]{1,0:T(8,128)(2,1)} %copy-done.7, ...), custom_call_target="tpu_custom_call" | custom-call | flops 42949672960 | bytes 12582912 | tf_op jit(solution)/shard_map/attend_back/pallas_call | solution.py:319
  319.3 3.8 fusion.29
  323.1 3.8 fusion.28
  326.9 3.9 fusion.27
  330.9 3.9 fusion.26
  334.8 3.9 fusion.25
  338.7 4.0 fusion.24
  347.2 8.3 %gather_fusion.3 = bf16[16,512,512]{2,1,0:T(8,128)(2,1)} fusion(bf16[16,512,512]{2,1,0:T(8,128)(2,1)} %bitcast.132, s32[1024]{0:T(1024)S(1)} %pad_clamp_fusion), kind=kCustom, calls=%fused_computation.3 | custom fusion | bytes 16777280 | tf_op jit(solution)/shard_map/jit(_take)/gather | solution.py:398
  355.6 4.3 slice_bitcast_fusion
  367.4 3.9 maximum_select_fusion.2
  371.3 9.0 %collective-permute-done.62 = bf16[1,2,2,160,512]{4,3,2,1,0:T(8,128)(2,1)S(1)} collective-permute-done((bf16[1,2,2,160,512]{4,3,2,1,0:T(8,128)(2,1)S(1)}, bf16[1,2,2,160,512]{4,3,2,1,0:T(8,128)(2,1)S(1)}, u32[]{:S(2)}, u32[]{:S(2)}) %collective-permute-start.62) | collective-permute-done | bytes 655392 | tf_op jit(solution)/shard_map/ppermute | solution.py:35
  381.0 12.7 %collective-permute-done.59 = bf16[1,2,2,160,512]{4,3,1,2,0:T(8,128)(2,1)S(1)} collective-permute-done((bf16[1,2,2,160,512]{4,3,1,2,0:T(8,128)(2,1)S(1)}, bf16[1,2,2,160,512]{4,3,1,2,0:T(8,128)(2,1)S(1)}, u32[]{:S(2)}, u32[]{:S(2)}) %collective-permute-start.59) | collective-permute-done | bytes 655392 | tf_op jit(solution)/shard_map/ppermute | solution.py:35
  401.6 11.1 %collective-permute-done.58 = bf16[1,2,2,176,512]{4,3,1,2,0:T(8,128)(2,1)S(1)} collective-permute-done((bf16[1,2,2,176,512]{4,3,1,2,0:T(8,128)(2,1)S(1)}, bf16[1,2,2,176,512]{4,3,1,2,0:T(8,128)(2,1)S(1)}, u32[]{:S(2)}, u32[]{:S(2)}) %collective-permute-start.58) | collective-permute-done | bytes 720928 | tf_op jit(solution)/shard_map/ppermute | solution.py:35
  428.5 3.9 fusion.180
  432.5 2.8 multiply_reduce_fusion.11
  437.4 3.0 multiply_reduce_fusion.12
  447.8 2.5 fusion.186
  456.2 2.6 collective-permute-done.98
  461.4 2.9 collective-permute-done.66
  467.9 5.3 collective-permute-done.100
  474.1 6.2 %collective-permute-done.101 = f32[226,128]{1,0:T(8,128)S(1)} collective-permute-done((f32[226,128]{1,0:T(8,128)S(1)}, f32[226,128]{1,0:T(8,128)S(1)}, u32[]{:S(2)}, u32[]{:S(2)}) %collective-permute-start.101) | collective-permute-done | bytes 115744 | tf_op jit(solution)/shard_map/ppermute | solution.py:35
  483.2 8.2 %collective-permute-done.69 = bf16[1,2,176,512]{3,2,1,0:T(8,128)(2,1)S(1)} collective-permute-done((bf16[1,2,176,512]{3,2,1,0:T(8,128)(2,1)S(1)}, bf16[1,2,176,512]{3,2,1,0:T(8,128)(2,1)S(1)}, u32[]{:S(2)}, u32[]{:S(2)}) %collective-permute-start.69) | collective-permute-done | bytes 360480 | tf_op jit(solution)/shard_map/ppermute | solution.py:35
  505.1 6.3 %multiply_subtract_fusion = (f32[64,6144]{1,0:T(8,128)}, f32[64,6144]{1,0:T(8,128)}, f32[64,6144]{1,0:T(8,128)}) fusion(f32[64,6144]{1,0:T(8,128)} %param.38, f32[64,6144]{1,0:T(8,128)} %param.39, f32[64,6144]{1,0:T(8,128)} %param.40, f32[8,6144]{1,0:T(8,128)} %constant_dynamic-update-slice_fusion.2, f32[8,1024]{1,0:T(8,128)} %copy-done.110, s32[]{:T(128)S(6)} %select_n.151), kind=kOutput, calls=%fused_computation.84 | convolution fusion | flops 12634624 | bytes 9637892 | tf_op jit(solution)/shard_map/dot_general | solution.py:667
  514.3 4.7 collective-permute-done.73
  520.0 5.3 collective-permute-done.72
  531.1 3.2 fusion.37
  534.3 4.2 maximum_select_fusion.3
  538.5 3.2 fusion
  541.7 3.4 gather_fusion.4
  582.2 5.3 maximum_select_fusion
  (735 shorter events, 250.0 us)
Async XLA Ops:
  3.6 52.9 %collective-permute-start.21 = (f32[8,3072]{1,0:T(8,128)}, f32[8,3072]{1,0:T(8,128)}, u32[]{:S(2)}, u32[]{:S(2)}) collective-permute-start(f32[8,3072]{1,0:T(8,128)} %fusion.125), channel_id=1, source_target_pairs={{0,2},{2,0},{4,6},{6,4},{8,10},{10,8},{12,14},{14,12},{16,18},{18,... | collective-permute-start | bytes 294920 | tf_op jit(solution)/shard_map/ppermute | solution.py:35
  8.1 44.4 %collective-permute-start = (bf16[1,48,1024]{2,1,0:T(8,128)(2,1)}, bf16[1,48,1024]{2,1,0:T(8,128)(2,1)}, u32[]{:S(2)}, u32[]{:S(2)}) collective-permute-start(bf16[1,48,1024]{2,1,0:T(8,128)(2,1)} %fusion.147), channel_id=1, source_target_pairs={{0,16},{2,18},{4,20},{6,22},{8,24},{10,26},{12,28},{14,30},{16,0},... | collective-permute-start | bytes 294920 | tf_op jit(solution)/shard_map/ppermute | solution.py:35
  12.2 18.4 %collective-permute-start.3 = (bf16[1,16,1024]{2,1,0:T(8,128)(2,1)}, bf16[1,16,1024]{2,1,0:T(8,128)(2,1)}, u32[]{:S(2)}, u32[]{:S(2)}) collective-permute-start(bf16[1,16,1024]{2,1,0:T(8,128)(2,1)} %get-tuple-element.247), channel_id=1, source_target_pairs={{0,8},{2,10},{4,12},{6,14},{8,0},{10,2},{12,4},{14,6},{16,24},{18,... | collective-permute-start | bytes 98312 | tf_op jit(solution)/shard_map/ppermute | solution.py:35
  13.8 18.2 %collective-permute-start.2 = (bf16[1,16,1024]{2,1,0:T(8,128)(2,1)}, bf16[1,16,1024]{2,1,0:T(8,128)(2,1)}, u32[]{:S(2)}, u32[]{:S(2)}) collective-permute-start(bf16[1,16,1024]{2,1,0:T(8,128)(2,1)} %get-tuple-element.248), channel_id=1, source_target_pairs={{0,4},{2,6},{4,0},{6,2},{8,12},{10,14},{12,8},{14,10},{16,20},{18,... | collective-permute-start | bytes 98312 | tf_op jit(solution)/shard_map/ppermute | solution.py:35
  17.4 94.8 %collective-permute-start.27 = (bf16[1,512,512]{2,1,0:T(8,128)(2,1)}, bf16[1,512,512]{2,1,0:T(8,128)(2,1)}, u32[]{:S(2)}, u32[]{:S(2)}) collective-permute-start(bf16[1,512,512]{2,1,0:T(8,128)(2,1)} %convert_bitcast_fusion), channel_id=1, source_target_pairs={{0,16},{2,18},{4,20},{6,22},{8,24},{10,26},{12,28},{14,30},{16,0},... | collective-permute-start | bytes 1572872 | tf_op jit(solution)/shard_map/ppermute | solution.py:35
  32.0 42.2 %collective-permute-start.30 = (bf16[1,160,512]{2,1,0:T(8,128)(2,1)}, bf16[1,160,512]{2,1,0:T(8,128)(2,1)}, u32[]{:S(2)}, u32[]{:S(2)}) collective-permute-start(bf16[1,160,512]{2,1,0:T(8,128)(2,1)} %get-tuple-element.233), channel_id=1, source_target_pairs={{0,8},{2,10},{4,12},{6,14},{8,0},{10,2},{12,4},{14,6},{16,24},{18,... | collective-permute-start | bytes 491528 | tf_op jit(solution)/shard_map/ppermute | solution.py:35
  38.9 8.1 %collective-permute-start.5 = (bf16[2,1,16,1024]{3,2,0,1:T(8,128)(2,1)S(1)}, bf16[2,1,16,1024]{3,2,0,1:T(8,128)(2,1)S(1)}, u32[]{:S(2)}, u32[]{:S(2)}) collective-permute-start(bf16[2,1,16,1024]{3,2,0,1:T(8,128)(2,1)S(1)} %pad_maximum_fusion.40), channel_id=1, source_target_pairs={{0,8},{2,10},{4,12},{6,14},{8,0},{10,2},{12,4},{14,6},{16,24},{18,... | collective-permute-start | bytes 196616 | tf_op jit(solution)/shard_map/ppermute | solution.py:35
  51.3 39.1 %collective-permute-start.29 = (bf16[1,176,512]{2,1,0:T(8,128)(2,1)}, bf16[1,176,512]{2,1,0:T(8,128)(2,1)}, u32[]{:S(2)}, u32[]{:S(2)}) collective-permute-start(bf16[1,176,512]{2,1,0:T(8,128)(2,1)} %get-tuple-element.236), channel_id=1, source_target_pairs={{0,4},{2,6},{4,0},{6,2},{8,12},{10,14},{12,8},{14,10},{16,20},{18,... | collective-permute-start | bytes 540680 | tf_op jit(solution)/shard_map/ppermute | solution.py:35
  63.5 6.1 %collective-permute-start.8 = (bf16[2,2,1,16,1024]{4,3,0,1,2:T(8,128)(2,1)}, bf16[2,2,1,16,1024]{4,3,0,1,2:T(8,128)(2,1)S(1)}, u32[]{:S(2)}, u32[]{:S(2)}) collective-permute-start(bf16[2,2,1,16,1024]{4,3,0,1,2:T(8,128)(2,1)} %pad_maximum_fusion.33), channel_id=1, source_target_pairs={{0,2},{2,0},{4,6},{6,4},{8,10},{10,8},{12,14},{14,12},{16,18},{18,... | collective-permute-start | bytes 393224 | tf_op jit(solution)/shard_map/ppermute | solution.py:35
  65.9 6.3 %collective-permute-start.9 = (bf16[2,2,1,16,1024]{4,3,1,2,0:T(8,128)(2,1)}, bf16[2,2,1,16,1024]{4,3,1,2,0:T(8,128)(2,1)S(1)}, u32[]{:S(2)}, u32[]{:S(2)}) collective-permute-start(bf16[2,2,1,16,1024]{4,3,1,2,0:T(8,128)(2,1)} %pad_maximum_fusion.34), channel_id=1, source_target_pairs={{0,4},{2,6},{4,0},{6,2},{8,12},{10,14},{12,8},{14,10},{16,20},{18,... | collective-permute-start | bytes 393224 | tf_op jit(solution)/shard_map/ppermute | solution.py:35
  69.6 23.2 %collective-permute-start.28 = (bf16[1,176,512]{2,1,0:T(8,128)(2,1)}, bf16[1,176,512]{2,1,0:T(8,128)(2,1)S(1)}, u32[]{:S(2)}, u32[]{:S(2)}) collective-permute-start(bf16[1,176,512]{2,1,0:T(8,128)(2,1)} %get-tuple-element.237), channel_id=1, source_target_pairs={{0,2},{2,0},{4,6},{6,4},{8,10},{10,8},{12,14},{14,12},{16,18},{18,... | collective-permute-start | bytes 540680 | tf_op jit(solution)/shard_map/ppermute | solution.py:35
  76.8 14.6 %collective-permute-start.23 = (f32[8,3072]{1,0:T(8,128)S(1)}, f32[8,3072]{1,0:T(8,128)S(1)}, u32[]{:S(2)}, u32[]{:S(2)}) collective-permute-start(f32[8,3072]{1,0:T(8,128)S(1)} %add.562), channel_id=1, source_target_pairs={{0,8},{2,10},{4,12},{6,14},{8,0},{10,2},{12,4},{14,6},{16,24},{18,... | collective-permute-start | bytes 294920 | tf_op jit(solution)/shard_map/ppermute | solution.py:35
  89.1 10.3 %collective-permute-start.16 = (bf16[2,2,1,16,1024]{4,3,1,2,0:T(8,128)(2,1)S(1)}, bf16[2,2,1,16,1024]{4,3,1,2,0:T(8,128)(2,1)S(1)}, u32[]{:S(2)}, u32[]{:S(2)}) collective-permute-start(bf16[2,2,1,16,1024]{4,3,1,2,0:T(8,128)(2,1)S(1)} %pad_maximum_fusion.35), channel_id=1, source_target_pairs={{0,8},{2,10},{4,12},{6,14},{8,0},{10,2},{12,4},{14,6},{16,24},{18,... | collective-permute-start | bytes 393224 | tf_op jit(solution)/shard_map/ppermute | solution.py:35
  91.4 6.6 %collective-permute-start.24 = (f32[8,3072]{1,0:T(8,128)S(1)}, f32[8,3072]{1,0:T(8,128)S(1)}, u32[]{:S(2)}, u32[]{:S(2)}) collective-permute-start(f32[8,3072]{1,0:T(8,128)S(1)} %add.563), channel_id=1, source_target_pairs={{0,16},{2,18},{4,20},{6,22},{8,24},{10,26},{12,28},{14,30},{16,0},... | collective-permute-start | bytes 294920 | tf_op jit(solution)/shard_map/ppermute | solution.py:35
  91.5 9.2 %collective-permute-start.18 = (bf16[2,2,1,16,1024]{4,3,0,1,2:T(8,128)(2,1)S(1)}, bf16[2,2,1,16,1024]{4,3,0,1,2:T(8,128)(2,1)S(1)}, u32[]{:S(2)}, u32[]{:S(2)}) collective-permute-start(bf16[2,2,1,16,1024]{4,3,0,1,2:T(8,128)(2,1)S(1)} %pad_maximum_fusion.37), channel_id=1, source_target_pairs={{0,4},{2,6},{4,0},{6,2},{8,12},{10,14},{12,8},{14,10},{16,20},{18,... | collective-permute-start | bytes 393224 | tf_op jit(solution)/shard_map/ppermute | solution.py:35
  92.8 11.7 %collective-permute-start.33 = (bf16[2,1,160,512]{3,2,1,0:T(8,128)(2,1)S(1)}, bf16[2,1,160,512]{3,2,1,0:T(8,128)(2,1)S(1)}, u32[]{:S(2)}, u32[]{:S(2)}) collective-permute-start(bf16[2,1,160,512]{3,2,1,0:T(8,128)(2,1)S(1)} %pad_maximum_fusion.27), channel_id=1, source_target_pairs={{0,2},{2,0},{4,6},{6,4},{8,10},{10,8},{12,14},{14,12},{16,18},{18,... | collective-permute-start | bytes 983048 | tf_op jit(solution)/shard_map/ppermute | solution.py:35
  98.1 10.9 %collective-permute-start.31 = (bf16[2,1,176,512]{3,2,0,1:T(8,128)(2,1)S(1)}, bf16[2,1,176,512]{3,2,0,1:T(8,128)(2,1)S(1)}, u32[]{:S(2)}, u32[]{:S(2)}) collective-permute-start(bf16[2,1,176,512]{3,2,0,1:T(8,128)(2,1)S(1)} %pad_maximum_fusion.23), channel_id=1, source_target_pairs={{0,4},{2,6},{4,0},{6,2},{8,12},{10,14},{12,8},{14,10},{16,20},{18,... | collective-permute-start | bytes 1081352 | tf_op jit(solution)/shard_map/ppermute | solution.py:35
  100.7 11.4 %collective-permute-start.32 = (bf16[2,1,176,512]{3,2,1,0:T(8,128)(2,1)S(1)}, bf16[2,1,176,512]{3,2,1,0:T(8,128)(2,1)S(1)}, u32[]{:S(2)}, u32[]{:S(2)}) collective-permute-start(bf16[2,1,176,512]{3,2,1,0:T(8,128)(2,1)S(1)} %pad_maximum_fusion.24), channel_id=1, source_target_pairs={{0,8},{2,10},{4,12},{6,14},{8,0},{10,2},{12,4},{14,6},{16,24},{18,... | collective-permute-start | bytes 1081352 | tf_op jit(solution)/shard_map/ppermute | solution.py:35
  113.1 6.2 %collective-permute-start.39 = (bf16[1,160,512]{2,1,0:T(8,128)(2,1)S(1)}, bf16[1,160,512]{2,1,0:T(8,128)(2,1)S(1)}, u32[]{:S(2)}, u32[]{:S(2)}) collective-permute-start(bf16[1,160,512]{2,1,0:T(8,128)(2,1)S(1)} %get-tuple-element.227), channel_id=1, source_target_pairs={{0,8},{2,10},{4,12},{6,14},{8,0},{10,2},{12,4},{14,6},{16,24},{18,... | collective-permute-start | bytes 491528 | tf_op jit(solution)/shard_map/ppermute | solution.py:35
  113.2 18.4 %collective-permute-start.36 = (bf16[2,2,1,160,512]{4,3,1,2,0:T(8,128)(2,1)S(1)}, bf16[2,2,1,160,512]{4,3,1,2,0:T(8,128)(2,1)S(1)}, u32[]{:S(2)}, u32[]{:S(2)}) collective-permute-start(bf16[2,2,1,160,512]{4,3,1,2,0:T(8,128)(2,1)S(1)} %pad_maximum_fusion.18), channel_id=1, source_target_pairs={{0,4},{2,6},{4,0},{6,2},{8,12},{10,14},{12,8},{14,10},{16,20},{18,... | collective-permute-start | bytes 1966088 | tf_op jit(solution)/shard_map/ppermute | solution.py:35
  114.3 18.5 %collective-permute-start.34 = (bf16[2,2,1,176,512]{4,3,0,1,2:T(8,128)(2,1)S(1)}, bf16[2,2,1,176,512]{4,3,0,1,2:T(8,128)(2,1)S(1)}, u32[]{:S(2)}, u32[]{:S(2)}) collective-permute-start(bf16[2,2,1,176,512]{4,3,0,1,2:T(8,128)(2,1)S(1)} %pad_maximum_fusion.14), channel_id=1, source_target_pairs={{0,8},{2,10},{4,12},{6,14},{8,0},{10,2},{12,4},{14,6},{16,24},{18,... | collective-permute-start | bytes 2162696 | tf_op jit(solution)/shard_map/ppermute | solution.py:35
  116.3 9.5 %collective-permute-start.38 = (bf16[1,176,512]{2,1,0:T(8,128)(2,1)S(1)}, bf16[1,176,512]{2,1,0:T(8,128)(2,1)S(1)}, u32[]{:S(2)}, u32[]{:S(2)}) collective-permute-start(bf16[1,176,512]{2,1,0:T(8,128)(2,1)S(1)} %get-tuple-element.230), channel_id=1, source_target_pairs={{0,4},{2,6},{4,0},{6,2},{8,12},{10,14},{12,8},{14,10},{16,20},{18,... | collective-permute-start | bytes 540680 | tf_op jit(solution)/shard_map/ppermute | solution.py:35
  118.4 15.7 %collective-permute-start.35 = (bf16[2,2,1,176,512]{4,3,1,2,0:T(8,128)(2,1)S(1)}, bf16[2,2,1,176,512]{4,3,1,2,0:T(8,128)(2,1)S(1)}, u32[]{:S(2)}, u32[]{:S(2)}) collective-permute-start(bf16[2,2,1,176,512]{4,3,1,2,0:T(8,128)(2,1)S(1)} %pad_maximum_fusion.15), channel_id=1, source_target_pairs={{0,2},{2,0},{4,6},{6,4},{8,10},{10,8},{12,14},{14,12},{16,18},{18,... | collective-permute-start | bytes 2162696 | tf_op jit(solution)/shard_map/ppermute | solution.py:35
  119.4 12.2 %collective-permute-start.37 = (bf16[1,176,512]{2,1,0:T(8,128)(2,1)S(1)}, bf16[1,176,512]{2,1,0:T(8,128)(2,1)S(1)}, u32[]{:S(2)}, u32[]{:S(2)}) collective-permute-start(bf16[1,176,512]{2,1,0:T(8,128)(2,1)S(1)} %get-tuple-element.231), channel_id=1, source_target_pairs={{0,2},{2,0},{4,6},{6,4},{8,10},{10,8},{12,14},{14,12},{16,18},{18,... | collective-permute-start | bytes 540680 | tf_op jit(solution)/shard_map/ppermute | solution.py:35
  125.8 11.1 %collective-permute-start.25 = (f32[8,3072]{1,0:T(8,128)S(1)}, f32[8,3072]{1,0:T(8,128)S(1)}, u32[]{:S(2)}, u32[]{:S(2)}) collective-permute-start(f32[8,3072]{1,0:T(8,128)S(1)} %add.564), channel_id=1, source_target_pairs={{0,1},{1,0},{2,3},{3,2},{4,5},{5,4},{6,7},{7,6},{8,9},{9,8},{10,11... | collective-permute-start | bytes 294920 | tf_op jit(solution)/shard_map/ppermute | solution.py:30
  131.6 16.0 %collective-permute-start.19 = (bf16[16,48,1024]{2,1,0:T(8,128)(2,1)S(1)}, bf16[16,48,1024]{2,1,0:T(8,128)(2,1)S(1)}, u32[]{:S(2)}, u32[]{:S(2)}) collective-permute-start(bf16[16,48,1024]{2,1,0:T(8,128)(2,1)S(1)} %bitcast.547), channel_id=1, source_target_pairs={{0,1},{1,0},{2,3},{3,2},{4,5},{5,4},{6,7},{7,6},{8,9},{9,8},{10,11... | collective-permute-start | bytes 4718600 | tf_op jit(solution)/shard_map/ppermute | solution.py:30
  135.3 10.1 %collective-permute-start.42 = (bf16[2,1,160,512]{3,2,0,1:T(8,128)(2,1)S(1)}, bf16[2,1,160,512]{3,2,0,1:T(8,128)(2,1)S(1)}, u32[]{:S(2)}, u32[]{:S(2)}) collective-permute-start(bf16[2,1,160,512]{3,2,0,1:T(8,128)(2,1)S(1)} %pad_maximum_fusion.28), channel_id=1, source_target_pairs={{0,2},{2,0},{4,6},{6,4},{8,10},{10,8},{12,14},{14,12},{16,18},{18,... | collective-permute-start | bytes 983048 | tf_op jit(solution)/shard_map/ppermute | solution.py:35
  136.1 10.5 %collective-permute-start.40 = (bf16[2,1,176,512]{3,2,1,0:T(8,128)(2,1)S(1)}, bf16[2,1,176,512]{3,2,1,0:T(8,128)(2,1)S(1)}, u32[]{:S(2)}, u32[]{:S(2)}) collective-permute-start(bf16[2,1,176,512]{3,2,1,0:T(8,128)(2,1)S(1)} %pad_maximum_fusion.25), channel_id=1, source_target_pairs={{0,4},{2,6},{4,0},{6,2},{8,12},{10,14},{12,8},{14,10},{16,20},{18,... | collective-permute-start | bytes 1081352 | tf_op jit(solution)/shard_map/ppermute | solution.py:35
  137.5 22.1 %collective-permute-start.41 = (bf16[2,1,176,512]{3,2,1,0:T(8,128)(2,1)S(1)}, bf16[2,1,176,512]{3,2,1,0:T(8,128)(2,1)}, u32[]{:S(2)}, u32[]{:S(2)}) collective-permute-start(bf16[2,1,176,512]{3,2,1,0:T(8,128)(2,1)S(1)} %pad_maximum_fusion.26), channel_id=1, source_target_pairs={{0,8},{2,10},{4,12},{6,14},{8,0},{10,2},{12,4},{14,6},{16,24},{18,... | collective-permute-start | bytes 1081352 | tf_op jit(solution)/shard_map/ppermute | solution.py:35
  161.5 17.5 %collective-permute-start.45 = (bf16[2,2,1,160,512]{4,3,0,1,2:T(8,128)(2,1)}, bf16[2,2,1,160,512]{4,3,0,1,2:T(8,128)(2,1)}, u32[]{:S(2)}, u32[]{:S(2)}) collective-permute-start(bf16[2,2,1,160,512]{4,3,0,1,2:T(8,128)(2,1)} %pad_maximum_fusion.19), channel_id=1, source_target_pairs={{0,4},{2,6},{4,0},{6,2},{8,12},{10,14},{12,8},{14,10},{16,20},{18,... | collective-permute-start | bytes 1966088 | tf_op jit(solution)/shard_map/ppermute | solution.py:35
  162.3 18.6 %collective-permute-start.43 = (bf16[2,2,1,176,512]{4,3,1,2,0:T(8,128)(2,1)}, bf16[2,2,1,176,512]{4,3,1,2,0:T(8,128)(2,1)}, u32[]{:S(2)}, u32[]{:S(2)}) collective-permute-start(bf16[2,2,1,176,512]{4,3,1,2,0:T(8,128)(2,1)} %pad_maximum_fusion.16), channel_id=1, source_target_pairs={{0,8},{2,10},{4,12},{6,14},{8,0},{10,2},{12,4},{14,6},{16,24},{18,... | collective-permute-start | bytes 2162696 | tf_op jit(solution)/shard_map/ppermute | solution.py:35
  162.7 19.6 %collective-permute-start.44 = (bf16[2,2,1,176,512]{4,3,1,2,0:T(8,128)(2,1)}, bf16[2,2,1,176,512]{4,3,1,2,0:T(8,128)(2,1)}, u32[]{:S(2)}, u32[]{:S(2)}) collective-permute-start(bf16[2,2,1,176,512]{4,3,1,2,0:T(8,128)(2,1)} %pad_maximum_fusion.17), channel_id=1, source_target_pairs={{0,2},{2,0},{4,6},{6,4},{8,10},{10,8},{12,14},{14,12},{16,18},{18,... | collective-permute-start | bytes 2162696 | tf_op jit(solution)/shard_map/ppermute | solution.py:35
  173.6 28.7 %collective-permute-start.26 = (bf16[512,1024]{1,0:T(8,128)(2,1)}, bf16[512,1024]{1,0:T(8,128)(2,1)}, u32[]{:S(2)}, u32[]{:S(2)}) collective-permute-start(bf16[512,1024]{1,0:T(8,128)(2,1)} %add_convert_fusion.5), channel_id=1, source_target_pairs={{0,1},{1,0},{2,3},{3,2},{4,5},{5,4},{6,7},{7,6},{8,9},{9,8},{10,11... | collective-permute-start | bytes 3145736 | tf_op jit(solution)/shard_map/ppermute | solution.py:30
  283.0 83.2 %collective-permute-start.49 = (bf16[512,1024]{1,0:T(8,128)(2,1)}, bf16[512,1024]{1,0:T(8,128)(2,1)}, u32[]{:S(2)}, u32[]{:S(2)}) collective-permute-start(bf16[512,1024]{1,0:T(8,128)(2,1)} %get-tuple-element.214), channel_id=1, source_target_pairs={{0,1},{1,0},{2,3},{3,2},{4,5},{5,4},{6,7},{7,6},{8,9},{9,8},{10,11... | collective-permute-start | bytes 3145736 | tf_op jit(solution)/shard_map/ppermute | solution.py:30
  362.0 51.8 %collective-permute-start.52 = (bf16[512,1024]{1,0:T(8,128)(2,1)S(1)}, bf16[512,1024]{1,0:T(8,128)(2,1)S(1)}, u32[]{:S(2)}, u32[]{:S(2)}) collective-permute-start(bf16[512,1024]{1,0:T(8,128)(2,1)S(1)} %add_convert_fusion), channel_id=1, source_target_pairs={{0,1},{1,0},{2,3},{3,2},{4,5},{5,4},{6,7},{7,6},{8,9},{9,8},{10,11... | collective-permute-start | bytes 3145736 | tf_op jit(solution)/shard_map/ppermute | solution.py:30
  362.7 17.6 %collective-permute-start.62 = (bf16[1,2,2,160,512]{4,3,2,1,0:T(8,128)(2,1)S(1)}, bf16[1,2,2,160,512]{4,3,2,1,0:T(8,128)(2,1)S(1)}, u32[]{:S(2)}, u32[]{:S(2)}) collective-permute-start(bf16[1,2,2,160,512]{4,3,2,1,0:T(8,128)(2,1)S(1)} %slice_bitcast_fusion.10), channel_id=1, source_target_pairs={{0,4},{2,6},{4,0},{6,2},{8,12},{10,14},{12,8},{14,10},{16,20},{18,... | collective-permute-start | bytes 1966088 | tf_op jit(solution)/shard_map/ppermute | solution.py:35
  364.1 29.5 %collective-permute-start.59 = (bf16[1,2,2,160,512]{4,3,1,2,0:T(8,128)(2,1)S(1)}, bf16[1,2,2,160,512]{4,3,1,2,0:T(8,128)(2,1)S(1)}, u32[]{:S(2)}, u32[]{:S(2)}) collective-permute-start(bf16[1,2,2,160,512]{4,3,1,2,0:T(8,128)(2,1)S(1)} %slice_bitcast_fusion.12), channel_id=1, source_target_pairs={{0,4},{2,6},{4,0},{6,2},{8,12},{10,14},{12,8},{14,10},{16,20},{18,... | collective-permute-start | bytes 1966088 | tf_op jit(solution)/shard_map/ppermute | solution.py:35
  364.8 30.6 %collective-permute-start.60 = (bf16[1,2,2,176,512]{4,3,2,1,0:T(8,128)(2,1)S(1)}, bf16[1,2,2,176,512]{4,3,2,1,0:T(8,128)(2,1)S(1)}, u32[]{:S(2)}, u32[]{:S(2)}) collective-permute-start(bf16[1,2,2,176,512]{4,3,2,1,0:T(8,128)(2,1)S(1)} %slice_bitcast_fusion.4), channel_id=1, source_target_pairs={{0,8},{2,10},{4,12},{6,14},{8,0},{10,2},{12,4},{14,6},{16,24},{18,... | collective-permute-start | bytes 2162696 | tf_op jit(solution)/shard_map/ppermute | solution.py:35
  366.2 29.2 %collective-permute-start.61 = (bf16[1,2,2,176,512]{4,3,2,1,0:T(8,128)(2,1)S(1)}, bf16[1,2,2,176,512]{4,3,2,1,0:T(8,128)(2,1)S(1)}, u32[]{:S(2)}, u32[]{:S(2)}) collective-permute-start(bf16[1,2,2,176,512]{4,3,2,1,0:T(8,128)(2,1)S(1)} %slice_bitcast_fusion.2), channel_id=1, source_target_pairs={{0,2},{2,0},{4,6},{6,4},{8,10},{10,8},{12,14},{14,12},{16,18},{18,... | collective-permute-start | bytes 2162696 | tf_op jit(solution)/shard_map/ppermute | solution.py:35
  380.4 18.8 %collective-permute-start.57 = (bf16[1,2,2,176,512]{4,3,2,1,0:T(8,128)(2,1)S(1)}, bf16[1,2,2,176,512]{4,3,2,1,0:T(8,128)(2,1)S(1)}, u32[]{:S(2)}, u32[]{:S(2)}) collective-permute-start(bf16[1,2,2,176,512]{4,3,2,1,0:T(8,128)(2,1)S(1)} %slice_bitcast_fusion.8), channel_id=1, source_target_pairs={{0,8},{2,10},{4,12},{6,14},{8,0},{10,2},{12,4},{14,6},{16,24},{18,... | collective-permute-start | bytes 2162696 | tf_op jit(solution)/shard_map/ppermute | solution.py:35
  393.6 19.1 %collective-permute-start.58 = (bf16[1,2,2,176,512]{4,3,1,2,0:T(8,128)(2,1)S(1)}, bf16[1,2,2,176,512]{4,3,1,2,0:T(8,128)(2,1)S(1)}, u32[]{:S(2)}, u32[]{:S(2)}) collective-permute-start(bf16[1,2,2,176,512]{4,3,1,2,0:T(8,128)(2,1)S(1)} %slice_bitcast_fusion.6), channel_id=1, source_target_pairs={{0,2},{2,0},{4,6},{6,4},{8,10},{10,8},{12,14},{14,12},{16,18},{18,... | collective-permute-start | bytes 2162696 | tf_op jit(solution)/shard_map/ppermute | solution.py:35
  395.9 29.8 %collective-permute-start.65 = (bf16[1,2,160,512]{3,2,1,0:T(8,128)(2,1)S(1)}, bf16[1,2,160,512]{3,2,1,0:T(8,128)(2,1)S(1)}, u32[]{:S(2)}, u32[]{:S(2)}) collective-permute-start(bf16[1,2,160,512]{3,2,1,0:T(8,128)(2,1)S(1)} %slice_bitcast_fusion.21), channel_id=1, source_target_pairs={{0,2},{2,0},{4,6},{6,4},{8,10},{10,8},{12,14},{14,12},{16,18},{18,... | collective-permute-start | bytes 983048 | tf_op jit(solution)/shard_map/ppermute | solution.py:35
  398.0 52.8 %collective-permute-start.64 = (bf16[1,2,176,512]{3,2,1,0:T(8,128)(2,1)}, bf16[1,2,176,512]{3,2,1,0:T(8,128)(2,1)}, u32[]{:S(2)}, u32[]{:S(2)}) collective-permute-start(bf16[1,2,176,512]{3,2,1,0:T(8,128)(2,1)} %slice_bitcast_fusion.17), channel_id=1, source_target_pairs={{0,8},{2,10},{4,12},{6,14},{8,0},{10,2},{12,4},{14,6},{16,24},{18,... | collective-permute-start | bytes 1081352 | tf_op jit(solution)/shard_map/ppermute | solution.py:35
  399.2 52.7 %collective-permute-start.63 = (bf16[1,2,176,512]{3,2,1,0:T(8,128)(2,1)}, bf16[1,2,176,512]{3,2,1,0:T(8,128)(2,1)}, u32[]{:S(2)}, u32[]{:S(2)}) collective-permute-start(bf16[1,2,176,512]{3,2,1,0:T(8,128)(2,1)} %slice_bitcast_fusion.18), channel_id=1, source_target_pairs={{0,4},{2,6},{4,0},{6,2},{8,12},{10,14},{12,8},{14,10},{16,20},{18,... | collective-permute-start | bytes 1081352 | tf_op jit(solution)/shard_map/ppermute | solution.py:35
  423.3 158.9 %collective-permute-start.53 = (f32[512,1024]{1,0:T(8,128)S(1)}, f32[512,1024]{1,0:T(8,128)}, u32[]{:S(2)}, u32[]{:S(2)}) collective-permute-start(f32[512,1024]{1,0:T(8,128)S(1)} %multiply_add_fusion), channel_id=1, source_target_pairs={{0,1},{1,0},{2,3},{3,2},{4,5},{5,4},{6,7},{7,6},{8,9},{9,8},{10,11... | collective-permute-start | bytes 6291464 | tf_op jit(solution)/shard_map/ppermute | solution.py:30
  442.0 5.7 collective-permute-start.55
  447.4 91.0 %collective-permute-start.76 = (bf16[16,48,1024]{2,1,0:T(8,128)(2,1)}, bf16[16,48,1024]{2,1,0:T(8,128)(2,1)}, u32[]{:S(2)}, u32[]{:S(2)}) collective-permute-start(bf16[16,48,1024]{2,1,0:T(8,128)(2,1)} %dynamic-slice_bitcast_fusion), channel_id=1, source_target_pairs={{0,1},{1,0},{2,3},{3,2},{4,5},{5,4},{6,7},{7,6},{8,9},{9,8},{10,11... | collective-permute-start | bytes 4718600 | tf_op jit(solution)/shard_map/ppermute | solution.py:30
  453.0 6.9 %collective-permute-start.68 = (bf16[1,160,512]{2,1,0:T(8,128)(2,1)S(1)}, bf16[1,160,512]{2,1,0:T(8,128)(2,1)S(1)}, u32[]{:S(2)}, u32[]{:S(2)}) collective-permute-start(bf16[1,160,512]{2,1,0:T(8,128)(2,1)S(1)} %slice_bitcast_fusion.27), channel_id=1, source_target_pairs={{0,8},{2,10},{4,12},{6,14},{8,0},{10,2},{12,4},{14,6},{16,24},{18,... | collective-permute-start | bytes 491528 | tf_op jit(solution)/shard_map/ppermute | solution.py:35
  455.0 6.4 %collective-permute-start.67 = (bf16[1,176,512]{2,1,0:T(8,128)(2,1)S(1)}, bf16[1,176,512]{2,1,0:T(8,128)(2,1)S(1)}, u32[]{:S(2)}, u32[]{:S(2)}) collective-permute-start(bf16[1,176,512]{2,1,0:T(8,128)(2,1)S(1)} %slice_bitcast_fusion.24), channel_id=1, source_target_pairs={{0,4},{2,6},{4,0},{6,2},{8,12},{10,14},{12,8},{14,10},{16,20},{18,... | collective-permute-start | bytes 540680 | tf_op jit(solution)/shard_map/ppermute | solution.py:35
  464.4 16.0 %collective-permute-start.71 = (bf16[1,2,160,512]{3,2,1,0:T(8,128)(2,1)S(1)}, bf16[1,2,160,512]{3,2,1,0:T(8,128)(2,1)S(1)}, u32[]{:S(2)}, u32[]{:S(2)}) collective-permute-start(bf16[1,2,160,512]{3,2,1,0:T(8,128)(2,1)S(1)} %slice_bitcast_fusion.20), channel_id=1, source_target_pairs={{0,2},{2,0},{4,6},{6,4},{8,10},{10,8},{12,14},{14,12},{16,18},{18,... | collective-permute-start | bytes 983048 | tf_op jit(solution)/shard_map/ppermute | solution.py:35
  465.7 7.5 %collective-permute-start.100 = (f32[226,128]{1,0:T(8,128)S(1)}, f32[226,128]{1,0:T(8,128)S(1)}, u32[]{:S(2)}, u32[]{:S(2)}) collective-permute-start(f32[226,128]{1,0:T(8,128)S(1)} %fusion.238), channel_id=1, source_target_pairs={{0,8},{2,10},{4,12},{6,14},{8,0},{10,2},{12,4},{14,6},{16,24},{18,... | collective-permute-start | bytes 347144 | tf_op jit(solution)/shard_map/ppermute | solution.py:35
  467.0 14.9 %collective-permute-start.70 = (bf16[1,2,176,512]{3,2,1,0:T(8,128)(2,1)S(1)}, bf16[1,2,176,512]{3,2,1,0:T(8,128)(2,1)S(1)}, u32[]{:S(2)}, u32[]{:S(2)}) collective-permute-start(bf16[1,2,176,512]{3,2,1,0:T(8,128)(2,1)S(1)} %slice_bitcast_fusion.15), channel_id=1, source_target_pairs={{0,8},{2,10},{4,12},{6,14},{8,0},{10,2},{12,4},{14,6},{16,24},{18,... | collective-permute-start | bytes 1081352 | tf_op jit(solution)/shard_map/ppermute | solution.py:35
  473.2 7.1 %collective-permute-start.101 = (f32[226,128]{1,0:T(8,128)S(1)}, f32[226,128]{1,0:T(8,128)S(1)}, u32[]{:S(2)}, u32[]{:S(2)}) collective-permute-start(f32[226,128]{1,0:T(8,128)S(1)} %add.671), channel_id=1, source_target_pairs={{0,16},{2,18},{4,20},{6,22},{8,24},{10,26},{12,28},{14,30},{16,0},... | collective-permute-start | bytes 347144 | tf_op jit(solution)/shard_map/ppermute | solution.py:35
  480.3 54.0 %collective-permute-start.56 = (f32[512,512]{1,0:T(8,128)}, f32[512,512]{1,0:T(8,128)}, u32[]{:S(2)}, u32[]{:S(2)}) collective-permute-start(f32[512,512]{1,0:T(8,128)} %get-tuple-element.218), channel_id=1, source_target_pairs={{0,1},{1,0},{2,3},{3,2},{4,5},{5,4},{6,7},{7,6},{8,9},{9,8},{10,11... | collective-permute-start | bytes 3145736 | tf_op jit(solution)/shard_map/ppermute | solution.py:30
  480.4 10.9 %collective-permute-start.69 = (bf16[1,2,176,512]{3,2,1,0:T(8,128)(2,1)S(1)}, bf16[1,2,176,512]{3,2,1,0:T(8,128)(2,1)S(1)}, u32[]{:S(2)}, u32[]{:S(2)}) collective-permute-start(bf16[1,2,176,512]{3,2,1,0:T(8,128)(2,1)S(1)} %slice_bitcast_fusion.16), channel_id=1, source_target_pairs={{0,4},{2,6},{4,0},{6,2},{8,12},{10,14},{12,8},{14,10},{16,20},{18,... | collective-permute-start | bytes 1081352 | tf_op jit(solution)/shard_map/ppermute | solution.py:35
  481.8 43.5 %collective-permute-start.75 = (bf16[1,512,512]{2,1,0:T(8,128)(2,1)}, bf16[1,512,512]{2,1,0:T(8,128)(2,1)}, u32[]{:S(2)}, u32[]{:S(2)}) collective-permute-start(bf16[1,512,512]{2,1,0:T(8,128)(2,1)} %pad_maximum_fusion.22), channel_id=1, source_target_pairs={{0,16},{2,18},{4,20},{6,22},{8,24},{10,26},{12,28},{14,30},{16,0},... | collective-permute-start | bytes 1572872 | tf_op jit(solution)/shard_map/ppermute | solution.py:35
  494.2 17.9 %collective-permute-start.74 = (bf16[1,160,512]{2,1,0:T(8,128)(2,1)}, bf16[1,160,512]{2,1,0:T(8,128)(2,1)}, u32[]{:S(2)}, u32[]{:S(2)}) collective-permute-start(bf16[1,160,512]{2,1,0:T(8,128)(2,1)} %slice_bitcast_fusion.26), channel_id=1, source_target_pairs={{0,8},{2,10},{4,12},{6,14},{8,0},{10,2},{12,4},{14,6},{16,24},{18,... | collective-permute-start | bytes 491528 | tf_op jit(solution)/shard_map/ppermute | solution.py:35
  512.1 7.0 %collective-permute-start.73 = (bf16[1,176,512]{2,1,0:T(8,128)(2,1)S(1)}, bf16[1,176,512]{2,1,0:T(8,128)(2,1)S(1)}, u32[]{:S(2)}, u32[]{:S(2)}) collective-permute-start(bf16[1,176,512]{2,1,0:T(8,128)(2,1)S(1)} %copy-done.93), channel_id=1, source_target_pairs={{0,4},{2,6},{4,0},{6,2},{8,12},{10,14},{12,8},{14,10},{16,20},{18,... | collective-permute-start | bytes 540680 | tf_op jit(solution)/shard_map/ppermute | solution.py:35
  519.1 6.2 %collective-permute-start.72 = (bf16[1,176,512]{2,1,0:T(8,128)(2,1)S(1)}, bf16[1,176,512]{2,1,0:T(8,128)(2,1)S(1)}, u32[]{:S(2)}, u32[]{:S(2)}) collective-permute-start(bf16[1,176,512]{2,1,0:T(8,128)(2,1)S(1)} %copy-done.92), channel_id=1, source_target_pairs={{0,2},{2,0},{4,6},{6,4},{8,10},{10,8},{12,14},{14,12},{16,18},{18,... | collective-permute-start | bytes 540680 | tf_op jit(solution)/shard_map/ppermute | solution.py:35
  546.7 6.2 %collective-permute-start.80 = (bf16[1,2,2,16,1024]{4,3,2,1,0:T(8,128)(2,1)S(1)}, bf16[1,2,2,16,1024]{4,3,2,1,0:T(8,128)(2,1)S(1)}, u32[]{:S(2)}, u32[]{:S(2)}) collective-permute-start(bf16[1,2,2,16,1024]{4,3,2,1,0:T(8,128)(2,1)S(1)} %slice_bitcast_fusion.32), channel_id=1, source_target_pairs={{0,8},{2,10},{4,12},{6,14},{8,0},{10,2},{12,4},{14,6},{16,24},{18,... | collective-permute-start | bytes 393224 | tf_op jit(solution)/shard_map/ppermute | solution.py:35
  548.2 6.0 %collective-permute-start.81 = (bf16[1,2,2,16,1024]{4,3,2,1,0:T(8,128)(2,1)S(1)}, bf16[1,2,2,16,1024]{4,3,2,1,0:T(8,128)(2,1)S(1)}, u32[]{:S(2)}, u32[]{:S(2)}) collective-permute-start(bf16[1,2,2,16,1024]{4,3,2,1,0:T(8,128)(2,1)S(1)} %slice_bitcast_fusion.30), channel_id=1, source_target_pairs={{0,2},{2,0},{4,6},{6,4},{8,10},{10,8},{12,14},{14,12},{16,18},{18,... | collective-permute-start | bytes 393224 | tf_op jit(solution)/shard_map/ppermute | solution.py:35
  549.1 5.7 collective-permute-start.82
  550.3 9.9 %collective-permute-start.77 = (bf16[1,2,2,16,1024]{4,3,2,1,0:T(8,128)(2,1)S(1)}, bf16[1,2,2,16,1024]{4,3,2,1,0:T(8,128)(2,1)S(1)}, u32[]{:S(2)}, u32[]{:S(2)}) collective-permute-start(bf16[1,2,2,16,1024]{4,3,2,1,0:T(8,128)(2,1)S(1)} %slice_bitcast_fusion.38), channel_id=1, source_target_pairs={{0,8},{2,10},{4,12},{6,14},{8,0},{10,2},{12,4},{14,6},{16,24},{18,... | collective-permute-start | bytes 393224 | tf_op jit(solution)/shard_map/ppermute | solution.py:35
  573.6 8.4 %collective-permute-start.95 = (bf16[1,48,1024]{2,1,0:T(8,128)(2,1)S(1)}, bf16[1,48,1024]{2,1,0:T(8,128)(2,1)S(1)}, u32[]{:S(2)}, u32[]{:S(2)}) collective-permute-start(bf16[1,48,1024]{2,1,0:T(8,128)(2,1)S(1)} %pad_maximum_fusion.38), channel_id=1, source_target_pairs={{0,16},{2,18},{4,20},{6,22},{8,24},{10,26},{12,28},{14,30},{16,0},... | collective-permute-start | bytes 294920 | tf_op jit(solution)/shard_map/ppermute | solution.py:35
  (194 other events, 2413.5 us)

commit v2 on v1

--- a/solution.py
+++ b/solution.py
@@ -68,37 +68,29 @@
     ]
 
 
-def spread_close(parts):
+def spread_last(parts):
+    return [(part, swap_bit(part, axis_orders[index][2])) for index, part in enumerate(parts)]
+
+
+def split_rows(array, cuts):
+    return [array[..., cuts[i] : cuts[i + 1], :] for i in range(3)]
+
+
+def spread_close(pairs):
     pieces = []
-    for index, part in enumerate(parts):
+    for index, pair in enumerate(pairs):
         order = axis_orders[index]
         held = [order[2], order[1], order[0]]
         axes = [3] + [held.index(bit) for bit in (2, 1, 0)] + [4, 5]
-        pieces.append(part.transpose(axes))
+        pieces.append(jnp.stack(pair).transpose(axes))
     return jnp.concatenate(pieces, axis=4)
 
 
-def gather_relative(block):
-    count = lax.axis_size("dp")
-    rows, columns = block.shape
+def spread_high(block):
     held = block[None]
-    for bit in range(4, bit_count(count)):
+    for bit in range(4, bit_count(lax.axis_size("dp"))):
         held = jnp.concatenate([held, swap_bit(held, bit)], axis=0)
-    cuts = third_cuts(rows)
-    split = lambda array: [array[:, cuts[i] : cuts[i + 1]] for i in range(3)]
-    far = swap_bit(held, 3)
-    near_parts = spread_step(split(held), 0)
-    near_parts = spread_step(list(tie(*near_parts)), 1)
-    tied = tie(far, *near_parts)
-    far, near_parts = tied[0], list(tied[1:])
-    near_parts = spread_step(near_parts, 2)
-    far_parts = spread_step(split(far), 0)
-    tied = tie(*near_parts, *far_parts)
-    near_parts, far_parts = list(tied[:3]), list(tied[3:])
-    far_parts = spread_step(far_parts, 1)
-    far_parts = spread_step(list(tie(*far_parts)), 2)
-    near, far = spread_close(near_parts), spread_close(far_parts)
-    return jnp.stack([near, far], axis=1).reshape(count, rows, columns)
+    return held
 
 
 def add_low(left, right):
@@ -117,35 +109,21 @@
     return folded
 
 
-def scatter_relative(full):
-    count, rows, columns = full.shape
-    bits = bit_count(count)
-    near, far = [
-        full.reshape(count // 16, 2, 2, 2, 2, rows, columns)[:, i] for i in range(2)
-    ]
-    cuts = third_cuts(rows)
-    split = lambda array: [array[..., cuts[i] : cuts[i + 1], :] for i in range(3)]
-    near_parts, far_parts = split(near), split(far)
-    near_held = [[2, 1, 0] for _ in range(3)]
-    far_held = [[2, 1, 0] for _ in range(3)]
-    far_parts = fold_step(far_parts, far_held, 2)
-    far_parts = fold_step(list(tie(*far_parts)), far_held, 1)
-    far_parts = fold_step(list(tie(*far_parts)), far_held, 0)
-    near_parts = fold_step(near_parts, near_held, 2)
-    tied = tie(*near_parts, *far_parts)
-    near_parts, far_parts = list(tied[:3]), list(tied[3:])
-    far_sum = swap_bit(jnp.concatenate(far_parts, axis=-2), 3)
-    near_parts = fold_step(near_parts, near_held, 1)
-    near_parts = fold_step(list(tie(*near_parts)), near_held, 0)
-    near_sum = jnp.concatenate(near_parts, axis=-2)
-    if bits == 4:
-        return near_sum[0].astype(f32) + far_sum[0].astype(f32)
-    total = add_low(near_sum, far_sum)
-    for bit in range(bits - 1, 3, -1):
-        half = 1 << (bit - 4)
-        total = total[:half].astype(f32) + swap_bit(total[half:], bit).astype(f32)
-        if bit > 4:
-            total = total.astype(bf16)
+def fold_first(pairs):
+    return [add_low(keep, swap_bit(send, axis_orders[index][2])) for index, (keep, send) in enumerate(pairs)]
+
+
+def fold_next(parts, phase):
+    return [add_low(part[0], swap_bit(part[1], axis_orders[index][phase])) for index, part in enumerate(parts)]
+
+
+def fold_high(total):
+    count = total.shape[0]
+    if count == 1:
+        return total[0]
+    for bit in range(bit_count(count) - 1, -1, -1):
+        half = 1 << bit
+        total = total[:half] + swap_bit(total[half:].astype(bf16), bit + 4).astype(f32)
     return total[0]
 
 
@@ -182,15 +160,12 @@
     return values * cosine + partner * sine
 
 
-def attend_kernel(q_ref, k_ref, v_ref, cos_ref, sin_ref, bias_ref, o_ref, qa_ref, kr_ref):
+def attend_kernel(q_ref, k_ref, v_ref, bias_ref, o_ref, qa_ref):
     lane = lax.broadcasted_iota(jnp.int32, (LEN, PAIR), 1)
     lane_rows = lax.broadcasted_iota(jnp.int32, (ROWS, PAIR), 1)
     row_index = lax.broadcasted_iota(jnp.int32, (PAIR, ROWS), 0)
-    cosine, sine = cos_ref[...], sin_ref[...]
-    q_turned = (rotate(q_ref[...], cosine, sine, lane).astype(bf16).astype(f32) * 0.125)
-    k_turned = rotate(k_ref[...], cosine, sine, lane).astype(bf16)
-    kr_ref[...] = k_turned
-    k_wide = k_turned.astype(f32)
+    q_wide = q_ref[...].astype(f32)
+    k_wide = k_ref[...].astype(f32)
     values_t = v_ref[...].T
     bias = bias_ref[...].astype(f32)
     keys = []
@@ -198,28 +173,36 @@
         own = lane // HEAD == head
         spare = (1 - head) * HEAD
         keys.append(
-            jnp.where(
-                own, k_wide, jnp.where(lane == spare, bias, 0.0)
-            ).astype(bf16)
+            jnp.where(own, k_wide, jnp.where(lane == spare, bias, 0.0)).astype(bf16)
         )
         qa_ref[:, head * PAIR : (head + 1) * PAIR] = jnp.where(
-            own, q_turned, jnp.where(lane == spare, 1.0, 0.0)
+            own, q_wide, jnp.where(lane == spare, 1.0, 0.0)
         ).astype(bf16)
-    for block in range(LEN // ROWS):
+    steps = [(block, head) for block in range(LEN // ROWS) for head in range(2)]
+
+    def scores_of(step):
+        block, head = step
         rows = slice(block * ROWS, (block + 1) * ROWS)
-        outs = []
-        extra = jnp.zeros((PAIR, ROWS), f32)
-        for head in range(2):
-            spare = (1 - head) * HEAD
-            q_block = qa_ref[rows, head * PAIR : (head + 1) * PAIR]
-            scores = dot32(keys[head], q_block, NT)
-            highest = jnp.max(scores, axis=0, keepdims=True)
-            weights = jnp.exp(scores - highest)
-            total = jnp.sum(weights, axis=0, keepdims=True)
-            out_t = dot32(values_t[head * HEAD : (head + 1) * HEAD], weights.astype(bf16))
-            outs.append(out_t / total)
-            for place, term in enumerate(three_terms(highest + jnp.log(total))):
-                extra = jnp.where(row_index == spare + 1 + place, -term, extra)
+        return dot32(keys[head], qa_ref[rows, head * PAIR : (head + 1) * PAIR], NT)
+
+    following = scores_of(steps[0])
+    for position, (block, head) in enumerate(steps):
+        scores = following
+        if position + 1 < len(steps):
+            following = scores_of(steps[position + 1])
+        rows = slice(block * ROWS, (block + 1) * ROWS)
+        if head == 0:
+            outs, extra = [], jnp.zeros((PAIR, ROWS), f32)
+        spare = (1 - head) * HEAD
+        highest = jnp.max(scores, axis=0, keepdims=True)
+        weights = jnp.exp(scores - highest)
+        total = jnp.sum(weights, axis=0, keepdims=True)
+        out_t = dot32(values_t[head * HEAD : (head + 1) * HEAD], weights.astype(bf16))
+        outs.append(out_t / total)
+        for place, term in enumerate(three_terms(highest + jnp.log(total))):
+            extra = jnp.where(row_index == spare + 1 + place, -term, extra)
+        if head == 0:
+            continue
         o_ref[rows, :] = jnp.concatenate(outs, axis=0).T.astype(bf16)
         extra_t = extra.T
         for head in range(2):
@@ -231,7 +214,7 @@
             ).astype(bf16)
 
 
-def attend_forward(queries, keys, values, cosine, sine, bias):
+def attend_forward(queries, keys, values, bias):
     width = values.shape[1]
     pairs = width // PAIR
     tall = lambda columns: pl.BlockSpec((LEN, columns), lambda pair: (0, pair))
@@ -239,25 +222,24 @@
     return pl.pallas_call(
         attend_kernel,
         grid=(pairs,),
-        in_specs=[tall(PAIR), tall(PAIR), tall(PAIR), whole, whole, whole],
-        out_specs=[tall(PAIR), tall(2 * PAIR), tall(PAIR)],
+        in_specs=[tall(PAIR), tall(PAIR), tall(PAIR), whole],
+        out_specs=[tall(PAIR), tall(2 * PAIR)],
         out_shape=[
             jax.ShapeDtypeStruct((LEN, width), bf16),
             jax.ShapeDtypeStruct((LEN, 2 * width), bf16),
-            jax.ShapeDtypeStruct((LEN, width), bf16),
         ],
         compiler_params=pltpu.CompilerParams(vmem_limit_bytes=vmem_bytes),
         cost_estimate=pl.CostEstimate(
             flops=2 * 4 * LEN * LEN * width * 4,
-            bytes_accessed=10 * LEN * width * 2,
+            bytes_accessed=6 * LEN * width * 2,
             transcendentals=LEN * LEN * width // HEAD,
         ),
         name="attend",
-    )(queries, keys, values, cosine, sine, bias)
+    )(queries, keys, values, bias)
 
 
 def attend_back_kernel(
-    qa_ref, kr_ref, v_ref, do_ref, o_ref, cos_ref, sin_ref, bias_ref,
+    qa_ref, kr_ref, v_ref, o_ref, mine_ref, other_ref, weight_ref, cos_ref, sin_ref, bias_ref,
     dq_ref, dk_ref, dv_ref, doa_ref, dka_ref, dva_ref,
 ):
     lane = lax.broadcasted_iota(jnp.int32, (LEN, PAIR), 1)
@@ -266,7 +248,10 @@
     k_wide = kr_ref[...].astype(f32)
     keys_t = kr_ref[...].T
     v_wide = v_ref[...].astype(f32)
-    do_wide = do_ref[...].astype(f32)
+    do_wide = jnp.concatenate(
+        [dot32(ref[...], weight_ref[0]).astype(bf16).astype(f32) for ref in (mine_ref, other_ref)],
+        axis=0,
+    )
     bias = bias_ref[...].astype(f32)
     product = do_wide * o_ref[...].astype(f32)
     keys, values = [], []
@@ -311,15 +296,19 @@
     dv_ref[...] = jnp.where(first, dva_ref[:, :PAIR], dva_ref[:, PAIR:]).astype(bf16)
 
 
-def attend_backward(queries, keys, values, grads, outputs, cosine, sine, bias):
+def attend_backward(queries, keys, values, outputs, grad_mine, grad_other, stacked, cosine, sine, bias):
     width = values.shape[1]
     pairs = width // PAIR
     tall = lambda columns: pl.BlockSpec((LEN, columns), lambda pair: (0, pair))
-    whole = pl.BlockSpec((LEN, PAIR), lambda pair: (0, 0))
+    whole = lambda shape: pl.BlockSpec(shape, lambda pair: (0, 0))
     return pl.pallas_call(
         attend_back_kernel,
         grid=(pairs,),
-        in_specs=[tall(2 * PAIR)] + [tall(PAIR)] * 4 + [whole] * 3,
+        in_specs=[tall(2 * PAIR)]
+        + [tall(PAIR)] * 3
+        + [whole(grad_mine.shape)] * 2
+        + [pl.BlockSpec((1, D, PAIR), lambda pair: (3, 0, pair))]
+        + [whole((LEN, PAIR))] * 3,
         out_specs=[tall(PAIR)] * 3,
         out_shape=[jax.ShapeDtypeStruct((LEN, width), bf16)] * 3,
         scratch_shapes=[
@@ -334,7 +323,275 @@
             transcendentals=LEN * LEN * width // HEAD,
         ),
         name="attend_back",
-    )(queries, keys, values, grads, outputs, cosine, sine, bias)
+    )(queries, keys, values, outputs, grad_mine, grad_other, stacked, cosine, sine, bias)
+
+
+def part_place(slot, index, high_count):
+    bit = lambda which: (slot >> which) & 1
+    order = axis_orders[index]
+    lead = (bit(order[1]) * 2 + bit(order[0])) * high_count + (slot >> 4)
+    return bit(3), bit(order[2]), lead
+
+
+def project_kernel(high_count, panel_rows, cuts, slots_ref, *refs):
+    parts, refs = refs[:12], refs[12:]
+    mine_ref, other_ref, cos_ref, sin_ref, q_ref, k_ref, v_ref, out_ref, held, in_sems, out_sem = refs
+    per_block = D // panel_rows
+
+    def fetch(panel, carry):
+        slot = slots_ref[panel]
+        group = jnp.minimum(panel // per_block, 3)
+        for index in range(3):
+            far, last, lead = part_place(slot, index, high_count)
+            rows = cuts[index + 1] - cuts[index]
+            start = pl.multiple_of(panel * panel_rows + cuts[index], 16)
+            for which in range(4):
+
+                @pl.when(far * 2 + last == which)
+                def _():
+                    pltpu.make_async_copy(
+                        parts[which * 3 + index].at[lead], held.at[pl.ds(start, rows)], in_sems.at[group]
+                    ).start()
+
+        return carry
+
+    lax.fori_loop(0, 8 * per_block, fetch, 0)
+    half = mine_ref.shape[0]
+    width = held.shape[1]
+    lane = lax.broadcasted_iota(jnp.int32, (half, PAIR), 1)
+    for block, ref in enumerate((q_ref, k_ref, v_ref)):
+        place = pl.ds(block * D, D)
+        pltpu.make_async_copy(held.at[place], held.at[place], in_sems.at[block]).wait()
+        pltpu.make_async_copy(held.at[place], out_ref.at[place], out_sem).start()
+        for part, rows_ref in enumerate((mine_ref, other_ref)):
+            rows = slice(part * half, (part + 1) * half)
+            product = dot32(rows_ref[...], held[block * D : (block + 1) * D])
+            if block == 2:
+                ref[rows, :] = product.astype(bf16)
+                continue
+            cosine, sine = cos_ref[rows, :], sin_ref[rows, :]
+            for pair in range(width // PAIR):
+                columns = slice(pair * PAIR, (pair + 1) * PAIR)
+                turned = rotate(product[:, columns], cosine, sine, lane).astype(bf16)
+                if block == 0:
+                    turned = (turned.astype(f32) * 0.125).astype(bf16)
+                ref[rows, columns] = turned
+    place = pl.ds(3 * D, 5 * D)
+    pltpu.make_async_copy(held.at[place], held.at[place], in_sems.at[3]).wait()
+    pltpu.make_async_copy(held.at[place], out_ref.at[place], out_sem).start()
+    pltpu.make_async_copy(held, out_ref, out_sem).wait()
+
+
+def project(near_pairs, far_pairs, slots, panel_rows, cuts, mine, other, cosine, sine):
+    high_count, width = near_pairs[0][0].shape[2], near_pairs[0][0].shape[-1]
+    parts = [
+        pairs[index][last].reshape(-1, cuts[index + 1] - cuts[index], width)
+        for pairs in (near_pairs, far_pairs)
+        for last in range(2)
+        for index in range(3)
+    ]
+    whole = pl.BlockSpec(memory_space=pltpu.VMEM)
+    anywhere = pl.BlockSpec(memory_space=pl.ANY)
+    tall = jax.ShapeDtypeStruct((LEN, width), bf16)
+    return pl.pallas_call(
+        lambda *refs: project_kernel(high_count, panel_rows, cuts, *refs),
+        in_specs=[pl.BlockSpec(memory_space=pltpu.SMEM)] + [anywhere] * 12 + [whole] * 4,
+        out_specs=[whole] * 3 + [anywhere],
+        out_shape=[tall] * 3 + [jax.ShapeDtypeStruct((8 * D, width), bf16)],
+        scratch_shapes=[
+            pltpu.VMEM((8 * D, width), bf16),
+            pltpu.SemaphoreType.DMA((4,)),
+            pltpu.SemaphoreType.DMA,
+        ],
+        compiler_params=pltpu.CompilerParams(vmem_limit_bytes=vmem_bytes),
+        cost_estimate=pl.CostEstimate(
+            flops=2 * LEN * 3 * D * width, bytes_accessed=48 * D * width, transcendentals=0
+        ),
+        name="project",
+    )(slots, *parts, mine, other, cosine, sine)
+
+
+def feed_kernel(n_ref, g_ref, w_ref, f_ref, d_ref, a_ref, u_ref):
+    width = w_ref.shape[2]
+    rows, grads = n_ref[...], g_ref[...]
+    pre = [dot32(rows, w_ref[i]) for i in range(2)]
+    act_grad = [dot32(grads, w_ref[2 + i]) for i in range(2)]
+    acts, pre_grads = [], []
+    for i in range(2):
+        value = pre[i]
+        square = value * value
+        turn = jnp.tanh(0.7978845608028654 * (value + 0.044715 * (square * value)))
+        share = 0.5 * (1.0 + turn)
+        slope = share + (0.5 * value) * (1.0 - turn * turn) * (
+            0.7978845608028654 + (3 * 0.044715 * 0.7978845608028654) * square
+        )
+        acts.append((value * share).astype(bf16))
+        pre_grads.append((act_grad[i] * slope).astype(bf16))
+        a_ref[:, i * width : (i + 1) * width] = acts[i]
+        u_ref[:, i * width : (i + 1) * width] = pre_grads[i]
+    f_ref[...] = (dot32(acts[0], w_ref[2], NT) + dot32(acts[1], w_ref[3], NT)).astype(f_ref.dtype)
+    d_ref[...] = (dot32(pre_grads[0], w_ref[0], NT) + dot32(pre_grads[1], w_ref[1], NT)).astype(d_ref.dtype)
+
+
+def feed(rows, grads, stacked, kind):
+    half, width = rows.shape[0], stacked.shape[2]
+    whole = pl.BlockSpec((half, D), lambda step: (0, 0))
+    low, sums = jax.ShapeDtypeStruct((half, D), bf16), jax.ShapeDtypeStruct((half, D), kind)
+    return pl.pallas_call(
+        feed_kernel,
+        grid=(1,),
+        in_specs=[whole, whole, pl.BlockSpec((4, D, width), lambda step: (1, 0, 0))],
+        out_specs=[whole] * 4,
+        out_shape=[sums, sums, low, low],
+        compiler_params=pltpu.CompilerParams(vmem_limit_bytes=vmem_bytes),
+        cost_estimate=pl.CostEstimate(
+            flops=2 * 4 * half * D * D, bytes_accessed=16 * D * width, transcendentals=half * D
+        ),
+        name="feed",
+    )(rows, grads, stacked)
+
+
+def inputs_grad_kernel(q_ref, k_ref, v_ref, w_ref, mine_ref, other_ref):
+    half = mine_ref.shape[0]
+    for start, out_ref in ((half, other_ref), (0, mine_ref)):
+        rows = slice(start, start + half)
+        total = dot32(q_ref[rows, :], w_ref[0], NT)
+        total = total + dot32(k_ref[rows, :], w_ref[1], NT)
+        total = total + dot32(v_ref[rows, :], w_ref[2], NT)
+        out_ref[...] = total.astype(out_ref.dtype)
+
+
+def inputs_grad(query_grad, key_grad, value_grad, stacked):
+    width = stacked.shape[2]
+    half = LEN // 2
+    tall = pl.BlockSpec((LEN, width), lambda step: (0, 0))
+    out = pl.BlockSpec((half, D), lambda step: (0, 0))
+    return pl.pallas_call(
+        inputs_grad_kernel,
+        grid=(1,),
+        in_specs=[tall] * 3 + [pl.BlockSpec((3, D, width), lambda step: (0, 0, 0))],
+        out_specs=[out, out],
+        out_shape=[jax.ShapeDtypeStruct((half, D), f32), jax.ShapeDtypeStruct((half, D), bf16)],
+        compiler_params=pltpu.CompilerParams(vmem_limit_bytes=vmem_bytes),
+        cost_estimate=pl.CostEstimate(
+            flops=2 * 3 * LEN * D * width, bytes_accessed=12 * LEN * D, transcendentals=0
+        ),
+        name="inputs_grad",
+    )(query_grad, key_grad, value_grad, stacked)
+
+
+def gradients_kernel(high_count, panel_rows, cuts, lefts, rights, uses, slots_ref, *refs):
+    in_count = sum(len(pieces) for pieces in lefts + rights)
+    inputs, refs = refs[:in_count], refs[in_count:]
+    parts, refs = refs[:12], refs[12:]
+    left_held, right_held = refs[: len(lefts)], refs[len(lefts) : len(lefts) + len(rights)]
+    turned, block_ref, in_sems, out_sems = refs[len(lefts) + len(rights) :]
+    side = block_ref.shape[1]
+    operands = [(held, pieces) for held, pieces in zip(left_held + right_held, lefts + rights)]
+
+    def load(operand):
+        held, pieces = operands[operand]
+        return [
+            pltpu.make_async_copy(
+                inputs[which],
+                held.at[pl.ds(row, inputs[which].shape[0]), pl.ds(column, inputs[which].shape[1])],
+                in_sems.at[operand],
+            )
+            for row, column, which in pieces
+        ]
+
+    order = []
+    for left, right, right_start in uses:
+        for operand in (left, len(lefts) + right):
+            if operand not in order:
+                order.append(operand)
+    for operand in order:
+        for copy in load(operand):
+            copy.start()
+    ready = set()
+    pieces = side // panel_rows
+    block = 0
+    for left, right, right_start in uses:
+        for operand in (left, len(lefts) + right):
+            if operand not in ready:
+                held = operands[operand][0]
+                pltpu.make_async_copy(held, held, in_sems.at[operand]).wait()
+                ready.add(operand)
+                if operand < len(lefts):
+                    turned[left % 2] = held[...].T
+        for left_start in range(0, D, side):
+            place = block % 2
+            if block >= 2:
+                pltpu.make_async_copy(block_ref.at[place], block_ref.at[place], out_sems.at[place]).wait()
+            block_ref[place] = dot32(
+                turned[left % 2, left_start : left_start + side],
+                right_held[right][:, right_start : right_start + side],
+            ).astype(bf16)
+
+            def send(piece, carry, block=block, place=place):
+                slot = slots_ref[block * pieces + piece]
+                for index in range(3):
+                    far, last, lead = part_place(slot, index, high_count)
+                    rows = cuts[index + 1] - cuts[index]
+                    start = pl.multiple_of(piece * panel_rows + cuts[index], 16)
+                    for which in range(4):
+
+                        @pl.when(far * 2 + last == which)
+                        def _():
+                            pltpu.make_async_copy(
+                                block_ref.at[place, pl.ds(start, rows)],
+                                parts[which * 3 + index].at[lead],
+                                out_sems.at[place],
+                            ).start()
+
+                return carry
+
+            lax.fori_loop(0, pieces, send, 0)
+            block += 1
+    for place in range(2):
+        pltpu.make_async_copy(block_ref.at[place], block_ref.at[place], out_sems.at[place]).wait()
+
+
+def panel_gradients(lefts, rights, uses, slots, panel_rows, cuts, high_count, width):
+    arrays, numbered = [], []
+    for operands in (lefts, rights):
+        made = []
+        for pieces in operands:
+            made.append([(row, column, len(arrays) + i) for i, (row, column, _) in enumerate(pieces)])
+            arrays.extend(array for _, _, array in pieces)
+        numbered.append(made)
+    extent = lambda pieces: max(column + array.shape[1] for _, column, array in pieces)
+    outs = [
+        jax.ShapeDtypeStruct((4 * high_count, cuts[index + 1] - cuts[index], width), bf16)
+        for _ in range(4)
+        for index in range(3)
+    ]
+    outs = pl.pallas_call(
+        lambda *refs: gradients_kernel(
+            high_count, panel_rows, cuts, numbered[0], numbered[1], uses, *refs
+        ),
+        in_specs=[pl.BlockSpec(memory_space=pltpu.SMEM)]
+        + [pl.BlockSpec(memory_space=pl.ANY)] * len(arrays),
+        out_specs=[pl.BlockSpec(memory_space=pl.ANY)] * 12,
+        out_shape=outs,
+        scratch_shapes=[pltpu.VMEM((LEN, extent(pieces)), bf16) for pieces in list(lefts) + list(rights)]
+        + [
+            pltpu.VMEM((2, D, LEN), bf16),
+            pltpu.VMEM((2, width, width), bf16),
+            pltpu.SemaphoreType.DMA((len(lefts) + len(rights),)),
+            pltpu.SemaphoreType.DMA((2,)),
+        ],
+        compiler_params=pltpu.CompilerParams(vmem_limit_bytes=vmem_bytes),
+        cost_estimate=pl.CostEstimate(
+            flops=2 * LEN * len(uses) * D * width,
+            bytes_accessed=24 * LEN * D,
+            transcendentals=0,
+        ),
+        name="gradients",
+    )(slots, *arrays)
+    shaped = [out.reshape((2, 2, high_count) + out.shape[1:]) for out in outs]
+    pairs = lambda far: [(shaped[far * 6 + index], shaped[far * 6 + 3 + index]) for index in range(3)]
+    return pairs(0), pairs(1)
 
 
 def vector_parts(vectors):
@@ -442,21 +699,50 @@
     text_half = text_rows // 2
     relative = jnp.arange(count) ^ me
 
+    high_count = count // 16
+    cuts, text_cuts = third_cuts(panel_rows), third_cuts(text_half)
+    silu_time = jax.nn.silu(time_embedding.astype(f32)).astype(bf16)
+    time_rows = lax.dynamic_slice_in_dim(silu_time, me * share_rows, share_rows, 1)
+    weight_half = lax.dynamic_slice_in_dim(modulation_weight, core * 3 * D, 3 * D, 1).astype(bf16)
     own_rows = lax.dynamic_slice_in_dim(text_matrices, core * text_half, text_half, 0)
-    text_half_all = gather_relative(own_rows.astype(bf16))
+    text_held = spread_high(own_rows.astype(bf16))
+    near_held = spread_high(soap_master.astype(bf16))
+    text_far = swap_bit(text_held, 3)
+    near = spread_step(split_rows(near_held, cuts), 0)
+    text_far, near_held, near_a, near_b, near_c = tie(text_far, near_held, *near)
+    near = [near_a, near_b, near_c]
+    text_parts = split_rows(jnp.concatenate([text_held, text_far], axis=0), text_cuts)
+    far_held = swap_bit(near_held, 3)
+    text_parts = spread_step(text_parts, 0)
+    partial = dot32(time_rows, weight_half)
+    *text_parts, partial = tie(*text_parts, partial)
+    text_parts = spread_step(text_parts, 1)
+    near = spread_step(near, 1)
+    *text_parts, partial = tie(*text_parts, partial)
+    text_pairs = spread_last(text_parts)
+    partial = partial + swap_bit(partial, 0)
+    text_tied = tie(*[part for pair in text_pairs for part in pair], *near, far_held, partial)
+    text_pairs = [text_tied[0:2], text_tied[2:4], text_tied[4:6]]
+    near, far_held, partial = list(text_tied[6:9]), text_tied[9], text_tied[10]
+    near_pairs = spread_last(near)
+    far = spread_step(split_rows(far_held, cuts), 0)
+    partial = partial + swap_bit(partial, 1)
+    *far, partial = tie(*far, partial)
+    far = spread_step(far, 1)
+    partial = partial + swap_bit(partial, 2)
+    *far, partial = tie(*far, partial)
+    far_pairs = spread_last(far)
+    partial = partial + swap_bit(partial, 3)
+    for bit in range(4, bit_count(count)):
+        partial = partial + swap_bit(partial, bit)
+    modulation_half = partial
+    text_half_all = spread_close([[part for part in pair] for pair in text_pairs])
+    text_half_all = text_half_all.reshape(2, high_count, 2, 2, 2, text_half, D)
+    text_half_all = jnp.moveaxis(text_half_all, 0, 1).reshape(count, text_half, D)
     text_other = swap_core(text_half_all)
-    slots = gather_relative(soap_master.astype(bf16))
     texts = take_blocks(by_core(core, text_half_all, text_other, axis=1), relative)
     texts = texts.reshape(3 * TEXT, D)
     expand_weight, shrink_rows, text_to_model = texts[:TEXT], texts[TEXT : 2 * TEXT], texts[2 * TEXT :]
-    stacked = take_blocks(slots, owner_list ^ me).reshape(8, D, width)
-    query_weight, key_weight, value_weight, out_weight = (stacked[i] for i in range(4))
-    hidden_in, hidden_out = stacked[4:6], stacked[6:8]
-
-    silu_time = jax.nn.silu(time_embedding.astype(f32)).astype(bf16)
-    time_rows = lax.dynamic_slice_in_dim(silu_time, me * share_rows, share_rows, 1)
-    weight_half = lax.dynamic_slice_in_dim(modulation_weight, core * 3 * D, 3 * D, 1).astype(bf16)
-    modulation_half = sum_dp(dot32(time_rows, weight_half))
     modulation = by_core(core, modulation_half, swap_core(modulation_half), axis=1)
     (
         kernel,
@@ -504,49 +790,36 @@
     stream = mel_mine + dot32(text_low, text_to_model)
 
     normed_one, scale_norm_one = normalise(stream)
-    first_normed = both_halves((normed_one * (1.0 + scale_one) + shift_one).astype(bf16))
+    first_mine = (normed_one * (1.0 + scale_one) + shift_one).astype(bf16)
+    first_other = swap_core(first_mine)
     cosine, sine = rotary_tables(core, half)
     position = (jnp.arange(LEN) + first) % LEN
     bias = jnp.where(position < lengths[0], 0.0, -1e30).astype(bf16)
     bias = jnp.broadcast_to(bias[:, None], (LEN, PAIR))
-    queries = dot32(first_normed, query_weight)
-    keys = dot32(first_normed, key_weight)
-    value_rows = dot32(first_normed, value_weight).astype(bf16)
-    attended, query_aug, key_rot = attend_forward(queries, keys, value_rows, cosine, sine, bias)
-    attention_out = sum_halves(lambda rows: dot32(rows, out_weight, NT), attended, half)
+    queries, keys, value_rows, stacked = project(
+        near_pairs, far_pairs, owner_list ^ me, panel_rows, cuts, first_mine, first_other, cosine, sine
+    )
+    stacked = stacked.reshape(8, D, width)
+    attended, query_aug = attend_forward(queries, keys, value_rows, bias)
+    attention_out = sum_halves(lambda rows: dot32(rows, stacked[3], NT), attended, half)
     stream_one = stream + gate_one * attention_out
 
     normed_two, scale_norm_two = normalise(stream_one)
-    second_normed = both_halves((normed_two * (1.0 + scale_two) + shift_two).astype(bf16))
-    unit_pre = [dot32(second_normed, hidden_in[i]) for i in range(2)]
-    unit_act, unit_back = zip(*[jax.vjp(gelu_tanh, pre) for pre in unit_pre])
-    unit_low = jnp.concatenate([act.astype(bf16) for act in unit_act], axis=1)
-    unit_out = sum_halves(
-        lambda rows: dot32(rows[:, :width], hidden_out[0], NT) + dot32(rows[:, width:], hidden_out[1], NT),
-        unit_low,
-        half,
-    )
-    output_mine = (stream_one + gate_two * unit_out).astype(bf16)
-    block_output = by_core(core, output_mine, swap_core(output_mine))
-
+    second_mine = (normed_two * (1.0 + scale_two) + shift_two).astype(bf16)
+    second_other = swap_core(second_mine)
     cot_mine = lax.dynamic_slice_in_dim(cotangent, first, half, 0)
     cot_other = lax.dynamic_slice_in_dim(cotangent, half - first, half, 0)
     out_grad = cot_mine.astype(f32)
+    hidden_mine = (gate_two * out_grad).astype(bf16)
+    hidden_other = (gate_two * cot_other.astype(f32)).astype(bf16)
+    their_out, their_grad, act_other, pre_other = feed(second_other, hidden_other, stacked, bf16)
+    their_out, their_grad = swap_core(their_out), swap_core(their_grad)
+    my_out, my_grad, act_mine, pre_mine = feed(second_mine, hidden_mine, stacked, f32)
+    unit_out = my_out + their_out.astype(f32)
+    normed_two_grad = my_grad + their_grad.astype(f32)
+    output_mine = (stream_one + gate_two * unit_out).astype(bf16)
+    block_output = by_core(core, output_mine, swap_core(output_mine))
     gate_two_grad = jnp.sum(out_grad * unit_out, axis=0)
-    hidden_out_grad = jnp.concatenate(
-        [(gate_two * out_grad).astype(bf16), (gate_two * cot_other.astype(f32)).astype(bf16)], axis=0
-    )
-    TN = (((0,), (0,)), ((), ()))
-    out_blocks_grad = [dot32(hidden_out_grad, unit_low[:, i * width : (i + 1) * width], TN) for i in range(2)]
-    pre_grad = [
-        unit_back[i](dot32(hidden_out_grad, hidden_out[i]))[0].astype(bf16) for i in range(2)
-    ]
-    in_blocks_grad = [dot32(second_normed, pre_grad[i], TN) for i in range(2)]
-    normed_two_grad = sum_halves(
-        lambda rows: dot32(rows[:, :width], hidden_in[0], NT) + dot32(rows[:, width:], hidden_in[1], NT),
-        jnp.concatenate(pre_grad, axis=1),
-        half,
-    )
     shift_two_grad = jnp.sum(normed_two_grad, axis=0)
     scale_two_grad = jnp.sum(normed_two_grad * normed_two, axis=0)
     stream_one_grad = out_grad + normalise_back(
@@ -554,27 +827,47 @@
     )
 
     gate_one_grad = jnp.sum(stream_one_grad * attention_out, axis=0)
-    attention_grad = both_halves((gate_one * stream_one_grad).astype(bf16))
-    out_weight_grad = dot32(attention_grad, attended, TN)
-    attended_grad = dot32(attention_grad, out_weight).astype(bf16)
+    TN = (((0,), (0,)), ((), ()))
+    attention_mine = (gate_one * stream_one_grad).astype(bf16)
+    attention_other = swap_core(attention_mine)
     query_grad, key_grad, value_grad = attend_backward(
-        query_aug, key_rot, value_rows, attended_grad, attended, cosine, sine, bias
-    )
-    head_grads = [dot32(first_normed, grad, TN) for grad in (query_grad, key_grad, value_grad)]
-    normed_one_grad = sum_halves(
-        lambda rows: dot32(rows[:, :width], query_weight, NT)
-        + dot32(rows[:, width : 2 * width], key_weight, NT)
-        + dot32(rows[:, 2 * width :], value_weight, NT),
-        jnp.concatenate([query_grad, key_grad, value_grad], axis=1),
-        half,
-    )
-    panel_grad = jnp.concatenate(
-        [grad.astype(bf16) for grad in head_grads + [out_weight_grad] + in_blocks_grad + out_blocks_grad],
-        axis=0,
-    ).reshape(count, panel_rows, width)
-    slot_index = jnp.arange(count)
-    inverse = jnp.sum(jnp.where(owner_list[None, :] == slot_index[:, None], slot_index[None, :], 0), axis=1)
-    own_panel = scatter_relative(take_blocks(panel_grad, jnp.take(inverse, relative, mode="clip")))
+        query_aug, keys, value_rows, attended, attention_mine, attention_other, stacked, cosine, sine, bias
+    )
+    my_grad, their_grad = inputs_grad(query_grad, key_grad, value_grad, stacked)
+    their_grad = swap_core(their_grad)
+    halves = lambda mine, other: [(0, 0, mine), (half, 0, other)]
+    whole = lambda array: [(0, 0, array)]
+    near_pairs, far_pairs = panel_gradients(
+        [
+            halves(first_mine, first_other),
+            halves(attention_mine, attention_other),
+            halves(second_mine, second_other),
+            halves(hidden_mine, hidden_other),
+        ],
+        [
+            whole(query_grad),
+            whole(key_grad),
+            whole(value_grad),
+            whole(attended),
+            halves(pre_mine, pre_other),
+            halves(act_mine, act_other),
+        ],
+        ((0, 0, 0), (0, 1, 0), (0, 2, 0), (1, 3, 0), (2, 4, 0), (2, 4, width), (3, 5, 0), (3, 5, width)),
+        owner_list ^ me,
+        panel_rows,
+        cuts,
+        high_count,
+        width,
+    )
+    normed_one_grad = my_grad + their_grad.astype(f32)
+    far = fold_first(far_pairs)
+    far = fold_next(tie(*far), 1)
+    far = fold_next(tie(*far), 0)
+    near = fold_first(near_pairs)
+    *far, near_a, near_b, near_c = tie(*far, *near)
+    far_sum = swap_bit(jnp.concatenate(far, axis=-2), 3)
+    near = fold_next([near_a, near_b, near_c], 1)
+    near_last = tie(*near)
 
     shift_one_grad = jnp.sum(normed_one_grad, axis=0)
     scale_one_grad = jnp.sum(normed_one_grad * normed_one, axis=0)
@@ -607,9 +900,8 @@
     text_keep_half = lax.dynamic_index_in_dim(text_grads, core, 1, keepdims=False)
     text_send_half = lax.dynamic_index_in_dim(text_grads, 1 - core, 1, keepdims=False)
     text_sum = add_low(text_keep_half, swap_core(text_send_half))
-    own_text = scatter_relative(take_blocks(text_sum, relative))
-    own_text = by_core(core, own_text, swap_core(own_text))
-
+    text_full = take_blocks(text_sum, relative).reshape(high_count, 2, 2, 2, 2, text_half, D)
+    text_full = text_full.transpose(1, 0, 2, 3, 4, 5, 6).reshape(2 * high_count, 2, 2, 2, text_half, D)
     normed_text_grad = dot32(expand_low, expand_weight, NT)
     gain_grad = jnp.sum(normed_text_grad * conv_normed, axis=0)
     norm_bias_grad = jnp.sum(normed_text_grad, axis=0)
@@ -657,7 +949,27 @@
     small = half_of(core) + swap_core(half_of(1 - core))
     in_group = (jnp.arange(GROUPS) == group).astype(f32)
     table = in_group[:, None] * small[None, vector_half:]
-    small = sum_dp(jnp.concatenate([small[:vector_half], table.reshape(-1)]).reshape(-1, 128))
+    small = jnp.concatenate([small[:vector_half], table.reshape(-1)]).reshape(-1, 128)
+
+    text_held = [[2, 1, 0] for _ in range(3)]
+    text_parts = fold_step(split_rows(text_full, text_cuts), text_held, 2)
+    small = small + swap_bit(small, 0)
+    *text_parts, small = tie(*text_parts, small)
+    text_parts = fold_step(text_parts, text_held, 1)
+    small = small + swap_bit(small, 1)
+    near = fold_next(near_last, 0)
+    *text_parts, small = tie(*text_parts, small)
+    text_parts = fold_step(text_parts, text_held, 0)
+    small = small + swap_bit(small, 2)
+    *text_parts, small = tie(*text_parts, small)
+    text_near = jnp.concatenate(text_parts, axis=-2)
+    text_near, text_far = text_near[:high_count], text_near[high_count:]
+    own_text = fold_high(text_near.astype(f32) + swap_bit(text_far, 3).astype(f32))
+    small = small + swap_bit(small, 3)
+    for bit in range(4, bit_count(count)):
+        small = small + swap_bit(small, bit)
+    own_text = by_core(core, own_text, swap_core(own_text))
+    own_panel = fold_high(jnp.concatenate(near, axis=-2).astype(f32) + far_sum.astype(f32))
     small = by_core(core, small[None], swap_core(small)[None]).reshape(2, -1)
     vector_sum = small[:, :vector_half].reshape(-1)
     tables = small[:, vector_half:].reshape(2, GROUPS, token_half)

time: 599 us -> 506 us (0.84)
  matrix products: 114 us -> 38.2 us
  Pallas kernels: 51.8 us -> 107 us
  local copies, waits for them, and re-layouts: 78 us -> 50 us
  other arithmetic: 96.5 us -> 79.6 us
  waiting for transfers between devices: 153 us -> 140 us
  starting transfers between devices: 89.4 us -> 78.4 us
    dot_general x42 -> x12, matrix products: 99.3 us -> 25 us  [dot32(): return lax.dot_general(left, right, dims, preferred_element_type=f32)]
    pallas_call x0 -> x5, Pallas kernels: none -> 62 us  [the longest x1 23.4 us: panel_gradients(): pl.pallas_call(lambda *refs: gradients_kernel(high_count, panel_rows, cut...]
    gather x4 -> x2, local copies, waits for them, and re-layouts: 24.6 us -> 7.74 us  [take_blocks(): return jnp.take(blocks, index, axis=0, mode='clip')]
    ppermute x84 -> x66, waiting for transfers between devices: 147 us -> 132 us  [swap_bit(): return lax.ppermute(array, 'dp', [(i, i ^ 1 << bit) for i in range(count)])]
    unnamed x328 -> x276, local copies, waits for them, and re-layouts: 14.5 us -> 27.4 us
    ppermute x84 -> x66, starting transfers between devices: 86.1 us -> 74.8 us  [swap_bit(): return lax.ppermute(array, 'dp', [(i, i ^ 1 << bit) for i in range(count)])]
    pallas_call x1, Pallas kernels: 26.7 us -> 16.9 us  [attend_forward(): pl.pallas_call(attend_kernel, grid=(pairs,), in_specs=[tall(PAIR), tall(P...]
    another operation x30 -> x18, other arithmetic: 18.3 us -> 10.1 us  [spread_step(): jnp.stack([part, swap_bit(part, axis_orders[index][phase])])]
  transfers between devices with their start and end apart: 103 -> 85, of which waited for: 49 -> 39; matrix products, arithmetic and copies ran while one was open for 40% -> 25% of each run, Pallas kernels for 4% -> 13%
where the time goes in v2:
time: 506 us; the launch traced here: 500 us
  waiting for transfers between devices  140 us (28%)
  Pallas kernels  107 us (21%)
  other arithmetic  79.6 us (16%)
  starting transfers between devices  78.4 us (15%)
  local copies, waits for them, and re-layouts  50 us (10%)
  matrix products  38.2 us (8%)
  between operations  6.41 us (1%)
    ppermute x66, waiting for transfers between devices, swap_bit(): return lax.ppermute(array, 'dp', [(i, i ^ 1 << bit) for i in range(count)])  132 us
    ppermute x66, starting transfers between devices, swap_bit(): return lax.ppermute(array, 'dp', [(i, i ^ 1 << bit) for i in range(count)])  74.8 us
    pallas_call x1, Pallas kernels, attend_backward(): pl.pallas_call(attend_back_kernel, grid=(pairs,), in_specs=[tall(2 * PAIR...  28.5 us
    unnamed x276, local copies, waits for them, and re-layouts  27.4 us
    dot_general x12, matrix products, dot32(): return lax.dot_general(left, right, dims, preferred_element_type=f32)  25 us
    pallas_call x1, Pallas kernels, panel_gradients(): pl.pallas_call(lambda *refs: gradients_kernel(high_count, panel_rows, cut...  23.4 us
    pallas_call x1, Pallas kernels, attend_forward(): pl.pallas_call(attend_kernel, grid=(pairs,), in_specs=[tall(PAIR), tall(P...  16.9 us
    pallas_call x2, Pallas kernels, feed(): pl.pallas_call(feed_kernel, grid=(1,), in_specs=[whole, whole, pl.BlockSp...  16.2 us
  transfers between devices with their start and end apart: 85, of which 39 were waited for; matrix products, arithmetic and copies ran while one was open for 25% of the time, Pallas kernels for 13%

profile of v2, /device:TPU:0, one launch (start us, length us, event | category | flops | bytes accessed | tf_op | source)
XLA Modules:
  0.0 500.1 jit_solution(477896044528034196)
XLA Ops:
  2.4 4.0 collective-permute-start
  6.5 2.1 convert_bitcast_fusion
  29.1 3.0 collective-permute-done.5
  41.9 4.6 collective-permute-done.7
  49.8 2.3 collective-permute-done.17
  57.6 7.9 %collective-permute-done.10 = bf16[2,2,2,16,1024]{4,3,2,1,0:T(8,128)(2,1)S(1)} collective-permute-done((bf16[2,2,2,16,1024]{4,3,2,1,0:T(8,128)(2,1)}, bf16[2,2,2,16,1024]{4,3,2,1,0:T(8,128)(2,1)S(1)}, u32[]{:S(2)}, u32[]{:S(2)}) %collective-permute-start.10) | collective-permute-done | bytes 262176 | tf_op jit(solution)/shard_map/ppermute | solution.py:35
  70.8 4.8 collective-permute-done.23
  75.7 3.7 collective-permute-start.26
  80.4 2.1 collective-permute-start.27
  86.0 3.9 collective-permute-done.25
  91.9 6.6 %collective-permute-done.28 = f32[8,3072]{1,0:T(8,128)S(1)} collective-permute-done((f32[8,3072]{1,0:T(8,128)S(1)}, f32[8,3072]{1,0:T(8,128)S(1)}, u32[]{:S(2)}, u32[]{:S(2)}) %collective-permute-start.28) | collective-permute-done | bytes 98336 | tf_op jit(solution)/shard_map/ppermute | solution.py:35
  99.8 3.0 maximum_select_fusion.1
  102.9 4.4 gather_fusion
  107.3 4.6 multiply_reduce_fusion.8
  114.4 2.9 add_convert_fusion.3
  122.8 1.8 collective-permute-start.33
  124.6 1.9 collective-permute-start.34
  127.7 1.9 fusion.97
  130.5 11.2 %collective-permute-done.31 = bf16[2,2,1,176,512]{4,3,1,2,0:T(8,128)(2,1)S(1)} collective-permute-done((bf16[2,2,1,176,512]{4,3,1,2,0:T(8,128)(2,1)S(1)}, bf16[2,2,1,176,512]{4,3,1,2,0:T(8,128)(2,1)S(1)}, u32[]{:S(2)}, u32[]{:S(2)}) %collective-permute-start.31) | collective-permute-done | bytes 720928 | tf_op jit(solution)/shard_map/ppermute | solution.py:35
  142.5 13.9 %collective-permute-done.34 = bf16[2,2,1,176,512]{4,3,1,2,0:T(8,128)(2,1)S(1)} collective-permute-done((bf16[2,2,1,176,512]{4,3,1,2,0:T(8,128)(2,1)S(1)}, bf16[2,2,1,176,512]{4,3,1,2,0:T(8,128)(2,1)S(1)}, u32[]{:S(2)}, u32[]{:S(2)}) %collective-permute-start.34) | collective-permute-done | bytes 720928 | tf_op jit(solution)/shard_map/ppermute | solution.py:35
  157.6 15.7 %project.1 = (bf16[1024,512]{1,0:T(8,128)(2,1)}, bf16[1024,512]{1,0:T(8,128)(2,1)}, bf16[1024,512]{1,0:T(8,128)(2,1)}, bf16[8192,512]{1,0:T(8,128)(2,1)}) custom-call(s32[16]{0:T(128)S(1)} %broadcast_xor_fusion.refs_0_, bf16[4,176,512]{2,1,0:T(8,128)(2,1)S(1)} %bitcast.334, bf16[4,176,512]{2,1,0:T(8,128)(2,1)S(1)} %bitcast.333, ...), custom_call_target="tpu_custom_call" | custom-call | flops 3221225472 | bytes 25165824 | tf_op jit(solution)/shard_map/project/pallas_call | solution.py:396
  177.2 16.9 %attend.1 = (bf16[1024,512]{1,0:T(8,128)(2,1)S(1)}, bf16[1024,1024]{1,0:T(8,128)(2,1)}) custom-call(bf16[1024,512]{1,0:T(8,128)(2,1)S(1)} %copy-done.20, bf16[1024,512]{1,0:T(8,128)(2,1)S(1)} %copy-done.17, bf16[1024,512]{1,0:T(8,128)(2,1)S(1)} %copy-done.19, bf16[1024,128]{1,0:T(8,128)(2,1)S(1)} %broadcast_in_dim.35.bias_ref), custom_call_target="tpu_custom_call" | custom-call | flops 17179869184 | bytes 6291456 | tf_op jit(solution)/shard_map/attend/pallas_call | solution.py:222
  194.1 2.3 convolution_convert_fusion.3
  196.6 2.6 collective-permute-done.37
  199.2 3.4 fusion.126
  204.1 3.3 multiply_convert_fusion.1
  207.4 7.9 %feed.3 = (bf16[512,1024]{1,0:T(8,128)(2,1)S(1)}, bf16[512,1024]{1,0:T(8,128)(2,1)S(1)}, bf16[512,1024]{1,0:T(8,128)(2,1)S(1)}, bf16[512,1024]{1,0:T(8,128)(2,1)S(1)}) custom-call(bf16[512,1024]{1,0:T(8,128)(2,1)S(1)} %collective-permute-done.38.n_ref.refs_6_, bf16[512,1024]{1,0:T(8,128)(2,1)} %get-tuple-element.247.g_ref.refs_8_, ...), custom_call_target="tpu_custom_call" | custom-call | flops 4294967296 | bytes 8388608 | tf_op jit(solution)/shard_map/feed/pallas_call | solution.py:440
  217.8 8.3 %feed.2 = (f32[512,1024]{1,0:T(8,128)}, f32[512,1024]{1,0:T(8,128)}, bf16[512,1024]{1,0:T(8,128)(2,1)S(1)}, bf16[512,1024]{1,0:T(8,128)(2,1)S(1)}) custom-call(bf16[512,1024]{1,0:T(8,128)(2,1)S(1)} %add_convert_fusion.1.n_ref.refs_5_, bf16[512,1024]{1,0:T(8,128)(2,1)S(1)} %get-tuple-element.248.g_ref.refs_7_, bf16[8,1024,512]{2,1,0:T(8,128)(2,1)} %bitcast.399), custom_call_target="tpu_custom_call" | custom-call | flops 4294967296 | bytes 8388608 | tf_op jit(solution)/shard_map/feed/pallas_call | solution.py:440
  227.2 3.0 multiply_reduce_fusion
  230.6 4.1 fusion.2
  235.6 2.4 collective-permute-done.42.other_ref.refs_4_
  239.0 28.5 %attend_back.1 = (bf16[1024,512]{1,0:T(8,128)(2,1)S(1)}, bf16[1024,512]{1,0:T(8,128)(2,1)S(1)}, bf16[1024,512]{1,0:T(8,128)(2,1)S(1)}) custom-call(bf16[1024,1024]{1,0:T(8,128)(2,1)} %get-tuple-element.146.qa_ref, bf16[1024,512]{1,0:T(8,128)(2,1)S(1)} %copy-done.18, bf16[1024,512]{1,0:T(8,128)(2,1)} %get-tuple-element.139.v_ref, ...), custom_call_target="tpu_custom_call" | custom-call | flops 42949672960 | bytes 12582912 | tf_op jit(solution)/shard_map/attend_back/pallas_call | solution.py:304
  270.5 23.4 %gradients.1 = (bf16[4,176,512]{2,1,0:T(8,128)(2,1)S(1)}, bf16[4,176,512]{2,1,0:T(8,128)(2,1)S(1)}, bf16[4,160,512]{2,1,0:T(8,128)(2,1)S(1)}, bf16[4,176,512]{2,...) custom-call(s32[16]{0:T(128)S(1)} %broadcast_xor_fusion.refs_0_, ...), custom_call_target="tpu_custom_call" | custom-call | flops 8589934592 | bytes 25165824 | tf_op jit(solution)/shard_map/gradients/pallas_call | solution.py:569
  303.6 6.7 %inputs_grad.1 = (f32[512,1024]{1,0:T(8,128)}, bf16[512,1024]{1,0:T(8,128)(2,1)S(1)}) custom-call(bf16[1024,512]{1,0:T(8,128)(2,1)S(1)} %copy-done.22, bf16[1024,512]{1,0:T(8,128)(2,1)S(1)} %copy-done.24, bf16[1024,512]{1,0:T(8,128)(2,1)S(1)} %copy-done.26, bf16[8,1024,512]{2,1,0:T(8,128)(2,1)} %bitcast.401), custom_call_target="tpu_custom_call" | custom-call | flops 3221225472 | bytes 12582912 | tf_op jit(solution)/shard_map/inputs_grad/pallas_call | solution.py:469
  312.5 4.8 maximum_select_fusion.2
  317.2 1.8 collective-permute-start.48
  319.1 2.1 fusion.16
  321.2 7.2 %collective-permute-done.50 = bf16[2,2,1,160,512]{4,3,1,0,2:T(8,128)(2,1)S(1)} collective-permute-done((bf16[2,2,1,160,512]{4,3,1,0,2:T(8,128)(2,1)}, bf16[2,2,1,160,512]{4,3,1,0,2:T(8,128)(2,1)S(1)}, u32[]{:S(2)}, u32[]{:S(2)}) %collective-permute-start.50) | collective-permute-done | bytes 655392 | tf_op jit(solution)/shard_map/ppermute | solution.py:35
  330.3 14.0 %collective-permute-done.49 = bf16[2,2,1,176,512]{4,3,1,0,2:T(8,128)(2,1)S(1)} collective-permute-done((bf16[2,2,1,176,512]{4,3,1,0,2:T(8,128)(2,1)S(1)}, bf16[2,2,1,176,512]{4,3,1,0,2:T(8,128)(2,1)S(1)}, u32[]{:S(2)}, u32[]{:S(2)}) %collective-permute-start.49) | collective-permute-done | bytes 720928 | tf_op jit(solution)/shard_map/ppermute | solution.py:35
  358.6 2.8 fusion.123
  368.8 3.9 fusion.124
  372.8 3.0 multiply_reduce_fusion.11
  375.8 1.8 convolution_convert_fusion.2
  377.7 3.0 multiply_reduce_fusion.12
  382.5 2.0 pad_maximum_fusion
  390.9 1.8 collective-permute-start.56
  393.2 4.7 collective-permute-done.72
  400.0 5.2 %collective-permute-done.54 = bf16[1,176,512]{2,1,0:T(8,128)(2,1)S(1)} collective-permute-done((bf16[1,176,512]{2,1,0:T(8,128)(2,1)S(1)}, bf16[1,176,512]{2,1,0:T(8,128)(2,1)S(1)}, u32[]{:S(2)}, u32[]{:S(2)}) %collective-permute-start.54) | collective-permute-done | bytes 180256 | tf_op jit(solution)/shard_map/ppermute | solution.py:35
  406.9 6.0 %collective-permute-done.62 = bf16[2,1,160,512]{3,2,1,0:T(8,128)(2,1)S(1)} collective-permute-done((bf16[2,1,160,512]{3,2,1,0:T(8,128)(2,1)S(1)}, bf16[2,1,160,512]{3,2,1,0:T(8,128)(2,1)S(1)}, u32[]{:S(2)}, u32[]{:S(2)}) %collective-permute-start.62) | collective-permute-done | bytes 327712 | tf_op jit(solution)/shard_map/ppermute | solution.py:35
  414.1 6.2 %collective-permute-done.60 = bf16[2,1,176,512]{3,2,1,0:T(8,128)(2,1)S(1)} collective-permute-done((bf16[2,1,176,512]{3,2,1,0:T(8,128)(2,1)S(1)}, bf16[2,1,176,512]{3,2,1,0:T(8,128)(2,1)S(1)}, u32[]{:S(2)}, u32[]{:S(2)}) %collective-permute-start.60) | collective-permute-done | bytes 360480 | tf_op jit(solution)/shard_map/ppermute | solution.py:35
  421.0 6.0 %collective-permute-done.65 = bf16[1,160,512]{2,1,0:T(8,128)(2,1)S(1)} collective-permute-done((bf16[1,160,512]{2,1,0:T(8,128)(2,1)S(1)}, bf16[1,160,512]{2,1,0:T(8,128)(2,1)S(1)}, u32[]{:S(2)}, u32[]{:S(2)}) %collective-permute-start.65) | collective-permute-done | bytes 163872 | tf_op jit(solution)/shard_map/ppermute | solution.py:35
  428.3 4.2 collective-permute-done.63
  433.6 4.4 collective-permute-done.64
  440.5 2.3 fusion.40
  442.8 2.9 fusion.15
  447.2 1.9 fusion
  449.1 3.3 gather_fusion.1
  456.9 2.5 collective-permute-start.68
  460.3 1.9 collective-permute-done.69
  466.0 2.5 collective-permute-start.74
  478.1 1.8 collective-permute-done.79
  482.2 1.9 collective-permute-start.81
  484.1 5.4 %maximum_select_fusion = f32[1024,1024]{1,0:T(8,128)} fusion(f32[512,1024]{1,0:T(8,128)} %collective-permute-done.44, f32[512,1024]{1,0:T(8,128)S(1)} %multiply_add_fusion, pred[]{:T(512)S(6)} %eq.26), kind=kLoop, calls=%fused_computation.2 | loop fusion | flops 3145728 | bytes 8388609 | tf_op jit(solution)/shard_map/jit(_where)/select_n | solution.py:39
  492.2 5.8 %multiply_subtract_fusion = (f32[64,6144]{1,0:T(8,128)}, f32[64,6144]{1,0:T(8,128)}, f32[64,6144]{1,0:T(8,128)}) fusion(f32[64,6144]{1,0:T(8,128)S(1)} %copy-done.89, f32[64,6144]{1,0:T(8,128)} %param.39, f32[64,6144]{1,0:T(8,128)} %param.40, f32[8,6144]{1,0:T(8,128)S(1)} %constant_dynamic-update-slice_fusion.5, f32[8,1024]{1,0:T(8,128)} %convert_element_type.624, ...), kind=kOutput, calls=%fused_computation.49 | convolution fusion | flops 12634624 | bytes 9637892 | tf_op jit(solution)/shard_map/dot_general | solution.py:979
  (579 shorter events, 157.4 us)
Async XLA Ops:
  2.4 21.4 %collective-permute-start = (bf16[1,48,1024]{2,1,0:T(8,128)(2,1)}, bf16[1,48,1024]{2,1,0:T(8,128)(2,1)}, u32[]{:S(2)}, u32[]{:S(2)}) collective-permute-start(bf16[1,48,1024]{2,1,0:T(8,128)(2,1)} %fusion.101), channel_id=1, source_target_pairs={{0,16},{2,18},{4,20},{6,22},{8,24},{10,26},{12,28},{14,30},{16,0},... | collective-permute-start | bytes 294920 | tf_op jit(solution)/shard_map/ppermute | solution.py:35
  10.3 11.0 %collective-permute-start.2 = (bf16[1,176,512]{2,1,0:T(8,128)(2,1)}, bf16[1,176,512]{2,1,0:T(8,128)(2,1)}, u32[]{:S(2)}, u32[]{:S(2)}) collective-permute-start(bf16[1,176,512]{2,1,0:T(8,128)(2,1)} %get-tuple-element.267), channel_id=1, source_target_pairs={{0,4},{2,6},{4,0},{6,2},{8,12},{10,14},{12,8},{14,10},{16,20},{18,... | collective-permute-start | bytes 540680 | tf_op jit(solution)/shard_map/ppermute | solution.py:35
  11.8 10.4 %collective-permute-start.1 = (bf16[1,176,512]{2,1,0:T(8,128)(2,1)S(1)}, bf16[1,176,512]{2,1,0:T(8,128)(2,1)S(1)}, u32[]{:S(2)}, u32[]{:S(2)}) collective-permute-start(bf16[1,176,512]{2,1,0:T(8,128)(2,1)S(1)} %get-tuple-element.268), channel_id=1, source_target_pairs={{0,2},{2,0},{4,6},{6,4},{8,10},{10,8},{12,14},{14,12},{16,18},{18,... | collective-permute-start | bytes 540680 | tf_op jit(solution)/shard_map/ppermute | solution.py:35
  33.3 6.0 %collective-permute-start.9 = (bf16[2,2,16,1024]{3,2,0,1:T(8,128)(2,1)S(1)}, bf16[2,2,16,1024]{3,2,0,1:T(8,128)(2,1)S(1)}, u32[]{:S(2)}, u32[]{:S(2)}) collective-permute-start(bf16[2,2,16,1024]{3,2,0,1:T(8,128)(2,1)S(1)} %pad_maximum_fusion.24), channel_id=1, source_target_pairs={{0,2},{2,0},{4,6},{6,4},{8,10},{10,8},{12,14},{14,12},{16,18},{18,... | collective-permute-start | bytes 393224 | tf_op jit(solution)/shard_map/ppermute | solution.py:35
  33.9 7.0 %collective-permute-start.8 = (bf16[2,2,16,1024]{3,2,1,0:T(8,128)(2,1)S(1)}, bf16[2,2,16,1024]{3,2,1,0:T(8,128)(2,1)S(1)}, u32[]{:S(2)}, u32[]{:S(2)}) collective-permute-start(bf16[2,2,16,1024]{3,2,1,0:T(8,128)(2,1)S(1)} %pad_maximum_fusion.23), channel_id=1, source_target_pairs={{0,8},{2,10},{4,12},{6,14},{8,0},{10,2},{12,4},{14,6},{16,24},{18,... | collective-permute-start | bytes 393224 | tf_op jit(solution)/shard_map/ppermute | solution.py:35
  34.6 19.5 %collective-permute-start.14 = (bf16[2,1,176,512]{3,2,1,0:T(8,128)(2,1)S(1)}, bf16[2,1,176,512]{3,2,1,0:T(8,128)(2,1)}, u32[]{:S(2)}, u32[]{:S(2)}) collective-permute-start(bf16[2,1,176,512]{3,2,1,0:T(8,128)(2,1)S(1)} %pad_maximum_fusion.14), channel_id=1, source_target_pairs={{0,8},{2,10},{4,12},{6,14},{8,0},{10,2},{12,4},{14,6},{16,24},{18,... | collective-permute-start | bytes 1081352 | tf_op jit(solution)/shard_map/ppermute | solution.py:35
  36.2 17.2 %collective-permute-start.15 = (bf16[2,1,160,512]{3,2,1,0:T(8,128)(2,1)S(1)}, bf16[2,1,160,512]{3,2,1,0:T(8,128)(2,1)S(1)}, u32[]{:S(2)}, u32[]{:S(2)}) collective-permute-start(bf16[2,1,160,512]{3,2,1,0:T(8,128)(2,1)S(1)} %pad_maximum_fusion.17), channel_id=1, source_target_pairs={{0,2},{2,0},{4,6},{6,4},{8,10},{10,8},{12,14},{14,12},{16,18},{18,... | collective-permute-start | bytes 983048 | tf_op jit(solution)/shard_map/ppermute | solution.py:35
  37.7 18.8 %collective-permute-start.13 = (bf16[2,1,176,512]{3,2,1,0:T(8,128)(2,1)S(1)}, bf16[2,1,176,512]{3,2,1,0:T(8,128)(2,1)}, u32[]{:S(2)}, u32[]{:S(2)}) collective-permute-start(bf16[2,1,176,512]{3,2,1,0:T(8,128)(2,1)S(1)} %pad_maximum_fusion.13), channel_id=1, source_target_pairs={{0,4},{2,6},{4,0},{6,2},{8,12},{10,14},{12,8},{14,10},{16,20},{18,... | collective-permute-start | bytes 1081352 | tf_op jit(solution)/shard_map/ppermute | solution.py:35
  39.2 7.3 %collective-permute-start.7 = (bf16[2,2,16,1024]{3,2,1,0:T(8,128)(2,1)S(1)}, bf16[2,2,16,1024]{3,2,1,0:T(8,128)(2,1)S(1)}, u32[]{:S(2)}, u32[]{:S(2)}) collective-permute-start(bf16[2,2,16,1024]{3,2,1,0:T(8,128)(2,1)S(1)} %pad_maximum_fusion.22), channel_id=1, source_target_pairs={{0,4},{2,6},{4,0},{6,2},{8,12},{10,14},{12,8},{14,10},{16,20},{18,... | collective-permute-start | bytes 393224 | tf_op jit(solution)/shard_map/ppermute | solution.py:35
  40.9 24.6 %collective-permute-start.16 = (bf16[1,512,512]{2,1,0:T(8,128)(2,1)}, bf16[1,512,512]{2,1,0:T(8,128)(2,1)}, u32[]{:S(2)}, u32[]{:S(2)}) collective-permute-start(bf16[1,512,512]{2,1,0:T(8,128)(2,1)} %convert_bitcast_fusion), channel_id=1, source_target_pairs={{0,16},{2,18},{4,20},{6,22},{8,24},{10,26},{12,28},{14,30},{16,0},... | collective-permute-start | bytes 1572872 | tf_op jit(solution)/shard_map/ppermute | solution.py:35
  52.1 13.4 %collective-permute-start.10 = (bf16[2,2,2,16,1024]{4,3,2,1,0:T(8,128)(2,1)}, bf16[2,2,2,16,1024]{4,3,2,1,0:T(8,128)(2,1)S(1)}, u32[]{:S(2)}, u32[]{:S(2)}) collective-permute-start(bf16[2,2,2,16,1024]{4,3,2,1,0:T(8,128)(2,1)} %pad_maximum_fusion.19), channel_id=1, source_target_pairs={{0,8},{2,10},{4,12},{6,14},{8,0},{10,2},{12,4},{14,6},{16,24},{18,... | collective-permute-start | bytes 786440 | tf_op jit(solution)/shard_map/ppermute | solution.py:35
  53.5 12.0 %collective-permute-start.11 = (bf16[2,2,2,16,1024]{4,3,2,1,0:T(8,128)(2,1)}, bf16[2,2,2,16,1024]{4,3,2,1,0:T(8,128)(2,1)S(1)}, u32[]{:S(2)}, u32[]{:S(2)}) collective-permute-start(bf16[2,2,2,16,1024]{4,3,2,1,0:T(8,128)(2,1)} %pad_maximum_fusion.20), channel_id=1, source_target_pairs={{0,2},{2,0},{4,6},{6,4},{8,10},{10,8},{12,14},{14,12},{16,18},{18,... | collective-permute-start | bytes 786440 | tf_op jit(solution)/shard_map/ppermute | solution.py:35
  54.0 11.5 %collective-permute-start.12 = (bf16[2,2,2,16,1024]{4,3,0,1,2:T(8,128)(2,1)}, bf16[2,2,2,16,1024]{4,3,0,1,2:T(8,128)(2,1)S(1)}, u32[]{:S(2)}, u32[]{:S(2)}) collective-permute-start(bf16[2,2,2,16,1024]{4,3,0,1,2:T(8,128)(2,1)} %pad_maximum_fusion.21), channel_id=1, source_target_pairs={{0,4},{2,6},{4,0},{6,2},{8,12},{10,14},{12,8},{14,10},{16,20},{18,... | collective-permute-start | bytes 786440 | tf_op jit(solution)/shard_map/ppermute | solution.py:35
  66.4 9.1 %collective-permute-start.22 = (bf16[1,160,512]{2,1,0:T(8,128)(2,1)S(1)}, bf16[1,160,512]{2,1,0:T(8,128)(2,1)S(1)}, u32[]{:S(2)}, u32[]{:S(2)}) collective-permute-start(bf16[1,160,512]{2,1,0:T(8,128)(2,1)S(1)} %get-tuple-element.258), channel_id=1, source_target_pairs={{0,8},{2,10},{4,12},{6,14},{8,0},{10,2},{12,4},{14,6},{16,24},{18,... | collective-permute-start | bytes 491528 | tf_op jit(solution)/shard_map/ppermute | solution.py:35
  67.6 8.0 %collective-permute-start.20 = (bf16[1,176,512]{2,1,0:T(8,128)(2,1)S(1)}, bf16[1,176,512]{2,1,0:T(8,128)(2,1)S(1)}, u32[]{:S(2)}, u32[]{:S(2)}) collective-permute-start(bf16[1,176,512]{2,1,0:T(8,128)(2,1)S(1)} %get-tuple-element.262), channel_id=1, source_target_pairs={{0,2},{2,0},{4,6},{6,4},{8,10},{10,8},{12,14},{14,12},{16,18},{18,... | collective-permute-start | bytes 540680 | tf_op jit(solution)/shard_map/ppermute | solution.py:35
  67.7 8.0 %collective-permute-start.21 = (bf16[1,176,512]{2,1,0:T(8,128)(2,1)S(1)}, bf16[1,176,512]{2,1,0:T(8,128)(2,1)S(1)}, u32[]{:S(2)}, u32[]{:S(2)}) collective-permute-start(bf16[1,176,512]{2,1,0:T(8,128)(2,1)S(1)} %get-tuple-element.261), channel_id=1, source_target_pairs={{0,4},{2,6},{4,0},{6,2},{8,12},{10,14},{12,8},{14,10},{16,20},{18,... | collective-permute-start | bytes 540680 | tf_op jit(solution)/shard_map/ppermute | solution.py:35
  68.7 6.9 %collective-permute-start.23 = (f32[8,3072]{1,0:T(8,128)S(1)}, f32[8,3072]{1,0:T(8,128)S(1)}, u32[]{:S(2)}, u32[]{:S(2)}) collective-permute-start(f32[8,3072]{1,0:T(8,128)S(1)} %add.477), channel_id=1, source_target_pairs={{0,4},{2,6},{4,0},{6,2},{8,12},{10,14},{12,8},{14,10},{16,20},{18,... | collective-permute-start | bytes 294920 | tf_op jit(solution)/shard_map/ppermute | solution.py:35
  75.7 9.4 %collective-permute-start.26 = (bf16[2,1,160,512]{3,2,1,0:T(8,128)(2,1)S(1)}, bf16[2,1,160,512]{3,2,1,0:T(8,128)(2,1)S(1)}, u32[]{:S(2)}, u32[]{:S(2)}) collective-permute-start(bf16[2,1,160,512]{3,2,1,0:T(8,128)(2,1)S(1)} %pad_maximum_fusion.18), channel_id=1, source_target_pairs={{0,2},{2,0},{4,6},{6,4},{8,10},{10,8},{12,14},{14,12},{16,18},{18,... | collective-permute-start | bytes 983048 | tf_op jit(solution)/shard_map/ppermute | solution.py:35
  82.5 7.4 %collective-permute-start.25 = (bf16[2,1,176,512]{3,2,1,0:T(8,128)(2,1)S(1)}, bf16[2,1,176,512]{3,2,1,0:T(8,128)(2,1)S(1)}, u32[]{:S(2)}, u32[]{:S(2)}) collective-permute-start(bf16[2,1,176,512]{3,2,1,0:T(8,128)(2,1)S(1)} %pad_maximum_fusion.16), channel_id=1, source_target_pairs={{0,8},{2,10},{4,12},{6,14},{8,0},{10,2},{12,4},{14,6},{16,24},{18,... | collective-permute-start | bytes 1081352 | tf_op jit(solution)/shard_map/ppermute | solution.py:35
  82.6 8.3 %collective-permute-start.24 = (bf16[2,1,176,512]{3,2,1,0:T(8,128)(2,1)S(1)}, bf16[2,1,176,512]{3,2,1,0:T(8,128)(2,1)S(1)}, u32[]{:S(2)}, u32[]{:S(2)}) collective-permute-start(bf16[2,1,176,512]{3,2,1,0:T(8,128)(2,1)S(1)} %pad_maximum_fusion.15), channel_id=1, source_target_pairs={{0,4},{2,6},{4,0},{6,2},{8,12},{10,14},{12,8},{14,10},{16,20},{18,... | collective-permute-start | bytes 1081352 | tf_op jit(solution)/shard_map/ppermute | solution.py:35
  84.7 15.2 %collective-permute-start.18 = (bf16[16,48,1024]{2,1,0:T(8,128)(2,1)S(1)}, bf16[16,48,1024]{2,1,0:T(8,128)(2,1)S(1)}, u32[]{:S(2)}, u32[]{:S(2)}) collective-permute-start(bf16[16,48,1024]{2,1,0:T(8,128)(2,1)S(1)} %bitcast.353), channel_id=1, source_target_pairs={{0,1},{1,0},{2,3},{3,2},{4,5},{5,4},{6,7},{7,6},{8,9},{9,8},{10,11... | collective-permute-start | bytes 4718600 | tf_op jit(solution)/shard_map/ppermute | solution.py:30
  91.8 6.6 %collective-permute-start.28 = (f32[8,3072]{1,0:T(8,128)S(1)}, f32[8,3072]{1,0:T(8,128)S(1)}, u32[]{:S(2)}, u32[]{:S(2)}) collective-permute-start(f32[8,3072]{1,0:T(8,128)S(1)} %add.494), channel_id=1, source_target_pairs={{0,16},{2,18},{4,20},{6,22},{8,24},{10,26},{12,28},{14,30},{16,0},... | collective-permute-start | bytes 294920 | tf_op jit(solution)/shard_map/ppermute | solution.py:35
  98.5 28.0 %collective-permute-start.30 = (bf16[2,2,1,176,512]{4,3,1,2,0:T(8,128)(2,1)S(1)}, bf16[2,2,1,176,512]{4,3,1,2,0:T(8,128)(2,1)}, u32[]{:S(2)}, u32[]{:S(2)}) collective-permute-start(bf16[2,2,1,176,512]{4,3,1,2,0:T(8,128)(2,1)S(1)} %pad_maximum_fusion.4), channel_id=1, source_target_pairs={{0,8},{2,10},{4,12},{6,14},{8,0},{10,2},{12,4},{14,6},{16,24},{18,... | collective-permute-start | bytes 2162696 | tf_op jit(solution)/shard_map/ppermute | solution.py:35
  98.8 25.9 %collective-permute-start.32 = (bf16[2,2,1,160,512]{4,3,1,2,0:T(8,128)(2,1)S(1)}, bf16[2,2,1,160,512]{4,3,1,2,0:T(8,128)(2,1)}, u32[]{:S(2)}, u32[]{:S(2)}) collective-permute-start(bf16[2,2,1,160,512]{4,3,1,2,0:T(8,128)(2,1)S(1)} %pad_maximum_fusion.8), channel_id=1, source_target_pairs={{0,4},{2,6},{4,0},{6,2},{8,12},{10,14},{12,8},{14,10},{16,20},{18,... | collective-permute-start | bytes 1966088 | tf_op jit(solution)/shard_map/ppermute | solution.py:35
  121.1 35.3 %collective-permute-start.36 = (bf16[512,1024]{1,0:T(8,128)(2,1)S(1)}, bf16[512,1024]{1,0:T(8,128)(2,1)S(1)}, u32[]{:S(2)}, u32[]{:S(2)}) collective-permute-start(bf16[512,1024]{1,0:T(8,128)(2,1)S(1)} %add_convert_fusion.2.refs_13_.refs_1_), channel_id=1, source_target_pairs={{0,1},{1,0},{2,3},{3,2},{4,5},{5,4},{6,7},{7,6},{8,9},{9,8},{10,11... | collective-permute-start | bytes 3145736 | tf_op jit(solution)/shard_map/ppermute | solution.py:30
  122.7 19.0 %collective-permute-start.31 = (bf16[2,2,1,176,512]{4,3,1,2,0:T(8,128)(2,1)S(1)}, bf16[2,2,1,176,512]{4,3,1,2,0:T(8,128)(2,1)S(1)}, u32[]{:S(2)}, u32[]{:S(2)}) collective-permute-start(bf16[2,2,1,176,512]{4,3,1,2,0:T(8,128)(2,1)S(1)} %pad_maximum_fusion.5), channel_id=1, source_target_pairs={{0,2},{2,0},{4,6},{6,4},{8,10},{10,8},{12,14},{14,12},{16,18},{18,... | collective-permute-start | bytes 2162696 | tf_op jit(solution)/shard_map/ppermute | solution.py:35
  122.8 19.7 %collective-permute-start.33 = (bf16[2,2,1,176,512]{4,3,1,2,0:T(8,128)(2,1)S(1)}, bf16[2,2,1,176,512]{4,3,1,2,0:T(8,128)(2,1)S(1)}, u32[]{:S(2)}, u32[]{:S(2)}) collective-permute-start(bf16[2,2,1,176,512]{4,3,1,2,0:T(8,128)(2,1)S(1)} %copy-done.77), channel_id=1, source_target_pairs={{0,8},{2,10},{4,12},{6,14},{8,0},{10,2},{12,4},{14,6},{16,24},{18,... | collective-permute-start | bytes 2162696 | tf_op jit(solution)/shard_map/ppermute | solution.py:35
  124.6 31.8 %collective-permute-start.34 = (bf16[2,2,1,176,512]{4,3,1,2,0:T(8,128)(2,1)S(1)}, bf16[2,2,1,176,512]{4,3,1,2,0:T(8,128)(2,1)S(1)}, u32[]{:S(2)}, u32[]{:S(2)}) collective-permute-start(bf16[2,2,1,176,512]{4,3,1,2,0:T(8,128)(2,1)S(1)} %copy-done.76), channel_id=1, source_target_pairs={{0,2},{2,0},{4,6},{6,4},{8,10},{10,8},{12,14},{14,12},{16,18},{18,... | collective-permute-start | bytes 2162696 | tf_op jit(solution)/shard_map/ppermute | solution.py:35
  126.6 16.0 %collective-permute-start.35 = (bf16[2,2,1,160,512]{4,3,1,2,0:T(8,128)(2,1)S(1)}, bf16[2,2,1,160,512]{4,3,1,2,0:T(8,128)(2,1)S(1)}, u32[]{:S(2)}, u32[]{:S(2)}) collective-permute-start(bf16[2,2,1,160,512]{4,3,1,2,0:T(8,128)(2,1)S(1)} %copy-done.3), channel_id=1, source_target_pairs={{0,4},{2,6},{4,0},{6,2},{8,12},{10,14},{12,8},{14,10},{16,20},{18,... | collective-permute-start | bytes 1966088 | tf_op jit(solution)/shard_map/ppermute | solution.py:35
  217.3 8.9 %collective-permute-start.41 = (bf16[512,1024]{1,0:T(8,128)(2,1)S(1)}, bf16[512,1024]{1,0:T(8,128)(2,1)S(1)}, u32[]{:S(2)}, u32[]{:S(2)}) collective-permute-start(bf16[512,1024]{1,0:T(8,128)(2,1)S(1)} %get-tuple-element.145), channel_id=1, source_target_pairs={{0,1},{1,0},{2,3},{3,2},{4,5},{5,4},{6,7},{7,6},{8,9},{9,8},{10,11... | collective-permute-start | bytes 3145736 | tf_op jit(solution)/shard_map/ppermute | solution.py:30
  217.4 12.8 %collective-permute-start.39 = (bf16[512,1024]{1,0:T(8,128)(2,1)S(1)}, bf16[512,1024]{1,0:T(8,128)(2,1)}, u32[]{:S(2)}, u32[]{:S(2)}) collective-permute-start(bf16[512,1024]{1,0:T(8,128)(2,1)S(1)} %get-tuple-element.143), channel_id=1, source_target_pairs={{0,1},{1,0},{2,3},{3,2},{4,5},{5,4},{6,7},{7,6},{8,9},{9,8},{10,11... | collective-permute-start | bytes 3145736 | tf_op jit(solution)/shard_map/ppermute | solution.py:30
  235.2 75.4 %collective-permute-start.40 = (bf16[512,1024]{1,0:T(8,128)(2,1)}, bf16[512,1024]{1,0:T(8,128)(2,1)}, u32[]{:S(2)}, u32[]{:S(2)}) collective-permute-start(bf16[512,1024]{1,0:T(8,128)(2,1)} %get-tuple-element.244), channel_id=1, source_target_pairs={{0,1},{1,0},{2,3},{3,2},{4,5},{5,4},{6,7},{7,6},{8,9},{9,8},{10,11... | collective-permute-start | bytes 3145736 | tf_op jit(solution)/shard_map/ppermute | solution.py:30
  297.4 19.9 %collective-permute-start.59 = (bf16[2,2,1,160,512]{4,3,1,2,0:T(8,128)(2,1)}, bf16[2,2,1,160,512]{4,3,1,2,0:T(8,128)(2,1)}, u32[]{:S(2)}, u32[]{:S(2)}) collective-permute-start(bf16[2,2,1,160,512]{4,3,1,2,0:T(8,128)(2,1)} %bitcast.117), channel_id=1, source_target_pairs={{0,4},{2,6},{4,0},{6,2},{8,12},{10,14},{12,8},{14,10},{16,20},{18,... | collective-permute-start | bytes 1966088 | tf_op jit(solution)/shard_map/ppermute | solution.py:35
  298.9 29.5 %collective-permute-start.50 = (bf16[2,2,1,160,512]{4,3,1,0,2:T(8,128)(2,1)}, bf16[2,2,1,160,512]{4,3,1,0,2:T(8,128)(2,1)S(1)}, u32[]{:S(2)}, u32[]{:S(2)}) collective-permute-start(bf16[2,2,1,160,512]{4,3,1,0,2:T(8,128)(2,1)} %bitcast.343), channel_id=1, source_target_pairs={{0,4},{2,6},{4,0},{6,2},{8,12},{10,14},{12,8},{14,10},{16,20},{18,... | collective-permute-start | bytes 1966088 | tf_op jit(solution)/shard_map/ppermute | solution.py:35
  310.3 42.5 %collective-permute-start.43 = (bf16[512,1024]{1,0:T(8,128)(2,1)S(1)}, bf16[512,1024]{1,0:T(8,128)(2,1)S(1)}, u32[]{:S(2)}, u32[]{:S(2)}) collective-permute-start(bf16[512,1024]{1,0:T(8,128)(2,1)S(1)} %get-tuple-element.151), channel_id=1, source_target_pairs={{0,1},{1,0},{2,3},{3,2},{4,5},{5,4},{6,7},{7,6},{8,9},{9,8},{10,11... | collective-permute-start | bytes 3145736 | tf_op jit(solution)/shard_map/ppermute | solution.py:30
  310.3 38.1 %collective-permute-start.58 = (bf16[2,2,1,176,512]{4,3,1,2,0:T(8,128)(2,1)S(1)}, bf16[2,2,1,176,512]{4,3,1,2,0:T(8,128)(2,1)S(1)}, u32[]{:S(2)}, u32[]{:S(2)}) collective-permute-start(bf16[2,2,1,176,512]{4,3,1,2,0:T(8,128)(2,1)S(1)} %bitcast.342), channel_id=1, source_target_pairs={{0,2},{2,0},{4,6},{6,4},{8,10},{10,8},{12,14},{14,12},{16,18},{18,... | collective-permute-start | bytes 2162696 | tf_op jit(solution)/shard_map/ppermute | solution.py:35
  310.6 33.7 %collective-permute-start.49 = (bf16[2,2,1,176,512]{4,3,1,0,2:T(8,128)(2,1)S(1)}, bf16[2,2,1,176,512]{4,3,1,0,2:T(8,128)(2,1)S(1)}, u32[]{:S(2)}, u32[]{:S(2)}) collective-permute-start(bf16[2,2,1,176,512]{4,3,1,0,2:T(8,128)(2,1)S(1)} %bitcast.442), channel_id=1, source_target_pairs={{0,2},{2,0},{4,6},{6,4},{8,10},{10,8},{12,14},{14,12},{16,18},{18,... | collective-permute-start | bytes 2162696 | tf_op jit(solution)/shard_map/ppermute | solution.py:35
  317.2 27.3 %collective-permute-start.48 = (bf16[2,2,1,176,512]{4,3,1,2,0:T(8,128)(2,1)S(1)}, bf16[2,2,1,176,512]{4,3,1,2,0:T(8,128)(2,1)S(1)}, u32[]{:S(2)}, u32[]{:S(2)}) collective-permute-start(bf16[2,2,1,176,512]{4,3,1,2,0:T(8,128)(2,1)S(1)} %bitcast.441), channel_id=1, source_target_pairs={{0,8},{2,10},{4,12},{6,14},{8,0},{10,2},{12,4},{14,6},{16,24},{18,... | collective-permute-start | bytes 2162696 | tf_op jit(solution)/shard_map/ppermute | solution.py:35
  328.4 23.4 %collective-permute-start.57 = (bf16[2,2,1,176,512]{4,3,1,2,0:T(8,128)(2,1)S(1)}, bf16[2,2,1,176,512]{4,3,1,2,0:T(8,128)(2,1)S(1)}, u32[]{:S(2)}, u32[]{:S(2)}) collective-permute-start(bf16[2,2,1,176,512]{4,3,1,2,0:T(8,128)(2,1)S(1)} %bitcast.341), channel_id=1, source_target_pairs={{0,8},{2,10},{4,12},{6,14},{8,0},{10,2},{12,4},{14,6},{16,24},{18,... | collective-permute-start | bytes 2162696 | tf_op jit(solution)/shard_map/ppermute | solution.py:35
  344.8 20.5 %collective-permute-start.53 = (bf16[2,1,160,512]{3,2,0,1:T(8,128)(2,1)S(1)}, bf16[2,1,160,512]{3,2,0,1:T(8,128)(2,1)S(1)}, u32[]{:S(2)}, u32[]{:S(2)}) collective-permute-start(bf16[2,1,160,512]{3,2,0,1:T(8,128)(2,1)S(1)} %slice_bitcast_fusion.7), channel_id=1, source_target_pairs={{0,2},{2,0},{4,6},{6,4},{8,10},{10,8},{12,14},{14,12},{16,18},{18,... | collective-permute-start | bytes 983048 | tf_op jit(solution)/shard_map/ppermute | solution.py:35
  345.9 43.8 %collective-permute-start.52 = (bf16[2,1,176,512]{3,2,0,1:T(8,128)(2,1)}, bf16[2,1,176,512]{3,2,0,1:T(8,128)(2,1)}, u32[]{:S(2)}, u32[]{:S(2)}) collective-permute-start(bf16[2,1,176,512]{3,2,0,1:T(8,128)(2,1)} %slice_bitcast_fusion.3), channel_id=1, source_target_pairs={{0,8},{2,10},{4,12},{6,14},{8,0},{10,2},{12,4},{14,6},{16,24},{18,... | collective-permute-start | bytes 1081352 | tf_op jit(solution)/shard_map/ppermute | solution.py:35
  348.4 39.8 %collective-permute-start.51 = (bf16[2,1,176,512]{3,2,1,0:T(8,128)(2,1)}, bf16[2,1,176,512]{3,2,1,0:T(8,128)(2,1)}, u32[]{:S(2)}, u32[]{:S(2)}) collective-permute-start(bf16[2,1,176,512]{3,2,1,0:T(8,128)(2,1)} %slice_bitcast_fusion.4), channel_id=1, source_target_pairs={{0,4},{2,6},{4,0},{6,2},{8,12},{10,14},{12,8},{14,10},{16,20},{18,... | collective-permute-start | bytes 1081352 | tf_op jit(solution)/shard_map/ppermute | solution.py:35
  363.1 121.1 %collective-permute-start.44 = (f32[512,1024]{1,0:T(8,128)S(1)}, f32[512,1024]{1,0:T(8,128)}, u32[]{:S(2)}, u32[]{:S(2)}) collective-permute-start(f32[512,1024]{1,0:T(8,128)S(1)} %multiply_add_fusion), channel_id=1, source_target_pairs={{0,1},{1,0},{2,3},{3,2},{4,5},{5,4},{6,7},{7,6},{8,9},{9,8},{10,11... | collective-permute-start | bytes 6291464 | tf_op jit(solution)/shard_map/ppermute | solution.py:30
  384.9 62.3 %collective-permute-start.67 = (bf16[16,48,1024]{2,1,0:T(8,128)(2,1)S(1)}, bf16[16,48,1024]{2,1,0:T(8,128)(2,1)S(1)}, u32[]{:S(2)}, u32[]{:S(2)}) collective-permute-start(bf16[16,48,1024]{2,1,0:T(8,128)(2,1)S(1)} %dynamic-slice_bitcast_fusion), channel_id=1, source_target_pairs={{0,1},{1,0},{2,3},{3,2},{4,5},{5,4},{6,7},{7,6},{8,9},{9,8},{10,11... | collective-permute-start | bytes 4718600 | tf_op jit(solution)/shard_map/ppermute | solution.py:30
  388.3 57.4 %collective-permute-start.47 = (f32[512,512]{1,0:T(8,128)S(1)}, f32[512,512]{1,0:T(8,128)S(1)}, u32[]{:S(2)}, u32[]{:S(2)}) collective-permute-start(f32[512,512]{1,0:T(8,128)S(1)} %get-tuple-element.254), channel_id=1, source_target_pairs={{0,1},{1,0},{2,3},{3,2},{4,5},{5,4},{6,7},{7,6},{8,9},{9,8},{10,11... | collective-permute-start | bytes 3145736 | tf_op jit(solution)/shard_map/ppermute | solution.py:30
  390.9 8.8 %collective-permute-start.56 = (bf16[1,160,512]{2,1,0:T(8,128)(2,1)S(1)}, bf16[1,160,512]{2,1,0:T(8,128)(2,1)S(1)}, u32[]{:S(2)}, u32[]{:S(2)}) collective-permute-start(bf16[1,160,512]{2,1,0:T(8,128)(2,1)S(1)} %slice_bitcast_fusion.17), channel_id=1, source_target_pairs={{0,8},{2,10},{4,12},{6,14},{8,0},{10,2},{12,4},{14,6},{16,24},{18,... | collective-permute-start | bytes 491528 | tf_op jit(solution)/shard_map/ppermute | solution.py:35
  398.0 7.3 %collective-permute-start.55 = (bf16[1,176,512]{2,1,0:T(8,128)(2,1)S(1)}, bf16[1,176,512]{2,1,0:T(8,128)(2,1)S(1)}, u32[]{:S(2)}, u32[]{:S(2)}) collective-permute-start(bf16[1,176,512]{2,1,0:T(8,128)(2,1)S(1)} %slice_bitcast_fusion.13), channel_id=1, source_target_pairs={{0,4},{2,6},{4,0},{6,2},{8,12},{10,14},{12,8},{14,10},{16,20},{18,... | collective-permute-start | bytes 540680 | tf_op jit(solution)/shard_map/ppermute | solution.py:35
  399.7 5.5 %collective-permute-start.54 = (bf16[1,176,512]{2,1,0:T(8,128)(2,1)S(1)}, bf16[1,176,512]{2,1,0:T(8,128)(2,1)S(1)}, u32[]{:S(2)}, u32[]{:S(2)}) collective-permute-start(bf16[1,176,512]{2,1,0:T(8,128)(2,1)S(1)} %slice_bitcast_fusion.14), channel_id=1, source_target_pairs={{0,2},{2,0},{4,6},{6,4},{8,10},{10,8},{12,14},{14,12},{16,18},{18,... | collective-permute-start | bytes 540680 | tf_op jit(solution)/shard_map/ppermute | solution.py:35
  405.3 7.5 %collective-permute-start.62 = (bf16[2,1,160,512]{3,2,1,0:T(8,128)(2,1)S(1)}, bf16[2,1,160,512]{3,2,1,0:T(8,128)(2,1)S(1)}, u32[]{:S(2)}, u32[]{:S(2)}) collective-permute-start(bf16[2,1,160,512]{3,2,1,0:T(8,128)(2,1)S(1)} %slice_bitcast_fusion.6), channel_id=1, source_target_pairs={{0,2},{2,0},{4,6},{6,4},{8,10},{10,8},{12,14},{14,12},{16,18},{18,... | collective-permute-start | bytes 983048 | tf_op jit(solution)/shard_map/ppermute | solution.py:35
  405.7 8.2 %collective-permute-start.61 = (bf16[2,1,176,512]{3,2,1,0:T(8,128)(2,1)S(1)}, bf16[2,1,176,512]{3,2,1,0:T(8,128)(2,1)S(1)}, u32[]{:S(2)}, u32[]{:S(2)}) collective-permute-start(bf16[2,1,176,512]{3,2,1,0:T(8,128)(2,1)S(1)} %slice_bitcast_fusion.1), channel_id=1, source_target_pairs={{0,8},{2,10},{4,12},{6,14},{8,0},{10,2},{12,4},{14,6},{16,24},{18,... | collective-permute-start | bytes 1081352 | tf_op jit(solution)/shard_map/ppermute | solution.py:35
  412.9 7.4 %collective-permute-start.60 = (bf16[2,1,176,512]{3,2,1,0:T(8,128)(2,1)S(1)}, bf16[2,1,176,512]{3,2,1,0:T(8,128)(2,1)S(1)}, u32[]{:S(2)}, u32[]{:S(2)}) collective-permute-start(bf16[2,1,176,512]{3,2,1,0:T(8,128)(2,1)S(1)} %slice_bitcast_fusion.2), channel_id=1, source_target_pairs={{0,4},{2,6},{4,0},{6,2},{8,12},{10,14},{12,8},{14,10},{16,20},{18,... | collective-permute-start | bytes 1081352 | tf_op jit(solution)/shard_map/ppermute | solution.py:35
  413.9 24.1 %collective-permute-start.66 = (bf16[1,512,512]{2,1,0:T(8,128)(2,1)S(1)}, bf16[1,512,512]{2,1,0:T(8,128)(2,1)S(1)}, u32[]{:S(2)}, u32[]{:S(2)}) collective-permute-start(bf16[1,512,512]{2,1,0:T(8,128)(2,1)S(1)} %pad_maximum_fusion.12), channel_id=1, source_target_pairs={{0,16},{2,18},{4,20},{6,22},{8,24},{10,26},{12,28},{14,30},{16,0},... | collective-permute-start | bytes 1572872 | tf_op jit(solution)/shard_map/ppermute | solution.py:35
  420.4 6.5 %collective-permute-start.65 = (bf16[1,160,512]{2,1,0:T(8,128)(2,1)S(1)}, bf16[1,160,512]{2,1,0:T(8,128)(2,1)S(1)}, u32[]{:S(2)}, u32[]{:S(2)}) collective-permute-start(bf16[1,160,512]{2,1,0:T(8,128)(2,1)S(1)} %slice_bitcast_fusion.16), channel_id=1, source_target_pairs={{0,8},{2,10},{4,12},{6,14},{8,0},{10,2},{12,4},{14,6},{16,24},{18,... | collective-permute-start | bytes 491528 | tf_op jit(solution)/shard_map/ppermute | solution.py:35
  427.0 5.5 %collective-permute-start.63 = (bf16[1,176,512]{2,1,0:T(8,128)(2,1)S(1)}, bf16[1,176,512]{2,1,0:T(8,128)(2,1)S(1)}, u32[]{:S(2)}, u32[]{:S(2)}) collective-permute-start(bf16[1,176,512]{2,1,0:T(8,128)(2,1)S(1)} %slice_bitcast_fusion.12), channel_id=1, source_target_pairs={{0,2},{2,0},{4,6},{6,4},{8,10},{10,8},{12,14},{14,12},{16,18},{18,... | collective-permute-start | bytes 540680 | tf_op jit(solution)/shard_map/ppermute | solution.py:35
  432.5 5.5 %collective-permute-start.64 = (bf16[1,176,512]{2,1,0:T(8,128)(2,1)S(1)}, bf16[1,176,512]{2,1,0:T(8,128)(2,1)S(1)}, u32[]{:S(2)}, u32[]{:S(2)}) collective-permute-start(bf16[1,176,512]{2,1,0:T(8,128)(2,1)S(1)} %slice_bitcast_fusion.11), channel_id=1, source_target_pairs={{0,4},{2,6},{4,0},{6,2},{8,12},{10,14},{12,8},{14,10},{16,20},{18,... | collective-permute-start | bytes 540680 | tf_op jit(solution)/shard_map/ppermute | solution.py:35
  453.5 6.7 %collective-permute-start.70 = (bf16[2,2,2,16,1024]{4,3,2,1,0:T(8,128)(2,1)S(1)}, bf16[2,2,2,16,1024]{4,3,2,1,0:T(8,128)(2,1)S(1)}, u32[]{:S(2)}, u32[]{:S(2)}) collective-permute-start(bf16[2,2,2,16,1024]{4,3,2,1,0:T(8,128)(2,1)S(1)} %slice_bitcast_fusion.8), channel_id=1, source_target_pairs={{0,4},{2,6},{4,0},{6,2},{8,12},{10,14},{12,8},{14,10},{16,20},{18,... | collective-permute-start | bytes 786440 | tf_op jit(solution)/shard_map/ppermute | solution.py:35
  455.8 6.5 %collective-permute-start.69 = (bf16[2,2,2,16,1024]{4,3,0,2,1:T(8,128)(2,1)S(1)}, bf16[2,2,2,16,1024]{4,3,0,2,1:T(8,128)(2,1)S(1)}, u32[]{:S(2)}, u32[]{:S(2)}) collective-permute-start(bf16[2,2,2,16,1024]{4,3,0,2,1:T(8,128)(2,1)S(1)} %bitcast.386), channel_id=1, source_target_pairs={{0,2},{2,0},{4,6},{6,4},{8,10},{10,8},{12,14},{14,12},{16,18},{18,... | collective-permute-start | bytes 786440 | tf_op jit(solution)/shard_map/ppermute | solution.py:35
  456.9 7.2 %collective-permute-start.68 = (bf16[2,2,2,16,1024]{4,3,0,2,1:T(8,128)(2,1)S(1)}, bf16[2,2,2,16,1024]{4,3,0,2,1:T(8,128)(2,1)S(1)}, u32[]{:S(2)}, u32[]{:S(2)}) collective-permute-start(bf16[2,2,2,16,1024]{4,3,0,2,1:T(8,128)(2,1)S(1)} %bitcast.387), channel_id=1, source_target_pairs={{0,8},{2,10},{4,12},{6,14},{8,0},{10,2},{12,4},{14,6},{16,24},{18,... | collective-permute-start | bytes 786440 | tf_op jit(solution)/shard_map/ppermute | solution.py:35
  466.0 6.1 %collective-permute-start.74 = (bf16[2,2,16,1024]{3,2,0,1:T(8,128)(2,1)S(1)}, bf16[2,2,16,1024]{3,2,0,1:T(8,128)(2,1)S(1)}, u32[]{:S(2)}, u32[]{:S(2)}) collective-permute-start(bf16[2,2,16,1024]{3,2,0,1:T(8,128)(2,1)S(1)} %slice_bitcast_fusion.20), channel_id=1, source_target_pairs={{0,8},{2,10},{4,12},{6,14},{8,0},{10,2},{12,4},{14,6},{16,24},{18,... | collective-permute-start | bytes 393224 | tf_op jit(solution)/shard_map/ppermute | solution.py:35
  473.6 7.4 %collective-permute-start.80 = (f32[226,128]{1,0:T(8,128)S(1)}, f32[226,128]{1,0:T(8,128)S(1)}, u32[]{:S(2)}, u32[]{:S(2)}) collective-permute-start(f32[226,128]{1,0:T(8,128)S(1)} %add.570), channel_id=1, source_target_pairs={{0,8},{2,10},{4,12},{6,14},{8,0},{10,2},{12,4},{14,6},{16,24},{18,... | collective-permute-start | bytes 347144 | tf_op jit(solution)/shard_map/ppermute | solution.py:35
  474.2 5.8 %collective-permute-start.79 = (bf16[2,16,1024]{2,1,0:T(8,128)(2,1)S(1)}, bf16[2,16,1024]{2,1,0:T(8,128)(2,1)S(1)}, u32[]{:S(2)}, u32[]{:S(2)}) collective-permute-start(bf16[2,16,1024]{2,1,0:T(8,128)(2,1)S(1)} %slice_bitcast_fusion.23), channel_id=1, source_target_pairs={{0,8},{2,10},{4,12},{6,14},{8,0},{10,2},{12,4},{14,6},{16,24},{18,... | collective-permute-start | bytes 196616 | tf_op jit(solution)/shard_map/ppermute | solution.py:35
  481.0 8.5 %collective-permute-start.83 = (f32[226,128]{1,0:T(8,128)S(1)}, f32[226,128]{1,0:T(8,128)S(1)}, u32[]{:S(2)}, u32[]{:S(2)}) collective-permute-start(f32[226,128]{1,0:T(8,128)S(1)} %add.574), channel_id=1, source_target_pairs={{0,16},{2,18},{4,20},{6,22},{8,24},{10,26},{12,28},{14,30},{16,0},... | collective-permute-start | bytes 347144 | tf_op jit(solution)/shard_map/ppermute | solution.py:35
  482.2 7.9 %collective-permute-start.81 = (bf16[1,48,1024]{2,1,0:T(8,128)(2,1)S(1)}, bf16[1,48,1024]{2,1,0:T(8,128)(2,1)S(1)}, u32[]{:S(2)}, u32[]{:S(2)}) collective-permute-start(bf16[1,48,1024]{2,1,0:T(8,128)(2,1)S(1)} %slice.487), channel_id=1, source_target_pairs={{0,16},{2,18},{4,20},{6,22},{8,24},{10,26},{12,28},{14,30},{16,0},... | collective-permute-start | bytes 294920 | tf_op jit(solution)/shard_map/ppermute | solution.py:35
  490.2 8.5 %collective-permute-start.82 = (f32[48,1024]{1,0:T(8,128)S(1)}, f32[48,1024]{1,0:T(8,128)S(1)}, u32[]{:S(2)}, u32[]{:S(2)}) collective-permute-start(f32[48,1024]{1,0:T(8,128)S(1)} %add_bitcast_fusion), channel_id=1, source_target_pairs={{0,1},{1,0},{2,3},{3,2},{4,5},{5,4},{6,7},{7,6},{8,9},{9,8},{10,11... | collective-permute-start | bytes 589832 | tf_op jit(solution)/shard_map/ppermute | solution.py:30
  (149 other events, 1301.3 us)

commit v3 on v2

--- a/solution.py
+++ b/solution.py
@@ -1,4 +1,5 @@
 import jax
+import numpy as np
 import jax.numpy as jnp
 from jax import lax
 from jax.experimental import pallas as pl
@@ -30,9 +31,16 @@
     return lax.ppermute(array, "mp", [(0, 1), (1, 0)])
 
 
+def swap_bits(array, bits):
+    count = lax.axis_size("dp")
+    pairs = [
+        (i * 2 + core, (i ^ (1 << bits[core])) * 2 + core) for i in range(count) for core in range(2)
+    ]
+    return lax.ppermute(array, ("dp", "mp"), pairs)
+
+
 def swap_bit(array, bit):
-    count = lax.axis_size("dp")
-    return lax.ppermute(array, "dp", [(i, i ^ (1 << bit)) for i in range(count)])
+    return swap_bits(array, (bit, bit))
 
 
 def by_core(core, mine, other, axis=0):
@@ -47,43 +55,46 @@
     return count.bit_length() - 1
 
 
-def third_cuts(rows):
-    step = rows // 3
-    if rows >= 48:
-        step = (rows + 24) // 48 * 16
-    return (0, step, 2 * step, rows)
-
-
-axis_orders = ((0, 1, 2), (1, 2, 0), (2, 0, 1))
+def row_cuts(rows):
+    return (0, (rows * 2 + 24) // 48 * 16, rows)
+
+
+axis_orders = (((0, 1, 2), (1, 2, 0)), ((2, 0, 1), (2, 0, 1)))
+text_orders = ((2, 0, 1), (2, 1, 0))
+
+
+def phase_bits(orders, phase):
+    return tuple(order[phase] for order in orders)
 
 
 def tie(*values):
     return lax.optimization_barrier(values)
 
 
+def tie_lists(*lists):
+    flat = [value for values in lists for value in values]
+    flat = list(lax.optimization_barrier(tuple(flat)))
+    out = []
+    for values in lists:
+        out.append(flat[: len(values)])
+        flat = flat[len(values) :]
+    return out
+
+
+def split_rows(array, cuts):
+    return [array[..., cuts[i] : cuts[i + 1], :] for i in range(len(cuts) - 1)]
+
+
+def spread(part, orders, phase):
+    return jnp.stack([part, swap_bits(part, phase_bits(orders, phase))])
+
+
 def spread_step(parts, phase):
-    return [
-        jnp.stack([part, swap_bit(part, axis_orders[index][phase])])
-        for index, part in enumerate(parts)
-    ]
+    return [spread(part, axis_orders[index], phase) for index, part in enumerate(parts)]
 
 
 def spread_last(parts):
-    return [(part, swap_bit(part, axis_orders[index][2])) for index, part in enumerate(parts)]
-
-
-def split_rows(array, cuts):
-    return [array[..., cuts[i] : cuts[i + 1], :] for i in range(3)]
-
-
-def spread_close(pairs):
-    pieces = []
-    for index, pair in enumerate(pairs):
-        order = axis_orders[index]
-        held = [order[2], order[1], order[0]]
-        axes = [3] + [held.index(bit) for bit in (2, 1, 0)] + [4, 5]
-        pieces.append(jnp.stack(pair).transpose(axes))
-    return jnp.concatenate(pieces, axis=4)
+    return [(part, swap_bits(part, phase_bits(axis_orders[index], 2))) for index, part in enumerate(parts)]
 
 
 def spread_high(block):
@@ -97,24 +108,24 @@
     return (left.astype(f32) + right.astype(f32)).astype(bf16)
 
 
-def fold_step(parts, held, phase):
-    folded = []
-    for index, part in enumerate(parts):
-        bit = axis_orders[index][phase]
-        axis = 1 + held[index].index(bit)
-        keep = lax.index_in_dim(part, 0, axis, keepdims=False)
-        send = lax.index_in_dim(part, 1, axis, keepdims=False)
-        folded.append(add_low(keep, swap_bit(send, bit)))
-        held[index].remove(bit)
-    return folded
-
-
-def fold_first(pairs):
-    return [add_low(keep, swap_bit(send, axis_orders[index][2])) for index, (keep, send) in enumerate(pairs)]
-
-
-def fold_next(parts, phase):
-    return [add_low(part[0], swap_bit(part[1], axis_orders[index][phase])) for index, part in enumerate(parts)]
+def receive(sends, phase):
+    return [swap_bits(send, phase_bits(axis_orders[index], phase)) for index, send in enumerate(sends)]
+
+
+def add_all(keeps, received):
+    return [add_low(keep, other) for keep, other in zip(keeps, received)]
+
+
+def firsts(parts):
+    return [part[0] for part in parts]
+
+
+def seconds(parts):
+    return [part[1] for part in parts]
+
+
+def fold(part, orders, phase):
+    return add_low(part[0], swap_bits(part[1], phase_bits(orders, phase)))
 
 
 def fold_high(total):
@@ -127,14 +138,56 @@
     return total[0]
 
 
-def sum_dp(array):
-    for bit in range(bit_count(lax.axis_size("dp"))):
-        array = array + swap_bit(array, bit)
-    return array
+def bit_of(values, which):
+    return (values >> which) & 1
+
+
+def lead_place(slots, order, high_count):
+    return (bit_of(slots, order[1]) * 2 + bit_of(slots, order[0])) * high_count + (slots >> 4)
+
+
+def panel_places(core, slots, high_count, apart):
+    rows = []
+    for orders in axis_orders:
+        far = bit_of(slots, 3)
+        which = [bit_of(slots, order[2]) + 2 * far * apart for order in orders]
+        lead = [
+            lead_place(slots, order, high_count)
+            if apart
+            else (bit_of(slots, order[1]) * 2 + bit_of(slots, order[0])) * 2 * high_count
+            + far * high_count
+            + (slots >> 4)
+            for order in orders
+        ]
+        rows += [jnp.where(core == 0, *which), jnp.where(core == 0, *lead)]
+    return jnp.concatenate(rows).astype(jnp.int32)
+
+
+def text_places(core, slots, high_count):
+    places = []
+    for order in text_orders:
+        high = bit_of(slots, 3) * high_count + (slots >> 4)
+        places.append(
+            ((bit_of(slots, order[2]) * 2 + bit_of(slots, order[1])) * 2 + bit_of(slots, order[0]))
+            * (2 * high_count)
+            + high
+        )
+    return jnp.where(core == 0, *places).astype(jnp.int32)
+
+
+def text_slots(core, places, high_count):
+    lead, rest = places // (2 * high_count), places % (2 * high_count)
+    high = ((rest // high_count) << 3) | ((rest % high_count) << 4)
+    slots = []
+    for order in text_orders:
+        low = (bit_of(lead, 2) << order[2]) | (bit_of(lead, 1) << order[1]) | (bit_of(lead, 0) << order[0])
+        slots.append(high | low)
+    return jnp.where(core == 0, *slots)
 
 
 NT = (((1,), (1,)), ((), ()))
 NN = (((1,), (0,)), ((), ()))
+TN = (((0,), (0,)), ((), ()))
 ROWS = 256
 PAIR = 2 * HEAD
 vmem_bytes = 48 * 1024 * 1024
@@ -326,33 +379,35 @@
     )(queries, keys, values, outputs, grad_mine, grad_other, stacked, cosine, sine, bias)
 
 
-def part_place(slot, index, high_count):
-    bit = lambda which: (slot >> which) & 1
-    order = axis_orders[index]
-    lead = (bit(order[1]) * 2 + bit(order[0])) * high_count + (slot >> 4)
-    return bit(3), bit(order[2]), lead
-
-
-def project_kernel(high_count, panel_rows, cuts, slots_ref, *refs):
-    parts, refs = refs[:12], refs[12:]
+PARTS = 2
+
+
+def part_copies(table_ref, panels, panel, cuts, start_row, copy, arrays=4):
+    for index in range(PARTS):
+        which = table_ref[2 * index * panels + panel]
+        lead = table_ref[(2 * index + 1) * panels + panel]
+        start = pl.multiple_of(start_row + cuts[index], 16)
+        for number in range(arrays):
+
+            @pl.when(which == number)
+            def _():
+                copy(number * PARTS + index, lead, start, cuts[index + 1] - cuts[index])
+
+
+def project_kernel(panel_rows, cuts, slots_ref, *refs):
+    parts, refs = refs[: 2 * PARTS], refs[2 * PARTS :]
     mine_ref, other_ref, cos_ref, sin_ref, q_ref, k_ref, v_ref, out_ref, held, in_sems, out_sem = refs
     per_block = D // panel_rows
 
     def fetch(panel, carry):
-        slot = slots_ref[panel]
         group = jnp.minimum(panel // per_block, 3)
-        for index in range(3):
-            far, last, lead = part_place(slot, index, high_count)
-            rows = cuts[index + 1] - cuts[index]
-            start = pl.multiple_of(panel * panel_rows + cuts[index], 16)
-            for which in range(4):
-
-                @pl.when(far * 2 + last == which)
-                def _():
-                    pltpu.make_async_copy(
-                        parts[which * 3 + index].at[lead], held.at[pl.ds(start, rows)], in_sems.at[group]
-                    ).start()
-
+
+        def copy(number, lead, start, rows):
+            pltpu.make_async_copy(
+                parts[number].at[lead], held.at[pl.ds(start, rows)], in_sems.at[group]
+            ).start()
+
+        part_copies(slots_ref, 8 * per_block, panel, cuts, panel * panel_rows, copy, 2)
         return carry
 
     lax.fori_loop(0, 8 * per_block, fetch, 0)
@@ -382,20 +437,19 @@
     pltpu.make_async_copy(held, out_ref, out_sem).wait()
 
 
-def project(near_pairs, far_pairs, slots, panel_rows, cuts, mine, other, cosine, sine):
-    high_count, width = near_pairs[0][0].shape[2], near_pairs[0][0].shape[-1]
+def project(part_pairs, slots, panel_rows, cuts, mine, other, cosine, sine):
+    width = part_pairs[0][0].shape[-1]
     parts = [
-        pairs[index][last].reshape(-1, cuts[index + 1] - cuts[index], width)
-        for pairs in (near_pairs, far_pairs)
+        part_pairs[index][last].reshape(-1, cuts[index + 1] - cuts[index], width)
         for last in range(2)
-        for index in range(3)
+        for index in range(PARTS)
     ]
     whole = pl.BlockSpec(memory_space=pltpu.VMEM)
     anywhere = pl.BlockSpec(memory_space=pl.ANY)
     tall = jax.ShapeDtypeStruct((LEN, width), bf16)
     return pl.pallas_call(
-        lambda *refs: project_kernel(high_count, panel_rows, cuts, *refs),
-        in_specs=[pl.BlockSpec(memory_space=pltpu.SMEM)] + [anywhere] * 12 + [whole] * 4,
+        lambda *refs: project_kernel(panel_rows, cuts, *refs),
+        in_specs=[pl.BlockSpec(memory_space=pltpu.SMEM)] + [anywhere] * (2 * PARTS) + [whole] * 4,
         out_specs=[whole] * 3 + [anywhere],
         out_shape=[tall] * 3 + [jax.ShapeDtypeStruct((8 * D, width), bf16)],
         scratch_shapes=[
@@ -480,10 +534,10 @@
     )(query_grad, key_grad, value_grad, stacked)
 
 
-def gradients_kernel(high_count, panel_rows, cuts, lefts, rights, uses, slots_ref, *refs):
+def gradients_kernel(panel_rows, cuts, lefts, rights, uses, slots_ref, *refs):
     in_count = sum(len(pieces) for pieces in lefts + rights)
     inputs, refs = refs[:in_count], refs[in_count:]
-    parts, refs = refs[:12], refs[12:]
+    parts, refs = refs[: 4 * PARTS], refs[4 * PARTS :]
     left_held, right_held = refs[: len(lefts)], refs[len(lefts) : len(lefts) + len(rights)]
     turned, block_ref, in_sems, out_sems = refs[len(lefts) + len(rights) :]
     side = block_ref.shape[1]
@@ -529,21 +583,14 @@
             ).astype(bf16)
 
             def send(piece, carry, block=block, place=place):
-                slot = slots_ref[block * pieces + piece]
-                for index in range(3):
-                    far, last, lead = part_place(slot, index, high_count)
-                    rows = cuts[index + 1] - cuts[index]
-                    start = pl.multiple_of(piece * panel_rows + cuts[index], 16)
-                    for which in range(4):
-
-                        @pl.when(far * 2 + last == which)
-                        def _():
-                            pltpu.make_async_copy(
-                                block_ref.at[place, pl.ds(start, rows)],
-                                parts[which * 3 + index].at[lead],
-                                out_sems.at[place],
-                            ).start()
-
+                def copy(number, lead, start, rows):
+                    pltpu.make_async_copy(
+                        block_ref.at[place, pl.ds(start, rows)], parts[number].at[lead], out_sems.at[place]
+                    ).start()
+
+                part_copies(
+                    slots_ref, 8 * D // panel_rows, block * pieces + piece, cuts, piece * panel_rows, copy
+                )
                 return carry
 
             lax.fori_loop(0, pieces, send, 0)
@@ -564,15 +611,13 @@
     outs = [
         jax.ShapeDtypeStruct((4 * high_count, cuts[index + 1] - cuts[index], width), bf16)
         for _ in range(4)
-        for index in range(3)
+        for index in range(PARTS)
     ]
     outs = pl.pallas_call(
-        lambda *refs: gradients_kernel(
-            high_count, panel_rows, cuts, numbered[0], numbered[1], uses, *refs
-        ),
+        lambda *refs: gradients_kernel(panel_rows, cuts, numbered[0], numbered[1], uses, *refs),
         in_specs=[pl.BlockSpec(memory_space=pltpu.SMEM)]
         + [pl.BlockSpec(memory_space=pl.ANY)] * len(arrays),
-        out_specs=[pl.BlockSpec(memory_space=pl.ANY)] * 12,
+        out_specs=[pl.BlockSpec(memory_space=pl.ANY)] * (4 * PARTS),
         out_shape=outs,
         scratch_shapes=[pltpu.VMEM((LEN, extent(pieces)), bf16) for pieces in list(lefts) + list(rights)]
         + [
@@ -590,8 +635,207 @@
         name="gradients",
     )(slots, *arrays)
     shaped = [out.reshape((2, 2, high_count) + out.shape[1:]) for out in outs]
-    pairs = lambda far: [(shaped[far * 6 + index], shaped[far * 6 + 3 + index]) for index in range(3)]
+    pairs = lambda far: [
+        (shaped[far * 2 * PARTS + index], shaped[far * 2 * PARTS + PARTS + index]) for index in range(PARTS)
+    ]
     return pairs(0), pairs(1)
+
+
+beside = pl.CostEstimate(flops=1000, bytes_accessed=1000, transcendentals=0)
+
+
+def gelu_parts(values):
+    share = 0.5 * (1.0 + lax.erf(values * 0.7071067811865476))
+    density = 0.3989422804014327 * jnp.exp(-0.5 * values * values)
+    return share, density
+
+
+def in_vmem(kernel, name, inputs, outs, scratch=(), specs=None, out_specs=None):
+    whole = pl.BlockSpec(memory_space=pltpu.VMEM)
+    return pl.pallas_call(
+        kernel,
+        in_specs=specs or [whole] * len(inputs),
+        out_specs=out_specs or [whole] * len(outs),
+        out_shape=[jax.ShapeDtypeStruct(shape, kind) for shape, kind in outs],
+        scratch_shapes=list(scratch),
+        compiler_params=pltpu.CompilerParams(vmem_limit_bytes=vmem_bytes),
+        cost_estimate=beside,
+        name=name,
+    )(*inputs)
+
+
+def text_forward_kernel(
+    core_ref, table_ref, mine_ref, other_ref, normed_ref, masked_ref, keep_ref, mel_mine_ref, mel_other_ref,
+    in_bias_ref, gamma_ref, beta_ref, bias_ref, shift_ref, scale_ref,
+    pre_ref, energy_ref, grn_ref, text_ref, stream_ref, first_ref, other_first_ref, texts_ref, hidden_held, held, sem, out_sem,
+):
+    rows = mine_ref.shape[1]
+    half = stream_ref.shape[0]
+
+    def fetch(block, carry):
+        place = held.at[pl.ds(pl.multiple_of(block * rows, 16), rows)]
+        for part, ref in enumerate((mine_ref, other_ref)):
+
+            @pl.when((block + core_ref[0]) % 2 == part)
+            def _():
+                pltpu.make_async_copy(ref.at[table_ref[block]], place, sem).start()
+
+        return carry
+
+    lax.fori_loop(0, table_ref.shape[0], fetch, 0)
+    pltpu.make_async_copy(held, held, sem).wait()
+    out = pltpu.make_async_copy(held, texts_ref, out_sem)
+    out.start()
+    energy_sum = jnp.zeros((1, TXT_FF), f32)
+    for part in range(2):
+        frames = slice(part * half, (part + 1) * half)
+        pre = dot32(normed_ref[frames, :], held[:TEXT]) + in_bias_ref[...]
+        if part == 0:
+            pre_ref[...] = pre
+        hidden = pre * gelu_parts(pre)[0]
+        hidden_held[frames, :] = hidden
+        energy_sum = energy_sum + jnp.sum(hidden * hidden, axis=0, keepdims=True)
+    energy_ref[...] = energy_sum
+    energy = jnp.sqrt(energy_sum)
+    ratio = energy / (jnp.mean(energy, axis=-1, keepdims=True) + norm_eps)
+    weight = gamma_ref[...] * ratio + 1.0
+    for part, mel_ref in enumerate((mel_mine_ref, mel_other_ref)):
+        frames = slice(part * half, (part + 1) * half)
+        grn_low = (weight * hidden_held[frames, :] + beta_ref[...]).astype(bf16)
+        text_out = masked_ref[frames, :] + dot32(grn_low, held[TEXT : 2 * TEXT], NT) + bias_ref[...]
+        text_low = (text_out * keep_ref[frames, :]).astype(bf16)
+        stream = mel_ref[...].astype(f32) + dot32(text_low, held[2 * TEXT :])
+        normed, _ = normalise(stream)
+        first = (normed * (1.0 + scale_ref[...]) + shift_ref[...]).astype(bf16)
+        if part == 0:
+            grn_ref[...] = grn_low
+            text_ref[...] = text_low
+            stream_ref[...] = stream
+            first_ref[...] = first
+        else:
+            other_first_ref[...] = first
+    out.wait()
+
+
+def text_forward(core, table, *inputs):
+    whole, anywhere = pl.BlockSpec(memory_space=pltpu.VMEM), pl.BlockSpec(memory_space=pl.ANY)
+    scalars = pl.BlockSpec(memory_space=pltpu.SMEM)
+    half = LEN // 2
+    return in_vmem(
+        text_forward_kernel,
+        "text_forward",
+        (core.reshape(1).astype(jnp.int32), table) + inputs,
+        [
+            ((half, TXT_FF), f32),
+            ((1, TXT_FF), f32),
+            ((half, TXT_FF), bf16),
+            ((half, TEXT), bf16),
+            ((half, D), f32),
+            ((half, D), bf16),
+            ((half, D), bf16),
+            ((3 * TEXT, D), bf16),
+        ],
+        [
+            pltpu.VMEM((LEN, TXT_FF), f32),
+            pltpu.VMEM((3 * TEXT, D), bf16),
+            pltpu.SemaphoreType.DMA,
+            pltpu.SemaphoreType.DMA,
+        ],
+        [scalars, scalars, anywhere, anywhere] + [whole] * (len(inputs) - 2),
+        [whole] * 7 + [anywhere],
+    )
+
+
+def stream_back_kernel(
+    core_ref, my_ref, their_ref, stream_ref, later_ref, scale_ref, texts_ref, keep_ref, pre_ref,
+    mel_ref, low_ref, shrink_ref, shrink_low_ref, grn_grad_ref, sums_ref, bias_sum_ref, full_ref, sem,
+):
+    half = mel_ref.shape[0]
+    grad = my_ref[...] + their_ref[...].astype(f32)
+    normed, scale = normalise(stream_ref[...])
+    sums_ref[0:1] = jnp.sum(grad, axis=0, keepdims=True)
+    sums_ref[1:2] = jnp.sum(grad * normed, axis=0, keepdims=True)
+    mel_grad = later_ref[...] + normalise_back(grad * (1.0 + scale_ref[...]), normed, scale)
+    mel_ref[...] = mel_grad
+    place = pl.ds(pl.multiple_of(core_ref[0] * half, half), half)
+    out = pltpu.make_async_copy(mel_ref, full_ref.at[place], sem)
+    out.start()
+    low = mel_grad.astype(bf16)
+    low_ref[...] = low
+    shrink_grad = dot32(low, texts_ref[2 * TEXT :], NT) * keep_ref[...]
+    shrink_ref[...] = shrink_grad
+    bias_sum_ref[...] = jnp.sum(shrink_grad, axis=0, keepdims=True)
+    shrink_low = shrink_grad.astype(bf16)
+    shrink_low_ref[...] = shrink_low
+    grn_grad = dot32(shrink_low, texts_ref[TEXT : 2 * TEXT])
+    grn_grad_ref[...] = grn_grad
+    pre = pre_ref[...]
+    sums_ref[2:3] = jnp.sum(grn_grad * (pre * gelu_parts(pre)[0]), axis=0, keepdims=True)
+    sums_ref[3:4] = jnp.sum(grn_grad, axis=0, keepdims=True)
+    sums_ref[4:8] = jnp.zeros((4, D), f32)
+    out.wait()
+
+
+def stream_back(core, *inputs):
+    half = inputs[0].shape[0]
+    whole = pl.BlockSpec(memory_space=pltpu.VMEM)
+    return in_vmem(
+        stream_back_kernel,
+        "stream_back",
+        (core.reshape(1).astype(jnp.int32),) + inputs,
+        [
+            ((half, D), f32),
+            ((half, D), bf16),
+            ((half, TEXT), f32),
+            ((half, TEXT), bf16),
+            ((half, TXT_FF), f32),
+            ((8, D), f32),
+            ((1, TEXT), f32),
+            ((2 * half, D), f32),
+        ],
+        [pltpu.SemaphoreType.DMA],
+        [pl.BlockSpec(memory_space=pltpu.SMEM)] + [whole] * len(inputs),
+        [whole] * 7 + [pl.BlockSpec(memory_space=pl.ANY)],
+    )
+
+
+def text_back_kernel(
+    pre_ref, grn_grad_ref, energy_ref, dot_ref, gamma_ref, texts_ref, normed_ref, conv_normed_ref, conv_scale_ref, gain_ref,
+    shrink_low_ref, grn_ref, text_ref, low_ref,
+    mixed_ref, sums_ref, wide_sums_ref, grads_ref,
+):
+    pre = pre_ref[...]
+    share, density = gelu_parts(pre)
+    energy = jnp.sqrt(energy_ref[...])
+    energy_mean = jnp.mean(energy, axis=-1, keepdims=True) + norm_eps
+    ratio = energy / energy_mean
+    ratio_grad = gamma_ref[...] * dot_ref[...]
+    energy_grad = (ratio_grad - jnp.mean(ratio_grad * ratio, axis=-1, keepdims=True)) / energy_mean
+    hidden_grad = grn_grad_ref[...] * (gamma_ref[...] * ratio + 1.0) + (pre * share) * (energy_grad / energy)
+    expand_grad = hidden_grad * (share + pre * density)
+    wide_sums_ref[0:1] = jnp.sum(expand_grad, axis=0, keepdims=True)
+    wide_sums_ref[1:2] = ratio
+    expand_low = expand_grad.astype(bf16)
+    grads_ref[:TEXT] = dot32(normed_ref[...], expand_low, TN).astype(bf16)
+    grads_ref[TEXT : 2 * TEXT] = dot32(shrink_low_ref[...], grn_ref[...], TN).astype(bf16)
+    grads_ref[2 * TEXT :] = dot32(text_ref[...], low_ref[...], TN).astype(bf16)
+    normed_grad = dot32(expand_low, texts_ref[:TEXT], NT)
+    conv_normed = conv_normed_ref[...]
+    sums_ref[0:1] = jnp.sum(normed_grad * conv_normed, axis=0, keepdims=True)
+    sums_ref[1:2] = jnp.sum(normed_grad, axis=0, keepdims=True)
+    mixed_grad = normalise_back(normed_grad * gain_ref[...], conv_normed, conv_scale_ref[...])
+    sums_ref[2:3] = jnp.sum(mixed_grad, axis=0, keepdims=True)
+    mixed_ref[...] = mixed_grad
+
+
+def text_back(*inputs):
+    half = inputs[0].shape[0]
+    return in_vmem(
+        text_back_kernel,
+        "text_back",
+        inputs,
+        [((half, TEXT), f32), ((3, TEXT), f32), ((2, TXT_FF), f32), ((3 * TEXT, D), bf16)],
+    )
 
 
 def vector_parts(vectors):
@@ -617,16 +861,6 @@
     return scale * (grad - mean_grad - normed * mean_dot)
 
 
-def gelu_parts(values):
-    share = 0.5 * (1.0 + lax.erf(values * 0.7071067811865476))
-    density = 0.3989422804014327 * jnp.exp(-0.5 * values * values)
-    return share, density
-
-
-def gelu_tanh(values):
-    return jax.nn.gelu(values, approximate=True)
-
-
 def moments(gradient, first_moment, second_moment):
     first_new = beta_one * first_moment + (1.0 - beta_one) * gradient
     second_new = beta_two * second_moment + (1.0 - beta_two) * gradient * gradient
@@ -640,15 +874,14 @@
     return weight - rate * (direction + weight_decay * weight)
 
 
-def rotary_tables(core, half):
-    position = ((jnp.arange(LEN) + core * half) % LEN).astype(f32)
-    frequency = 10000.0 ** (-jnp.arange(HEAD // 2, dtype=f32) * 2.0 / HEAD)
+def rotary_tables(first):
+    position = np.arange(LEN)
+    frequency = 10000.0 ** (-np.arange(HEAD // 2) * 2.0 / HEAD)
     angle = position[:, None] * frequency[None, :]
-    cosine, sine = jnp.cos(angle), jnp.sin(angle)
-    return (
-        jnp.concatenate([cosine] * 4, axis=1),
-        jnp.concatenate([-sine, sine, -sine, sine], axis=1),
-    )
+    cosine, sine = np.cos(angle), np.sin(angle)
+    tables = np.concatenate([cosine] * 4 + [-sine, sine, -sine, sine], axis=1).astype(np.float32)
+    tables = lax.dynamic_slice_in_dim(jnp.asarray(np.concatenate([tables, tables])), first, LEN, 0)
+    return tables[:, :PAIR], tables[:, PAIR:]
 
 
 def take_blocks(blocks, index):
@@ -700,49 +933,60 @@
     relative = jnp.arange(count) ^ me
 
     high_count = count // 16
-    cuts, text_cuts = third_cuts(panel_rows), third_cuts(text_half)
+    cuts = row_cuts(panel_rows)
+    gather_table = panel_places(core, owner_list ^ me, high_count, 0)
+    panel_table = panel_places(core, owner_list ^ me, high_count, 1)
     silu_time = jax.nn.silu(time_embedding.astype(f32)).astype(bf16)
     time_rows = lax.dynamic_slice_in_dim(silu_time, me * share_rows, share_rows, 1)
     weight_half = lax.dynamic_slice_in_dim(modulation_weight, core * 3 * D, 3 * D, 1).astype(bf16)
     own_rows = lax.dynamic_slice_in_dim(text_matrices, core * text_half, text_half, 0)
     text_held = spread_high(own_rows.astype(bf16))
-    near_held = spread_high(soap_master.astype(bf16))
-    text_far = swap_bit(text_held, 3)
-    near = spread_step(split_rows(near_held, cuts), 0)
-    text_far, near_held, near_a, near_b, near_c = tie(text_far, near_held, *near)
-    near = [near_a, near_b, near_c]
-    text_parts = split_rows(jnp.concatenate([text_held, text_far], axis=0), text_cuts)
-    far_held = swap_bit(near_held, 3)
-    text_parts = spread_step(text_parts, 0)
     partial = dot32(time_rows, weight_half)
-    *text_parts, partial = tie(*text_parts, partial)
-    text_parts = spread_step(text_parts, 1)
-    near = spread_step(near, 1)
-    *text_parts, partial = tie(*text_parts, partial)
-    text_pairs = spread_last(text_parts)
-    partial = partial + swap_bit(partial, 0)
-    text_tied = tie(*[part for pair in text_pairs for part in pair], *near, far_held, partial)
-    text_pairs = [text_tied[0:2], text_tied[2:4], text_tied[4:6]]
-    near, far_held, partial = list(text_tied[6:9]), text_tied[9], text_tied[10]
-    near_pairs = spread_last(near)
-    far = spread_step(split_rows(far_held, cuts), 0)
-    partial = partial + swap_bit(partial, 1)
-    *far, partial = tie(*far, partial)
-    far = spread_step(far, 1)
-    partial = partial + swap_bit(partial, 2)
-    *far, partial = tie(*far, partial)
-    far_pairs = spread_last(far)
-    partial = partial + swap_bit(partial, 3)
+    held = spread_high(soap_master.astype(bf16))
+    text_received, partial_received = tie(swap_bit(text_held, 3), swap_bit(partial, 3))
+    text_held = jnp.concatenate([text_held, text_received], axis=0)
+    partial = partial + partial_received
+    text_received, partial_received, held = tie(
+        swap_bits(text_held, phase_bits(text_orders, 0)), swap_bits(partial, phase_bits(text_orders, 0)), held
+    )
+    held = split_rows(held, cuts)
+    text_held = jnp.stack([text_held, text_received])
+    partial = partial + partial_received
+    text_received, partial_received, far_last = tie(
+        swap_bits(text_held, phase_bits(text_orders, 1)),
+        swap_bits(partial, phase_bits(text_orders, 1)),
+        swap_bit(held[1], 3),
+    )
+    text_held = jnp.stack([text_held, text_received])
+    partial = partial + partial_received
+    text_received, partial_received, far_first = tie(
+        swap_bits(text_held, phase_bits(text_orders, 2)),
+        swap_bits(partial, phase_bits(text_orders, 2)),
+        swap_bit(held[0], 3),
+    )
+    partial = partial + partial_received
+    parts = [jnp.concatenate(pair, axis=0) for pair in zip(held, (far_first, far_last))]
+    received = receive(parts, 0)
+    text_mine = jnp.stack([text_held, text_received]).reshape(count, text_half, D)
+    text_other = swap_core(text_mine)
+    received, (text_mine, text_other, partial, text_features, mel_frames, cotangent) = tie_lists(
+        received, (text_mine, text_other, partial, text_features, mel_frames, cotangent)
+    )
+    parts = [jnp.stack(pair) for pair in zip(parts, received)]
+    received = receive(parts, 1)
     for bit in range(4, bit_count(count)):
         partial = partial + swap_bit(partial, bit)
     modulation_half = partial
-    text_half_all = spread_close([[part for part in pair] for pair in text_pairs])
-    text_half_all = text_half_all.reshape(2, high_count, 2, 2, 2, text_half, D)
-    text_half_all = jnp.moveaxis(text_half_all, 0, 1).reshape(count, text_half, D)
-    text_other = swap_core(text_half_all)
-    texts = take_blocks(by_core(core, text_half_all, text_other, axis=1), relative)
-    texts = texts.reshape(3 * TEXT, D)
-    expand_weight, shrink_rows, text_to_model = texts[:TEXT], texts[TEXT : 2 * TEXT], texts[2 * TEXT :]
+    mine_places, other_places = text_places(core, relative, high_count), text_places(1 - core, relative, high_count)
+    text_table = jnp.where(
+        core == 0, jnp.stack([mine_places, other_places], 1), jnp.stack([other_places, mine_places], 1)
+    ).reshape(-1)
+    if text_half % 16:
+        source = jnp.arange(2 * count) % 2 != core
+        texts = take_blocks(jnp.concatenate([text_mine, text_other]), text_table + count * source)
+        text_mine = text_other = texts.reshape(1, 3 * TEXT, D)
+        text_table = jnp.zeros((1,), jnp.int32)
+
     modulation = by_core(core, modulation_half, swap_core(modulation_half), axis=1)
     (
         kernel,
@@ -757,47 +1001,68 @@
     ) = vector_parts(vectors)
     group = group_ids[0]
     modulation_row = lax.dynamic_slice_in_dim(modulation, group, 1, 0) + modulation_bias
-    shift_one, scale_one, gate_one, shift_two, scale_two, gate_two = (
-        modulation_row[:, i * D : (i + 1) * D] for i in range(6)
-    )
+
 
     first = core * half
     margin = KERNEL // 2
     edge = 8
     keep_all = jnp.pad(text_keep.astype(f32), (edge, edge))[:, None]
     text_all = jnp.pad(text_features, ((edge, edge), (0, 0)))
-    window = lax.dynamic_slice_in_dim(text_all, first, half + 2 * edge, 0).astype(f32)
-    window = window * lax.dynamic_slice_in_dim(keep_all, first, half + 2 * edge, 0)
-    keep = lax.dynamic_slice_in_dim(keep_all, first + edge, half, 0)
-    masked_text = window[edge : edge + half]
-    taps = [window[edge - margin + j : edge - margin + j + half] for j in range(KERNEL)]
-    mixed = conv_bias[None, :]
-    for j in range(KERNEL):
-        mixed = mixed + taps[j] * kernel[j][None, :]
-    conv_normed, conv_scale = normalise(mixed)
-    normed_low = (conv_normed * norm_gain + norm_bias).astype(bf16)
-    expand_pre = dot32(normed_low, expand_weight) + in_bias
-    share, density = gelu_parts(expand_pre)
-    hidden = expand_pre * share
-    energy_sum = jnp.sum(hidden * hidden, axis=0, keepdims=True)
-    energy = jnp.sqrt(energy_sum + swap_core(energy_sum))
-    energy_mean = jnp.mean(energy, axis=-1, keepdims=True) + norm_eps
-    ratio = energy / energy_mean
-    grn_low = (grn_gamma * (hidden * ratio) + grn_beta + hidden).astype(bf16)
-    text_out = (masked_text + dot32(grn_low, shrink_rows, NT) + out_bias) * keep
-    text_low = text_out.astype(bf16)
-    mel_mine = lax.dynamic_slice_in_dim(mel_frames, first, half, 0).astype(f32)
-    stream = mel_mine + dot32(text_low, text_to_model)
-
-    normed_one, scale_norm_one = normalise(stream)
-    first_mine = (normed_one * (1.0 + scale_one) + shift_one).astype(bf16)
-    first_other = swap_core(first_mine)
-    cosine, sine = rotary_tables(core, half)
+
+    def text_start(start):
+        window = lax.dynamic_slice_in_dim(text_all, start, half + 2 * edge, 0).astype(f32)
+        window = window * lax.dynamic_slice_in_dim(keep_all, start, half + 2 * edge, 0)
+        keep = lax.dynamic_slice_in_dim(keep_all, start + edge, half, 0)
+        taps = [window[edge - margin + j : edge - margin + j + half] for j in range(KERNEL)]
+        mixed = conv_bias[None, :]
+        for j in range(KERNEL):
+            mixed = mixed + taps[j] * kernel[j][None, :]
+        normed, scale = normalise(mixed)
+        return window[edge : edge + half], keep, taps, normed, scale, (normed * norm_gain + norm_bias).astype(bf16)
+
+    masked_text, keep, taps, conv_normed, conv_scale, normed_low = text_start(first)
+    masked_other, keep_other, _, _, _, normed_other = text_start(half - first)
+    masked_both = jnp.concatenate([masked_text, masked_other], axis=0)
+    keep_both = jnp.concatenate([keep, keep_other], axis=0)
+    normed_both = jnp.concatenate([normed_low, normed_other], axis=0)
+    mel_mine = lax.dynamic_slice_in_dim(mel_frames, first, half, 0)
+    mel_other = lax.dynamic_slice_in_dim(mel_frames, half - first, half, 0)
+    cosine, sine = rotary_tables(first)
+    received, (text_other, modulation_row, normed_both, masked_both, cosine, sine) = tie_lists(
+        received, (text_other, modulation_row, normed_both, masked_both, cosine, sine)
+    )
+    pairs = spread_last([jnp.stack(pair) for pair in zip(parts, received)])
+    shift_one, scale_one, gate_one, shift_two, scale_two, gate_two = (
+        modulation_row[:, i * D : (i + 1) * D] for i in range(6)
+    )
+    expand_pre, energy_sum, grn_low, text_low, stream, first_mine, first_other, texts = text_forward(
+        core,
+        text_table,
+        text_mine,
+        text_other,
+        normed_both,
+        masked_both,
+        keep_both,
+        mel_mine,
+        mel_other,
+        in_bias[None],
+        grn_gamma[None],
+        grn_beta[None],
+        out_bias[None],
+        shift_one,
+        scale_one,
+    )
+
+    cot_mine = lax.dynamic_slice_in_dim(cotangent, first, half, 0)
+    cot_other = lax.dynamic_slice_in_dim(cotangent, half - first, half, 0)
+    hidden_mine = (gate_two * cot_mine.astype(f32)).astype(bf16)
+    hidden_other = (gate_two * cot_other.astype(f32)).astype(bf16)
+    first_mine, hidden_mine, hidden_other = tie(first_mine, hidden_mine, hidden_other)
     position = (jnp.arange(LEN) + first) % LEN
     bias = jnp.where(position < lengths[0], 0.0, -1e30).astype(bf16)
     bias = jnp.broadcast_to(bias[:, None], (LEN, PAIR))
     queries, keys, value_rows, stacked = project(
-        near_pairs, far_pairs, owner_list ^ me, panel_rows, cuts, first_mine, first_other, cosine, sine
+        pairs, gather_table, panel_rows, cuts, first_mine, first_other, cosine, sine
     )
     stacked = stacked.reshape(8, D, width)
     attended, query_aug = attend_forward(queries, keys, value_rows, bias)
@@ -807,11 +1072,7 @@
     normed_two, scale_norm_two = normalise(stream_one)
     second_mine = (normed_two * (1.0 + scale_two) + shift_two).astype(bf16)
     second_other = swap_core(second_mine)
-    cot_mine = lax.dynamic_slice_in_dim(cotangent, first, half, 0)
-    cot_other = lax.dynamic_slice_in_dim(cotangent, half - first, half, 0)
     out_grad = cot_mine.astype(f32)
-    hidden_mine = (gate_two * out_grad).astype(bf16)
-    hidden_other = (gate_two * cot_other.astype(f32)).astype(bf16)
     their_out, their_grad, act_other, pre_other = feed(second_other, hidden_other, stacked, bf16)
     their_out, their_grad = swap_core(their_out), swap_core(their_grad)
     my_out, my_grad, act_mine, pre_mine = feed(second_mine, hidden_mine, stacked, f32)
@@ -827,13 +1088,13 @@
     )
 
     gate_one_grad = jnp.sum(stream_one_grad * attention_out, axis=0)
-    TN = (((0,), (0,)), ((), ()))
     attention_mine = (gate_one * stream_one_grad).astype(bf16)
     attention_other = swap_core(attention_mine)
     query_grad, key_grad, value_grad = attend_backward(
         query_aug, keys, value_rows, attended, attention_mine, attention_other, stacked, cosine, sine, bias
     )
     my_grad, their_grad = inputs_grad(query_grad, key_grad, value_grad, stacked)
+    their_grad, query_grad = tie(their_grad, query_grad)
     their_grad = swap_core(their_grad)
     halves = lambda mine, other: [(0, 0, mine), (half, 0, other)]
     whole = lambda array: [(0, 0, array)]
@@ -853,60 +1114,54 @@
             halves(act_mine, act_other),
         ],
         ((0, 0, 0), (0, 1, 0), (0, 2, 0), (1, 3, 0), (2, 4, 0), (2, 4, width), (3, 5, 0), (3, 5, width)),
-        owner_list ^ me,
+        panel_table,
         panel_rows,
         cuts,
         high_count,
         width,
     )
-    normed_one_grad = my_grad + their_grad.astype(f32)
-    far = fold_first(far_pairs)
-    far = fold_next(tie(*far), 1)
-    far = fold_next(tie(*far), 0)
-    near = fold_first(near_pairs)
-    *far, near_a, near_b, near_c = tie(*far, *near)
-    far_sum = swap_bit(jnp.concatenate(far, axis=-2), 3)
-    near = fold_next([near_a, near_b, near_c], 1)
-    near_last = tie(*near)
-
-    shift_one_grad = jnp.sum(normed_one_grad, axis=0)
-    scale_one_grad = jnp.sum(normed_one_grad * normed_one, axis=0)
-    mel_grad_mine = stream_one_grad + normalise_back(
-        normed_one_grad * (1.0 + scale_one), normed_one, scale_norm_one
-    )
-    mel_gradient = by_core(core, mel_grad_mine, swap_core(mel_grad_mine))
-
-    stream_grad = mel_grad_mine.astype(bf16)
-    text_to_model_grad = dot32(text_low, stream_grad, TN)
-    shrink_grad = dot32(stream_grad, text_to_model, NT) * keep
-    out_bias_grad = jnp.sum(shrink_grad, axis=0)
-    shrink_low = shrink_grad.astype(bf16)
-    shrink_rows_grad = dot32(shrink_low, grn_low, TN)
-    grn_grad = dot32(shrink_low, shrink_rows)
-    hidden_dot = jnp.sum(grn_grad * hidden, axis=0, keepdims=True)
+
+    far_keep, far_send = firsts(far_pairs), seconds(far_pairs)
+    near_keep, near_send = firsts(near_pairs), seconds(near_pairs)
+    far_received = receive(far_send, 2)
+    mel_grad_mine, stream_low, shrink_grad, shrink_low, grn_grad, sums, out_bias_grad, mel_gradient = stream_back(
+        core, my_grad, their_grad, stream, stream_one_grad, scale_one, texts, keep, expand_pre
+    )
+    far_received, (sums, mel_grad_mine) = tie_lists(far_received, (sums, mel_grad_mine))
+    shift_one_grad, scale_one_grad, hidden_dot, beta_grad = sums[0], sums[1], sums[2:3], sums[3]
+    out_bias_grad = out_bias_grad[0]
+    far = add_all(far_keep, far_received)
+    far_received = receive(seconds(far), 1)
     hidden_dot_all = hidden_dot + swap_core(hidden_dot)
-    ratio_grad = grn_gamma * hidden_dot_all
-    energy_grad = ratio_grad / energy_mean - jnp.mean(ratio_grad * ratio, axis=-1, keepdims=True) / energy_mean
-    gamma_grad = (ratio * hidden_dot)[0]
-    beta_grad = jnp.sum(grn_grad, axis=0)
-    hidden_grad = grn_grad * (grn_gamma * ratio + 1.0) + hidden * (energy_grad / energy)
-    expand_grad = hidden_grad * (share + expand_pre * density)
-    in_bias_grad = jnp.sum(expand_grad, axis=0)
-    expand_low = expand_grad.astype(bf16)
-    expand_weight_grad = dot32(normed_low, expand_low, TN)
-    text_grads = jnp.concatenate(
-        [grad.astype(bf16) for grad in (expand_weight_grad, shrink_rows_grad, text_to_model_grad)], axis=0
-    ).reshape(count, 2, text_half, D)
+    mixed_grad, text_sums, wide_sums, text_grads = text_back(
+        expand_pre,
+        grn_grad,
+        energy_sum,
+        hidden_dot_all,
+        grn_gamma[None],
+        texts,
+        normed_low,
+        conv_normed,
+        conv_scale,
+        norm_gain[None],
+        shrink_low,
+        grn_low,
+        text_low,
+        stream_low,
+    )
+    mel_grad_theirs = swap_core(mel_grad_mine)
+    gain_grad, norm_bias_grad, conv_bias_grad = text_sums[0], text_sums[1], text_sums[2]
+    in_bias_grad, gamma_grad = wide_sums[0], wide_sums[1] * hidden_dot[0]
+    far_received, near_send, (mixed_grad, text_grads, mel_grad_theirs) = tie_lists(
+        far_received, near_send, (mixed_grad, text_grads, mel_grad_theirs)
+    )
+    far = add_all(firsts(far), far_received)
+    far_received = receive(seconds(far), 0)
+    near_received = receive(near_send, 2)
+    text_grads = text_grads.reshape(count, 2, text_half, D)
     text_keep_half = lax.dynamic_index_in_dim(text_grads, core, 1, keepdims=False)
     text_send_half = lax.dynamic_index_in_dim(text_grads, 1 - core, 1, keepdims=False)
-    text_sum = add_low(text_keep_half, swap_core(text_send_half))
-    text_full = take_blocks(text_sum, relative).reshape(high_count, 2, 2, 2, 2, text_half, D)
-    text_full = text_full.transpose(1, 0, 2, 3, 4, 5, 6).reshape(2 * high_count, 2, 2, 2, text_half, D)
-    normed_text_grad = dot32(expand_low, expand_weight, NT)
-    gain_grad = jnp.sum(normed_text_grad * conv_normed, axis=0)
-    norm_bias_grad = jnp.sum(normed_text_grad, axis=0)
-    mixed_grad = normalise_back(normed_text_grad * norm_gain, conv_normed, conv_scale)
-    conv_bias_grad = jnp.sum(mixed_grad, axis=0)
+    text_received = swap_core(text_send_half)
     kernel_grad = jnp.stack([jnp.sum(mixed_grad * taps[j], axis=0) for j in range(KERNEL)])
     border = lax.dynamic_slice_in_dim(mixed_grad, (1 - core) * (half - edge), edge, 0)
     border = swap_core(border)
@@ -918,7 +1173,6 @@
         start = edge + margin - j
         masked_grad = masked_grad + wide_grad[start : start + half] * kernel[j][None, :]
     text_grad_mine = masked_grad * keep
-    text_gradient = by_core(core, text_grad_mine, swap_core(text_grad_mine))
 
     vector_mine = jnp.concatenate(
         [
@@ -946,30 +1200,55 @@
             ]
         )
 
-    small = half_of(core) + swap_core(half_of(1 - core))
+    small_send = half_of(1 - core)
+    small = half_of(core)
     in_group = (jnp.arange(GROUPS) == group).astype(f32)
+
+    far_received, near_received, (text_received, small, small_send) = tie_lists(
+        far_received, near_received, (text_received, small, small_send)
+    )
+    far = add_all(firsts(far), far_received)
+    far_last = swap_bit(far[1], 3)
+    near = add_all(near_keep, near_received)
+    near_received = receive(seconds(near), 1)
+    text_part = take_blocks(
+        add_low(text_keep_half, text_received), text_slots(core, jnp.arange(count), high_count) ^ me
+    )
+    text_part = text_part.reshape(2, 2, 2, 2 * high_count, text_half, D)
+    text_received = swap_bits(text_part[1], phase_bits(text_orders, 2))
+    small_received = swap_core(small_send)
+    mel_gradient = lax.dynamic_update_slice_in_dim(mel_gradient, mel_grad_theirs, half - first, 0)
+    near_received, (text_received, small_received, mel_gradient, far_last) = tie_lists(
+        near_received, (text_received, small_received, mel_gradient, far_last)
+    )
+    far_first = swap_bit(far[0], 3)
+    near = add_all(firsts(near), near_received)
+    near_received = receive(seconds(near), 0)
+    text_part = add_low(text_part[0], text_received)
+    text_part = fold(text_part, text_orders, 1)
+    small = small + small_received
     table = in_group[:, None] * small[None, vector_half:]
     small = jnp.concatenate([small[:vector_half], table.reshape(-1)]).reshape(-1, 128)
-
-    text_held = [[2, 1, 0] for _ in range(3)]
-    text_parts = fold_step(split_rows(text_full, text_cuts), text_held, 2)
-    small = small + swap_bit(small, 0)
-    *text_parts, small = tie(*text_parts, small)
-    text_parts = fold_step(text_parts, text_held, 1)
-    small = small + swap_bit(small, 1)
-    near = fold_next(near_last, 0)
-    *text_parts, small = tie(*text_parts, small)
-    text_parts = fold_step(text_parts, text_held, 0)
-    small = small + swap_bit(small, 2)
-    *text_parts, small = tie(*text_parts, small)
-    text_near = jnp.concatenate(text_parts, axis=-2)
-    text_near, text_far = text_near[:high_count], text_near[high_count:]
-    own_text = fold_high(text_near.astype(f32) + swap_bit(text_far, 3).astype(f32))
+    small = small + swap_bits(small, (2, 0))
+    text_gradient = by_core(core, text_grad_mine, swap_core(text_grad_mine))
+    near_received, (text_part, small, text_gradient, far_first, block_output) = tie_lists(
+        near_received, (text_part, small, text_gradient, far_first, block_output)
+    )
+    near = add_all(firsts(near), near_received)
+    own_panel = jnp.concatenate(
+        [keep.astype(f32) + other.astype(f32) for keep, other in zip(near, (far_first, far_last))], axis=-2
+    )
+    own_panel = fold_high(own_panel)
+    text_part = fold(text_part, text_orders, 0)
+    text_received = swap_bit(text_part[high_count:], 3)
+    small = small + swap_bits(small, (0, 1))
+    small = small + swap_bits(small, (1, 2))
     small = small + swap_bit(small, 3)
+    own_text = text_part[:high_count].astype(f32) + text_received.astype(f32)
     for bit in range(4, bit_count(count)):
         small = small + swap_bit(small, bit)
+    own_text = fold_high(own_text)
     own_text = by_core(core, own_text, swap_core(own_text))
-    own_panel = fold_high(jnp.concatenate(near, axis=-2).astype(f32) + far_sum.astype(f32))
     small = by_core(core, small[None], swap_core(small)[None]).reshape(2, -1)
     vector_sum = small[:, :vector_half].reshape(-1)
     tables = small[:, vector_half:].reshape(2, GROUPS, token_half)

time: 506 us -> 394 us (0.78)
  other arithmetic: 79.6 us -> 48.8 us
  starting transfers between devices: 78.4 us -> 47.7 us
  local copies, waits for them, and re-layouts: 50 us -> 23 us
  waiting for transfers between devices: 140 us -> 116 us
  Pallas kernels: 107 us -> 127 us
  matrix products: 38.2 us -> 20.8 us
    ppermute x66 -> x38, starting transfers between devices: 74.8 us -> 44.6 us  [swap_bits(): return lax.ppermute(array, ('dp', 'mp'), pairs)]
    ppermute x66 -> x38, waiting for transfers between devices: 132 us -> 102 us  [swap_bits(): return lax.ppermute(array, ('dp', 'mp'), pairs)]
    unnamed x276 -> x166, local copies, waits for them, and re-layouts: 27.4 us -> 5.12 us
    pallas_call x2 -> x5, Pallas kernels: 39.1 us -> 58 us  [the longest x3 29.9 us: in_vmem(): pl.pallas_call(kernel, in_specs=specs or [whole] * len(inputs), out_specs...]
    dot_general x12 -> x3, matrix products: 25 us -> 7.12 us  [dot32(): return lax.dot_general(left, right, dims, preferred_element_type=f32)]
    reduce_sum x5 -> x0, other arithmetic: 11.2 us -> none  [the longest x1 4.06 us: body(): gate_two_grad = jnp.sum(out_grad * unit_out, axis=0)]
    select_n x5 -> x3, other arithmetic: 15.1 us -> 6.85 us  [by_core(): jnp.where(core == 0, jnp.concatenate([mine, other], axis=axis), jnp.conca...]
    gather x2 -> x1, local copies, waits for them, and re-layouts: 7.74 us -> 1.79 us  [take_blocks(): return jnp.take(blocks, index, axis=0, mode='clip')]
  transfers between devices with their start and end apart: 85 -> 55, of which waited for: 39 -> 26; matrix products, arithmetic and copies ran while one was open for 25% -> 17% of each run, Pallas kernels for 13% -> 10%
where the time goes in v3:
time: 394 us; the launch traced here: 388 us
  Pallas kernels  127 us (32%)
  waiting for transfers between devices  116 us (29%)
  other arithmetic  48.8 us (12%)
  starting transfers between devices  47.7 us (12%)
  local copies, waits for them, and re-layouts  23 us (6%)
  matrix products  20.8 us (5%)
    ppermute x38, waiting for transfers between devices, swap_bits(): return lax.ppermute(array, ('dp', 'mp'), pairs)  102 us
    ppermute x38, starting transfers between devices, swap_bits(): return lax.ppermute(array, ('dp', 'mp'), pairs)  44.6 us
    pallas_call x3, Pallas kernels, in_vmem(): pl.pallas_call(kernel, in_specs=specs or [whole] * len(inputs), out_specs...  29.9 us
    pallas_call x1, Pallas kernels, attend_backward(): pl.pallas_call(attend_back_kernel, grid=(pairs,), in_specs=[tall(2 * PAIR...  28.7 us
    pallas_call x1, Pallas kernels, panel_gradients(): pl.pallas_call(lambda *refs: gradients_kernel(panel_rows, cuts, numbered[...  18.5 us
    pallas_call x1, Pallas kernels, attend_forward(): pl.pallas_call(attend_kernel, grid=(pairs,), in_specs=[tall(PAIR), tall(P...  16.9 us
    pallas_call x2, Pallas kernels, feed(): pl.pallas_call(feed_kernel, grid=(1,), in_specs=[whole, whole, pl.BlockSp...  15.7 us
    ppermute x17, waiting for transfers between devices, swap_core(): return lax.ppermute(array, 'mp', [(0, 1), (1, 0)])  14 us
  transfers between devices with their start and end apart: 55, of which 26 were waited for; matrix products, arithmetic and copies ran while one was open for 17% of the time, Pallas kernels for 10%

profile of v3, /device:TPU:0, one launch (start us, length us, event | category | flops | bytes accessed | tf_op | source)
XLA Modules:
  0.0 387.6 jit_solution(12606842687093896722)
XLA Ops:
  1.8 4.1 %collective-permute-start = (bf16[1,48,1024]{2,1,0:T(8,128)(2,1)S(1)}, bf16[1,48,1024]{2,1,0:T(8,128)(2,1)S(1)}, u32[]{:S(2)}, u32[]{:S(2)}) collective-permute-start(bf16[1,48,1024]{2,1,0:T(8,128)(2,1)S(1)} %fusion.66), channel_id=1, source_target_pairs={{0,16},{1,17},{2,18},{3,19},{4,20},{5,21},{6,22},{7,23},{8,24},{9,... | collective-permute-start | bytes 294920 | tf_op jit(solution)/shard_map/ppermute | solution.py:39
  8.0 2.7 collective-permute-done
  10.8 4.5 %collective-permute-done.1 = f32[8,3072]{1,0:T(8,128)S(1)} collective-permute-done((f32[8,3072]{1,0:T(8,128)S(1)}, f32[8,3072]{1,0:T(8,128)S(1)}, u32[]{:S(2)}, u32[]{:S(2)}) %collective-permute-start.1) | collective-permute-done | bytes 98336 | tf_op jit(solution)/shard_map/ppermute | solution.py:39
  15.8 1.7 collective-permute-start.3
  17.6 5.4 %collective-permute-done.3 = f32[8,3072]{1,0:T(8,128)S(1)} collective-permute-done((f32[8,3072]{1,0:T(8,128)S(1)}, f32[8,3072]{1,0:T(8,128)S(1)}, u32[]{:S(2)}, u32[]{:S(2)}) %collective-permute-start.3) | collective-permute-done | bytes 98336 | tf_op jit(solution)/shard_map/ppermute | solution.py:39
  23.1 1.6 collective-permute-start.4
  24.6 3.4 collective-permute-start.6
  28.7 4.1 %collective-permute-done.5 = f32[8,3072]{1,0:T(8,128)S(1)} collective-permute-done((f32[8,3072]{1,0:T(8,128)S(1)}, f32[8,3072]{1,0:T(8,128)S(1)}, u32[]{:S(2)}, u32[]{:S(2)}) %collective-permute-start.5) | collective-permute-done | bytes 98336 | tf_op jit(solution)/shard_map/ppermute | solution.py:39
  32.8 3.1 collective-permute-done.6
  39.0 17.0 %collective-permute-done.9 = bf16[1,336,512]{2,1,0:T(8,128)(2,1)S(1)} collective-permute-done((bf16[1,336,512]{2,1,0:T(8,128)(2,1)S(1)}, bf16[1,336,512]{2,1,0:T(8,128)(2,1)S(1)}, u32[]{:S(2)}, u32[]{:S(2)}) %collective-permute-start.9) | collective-permute-done | bytes 344096 | tf_op jit(solution)/shard_map/ppermute | solution.py:39
  59.7 2.2 fusion.100
  62.0 8.1 %collective-permute-done.11 = bf16[2,176,512]{2,1,0:T(8,128)(2,1)S(1)} collective-permute-done((bf16[2,176,512]{2,1,0:T(8,128)(2,1)S(1)}, bf16[2,176,512]{2,1,0:T(8,128)(2,1)S(1)}, u32[]{:S(2)}, u32[]{:S(2)}) %collective-permute-start.11) | collective-permute-done | bytes 360480 | tf_op jit(solution)/shard_map/ppermute | solution.py:39
  71.9 1.8 collective-permute-start.14
  76.9 1.5 pad_maximum_fusion.1.masked_ref
  79.9 9.4 %collective-permute-done.14 = bf16[2,2,176,512]{3,2,1,0:T(8,128)(2,1)S(1)} collective-permute-done((bf16[2,2,176,512]{3,2,1,0:T(8,128)(2,1)S(1)}, bf16[2,2,176,512]{3,2,1,0:T(8,128)(2,1)S(1)}, u32[]{:S(2)}, u32[]{:S(2)}) %collective-permute-start.14) | collective-permute-done | bytes 720928 | tf_op jit(solution)/shard_map/ppermute | solution.py:39
  89.8 1.8 pad_maximum_fusion
  92.8 2.3 pad_maximum_fusion.3
  95.1 1.6 collective-permute-start.17
  97.7 3.0 constant_dynamic-slice_fusion.1
  100.8 13.2 %text_forward.1 = (f32[512,1024]{1,0:T(8,128)}, f32[1,1024]{1,0:T(1,128)S(1)}, bf16[512,1024]{1,0:T(8,128)(2,1)S(1)}, bf16[512,512]{1,0:T(8,128)(2,1)S(1)}, f32[...) custom-call(s32[1]{0:T(128)} %bitcast.core_ref, ...), custom_call_target="tpu_custom_call" | custom-call | flops 1000 | bytes 1000 | tf_op jit(solution)/shard_map/text_forward/pallas_call | solution.py:655
  114.0 1.6 multiply_convert_fusion.1
  115.8 11.1 %collective-permute-done.17 = bf16[2,2,2,176,512]{4,3,2,1,0:T(8,128)(2,1)} collective-permute-done((bf16[2,2,2,176,512]{4,3,2,1,0:T(8,128)(2,1)}, bf16[2,2,2,176,512]{4,3,2,1,0:T(8,128)(2,1)}, u32[]{:S(2)}, u32[]{:S(2)}) %collective-permute-start.17) | collective-permute-done | bytes 1441824 | tf_op jit(solution)/shard_map/ppermute | solution.py:39
  126.9 9.6 %project.1 = (bf16[1024,512]{1,0:T(8,128)(2,1)S(1)}, bf16[1024,512]{1,0:T(8,128)(2,1)S(1)}, bf16[1024,512]{1,0:T(8,128)(2,1)S(1)}, bf16[8192,512]{1,0:T(8,128)(2,1)}) custom-call(s32[64]{0:T(128)S(1)} %pad_add_fusion.1.refs_0_, bf16[8,336,512]{2,1,0:T(8,128)(2,1)} %bitcast.26.refs_1_, bf16[8,176,512]{2,1,0:T(8,128)(2,1)} %bitcast.29.refs_2_, ...), custom_call_target="tpu_custom_call" | custom-call | flops 3221225472 | bytes 25165824 | tf_op jit(solution)/shard_map/project/pallas_call | solution.py:450
  136.7 16.9 %attend.1 = (bf16[1024,512]{1,0:T(8,128)(2,1)S(1)}, bf16[1024,1024]{1,0:T(8,128)(2,1)}) custom-call(bf16[1024,512]{1,0:T(8,128)(2,1)S(1)} %get-tuple-element.156.q_ref, bf16[1024,512]{1,0:T(8,128)(2,1)S(1)} %get-tuple-element.157.k_ref.kr_ref, bf16[1024,512]{1,0:T(8,128)(2,1)S(1)} %get-tuple-element.158.v_ref, bf16[1024,128]{1,0:T(8,128)(2,1)S(1)} %broadcast_in_dim.74.bias_ref), custom_call_target="tpu_custom_call" | custom-call | flops 17179869184 | bytes 6291456 | tf_op jit(solution)/shard_map/attend/pallas_call | solution.py:275
  153.7 2.4 convolution_convert_fusion
  156.1 2.6 collective-permute-done.18
  158.8 3.4 fusion.96
  163.2 2.5 collective-permute-done.19.n_ref.refs_6_
  165.7 7.5 %feed.3 = (bf16[512,1024]{1,0:T(8,128)(2,1)S(1)}, bf16[512,1024]{1,0:T(8,128)(2,1)S(1)}, bf16[512,1024]{1,0:T(8,128)(2,1)S(1)}, bf16[512,1024]{1,0:T(8,128)(2,1)S(1)}) custom-call(bf16[512,1024]{1,0:T(8,128)(2,1)S(1)} %collective-permute-done.19.n_ref.refs_6_, bf16[512,1024]{1,0:T(8,128)(2,1)} %get-tuple-element.163.g_ref.refs_8_, ...), custom_call_target="tpu_custom_call" | custom-call | flops 4294967296 | bytes 8388608 | tf_op jit(solution)/shard_map/feed/pallas_call | solution.py:494
  173.8 8.2 %feed.2 = (f32[512,1024]{1,0:T(8,128)}, f32[512,1024]{1,0:T(8,128)}, bf16[512,1024]{1,0:T(8,128)(2,1)S(1)}, bf16[512,1024]{1,0:T(8,128)(2,1)S(1)}) custom-call(bf16[512,1024]{1,0:T(8,128)(2,1)S(1)} %add_convert_fusion.1.n_ref.refs_5_, bf16[512,1024]{1,0:T(8,128)(2,1)S(1)} %get-tuple-element.161.g_ref.refs_7_, bf16[8,1024,512]{2,1,0:T(8,128)(2,1)} %bitcast.238), custom_call_target="tpu_custom_call" | custom-call | flops 4294967296 | bytes 8388608 | tf_op jit(solution)/shard_map/feed/pallas_call | solution.py:494
  182.1 3.6 multiply_reduce_fusion
  186.0 4.1 %add_convert_fusion = (bf16[512,1024]{1,0:T(8,128)(2,1)}, f32[1024]{0:T(1024)S(1)}, f32[1024]{0:T(1024)S(1)}, f32[512,1024]{1,0:T(8,128)S(1)}) fusion(f32[512,1024]{1,0:T(8,128)S(1)} %get-tuple-element.260, f32[512,1024]{1,0:T(8,128)} %get-tuple-element.209, bf16[512,1024]{1,0:T(8,128)(2,1)} %collective-permute-done.34, f32[1024]{0:T(1024)S(1)} %bitcast.249, ...), kind=kLoop, calls=%fused_computation.16 | loop fusion | flops 10483712 | bytes 14704644 | tf_op jit(solution)/shard_map/convert_element_type | solution.py:1081
  190.7 2.4 collective-permute-done.21.other_ref.refs_4_
  194.1 28.7 %attend_back.1 = (bf16[1024,512]{1,0:T(8,128)(2,1)S(1)}, bf16[1024,512]{1,0:T(8,128)(2,1)S(1)}, bf16[1024,512]{1,0:T(8,128)(2,1)S(1)}) custom-call(bf16[1024,1024]{1,0:T(8,128)(2,1)} %get-tuple-element.165.qa_ref, bf16[1024,512]{1,0:T(8,128)(2,1)S(1)} %get-tuple-element.157.k_ref.kr_ref, bf16[1024,512]{1,0:T(8,128)(2,1)} %copy-done.21, ...), custom_call_target="tpu_custom_call" | custom-call | flops 42949672960 | bytes 12582912 | tf_op jit(solution)/shard_map/attend_back/pallas_call | solution.py:357
  222.8 8.0 %inputs_grad.1 = (f32[512,1024]{1,0:T(8,128)}, bf16[512,1024]{1,0:T(8,128)(2,1)}) custom-call(bf16[1024,512]{1,0:T(8,128)(2,1)S(1)} %get-tuple-element.170.q_ref.refs_9_, bf16[1024,512]{1,0:T(8,128)(2,1)S(1)} %get-tuple-element.167.k_ref.refs_10_, bf16[1024,512]{1,0:T(8,128)(2,1)S(1)} %get-tuple-element.168.v_ref.refs_11_, bf16[8,1024,512]{2,1,0:T(8,128)(2,1)} %bitcast.240), custom_call_target="tpu_custom_call" | custom-call | flops 3221225472 | bytes 12582912 | tf_op jit(solution)/shard_map/inputs_grad/pallas_call | solution.py:523
  230.9 18.5 %gradients.1 = (bf16[4,336,512]{2,1,0:T(8,128)(2,1)}, bf16[4,176,512]{2,1,0:T(8,128)(2,1)S(1)}, bf16[4,336,512]{2,1,0:T(8,128)(2,1)}, bf16[4,176,512]{2,1,0:T(8,...) custom-call(s32[64]{0:T(128)S(1)} %pad_add_fusion.refs_0_, ...), custom_call_target="tpu_custom_call" | custom-call | flops 8589934592 | bytes 25165824 | tf_op jit(solution)/shard_map/gradients/pallas_call | solution.py:616
  251.2 2.5 collective-permute-start.22
  255.7 2.5 collective-permute-done.47
  258.2 4.7 %maximum_select_fusion.1 = bf16[1024,1024]{1,0:T(8,128)(2,1)} fusion(bf16[512,1024]{1,0:T(8,128)(2,1)} %collective-permute-done.47, bf16[512,1024]{1,0:T(8,128)(2,1)} %get-tuple-element.269, pred[]{:T(512)S(6)} %eq.18), kind=kLoop, calls=%fused_computation.15 | loop fusion | flops 9437184 | bytes 4194305 | tf_op jit(solution)/shard_map/jit(_where)/select_n | solution.py:47
  262.9 9.1 %stream_back.1 = (f32[512,1024]{1,0:T(8,128)S(1)}, bf16[512,1024]{1,0:T(8,128)(2,1)S(1)}, f32[512,512]{1,0:T(8,128)S(1)}, bf16[512,512]{1,0:T(8,128)(2,1)S(1)}, ...) custom-call(s32[1]{0:T(128)} %bitcast.core_ref, ...), custom_call_target="tpu_custom_call" | custom-call | flops 1000 | bytes 1000 | tf_op jit(solution)/shard_map/stream_back/pallas_call | solution.py:655
  272.6 1.8 fusion.1
  278.2 7.6 %text_back.1 = (f32[512,512]{1,0:T(8,128)S(1)}, f32[3,512]{1,0:T(4,128)S(1)}, f32[2,1024]{1,0:T(2,128)S(1)}, bf16[1536,1024]{1,0:T(8,128)(2,1)}) custom-call(f32[512,1024]{1,0:T(8,128)} %get-tuple-element.182.pre_ref, f32[512,1024]{1,0:T(8,128)} %get-tuple-element.190.grn_grad_ref, f32[1,1024]{1,0:T(1,128)S(1)} %get-tuple-element.191.energy_ref, ...), custom_call_target="tpu_custom_call" | custom-call | flops 1000 | bytes 1000 | tf_op jit(solution)/shard_map/text_back/pallas_call | solution.py:655
  285.9 2.1 collective-permute-done.26
  291.7 2.7 dynamic-slice_bitcast_fusion
  296.1 1.8 collective-permute-done.44
  297.9 2.2 fusion.16
  300.3 1.6 constant_dynamic-update-slice_fusion.9
  304.0 1.6 maximum_select_fusion
  305.6 6.3 %collective-permute-done.30 = bf16[1,176,512]{2,1,0:T(8,128)(2,1)S(1)} collective-permute-done((bf16[1,176,512]{2,1,0:T(8,128)(2,1)S(1)}, bf16[1,176,512]{2,1,0:T(8,128)(2,1)S(1)}, u32[]{:S(2)}, u32[]{:S(2)}) %collective-permute-start.30) | collective-permute-done | bytes 180256 | tf_op jit(solution)/shard_map/ppermute | solution.py:39
  311.9 1.9 fusion.2
  316.6 2.1 fusion
  318.7 1.8 gather_fusion
  320.5 1.6 fusion.101
  324.2 1.5 collective-permute-start.36
  327.0 2.0 collective-permute-start.46
  329.0 16.1 %collective-permute-done.39 = bf16[1,176,512]{2,1,0:T(8,128)(2,1)S(1)} collective-permute-done((bf16[1,176,512]{2,1,0:T(8,128)(2,1)S(1)}, bf16[1,176,512]{2,1,0:T(8,128)(2,1)S(1)}, u32[]{:S(2)}, u32[]{:S(2)}) %collective-permute-start.39) | collective-permute-done | bytes 180256 | tf_op jit(solution)/shard_map/ppermute | solution.py:39
  349.4 2.1 collective-permute-start.41
  351.4 4.1 %collective-permute-done.43 = f32[226,128]{1,0:T(8,128)S(1)} collective-permute-done((f32[226,128]{1,0:T(8,128)S(1)}, f32[226,128]{1,0:T(8,128)S(1)}, u32[]{:S(2)}, u32[]{:S(2)}) %collective-permute-start.43) | collective-permute-done | bytes 115744 | tf_op jit(solution)/shard_map/ppermute | solution.py:39
  355.5 3.8 collective-permute-done.42
  363.4 2.3 fusion.43
  368.6 2.0 collective-permute-done.52
  370.6 1.7 collective-permute-start.53
  372.3 2.9 fusion.11
  379.3 6.2 %multiply_subtract_fusion = (f32[64,6144]{1,0:T(8,128)}, f32[64,6144]{1,0:T(8,128)}, f32[64,6144]{1,0:T(8,128)}) fusion(f32[64,6144]{1,0:T(8,128)} %param.39, f32[64,6144]{1,0:T(8,128)} %param.40, f32[64,6144]{1,0:T(8,128)} %param.41, f32[8,6144]{1,0:T(8,128)S(1)} %constant_dynamic-update-slice_fusion.2, f32[8,1024]{1,0:T(8,128)} %copy-done.71, ...), kind=kOutput, calls=%fused_computation.33 | convolution fusion | flops 12634624 | bytes 9637892 | tf_op jit(solution)/shard_map/dot_general | solution.py:1258
  (367 shorter events, 61.5 us)
Async XLA Ops:
  0.6 361.1 %copy-start = (f32[512,512]{1,0:T(8,128)S(1)}, f32[512,512]{1,0:T(8,128)}, u32[]{:S(2)}) copy-start(f32[512,512]{1,0:T(8,128)} %param.35) | copy-start | bytes 3145732
  0.7 16.8 %copy-start.39 = (f32[512,512]{1,0:T(8,128)S(1)}, f32[512,512]{1,0:T(8,128)}, u32[]{:S(2)}) copy-start(f32[512,512]{1,0:T(8,128)} %param.31) | copy-start | bytes 3145732
  1.8 9.0 %collective-permute-start = (bf16[1,48,1024]{2,1,0:T(8,128)(2,1)S(1)}, bf16[1,48,1024]{2,1,0:T(8,128)(2,1)S(1)}, u32[]{:S(2)}, u32[]{:S(2)}) collective-permute-start(bf16[1,48,1024]{2,1,0:T(8,128)(2,1)S(1)} %fusion.66), channel_id=1, source_target_pairs={{0,16},{1,17},{2,18},{3,19},{4,20},{5,21},{6,22},{7,23},{8,24},{9,... | collective-permute-start | bytes 294920 | tf_op jit(solution)/shard_map/ppermute | solution.py:39
  6.6 18.0 %copy-start.71 = (f32[8,1024]{1,0:T(8,128)}, f32[8,1024]{1,0:T(8,128)S(1)}, u32[]{:S(2)}) copy-start(f32[8,1024]{1,0:T(8,128)S(1)} %convert_element_type.392) | copy-start | bytes 98308
  8.0 7.3 %collective-permute-start.1 = (f32[8,3072]{1,0:T(8,128)S(1)}, f32[8,3072]{1,0:T(8,128)S(1)}, u32[]{:S(2)}, u32[]{:S(2)}) collective-permute-start(f32[8,3072]{1,0:T(8,128)S(1)} %fusion.62), channel_id=1, source_target_pairs={{0,16},{1,17},{2,18},{3,19},{4,20},{5,21},{6,22},{7,23},{8,24},{9,... | collective-permute-start | bytes 294920 | tf_op jit(solution)/shard_map/ppermute | solution.py:39
  15.3 7.7 %collective-permute-start.2 = (bf16[2,48,1024]{2,1,0:T(8,128)(2,1)S(1)}, bf16[2,48,1024]{2,1,0:T(8,128)(2,1)S(1)}, u32[]{:S(2)}, u32[]{:S(2)}) collective-permute-start(bf16[2,48,1024]{2,1,0:T(8,128)(2,1)S(1)} %get-tuple-element.300), channel_id=1, source_target_pairs={{0,8},{1,9},{2,10},{3,11},{4,12},{5,13},{6,14},{7,15},{8,0},{9,1},... | collective-permute-start | bytes 589832 | tf_op jit(solution)/shard_map/ppermute | solution.py:39
  15.8 7.2 %collective-permute-start.3 = (f32[8,3072]{1,0:T(8,128)S(1)}, f32[8,3072]{1,0:T(8,128)S(1)}, u32[]{:S(2)}, u32[]{:S(2)}) collective-permute-start(f32[8,3072]{1,0:T(8,128)S(1)} %add.607), channel_id=1, source_target_pairs={{0,8},{1,9},{2,10},{3,11},{4,12},{5,13},{6,14},{7,15},{8,0},{9,1},... | collective-permute-start | bytes 294920 | tf_op jit(solution)/shard_map/ppermute | solution.py:39
  23.1 12.8 %collective-permute-start.4 = (bf16[2,2,48,1024]{3,2,1,0:T(8,128)(2,1)S(1)}, bf16[2,2,48,1024]{3,2,1,0:T(8,128)(2,1)S(1)}, u32[]{:S(2)}, u32[]{:S(2)}) collective-permute-start(bf16[2,2,48,1024]{3,2,1,0:T(8,128)(2,1)S(1)} %get-tuple-element.296), channel_id=1, source_target_pairs={{0,2},{1,5},{2,0},{3,7},{4,6},{5,1},{6,4},{7,3},{8,10},{9,13},{10,... | collective-permute-start | bytes 1179656 | tf_op jit(solution)/shard_map/ppermute | solution.py:39
  24.6 11.3 %collective-permute-start.6 = (bf16[1,176,512]{2,1,0:T(8,128)(2,1)S(1)}, bf16[1,176,512]{2,1,0:T(8,128)(2,1)S(1)}, u32[]{:S(2)}, u32[]{:S(2)}) collective-permute-start(bf16[1,176,512]{2,1,0:T(8,128)(2,1)S(1)} %slice.305), channel_id=1, source_target_pairs={{0,16},{1,17},{2,18},{3,19},{4,20},{5,21},{6,22},{7,23},{8,24},{9,... | collective-permute-start | bytes 540680 | tf_op jit(solution)/shard_map/ppermute | solution.py:39
  28.1 4.7 %collective-permute-start.5 = (f32[8,3072]{1,0:T(8,128)S(1)}, f32[8,3072]{1,0:T(8,128)S(1)}, u32[]{:S(2)}, u32[]{:S(2)}) collective-permute-start(f32[8,3072]{1,0:T(8,128)S(1)} %add.608), channel_id=1, source_target_pairs={{0,2},{1,5},{2,0},{3,7},{4,6},{5,1},{6,4},{7,3},{8,10},{9,13},{10,... | collective-permute-start | bytes 294920 | tf_op jit(solution)/shard_map/ppermute | solution.py:39
  36.7 19.3 %collective-permute-start.7 = (bf16[2,2,2,48,1024]{4,3,2,1,0:T(8,128)(2,1)S(1)}, bf16[2,2,2,48,1024]{4,3,2,1,0:T(8,128)(2,1)S(1)}, u32[]{:S(2)}, u32[]{:S(2)}) collective-permute-start(bf16[2,2,2,48,1024]{4,3,2,1,0:T(8,128)(2,1)S(1)} %get-tuple-element.290), channel_id=1, source_target_pairs={{0,4},{1,3},{2,6},{3,1},{4,0},{5,7},{6,2},{7,5},{8,12},{9,11},{10,... | collective-permute-start | bytes 2359304 | tf_op jit(solution)/shard_map/ppermute | solution.py:39
  37.3 18.7 %collective-permute-start.9 = (bf16[1,336,512]{2,1,0:T(8,128)(2,1)S(1)}, bf16[1,336,512]{2,1,0:T(8,128)(2,1)S(1)}, u32[]{:S(2)}, u32[]{:S(2)}) collective-permute-start(bf16[1,336,512]{2,1,0:T(8,128)(2,1)S(1)} %slice.304), channel_id=1, source_target_pairs={{0,16},{1,17},{2,18},{3,19},{4,20},{5,21},{6,22},{7,23},{8,24},{9,... | collective-permute-start | bytes 1032200 | tf_op jit(solution)/shard_map/ppermute | solution.py:39
  37.8 18.2 %collective-permute-start.8 = (f32[8,3072]{1,0:T(8,128)S(1)}, f32[8,3072]{1,0:T(8,128)S(1)}, u32[]{:S(2)}, u32[]{:S(2)}) collective-permute-start(f32[8,3072]{1,0:T(8,128)S(1)} %add.609), channel_id=1, source_target_pairs={{0,4},{1,3},{2,6},{3,1},{4,0},{5,7},{6,2},{7,5},{8,12},{9,11},{10,... | collective-permute-start | bytes 294920 | tf_op jit(solution)/shard_map/ppermute | solution.py:39
  56.2 14.0 %collective-permute-start.12 = (bf16[16,48,1024]{2,1,0:T(8,128)(2,1)S(1)}, bf16[16,48,1024]{2,1,0:T(8,128)(2,1)}, u32[]{:S(2)}, u32[]{:S(2)}) collective-permute-start(bf16[16,48,1024]{2,1,0:T(8,128)(2,1)S(1)} %bitcast.214), channel_id=1, source_target_pairs={{0,1},{1,0},{2,3},{3,2},{4,5},{5,4},{6,7},{7,6},{8,9},{9,8},{10,11... | collective-permute-start | bytes 4718600 | tf_op jit(solution)/shard_map/ppermute | solution.py:31
  57.5 12.6 %collective-permute-start.10 = (bf16[2,336,512]{2,1,0:T(8,128)(2,1)}, bf16[2,336,512]{2,1,0:T(8,128)(2,1)}, u32[]{:S(2)}, u32[]{:S(2)}) collective-permute-start(bf16[2,336,512]{2,1,0:T(8,128)(2,1)} %get-tuple-element.294), channel_id=1, source_target_pairs={{0,2},{1,5},{2,0},{3,7},{4,6},{5,1},{6,4},{7,3},{8,10},{9,13},{10,... | collective-permute-start | bytes 2064392 | tf_op jit(solution)/shard_map/ppermute | solution.py:39
  59.6 10.5 %collective-permute-start.11 = (bf16[2,176,512]{2,1,0:T(8,128)(2,1)S(1)}, bf16[2,176,512]{2,1,0:T(8,128)(2,1)S(1)}, u32[]{:S(2)}, u32[]{:S(2)}) collective-permute-start(bf16[2,176,512]{2,1,0:T(8,128)(2,1)S(1)} %get-tuple-element.298), channel_id=1, source_target_pairs={{0,8},{1,9},{2,10},{3,11},{4,12},{5,13},{6,14},{7,15},{8,0},{9,1},... | collective-permute-start | bytes 1081352 | tf_op jit(solution)/shard_map/ppermute | solution.py:39
  71.4 18.4 %collective-permute-start.13 = (bf16[2,2,336,512]{3,2,1,0:T(8,128)(2,1)S(1)}, bf16[2,2,336,512]{3,2,1,0:T(8,128)(2,1)S(1)}, u32[]{:S(2)}, u32[]{:S(2)}) collective-permute-start(bf16[2,2,336,512]{3,2,1,0:T(8,128)(2,1)S(1)} %get-tuple-element.282), channel_id=1, source_target_pairs={{0,4},{1,9},{2,6},{3,11},{4,0},{5,13},{6,2},{7,15},{8,12},{9,1},{1... | collective-permute-start | bytes 4128776 | tf_op jit(solution)/shard_map/ppermute | solution.py:39
  71.9 17.4 %collective-permute-start.14 = (bf16[2,2,176,512]{3,2,1,0:T(8,128)(2,1)S(1)}, bf16[2,2,176,512]{3,2,1,0:T(8,128)(2,1)S(1)}, u32[]{:S(2)}, u32[]{:S(2)}) collective-permute-start(bf16[2,2,176,512]{3,2,1,0:T(8,128)(2,1)S(1)} %get-tuple-element.292), channel_id=1, source_target_pairs={{0,2},{1,3},{2,0},{3,1},{4,6},{5,7},{6,4},{7,5},{8,10},{9,11},{10,... | collective-permute-start | bytes 2162696 | tf_op jit(solution)/shard_map/ppermute | solution.py:39
  73.7 6.1 %collective-permute-start.15 = (f32[8,3072]{1,0:T(8,128)S(1)}, f32[8,3072]{1,0:T(8,128)S(1)}, u32[]{:S(2)}, u32[]{:S(2)}) collective-permute-start(f32[8,3072]{1,0:T(8,128)S(1)} %add.610), channel_id=1, source_target_pairs={{0,1},{1,0},{2,3},{3,2},{4,5},{5,4},{6,7},{7,6},{8,9},{9,8},{10,11... | collective-permute-start | bytes 294920 | tf_op jit(solution)/shard_map/ppermute | solution.py:31
  91.6 35.4 %collective-permute-start.16 = (bf16[2,2,2,336,512]{4,3,2,1,0:T(8,128)(2,1)}, bf16[2,2,2,336,512]{4,3,2,1,0:T(8,128)(2,1)}, u32[]{:S(2)}, u32[]{:S(2)}) collective-permute-start(bf16[2,2,2,336,512]{4,3,2,1,0:T(8,128)(2,1)} %pad_maximum_fusion), channel_id=1, source_target_pairs={{0,8},{1,3},{2,10},{3,1},{4,12},{5,7},{6,14},{7,5},{8,0},{9,11},{1... | collective-permute-start | bytes 8257544 | tf_op jit(solution)/shard_map/ppermute | solution.py:39
  95.1 31.8 %collective-permute-start.17 = (bf16[2,2,2,176,512]{4,3,2,1,0:T(8,128)(2,1)}, bf16[2,2,2,176,512]{4,3,2,1,0:T(8,128)(2,1)}, u32[]{:S(2)}, u32[]{:S(2)}) collective-permute-start(bf16[2,2,2,176,512]{4,3,2,1,0:T(8,128)(2,1)} %pad_maximum_fusion.3), channel_id=1, source_target_pairs={{0,4},{1,5},{2,6},{3,7},{4,0},{5,1},{6,2},{7,3},{8,12},{9,13},{10,... | collective-permute-start | bytes 4325384 | tf_op jit(solution)/shard_map/ppermute | solution.py:39
  100.8 13.3 %copy-start.38 = (bf16[1024,1024]{1,0:T(8,128)(2,1)S(1)}, bf16[1024,1024]{1,0:T(8,128)(2,1)}, u32[]{:S(2)}) copy-start(bf16[1024,1024]{1,0:T(8,128)(2,1)} %param.25) | copy-start | bytes 6291460
  114.0 12.9 %copy-start.15 = (f32[1024,128]{1,0:T(8,128)S(1)}, f32[1024,128]{1,0:T(8,128)}, u32[]{:S(2)}) copy-start(f32[1024,128]{1,0:T(8,128)} %get-tuple-element.155.refs_8_.sin_ref) | copy-start | bytes 1572868
  114.0 12.9 %copy-start.16 = (f32[1024,128]{1,0:T(8,128)S(1)}, f32[1024,128]{1,0:T(8,128)}, u32[]{:S(2)}) copy-start(f32[1024,128]{1,0:T(8,128)} %get-tuple-element.154.refs_7_.cos_ref) | copy-start | bytes 1572868
  115.8 58.0 %copy-start.6 = (bf16[512,1024]{1,0:T(8,128)(2,1)}, bf16[512,1024]{1,0:T(8,128)(2,1)S(1)}, u32[]{:S(2)}) copy-start(bf16[512,1024]{1,0:T(8,128)(2,1)S(1)} %get-tuple-element.161.g_ref.refs_7_) | copy-start | bytes 3145732
  136.5 17.2 %copy-start.21 = (bf16[1024,512]{1,0:T(8,128)(2,1)}, bf16[1024,512]{1,0:T(8,128)(2,1)S(1)}, u32[]{:S(2)}) copy-start(bf16[1024,512]{1,0:T(8,128)(2,1)S(1)} %get-tuple-element.158.v_ref) | copy-start | bytes 3145732
  156.1 2.7 collective-permute-start.18
  163.0 2.7 collective-permute-start.19
  173.2 8.8 %collective-permute-start.20 = (bf16[512,1024]{1,0:T(8,128)(2,1)S(1)}, bf16[512,1024]{1,0:T(8,128)(2,1)}, u32[]{:S(2)}, u32[]{:S(2)}) collective-permute-start(bf16[512,1024]{1,0:T(8,128)(2,1)S(1)} %get-tuple-element.164), channel_id=1, source_target_pairs={{0,1},{1,0},{2,3},{3,2},{4,5},{5,4},{6,7},{7,6},{8,9},{9,8},{10,11... | collective-permute-start | bytes 3145736 | tf_op jit(solution)/shard_map/ppermute | solution.py:31
  173.4 12.3 %collective-permute-start.34 = (bf16[512,1024]{1,0:T(8,128)(2,1)S(1)}, bf16[512,1024]{1,0:T(8,128)(2,1)}, u32[]{:S(2)}, u32[]{:S(2)}) collective-permute-start(bf16[512,1024]{1,0:T(8,128)(2,1)S(1)} %get-tuple-element.210), channel_id=1, source_target_pairs={{0,1},{1,0},{2,3},{3,2},{4,5},{5,4},{6,7},{7,6},{8,9},{9,8},{10,11... | collective-permute-start | bytes 3145736 | tf_op jit(solution)/shard_map/ppermute | solution.py:31
  190.4 2.7 collective-permute-start.21
  251.2 21.4 %collective-permute-start.22 = (bf16[2,2,1,336,512]{4,3,1,0,2:T(8,128)(2,1)}, bf16[2,2,1,336,512]{4,3,1,0,2:T(8,128)(2,1)}, u32[]{:S(2)}, u32[]{:S(2)}) collective-permute-start(bf16[2,2,1,336,512]{4,3,1,0,2:T(8,128)(2,1)} %bitcast.270), channel_id=1, source_target_pairs={{0,8},{1,3},{2,10},{3,1},{4,12},{5,7},{6,14},{7,5},{8,0},{9,11},{1... | collective-permute-start | bytes 4128776 | tf_op jit(solution)/shard_map/ppermute | solution.py:39
  253.7 4.5 %collective-permute-start.47 = (bf16[512,1024]{1,0:T(8,128)(2,1)}, bf16[512,1024]{1,0:T(8,128)(2,1)}, u32[]{:S(2)}, u32[]{:S(2)}) collective-permute-start(bf16[512,1024]{1,0:T(8,128)(2,1)} %get-tuple-element.269), channel_id=1, source_target_pairs={{0,1},{1,0},{2,3},{3,2},{4,5},{5,4},{6,7},{7,6},{8,9},{9,8},{10,11... | collective-permute-start | bytes 3145736 | tf_op jit(solution)/shard_map/ppermute | solution.py:31
  253.7 9.2 %collective-permute-start.24 = (bf16[512,1024]{1,0:T(8,128)(2,1)}, bf16[512,1024]{1,0:T(8,128)(2,1)S(1)}, u32[]{:S(2)}, u32[]{:S(2)}) collective-permute-start(bf16[512,1024]{1,0:T(8,128)(2,1)} %get-tuple-element.180), channel_id=1, source_target_pairs={{0,1},{1,0},{2,3},{3,2},{4,5},{5,4},{6,7},{7,6},{8,9},{9,8},{10,11... | collective-permute-start | bytes 3145736 | tf_op jit(solution)/shard_map/ppermute | solution.py:31
  254.2 18.4 %collective-permute-start.23 = (bf16[2,2,1,176,512]{4,3,1,0,2:T(8,128)(2,1)}, bf16[2,2,1,176,512]{4,3,1,0,2:T(8,128)(2,1)}, u32[]{:S(2)}, u32[]{:S(2)}) collective-permute-start(bf16[2,2,1,176,512]{4,3,1,0,2:T(8,128)(2,1)} %bitcast.40), channel_id=1, source_target_pairs={{0,4},{1,5},{2,6},{3,7},{4,0},{5,1},{6,2},{7,3},{8,12},{9,13},{10,... | collective-permute-start | bytes 2162696 | tf_op jit(solution)/shard_map/ppermute | solution.py:39
  272.6 15.4 %collective-permute-start.28 = (f32[512,1024]{1,0:T(8,128)S(1)}, f32[512,1024]{1,0:T(8,128)S(1)}, u32[]{:S(2)}, u32[]{:S(2)}) collective-permute-start(f32[512,1024]{1,0:T(8,128)S(1)} %get-tuple-element.199), channel_id=1, source_target_pairs={{0,1},{1,0},{2,3},{3,2},{4,5},{5,4},{6,7},{7,6},{8,9},{9,8},{10,11... | collective-permute-start | bytes 6291464 | tf_op jit(solution)/shard_map/ppermute | solution.py:31
  274.5 13.5 %collective-permute-start.25 = (bf16[2,1,336,512]{3,2,0,1:T(8,128)(2,1)S(1)}, bf16[2,1,336,512]{3,2,0,1:T(8,128)(2,1)S(1)}, u32[]{:S(2)}, u32[]{:S(2)}) collective-permute-start(bf16[2,1,336,512]{3,2,0,1:T(8,128)(2,1)S(1)} %slice_bitcast_fusion.2), channel_id=1, source_target_pairs={{0,4},{1,9},{2,6},{3,11},{4,0},{5,13},{6,2},{7,15},{8,12},{9,1},{1... | collective-permute-start | bytes 2064392 | tf_op jit(solution)/shard_map/ppermute | solution.py:39
  275.7 2.4 collective-permute-start.27
  277.1 10.9 %collective-permute-start.26 = (bf16[2,1,176,512]{3,2,0,1:T(8,128)(2,1)S(1)}, bf16[2,1,176,512]{3,2,0,1:T(8,128)(2,1)S(1)}, u32[]{:S(2)}, u32[]{:S(2)}) collective-permute-start(bf16[2,1,176,512]{3,2,0,1:T(8,128)(2,1)S(1)} %slice_bitcast_fusion.9), channel_id=1, source_target_pairs={{0,2},{1,3},{2,0},{3,1},{4,6},{5,7},{6,4},{7,5},{8,10},{9,11},{10,... | collective-permute-start | bytes 1081352 | tf_op jit(solution)/shard_map/ppermute | solution.py:39
  288.9 22.9 %collective-permute-start.29 = (bf16[1,336,512]{2,1,0:T(8,128)(2,1)}, bf16[1,336,512]{2,1,0:T(8,128)(2,1)S(1)}, u32[]{:S(2)}, u32[]{:S(2)}) collective-permute-start(bf16[1,336,512]{2,1,0:T(8,128)(2,1)} %slice_bitcast_fusion.13), channel_id=1, source_target_pairs={{0,2},{1,5},{2,0},{3,7},{4,6},{5,1},{6,4},{7,3},{8,10},{9,13},{10,... | collective-permute-start | bytes 1032200 | tf_op jit(solution)/shard_map/ppermute | solution.py:39
  289.5 22.4 %collective-permute-start.31 = (bf16[2,2,1,336,512]{4,3,1,2,0:T(8,128)(2,1)}, bf16[2,2,1,336,512]{4,3,1,2,0:T(8,128)(2,1)}, u32[]{:S(2)}, u32[]{:S(2)}) collective-permute-start(bf16[2,2,1,336,512]{4,3,1,2,0:T(8,128)(2,1)} %bitcast.56), channel_id=1, source_target_pairs={{0,8},{1,3},{2,10},{3,1},{4,12},{5,7},{6,14},{7,5},{8,0},{9,11},{1... | collective-permute-start | bytes 4128776 | tf_op jit(solution)/shard_map/ppermute | solution.py:39
  290.8 21.1 %collective-permute-start.32 = (bf16[2,2,1,176,512]{4,3,1,2,0:T(8,128)(2,1)}, bf16[2,2,1,176,512]{4,3,1,2,0:T(8,128)(2,1)}, u32[]{:S(2)}, u32[]{:S(2)}) collective-permute-start(bf16[2,2,1,176,512]{4,3,1,2,0:T(8,128)(2,1)} %bitcast.57), channel_id=1, source_target_pairs={{0,4},{1,5},{2,6},{3,7},{4,0},{5,1},{6,2},{7,3},{8,12},{9,13},{10,... | collective-permute-start | bytes 2162696 | tf_op jit(solution)/shard_map/ppermute | solution.py:39
  294.5 17.4 %collective-permute-start.33 = (bf16[16,48,1024]{2,1,0:T(8,128)(2,1)}, bf16[16,48,1024]{2,1,0:T(8,128)(2,1)}, u32[]{:S(2)}, u32[]{:S(2)}) collective-permute-start(bf16[16,48,1024]{2,1,0:T(8,128)(2,1)} %dynamic-slice_bitcast_fusion), channel_id=1, source_target_pairs={{0,1},{1,0},{2,3},{3,2},{4,5},{5,4},{6,7},{7,6},{8,9},{9,8},{10,11... | collective-permute-start | bytes 4718600 | tf_op jit(solution)/shard_map/ppermute | solution.py:31
  295.5 2.4 collective-permute-start.44
  300.0 2.7 collective-permute-start.45
  302.8 9.1 %collective-permute-start.30 = (bf16[1,176,512]{2,1,0:T(8,128)(2,1)S(1)}, bf16[1,176,512]{2,1,0:T(8,128)(2,1)S(1)}, u32[]{:S(2)}, u32[]{:S(2)}) collective-permute-start(bf16[1,176,512]{2,1,0:T(8,128)(2,1)S(1)} %slice_bitcast_fusion.18), channel_id=1, source_target_pairs={{0,8},{1,9},{2,10},{3,11},{4,12},{5,13},{6,14},{7,15},{8,0},{9,1},... | collective-permute-start | bytes 540680 | tf_op jit(solution)/shard_map/ppermute | solution.py:39
  315.1 30.0 %collective-permute-start.35 = (bf16[2,1,336,512]{3,2,1,0:T(8,128)(2,1)}, bf16[2,1,336,512]{3,2,1,0:T(8,128)(2,1)}, u32[]{:S(2)}, u32[]{:S(2)}) collective-permute-start(bf16[2,1,336,512]{3,2,1,0:T(8,128)(2,1)} %slice_bitcast_fusion), channel_id=1, source_target_pairs={{0,4},{1,9},{2,6},{3,11},{4,0},{5,13},{6,2},{7,15},{8,12},{9,1},{1... | collective-permute-start | bytes 2064392 | tf_op jit(solution)/shard_map/ppermute | solution.py:39
  322.1 23.1 %collective-permute-start.37 = (bf16[2,2,2,48,1024]{4,3,2,1,0:T(8,128)(2,1)S(1)}, bf16[2,2,2,48,1024]{4,3,2,1,0:T(8,128)(2,1)S(1)}, u32[]{:S(2)}, u32[]{:S(2)}) collective-permute-start(bf16[2,2,2,48,1024]{4,3,2,1,0:T(8,128)(2,1)S(1)} %bitcast.228), channel_id=1, source_target_pairs={{0,4},{1,3},{2,6},{3,1},{4,0},{5,7},{6,2},{7,5},{8,12},{9,11},{10,... | collective-permute-start | bytes 2359304 | tf_op jit(solution)/shard_map/ppermute | solution.py:39
  322.8 22.4 %copy-start.37 = (bf16[2,2,1,336,512]{4,3,1,2,0:T(8,128)(2,1)S(1)}, bf16[2,2,1,336,512]{4,3,1,2,0:T(8,128)(2,1)}, u32[]{:S(2)}) copy-start(bf16[2,2,1,336,512]{4,3,1,2,0:T(8,128)(2,1)} %copy-done.36) | copy-start | bytes 4128772
  324.2 20.9 %collective-permute-start.36 = (bf16[2,1,176,512]{3,2,1,0:T(8,128)(2,1)S(1)}, bf16[2,1,176,512]{3,2,1,0:T(8,128)(2,1)S(1)}, u32[]{:S(2)}, u32[]{:S(2)}) collective-permute-start(bf16[2,1,176,512]{3,2,1,0:T(8,128)(2,1)S(1)} %slice_bitcast_fusion.7), channel_id=1, source_target_pairs={{0,2},{1,3},{2,0},{3,1},{4,6},{5,7},{6,4},{7,5},{8,10},{9,11},{10,... | collective-permute-start | bytes 1081352 | tf_op jit(solution)/shard_map/ppermute | solution.py:39
  325.8 1.2 collective-permute-start.38
  325.8 19.3 %collective-permute-start.39 = (bf16[1,176,512]{2,1,0:T(8,128)(2,1)S(1)}, bf16[1,176,512]{2,1,0:T(8,128)(2,1)S(1)}, u32[]{:S(2)}, u32[]{:S(2)}) collective-permute-start(bf16[1,176,512]{2,1,0:T(8,128)(2,1)S(1)} %fusion.65), channel_id=1, source_target_pairs={{0,16},{1,17},{2,18},{3,19},{4,20},{5,21},{6,22},{7,23},{8,24},{9,... | collective-permute-start | bytes 540680 | tf_op jit(solution)/shard_map/ppermute | solution.py:39
  327.0 32.5 %collective-permute-start.46 = (bf16[1,336,512]{2,1,0:T(8,128)(2,1)S(1)}, bf16[1,336,512]{2,1,0:T(8,128)(2,1)S(1)}, u32[]{:S(2)}, u32[]{:S(2)}) collective-permute-start(bf16[1,336,512]{2,1,0:T(8,128)(2,1)S(1)} %fusion.55), channel_id=1, source_target_pairs={{0,16},{1,17},{2,18},{3,19},{4,20},{5,21},{6,22},{7,23},{8,24},{9,... | collective-permute-start | bytes 1032200 | tf_op jit(solution)/shard_map/ppermute | solution.py:39
  346.5 13.0 %collective-permute-start.40 = (bf16[1,336,512]{2,1,0:T(8,128)(2,1)S(1)}, bf16[1,336,512]{2,1,0:T(8,128)(2,1)S(1)}, u32[]{:S(2)}, u32[]{:S(2)}) collective-permute-start(bf16[1,336,512]{2,1,0:T(8,128)(2,1)S(1)} %slice_bitcast_fusion.12), channel_id=1, source_target_pairs={{0,2},{1,5},{2,0},{3,7},{4,6},{5,1},{6,4},{7,3},{8,10},{9,13},{10,... | collective-permute-start | bytes 1032200 | tf_op jit(solution)/shard_map/ppermute | solution.py:39
  347.8 11.5 %collective-permute-start.42 = (bf16[2,2,48,1024]{3,2,1,0:T(8,128)(2,1)S(1)}, bf16[2,2,48,1024]{3,2,1,0:T(8,128)(2,1)S(1)}, u32[]{:S(2)}, u32[]{:S(2)}) collective-permute-start(bf16[2,2,48,1024]{3,2,1,0:T(8,128)(2,1)S(1)} %slice_bitcast_fusion.4), channel_id=1, source_target_pairs={{0,2},{1,5},{2,0},{3,7},{4,6},{5,1},{6,4},{7,3},{8,10},{9,13},{10,... | collective-permute-start | bytes 1179656 | tf_op jit(solution)/shard_map/ppermute | solution.py:39
  349.3 6.2 %collective-permute-start.43 = (f32[226,128]{1,0:T(8,128)S(1)}, f32[226,128]{1,0:T(8,128)S(1)}, u32[]{:S(2)}, u32[]{:S(2)}) collective-permute-start(f32[226,128]{1,0:T(8,128)S(1)} %maximum_bitcast_fusion), channel_id=1, source_target_pairs={{0,8},{1,3},{2,10},{3,1},{4,12},{5,7},{6,14},{7,5},{8,0},{9,11},{1... | collective-permute-start | bytes 347144 | tf_op jit(solution)/shard_map/ppermute | solution.py:39
  349.4 10.1 %collective-permute-start.41 = (bf16[1,176,512]{2,1,0:T(8,128)(2,1)S(1)}, bf16[1,176,512]{2,1,0:T(8,128)(2,1)S(1)}, u32[]{:S(2)}, u32[]{:S(2)}) collective-permute-start(bf16[1,176,512]{2,1,0:T(8,128)(2,1)S(1)} %slice_bitcast_fusion.16), channel_id=1, source_target_pairs={{0,8},{1,9},{2,10},{3,11},{4,12},{5,13},{6,14},{7,15},{8,0},{9,1},... | collective-permute-start | bytes 540680 | tf_op jit(solution)/shard_map/ppermute | solution.py:39
  359.5 7.6 %collective-permute-start.48 = (bf16[2,48,1024]{2,1,0:T(8,128)(2,1)S(1)}, bf16[2,48,1024]{2,1,0:T(8,128)(2,1)S(1)}, u32[]{:S(2)}, u32[]{:S(2)}) collective-permute-start(bf16[2,48,1024]{2,1,0:T(8,128)(2,1)S(1)} %slice_bitcast_fusion.14), channel_id=1, source_target_pairs={{0,8},{1,9},{2,10},{3,11},{4,12},{5,13},{6,14},{7,15},{8,0},{9,1},... | collective-permute-start | bytes 589832 | tf_op jit(solution)/shard_map/ppermute | solution.py:39
  359.6 6.1 %collective-permute-start.51 = (f32[226,128]{1,0:T(8,128)S(1)}, f32[226,128]{1,0:T(8,128)S(1)}, u32[]{:S(2)}, u32[]{:S(2)}) collective-permute-start(f32[226,128]{1,0:T(8,128)S(1)} %fusion.87), channel_id=1, source_target_pairs={{0,2},{1,5},{2,0},{3,7},{4,6},{5,1},{6,4},{7,3},{8,10},{9,13},{10,... | collective-permute-start | bytes 347144 | tf_op jit(solution)/shard_map/ppermute | solution.py:39
  365.7 4.9 %collective-permute-start.52 = (f32[226,128]{1,0:T(8,128)S(1)}, f32[226,128]{1,0:T(8,128)S(1)}, u32[]{:S(2)}, u32[]{:S(2)}) collective-permute-start(f32[226,128]{1,0:T(8,128)S(1)} %add.708), channel_id=1, source_target_pairs={{0,4},{1,9},{2,6},{3,11},{4,0},{5,13},{6,2},{7,15},{8,12},{9,1},{1... | collective-permute-start | bytes 347144 | tf_op jit(solution)/shard_map/ppermute | solution.py:39
  367.2 9.3 %collective-permute-start.49 = (bf16[1,48,1024]{2,1,0:T(8,128)(2,1)S(1)}, bf16[1,48,1024]{2,1,0:T(8,128)(2,1)S(1)}, u32[]{:S(2)}, u32[]{:S(2)}) collective-permute-start(bf16[1,48,1024]{2,1,0:T(8,128)(2,1)S(1)} %slice.437), channel_id=1, source_target_pairs={{0,16},{1,17},{2,18},{3,19},{4,20},{5,21},{6,22},{7,23},{8,24},{9,... | collective-permute-start | bytes 294920 | tf_op jit(solution)/shard_map/ppermute | solution.py:39
  370.6 5.8 %collective-permute-start.53 = (f32[226,128]{1,0:T(8,128)S(1)}, f32[226,128]{1,0:T(8,128)S(1)}, u32[]{:S(2)}, u32[]{:S(2)}) collective-permute-start(f32[226,128]{1,0:T(8,128)S(1)} %add.709), channel_id=1, source_target_pairs={{0,16},{1,17},{2,18},{3,19},{4,20},{5,21},{6,22},{7,23},{8,24},{9,... | collective-permute-start | bytes 347144 | tf_op jit(solution)/shard_map/ppermute | solution.py:39
  376.4 1.4 collective-permute-start.54
  376.5 9.6 %collective-permute-start.50 = (f32[48,1024]{1,0:T(8,128)S(1)}, f32[48,1024]{1,0:T(8,128)S(1)}, u32[]{:S(2)}, u32[]{:S(2)}) collective-permute-start(f32[48,1024]{1,0:T(8,128)S(1)} %add_bitcast_fusion), channel_id=1, source_target_pairs={{0,1},{1,0},{2,3},{3,2},{4,5},{5,4},{6,7},{7,6},{8,9},{9,8},{10,11... | collective-permute-start | bytes 589832 | tf_op jit(solution)/shard_map/ppermute | solution.py:31
  (66 other events, 294.0 us)

commit v4 on v3

--- a/solution.py
+++ b/solution.py
@@ -24,7 +24,6 @@
 learn_rate = 0.03
 vector_rate = 0.3
 norm_eps = 1e-06
-solver = lax.Precision.HIGH
 
 
 def swap_core(array):
@@ -142,23 +141,15 @@
     return (values >> which) & 1
 
 
-def lead_place(slots, order, high_count):
-    return (bit_of(slots, order[1]) * 2 + bit_of(slots, order[0])) * high_count + (slots >> 4)
-
-
-def panel_places(core, slots, high_count, apart):
+def panel_places(core, slots, high_count, apart=False):
     rows = []
     for orders in axis_orders:
         far = bit_of(slots, 3)
-        which = [bit_of(slots, order[2]) + 2 * far * apart for order in orders]
-        lead = [
-            lead_place(slots, order, high_count)
-            if apart
-            else (bit_of(slots, order[1]) * 2 + bit_of(slots, order[0])) * 2 * high_count
-            + far * high_count
-            + (slots >> 4)
-            for order in orders
-        ]
+        which = [bit_of(slots, order[2]) + (2 * far if apart else 0) for order in orders]
+        lead = [bit_of(slots, order[1]) * 2 + bit_of(slots, order[0]) for order in orders]
+        if not apart:
+            lead = [place * 2 + far for place in lead]
+        lead = [place * high_count + (slots >> 4) for place in lead]
         rows += [jnp.where(core == 0, *which), jnp.where(core == 0, *lead)]
     return jnp.concatenate(rows).astype(jnp.int32)
 
@@ -185,12 +176,16 @@
     return jnp.where(core == 0, *slots)
 
 
+beside = pl.CostEstimate(flops=1000, bytes_accessed=1000, transcendentals=0)
+
 NT = (((1,), (1,)), ((), ()))
 NN = (((1,), (0,)), ((), ()))
 TN = (((0,), (0,)), ((), ()))
 ROWS = 256
+LONG_ROWS = 512
 PAIR = 2 * HEAD
-vmem_bytes = 48 * 1024 * 1024
+vmem_bytes = 12 * 1024 * 1024
+gradient_bytes = 20 * 1024 * 1024
 
 
 def dot32(left, right, dims=NN):
@@ -215,8 +210,8 @@
 
 def attend_kernel(q_ref, k_ref, v_ref, bias_ref, o_ref, qa_ref):
     lane = lax.broadcasted_iota(jnp.int32, (LEN, PAIR), 1)
-    lane_rows = lax.broadcasted_iota(jnp.int32, (ROWS, PAIR), 1)
-    row_index = lax.broadcasted_iota(jnp.int32, (PAIR, ROWS), 0)
+    lane_rows = lax.broadcasted_iota(jnp.int32, (LONG_ROWS, PAIR), 1)
+    row_index = lax.broadcasted_iota(jnp.int32, (PAIR, LONG_ROWS), 0)
     q_wide = q_ref[...].astype(f32)
     k_wide = k_ref[...].astype(f32)
     values_t = v_ref[...].T
@@ -231,11 +226,11 @@
         qa_ref[:, head * PAIR : (head + 1) * PAIR] = jnp.where(
             own, q_wide, jnp.where(lane == spare, 1.0, 0.0)
         ).astype(bf16)
-    steps = [(block, head) for block in range(LEN // ROWS) for head in range(2)]
+    steps = [(block, head) for block in range(LEN // LONG_ROWS) for head in range(2)]
 
     def scores_of(step):
         block, head = step
-        rows = slice(block * ROWS, (block + 1) * ROWS)
+        rows = slice(block * LONG_ROWS, (block + 1) * LONG_ROWS)
         return dot32(keys[head], qa_ref[rows, head * PAIR : (head + 1) * PAIR], NT)
 
     following = scores_of(steps[0])
@@ -243,9 +238,9 @@
         scores = following
         if position + 1 < len(steps):
             following = scores_of(steps[position + 1])
-        rows = slice(block * ROWS, (block + 1) * ROWS)
+        rows = slice(block * LONG_ROWS, (block + 1) * LONG_ROWS)
         if head == 0:
-            outs, extra = [], jnp.zeros((PAIR, ROWS), f32)
+            outs, extra = [], jnp.zeros((PAIR, LONG_ROWS), f32)
         spare = (1 - head) * HEAD
         highest = jnp.max(scores, axis=0, keepdims=True)
         weights = jnp.exp(scores - highest)
@@ -349,10 +344,10 @@
     dv_ref[...] = jnp.where(first, dva_ref[:, :PAIR], dva_ref[:, PAIR:]).astype(bf16)
 
 
-def attend_backward(queries, keys, values, outputs, grad_mine, grad_other, stacked, cosine, sine, bias):
-    width = values.shape[1]
+def attend_backward(side, queries, keys, values, outputs, grad_mine, grad_other, stacked, cosine, sine, bias):
+    width = values.shape[1] // 2
     pairs = width // PAIR
-    tall = lambda columns: pl.BlockSpec((LEN, columns), lambda pair: (0, pair))
+    tall = lambda columns: pl.BlockSpec((LEN, columns), lambda pair: (0, pair + side * pairs))
     whole = lambda shape: pl.BlockSpec(shape, lambda pair: (0, 0))
     return pl.pallas_call(
         attend_back_kernel,
@@ -360,9 +355,9 @@
         in_specs=[tall(2 * PAIR)]
         + [tall(PAIR)] * 3
         + [whole(grad_mine.shape)] * 2
-        + [pl.BlockSpec((1, D, PAIR), lambda pair: (3, 0, pair))]
+        + [pl.BlockSpec((1, D, PAIR), lambda pair: (3, 0, pair + side * pairs))]
         + [whole((LEN, PAIR))] * 3,
-        out_specs=[tall(PAIR)] * 3,
+        out_specs=[pl.BlockSpec((LEN, PAIR), lambda pair: (0, pair))] * 3,
         out_shape=[jax.ShapeDtypeStruct((LEN, width), bf16)] * 3,
         scratch_shapes=[
             pltpu.VMEM((LEN, 2 * PAIR), bf16),
@@ -370,11 +365,7 @@
             pltpu.VMEM((LEN, 2 * PAIR), f32),
         ],
         compiler_params=pltpu.CompilerParams(vmem_limit_bytes=vmem_bytes),
-        cost_estimate=pl.CostEstimate(
-            flops=2 * 10 * LEN * LEN * width * 4,
-            bytes_accessed=12 * LEN * width * 2,
-            transcendentals=LEN * LEN * width // HEAD,
-        ),
+        cost_estimate=beside,
         name="attend_back",
     )(queries, keys, values, outputs, grad_mine, grad_other, stacked, cosine, sine, bias)
 
@@ -395,7 +386,7 @@
 
 
 def project_kernel(panel_rows, cuts, slots_ref, *refs):
-    parts, refs = refs[: 2 * PARTS], refs[2 * PARTS :]
+    parts, refs = refs[: 4 * PARTS], refs[4 * PARTS :]
     mine_ref, other_ref, cos_ref, sin_ref, q_ref, k_ref, v_ref, out_ref, held, in_sems, out_sem = refs
     per_block = D // panel_rows
 
@@ -407,7 +398,7 @@
                 parts[number].at[lead], held.at[pl.ds(start, rows)], in_sems.at[group]
             ).start()
 
-        part_copies(slots_ref, 8 * per_block, panel, cuts, panel * panel_rows, copy, 2)
+        part_copies(slots_ref, 8 * per_block, panel, cuts, panel * panel_rows, copy)
         return carry
 
     lax.fori_loop(0, 8 * per_block, fetch, 0)
@@ -437,19 +428,15 @@
     pltpu.make_async_copy(held, out_ref, out_sem).wait()
 
 
-def project(part_pairs, slots, panel_rows, cuts, mine, other, cosine, sine):
-    width = part_pairs[0][0].shape[-1]
-    parts = [
-        part_pairs[index][last].reshape(-1, cuts[index + 1] - cuts[index], width)
-        for last in range(2)
-        for index in range(PARTS)
-    ]
+def project(groups, slots, panel_rows, cuts, mine, other, cosine, sine):
+    width = groups[0][0].shape[-1]
+    parts = [array.reshape((-1,) + array.shape[-2:]) for group in groups for array in group]
     whole = pl.BlockSpec(memory_space=pltpu.VMEM)
     anywhere = pl.BlockSpec(memory_space=pl.ANY)
     tall = jax.ShapeDtypeStruct((LEN, width), bf16)
     return pl.pallas_call(
         lambda *refs: project_kernel(panel_rows, cuts, *refs),
-        in_specs=[pl.BlockSpec(memory_space=pltpu.SMEM)] + [anywhere] * (2 * PARTS) + [whole] * 4,
+        in_specs=[pl.BlockSpec(memory_space=pltpu.SMEM)] + [anywhere] * (4 * PARTS) + [whole] * 4,
         out_specs=[whole] * 3 + [anywhere],
         out_shape=[tall] * 3 + [jax.ShapeDtypeStruct((8 * D, width), bf16)],
         scratch_shapes=[
@@ -505,143 +492,113 @@
     )(rows, grads, stacked)
 
 
-def inputs_grad_kernel(q_ref, k_ref, v_ref, w_ref, mine_ref, other_ref):
+def inputs_grad_kernel(*refs):
+    grads, w_ref, mine_ref, other_ref = refs[:6], refs[6], refs[7], refs[8]
     half = mine_ref.shape[0]
+    narrow = grads[0].shape[1]
     for start, out_ref in ((half, other_ref), (0, mine_ref)):
         rows = slice(start, start + half)
-        total = dot32(q_ref[rows, :], w_ref[0], NT)
-        total = total + dot32(k_ref[rows, :], w_ref[1], NT)
-        total = total + dot32(v_ref[rows, :], w_ref[2], NT)
+        total = None
+        for which in range(3):
+            for side in range(2):
+                weight = w_ref[which, :, side * narrow : (side + 1) * narrow]
+                part = dot32(grads[side * 3 + which][rows, :], weight, NT)
+                total = part if total is None else total + part
         out_ref[...] = total.astype(out_ref.dtype)
 
 
-def inputs_grad(query_grad, key_grad, value_grad, stacked):
+def inputs_grad(grads, stacked):
     width = stacked.shape[2]
     half = LEN // 2
-    tall = pl.BlockSpec((LEN, width), lambda step: (0, 0))
     out = pl.BlockSpec((half, D), lambda step: (0, 0))
     return pl.pallas_call(
         inputs_grad_kernel,
         grid=(1,),
-        in_specs=[tall] * 3 + [pl.BlockSpec((3, D, width), lambda step: (0, 0, 0))],
+        in_specs=[pl.BlockSpec((LEN, width // 2), lambda step: (0, 0))] * 6
+        + [pl.BlockSpec((3, D, width), lambda step: (0, 0, 0))],
         out_specs=[out, out],
         out_shape=[jax.ShapeDtypeStruct((half, D), f32), jax.ShapeDtypeStruct((half, D), bf16)],
         compiler_params=pltpu.CompilerParams(vmem_limit_bytes=vmem_bytes),
-        cost_estimate=pl.CostEstimate(
-            flops=2 * 3 * LEN * D * width, bytes_accessed=12 * LEN * D, transcendentals=0
-        ),
+        cost_estimate=beside,
         name="inputs_grad",
-    )(query_grad, key_grad, value_grad, stacked)
+    )(*grads, stacked)
 
 
 def gradients_kernel(panel_rows, cuts, lefts, rights, uses, slots_ref, *refs):
-    in_count = sum(len(pieces) for pieces in lefts + rights)
+    in_count = 1 + max(max(max(pair) for pair in lefts), max(max(pair) for group in rights for _, pair in group))
     inputs, refs = refs[:in_count], refs[in_count:]
-    parts, refs = refs[: 4 * PARTS], refs[4 * PARTS :]
-    left_held, right_held = refs[: len(lefts)], refs[len(lefts) : len(lefts) + len(rights)]
-    turned, block_ref, in_sems, out_sems = refs[len(lefts) + len(rights) :]
-    side = block_ref.shape[1]
-    operands = [(held, pieces) for held, pieces in zip(left_held + right_held, lefts + rights)]
-
-    def load(operand):
-        held, pieces = operands[operand]
-        return [
+    parts, (block_ref, out_sems) = refs[: 2 * PARTS], refs[2 * PARTS :]
+    tall, side = block_ref.shape[2:]
+    half = LEN // 2
+    pieces = tall // panel_rows
+    step = 0
+    drained = {}
+
+    def rows_of(pair, part, columns):
+        if pair[0] == pair[1]:
+            return inputs[pair[0]][part * half : (part + 1) * half, columns]
+        return inputs[pair[part]][:, columns]
+
+    for left, right, blocks in uses:
+        for left_start in range(0, D, tall):
+            place = step % 2
+            for number in drained.get(place, ()):
+                pltpu.make_async_copy(
+                    block_ref.at[place, number], block_ref.at[place, number], out_sems.at[place]
+                ).wait()
+            product = None
+            for part in range(2):
+                columns = [rows_of(pair, part, slice(start, start + side)) for start, pair in rights[right]]
+                wide = columns[0] if len(columns) == 1 else jnp.concatenate(columns, axis=1)
+                term = dot32(rows_of(lefts[left], part, slice(left_start, left_start + tall)), wide, TN)
+                product = term if product is None else product + term
+            for number, block in enumerate(blocks):
+                block_ref[place, number] = product[:, number * side : (number + 1) * side].astype(bf16)
+
+            def send(piece, carry, place=place, left_start=left_start, blocks=blocks):
+                for number, block in enumerate(blocks):
+
+                    def copy(array, lead, start, rows):
+                        pltpu.make_async_copy(
+                            block_ref.at[place, number, pl.ds(start, rows)],
+                            parts[array].at[lead],
+                            out_sems.at[place],
+                        ).start()
+
+                    panel = (block * D + left_start) // panel_rows + piece
+                    part_copies(slots_ref, 8 * D // panel_rows, panel, cuts, piece * panel_rows, copy, 2)
+                return carry
+
+            lax.fori_loop(0, pieces, send, 0)
+            drained[place] = range(len(blocks))
+            step += 1
+    for place, numbers in drained.items():
+        for number in numbers:
             pltpu.make_async_copy(
-                inputs[which],
-                held.at[pl.ds(row, inputs[which].shape[0]), pl.ds(column, inputs[which].shape[1])],
-                in_sems.at[operand],
-            )
-            for row, column, which in pieces
-        ]
-
-    order = []
-    for left, right, right_start in uses:
-        for operand in (left, len(lefts) + right):
-            if operand not in order:
-                order.append(operand)
-    for operand in order:
-        for copy in load(operand):
-            copy.start()
-    ready = set()
-    pieces = side // panel_rows
-    block = 0
-    for left, right, right_start in uses:
-        for operand in (left, len(lefts) + right):
-            if operand not in ready:
-                held = operands[operand][0]
-                pltpu.make_async_copy(held, held, in_sems.at[operand]).wait()
-                ready.add(operand)
-                if operand < len(lefts):
-                    turned[left % 2] = held[...].T
-        for left_start in range(0, D, side):
-            place = block % 2
-            if block >= 2:
-                pltpu.make_async_copy(block_ref.at[place], block_ref.at[place], out_sems.at[place]).wait()
-            block_ref[place] = dot32(
-                turned[left % 2, left_start : left_start + side],
-                right_held[right][:, right_start : right_start + side],
-            ).astype(bf16)
-
-            def send(piece, carry, block=block, place=place):
-                def copy(number, lead, start, rows):
-                    pltpu.make_async_copy(
-                        block_ref.at[place, pl.ds(start, rows)], parts[number].at[lead], out_sems.at[place]
-                    ).start()
-
-                part_copies(
-                    slots_ref, 8 * D // panel_rows, block * pieces + piece, cuts, piece * panel_rows, copy
-                )
-                return carry
-
-            lax.fori_loop(0, pieces, send, 0)
-            block += 1
-    for place in range(2):
-        pltpu.make_async_copy(block_ref.at[place], block_ref.at[place], out_sems.at[place]).wait()
-
-
-def panel_gradients(lefts, rights, uses, slots, panel_rows, cuts, high_count, width):
-    arrays, numbered = [], []
-    for operands in (lefts, rights):
-        made = []
-        for pieces in operands:
-            made.append([(row, column, len(arrays) + i) for i, (row, column, _) in enumerate(pieces)])
-            arrays.extend(array for _, _, array in pieces)
-        numbered.append(made)
-    extent = lambda pieces: max(column + array.shape[1] for _, column, array in pieces)
+                block_ref.at[place, number], block_ref.at[place, number], out_sems.at[place]
+            ).wait()
+
+
+def panel_gradients(arrays, lefts, rights, uses, slots, panel_rows, cuts, high_count, width):
+    tall = LEN // 2
     outs = [
-        jax.ShapeDtypeStruct((4 * high_count, cuts[index + 1] - cuts[index], width), bf16)
-        for _ in range(4)
+        jax.ShapeDtypeStruct((8 * high_count, cuts[index + 1] - cuts[index], width), bf16)
+        for _ in range(2)
         for index in range(PARTS)
     ]
     outs = pl.pallas_call(
-        lambda *refs: gradients_kernel(panel_rows, cuts, numbered[0], numbered[1], uses, *refs),
+        lambda *refs: gradients_kernel(panel_rows, cuts, lefts, rights, uses, *refs),
         in_specs=[pl.BlockSpec(memory_space=pltpu.SMEM)]
-        + [pl.BlockSpec(memory_space=pl.ANY)] * len(arrays),
-        out_specs=[pl.BlockSpec(memory_space=pl.ANY)] * (4 * PARTS),
+        + [pl.BlockSpec(memory_space=pltpu.VMEM)] * len(arrays),
+        out_specs=[pl.BlockSpec(memory_space=pl.ANY)] * (2 * PARTS),
         out_shape=outs,
-        scratch_shapes=[pltpu.VMEM((LEN, extent(pieces)), bf16) for pieces in list(lefts) + list(rights)]
-        + [
-            pltpu.VMEM((2, D, LEN), bf16),
-            pltpu.VMEM((2, width, width), bf16),
-            pltpu.SemaphoreType.DMA((len(lefts) + len(rights),)),
-            pltpu.SemaphoreType.DMA((2,)),
-        ],
-        compiler_params=pltpu.CompilerParams(vmem_limit_bytes=vmem_bytes),
-        cost_estimate=pl.CostEstimate(
-            flops=2 * LEN * len(uses) * D * width,
-            bytes_accessed=24 * LEN * D,
-            transcendentals=0,
-        ),
+        scratch_shapes=[pltpu.VMEM((2, 2, tall, width), bf16), pltpu.SemaphoreType.DMA((2,))],
+        compiler_params=pltpu.CompilerParams(vmem_limit_bytes=gradient_bytes),
+        cost_estimate=beside,
         name="gradients",
     )(slots, *arrays)
-    shaped = [out.reshape((2, 2, high_count) + out.shape[1:]) for out in outs]
-    pairs = lambda far: [
-        (shaped[far * 2 * PARTS + index], shaped[far * 2 * PARTS + PARTS + index]) for index in range(PARTS)
-    ]
-    return pairs(0), pairs(1)
-
-
-beside = pl.CostEstimate(flops=1000, bytes_accessed=1000, transcendentals=0)
+    shaped = [out.reshape((2, 2, 2 * high_count) + out.shape[1:]) for out in outs]
+    return shaped[:PARTS], shaped[PARTS:]
 
 
 def gelu_parts(values):
@@ -801,9 +758,10 @@
 
 def text_back_kernel(
     pre_ref, grn_grad_ref, energy_ref, dot_ref, gamma_ref, texts_ref, normed_ref, conv_normed_ref, conv_scale_ref, gain_ref,
-    shrink_low_ref, grn_ref, text_ref, low_ref,
-    mixed_ref, sums_ref, wide_sums_ref, grads_ref,
+    shrink_low_ref, grn_ref, text_ref, low_ref, core_ref, table_ref,
+    mixed_ref, sums_ref, wide_sums_ref, *rest,
 ):
+    grads_ref = rest[2] if len(rest) > 1 else rest[0]
     pre = pre_ref[...]
     share, density = gelu_parts(pre)
     energy = jnp.sqrt(energy_ref[...])
@@ -826,16 +784,190 @@
     mixed_grad = normalise_back(normed_grad * gain_ref[...], conv_normed, conv_scale_ref[...])
     sums_ref[2:3] = jnp.sum(mixed_grad, axis=0, keepdims=True)
     mixed_ref[...] = mixed_grad
-
-
-def text_back(*inputs):
+    if len(rest) == 1:
+        return
+    keep_ref, send_ref, _, sem = rest
+    rows = keep_ref.shape[1]
+
+    def place(block, carry):
+        piece = grads_ref.at[pl.ds(pl.multiple_of(block * rows, 16), rows)]
+        for part, ref in enumerate((keep_ref, send_ref)):
+
+            @pl.when((block + core_ref[0]) % 2 == part)
+            def _():
+                pltpu.make_async_copy(piece, ref.at[table_ref[block]], sem).start()
+
+        return carry
+
+    lax.fori_loop(0, table_ref.shape[0], place, 0)
+    pltpu.make_async_copy(grads_ref, grads_ref, sem).wait()
+
+
+def text_back(core, table, rows, *inputs):
     half = inputs[0].shape[0]
+    whole, anywhere = pl.BlockSpec(memory_space=pltpu.VMEM), pl.BlockSpec(memory_space=pl.ANY)
+    scalars = pl.BlockSpec(memory_space=pltpu.SMEM)
+    outs = [((half, TEXT), f32), ((3, TEXT), f32), ((2, TXT_FF), f32)]
+    apart = rows % 16 == 0
+    blocks = ((3 * TEXT // (2 * rows), rows, D), bf16)
     return in_vmem(
         text_back_kernel,
         "text_back",
-        inputs,
-        [((half, TEXT), f32), ((3, TEXT), f32), ((2, TXT_FF), f32), ((3 * TEXT, D), bf16)],
-    )
+        inputs + (core.reshape(1).astype(jnp.int32), table),
+        outs + ([blocks] * 2 if apart else [((3 * TEXT, D), bf16)]),
+        [pltpu.VMEM((3 * TEXT, D), bf16), pltpu.SemaphoreType.DMA] if apart else [],
+        [whole] * len(inputs) + [scalars] * 2,
+        [whole] * 3 + ([anywhere] * 2 if apart else [whole]),
+    )
+
+
+def conv_back_kernel(
+    core_ref, mixed_ref, border_ref, window_ref, kernel_ref, shrink_ref, keep_ref,
+    mine_ref, kernel_grad_ref, full_ref, wide, sem,
+):
+    half = mixed_ref.shape[0]
+    edge, margin = border_ref.shape[0], KERNEL // 2
+    mixed = mixed_ref[...]
+    border = border_ref[...]
+    wide[:edge] = jnp.where(core_ref[0] == 1, border, 0.0)
+    wide[edge : edge + half] = mixed
+    wide[edge + half :] = jnp.where(core_ref[0] == 0, border, 0.0)
+    total = shrink_ref[...]
+    for j in range(KERNEL):
+        start = edge + margin - j
+        total = total + wide[start : start + half] * kernel_ref[j : j + 1]
+        tap = window_ref[edge - margin + j : edge - margin + j + half]
+        kernel_grad_ref[j : j + 1] = jnp.sum(mixed * tap, axis=0, keepdims=True)
+    mine_ref[...] = total * keep_ref[...]
+    place = pl.ds(pl.multiple_of(core_ref[0] * half, half), half)
+    out = pltpu.make_async_copy(mine_ref, full_ref.at[place], sem)
+    out.start()
+    out.wait()
+
+
+def conv_back(core, *inputs):
+    half = inputs[0].shape[0]
+    whole, anywhere = pl.BlockSpec(memory_space=pltpu.VMEM), pl.BlockSpec(memory_space=pl.ANY)
+    return in_vmem(
+        conv_back_kernel,
+        "conv_back",
+        (core.reshape(1).astype(jnp.int32),) + inputs,
+        [((half, TEXT), f32), ((KERNEL, TEXT), f32), ((2 * half, TEXT), f32)],
+        [pltpu.VMEM((half + 2 * inputs[1].shape[0], TEXT), f32), pltpu.SemaphoreType.DMA],
+        [pl.BlockSpec(memory_space=pltpu.SMEM)] + [whole] * len(inputs),
+        [whole] * 2 + [anywhere],
+    )
+
+
+def settle_kernel(
+    core_ref, my_out_ref, their_out_ref, my_grad_ref, their_grad_ref, stream_ref, attention_ref, cot_ref,
+    gate_one_ref, scale_ref, gate_two_ref,
+    output_ref, later_ref, attention_grad_ref, sums_ref, full_ref, sem,
+):
+    half = output_ref.shape[0]
+    unit_out = my_out_ref[...] + their_out_ref[...].astype(f32)
+    stream = stream_ref[...]
+    output_ref[...] = (stream + gate_two_ref[...] * unit_out).astype(bf16)
+    place = pl.ds(pl.multiple_of(core_ref[0] * half, half), half)
+    out = pltpu.make_async_copy(output_ref, full_ref.at[place], sem)
+    out.start()
+    out_grad = cot_ref[...].astype(f32)
+    sums_ref[0:1] = jnp.sum(out_grad * unit_out, axis=0, keepdims=True)
+    grad = my_grad_ref[...] + their_grad_ref[...].astype(f32)
+    normed, scale = normalise(stream)
+    sums_ref[1:2] = jnp.sum(grad, axis=0, keepdims=True)
+    sums_ref[2:3] = jnp.sum(grad * normed, axis=0, keepdims=True)
+    later = out_grad + normalise_back(grad * (1.0 + scale_ref[...]), normed, scale)
+    later_ref[...] = later
+    sums_ref[3:4] = jnp.sum(later * attention_ref[...], axis=0, keepdims=True)
+    attention_grad_ref[...] = (gate_one_ref[...] * later).astype(bf16)
+    out.wait()
+
+
+def settle(core, *inputs):
+    half = inputs[0].shape[0]
+    whole, anywhere = pl.BlockSpec(memory_space=pltpu.VMEM), pl.BlockSpec(memory_space=pl.ANY)
+    return in_vmem(
+        settle_kernel,
+        "settle",
+        (core.reshape(1).astype(jnp.int32),) + inputs,
+        [((half, D), bf16), ((half, D), f32), ((half, D), bf16), ((4, D), f32), ((2 * half, D), bf16)],
+        [pltpu.SemaphoreType.DMA],
+        [pl.BlockSpec(memory_space=pltpu.SMEM)] + [whole] * len(inputs),
+        [whole] * 4 + [anywhere],
+    )
+
+
+def dot_split(left, right, dims=NN):
+    split = lambda array: (array.astype(bf16), (array - array.astype(bf16).astype(f32)).astype(bf16))
+    left_high, left_low = split(left)
+    right_high, right_low = split(right)
+    return (
+        dot32(left_high, right_high, dims)
+        + dot32(left_high, right_low, dims)
+        + dot32(left_low, right_high, dims)
+    )
+
+
+def rotated_kernel(places, utterances, *refs):
+    pieces, refs = refs[: sum(count for _, _, count in places)], refs[sum(count for _, _, count in places) :]
+    left_ref, right_ref, master_ref, first_ref, second_ref, weights_ref, moment_ref, variance_ref, grad_ref = refs
+    which = 0
+    for row, column, count in places:
+        total = pieces[which][...].astype(f32)
+        for ref in pieces[which + 1 : which + count]:
+            total = total + ref[...].astype(f32)
+        rows, columns = total.shape
+        grad_ref[row : row + rows, column : column + columns] = total / utterances
+        which += count
+    left, right = left_ref[...], right_ref[...]
+    rotated = dot_split(dot_split(left, grad_ref[...], TN), right)
+    moment, variance, direction = moments(rotated, first_ref[...], second_ref[...])
+    moment_ref[...] = moment
+    variance_ref[...] = variance
+    turned = dot_split(dot_split(left, direction), right, NT)
+    master = master_ref[...]
+    weights_ref[...] = apply_step(master, turned, learn_rate)
+
+
+def rotated_step(pieces, utterances, left, right, master, first, second):
+    places = [(row, column, len(arrays)) for row, column, arrays in pieces]
+    arrays = [array for _, _, group in pieces for array in group]
+    return in_vmem(
+        lambda *refs: rotated_kernel(places, utterances, *refs),
+        "rotated_step",
+        tuple(arrays) + (left, right, master, first, second),
+        [(master.shape, f32)] * 3,
+        [pltpu.VMEM(master.shape, f32)],
+    )
+
+
+def modulation_kernel(utterances, time_ref, table_ref, old_ref, first_ref, second_ref, weights_ref, moment_ref, variance_ref):
+    grad = dot32(time_ref[...], table_ref[...], TN) / utterances
+    moment, variance, direction = moments(grad, first_ref[...], second_ref[...])
+    moment_ref[...] = moment
+    variance_ref[...] = variance
+    weights_ref[...] = apply_step(old_ref[...], direction, learn_rate)
+
+
+def modulation_step(utterances, time_rows, table, old, first, second):
+    rows, columns = old.shape
+    step = columns // 6
+    tall = pl.BlockSpec((rows, step), lambda i: (0, i))
+    return pl.pallas_call(
+        lambda *refs: modulation_kernel(utterances, *refs),
+        grid=(6,),
+        in_specs=[
+            pl.BlockSpec((GROUPS, rows), lambda i: (0, 0)),
+            pl.BlockSpec((GROUPS, step), lambda i: (0, i)),
+        ]
+        + [tall] * 3,
+        out_specs=[tall] * 3,
+        out_shape=[jax.ShapeDtypeStruct(old.shape, f32)] * 3,
+        compiler_params=pltpu.CompilerParams(vmem_limit_bytes=vmem_bytes),
+        cost_estimate=beside,
+        name="modulation_step",
+    )(time_rows, table, old, first, second)
 
 
 def vector_parts(vectors):
@@ -934,8 +1066,8 @@
 
     high_count = count // 16
     cuts = row_cuts(panel_rows)
-    gather_table = panel_places(core, owner_list ^ me, high_count, 0)
-    panel_table = panel_places(core, owner_list ^ me, high_count, 1)
+    panel_table = panel_places(core, owner_list ^ me, high_count)
+    gather_table = panel_places(core, owner_list ^ me, high_count, True)
     silu_time = jax.nn.silu(time_embedding.astype(f32)).astype(bf16)
     time_rows = lax.dynamic_slice_in_dim(silu_time, me * share_rows, share_rows, 1)
     weight_half = lax.dynamic_slice_in_dim(modulation_weight, core * 3 * D, 3 * D, 1).astype(bf16)
@@ -952,28 +1084,33 @@
     held = split_rows(held, cuts)
     text_held = jnp.stack([text_held, text_received])
     partial = partial + partial_received
-    text_received, partial_received, far_last = tie(
-        swap_bits(text_held, phase_bits(text_orders, 1)),
-        swap_bits(partial, phase_bits(text_orders, 1)),
-        swap_bit(held[1], 3),
-    )
+    received, (text_received, partial_received, far_last) = tie_lists(
+        receive(held, 0),
+        (
+            swap_bits(text_held, phase_bits(text_orders, 1)),
+            swap_bits(partial, phase_bits(text_orders, 1)),
+            swap_bit(held[1], 3),
+        ),
+    )
+    near = [jnp.stack(pair) for pair in zip(held, received)]
     text_held = jnp.stack([text_held, text_received])
     partial = partial + partial_received
-    text_received, partial_received, far_first = tie(
-        swap_bits(text_held, phase_bits(text_orders, 2)),
-        swap_bits(partial, phase_bits(text_orders, 2)),
-        swap_bit(held[0], 3),
+    received, (text_received, partial_received, far_first) = tie_lists(
+        receive(near, 1),
+        (
+            swap_bits(text_held, phase_bits(text_orders, 2)),
+            swap_bits(partial, phase_bits(text_orders, 2)),
+            swap_bit(held[0], 3),
+        ),
     )
     partial = partial + partial_received
-    parts = [jnp.concatenate(pair, axis=0) for pair in zip(held, (far_first, far_last))]
-    received = receive(parts, 0)
+    near = [jnp.stack(pair) for pair in zip(near, received)]
+    near_received = receive(near, 2)
+    far = spread_step([far_first, far_last], 0)
+    received = receive(far, 1)
     text_mine = jnp.stack([text_held, text_received]).reshape(count, text_half, D)
     text_other = swap_core(text_mine)
-    received, (text_mine, text_other, partial, text_features, mel_frames, cotangent) = tie_lists(
-        received, (text_mine, text_other, partial, text_features, mel_frames, cotangent)
-    )
-    parts = [jnp.stack(pair) for pair in zip(parts, received)]
-    received = receive(parts, 1)
+    text_features, mel_frames, cotangent, far = tie(text_features, mel_frames, cotangent, far)
     for bit in range(4, bit_count(count)):
         partial = partial + swap_bit(partial, bit)
     modulation_half = partial
@@ -1018,20 +1155,21 @@
         for j in range(KERNEL):
             mixed = mixed + taps[j] * kernel[j][None, :]
         normed, scale = normalise(mixed)
-        return window[edge : edge + half], keep, taps, normed, scale, (normed * norm_gain + norm_bias).astype(bf16)
-
-    masked_text, keep, taps, conv_normed, conv_scale, normed_low = text_start(first)
-    masked_other, keep_other, _, _, _, normed_other = text_start(half - first)
-    masked_both = jnp.concatenate([masked_text, masked_other], axis=0)
+        return window, keep, normed, scale, (normed * norm_gain + norm_bias).astype(bf16)
+
+    window, keep, conv_normed, conv_scale, normed_low = text_start(first)
+    window_other, keep_other, _, _, normed_other = text_start(half - first)
+    masked_both = jnp.concatenate([window[edge : edge + half], window_other[edge : edge + half]], axis=0)
     keep_both = jnp.concatenate([keep, keep_other], axis=0)
     normed_both = jnp.concatenate([normed_low, normed_other], axis=0)
     mel_mine = lax.dynamic_slice_in_dim(mel_frames, first, half, 0)
     mel_other = lax.dynamic_slice_in_dim(mel_frames, half - first, half, 0)
     cosine, sine = rotary_tables(first)
-    received, (text_other, modulation_row, normed_both, masked_both, cosine, sine) = tie_lists(
-        received, (text_other, modulation_row, normed_both, masked_both, cosine, sine)
-    )
-    pairs = spread_last([jnp.stack(pair) for pair in zip(parts, received)])
+    received, near_received, (text_other, modulation_row, normed_both, masked_both, cosine, sine) = tie_lists(
+        received, near_received, (text_other, modulation_row, normed_both, masked_both, cosine, sine)
+    )
+    far = [jnp.stack(pair) for pair in zip(far, received)]
+    far_received = receive(far, 2)
     shift_one, scale_one, gate_one, shift_two, scale_two, gate_two = (
         modulation_row[:, i * D : (i + 1) * D] for i in range(6)
     )
@@ -1062,78 +1200,98 @@
     bias = jnp.where(position < lengths[0], 0.0, -1e30).astype(bf16)
     bias = jnp.broadcast_to(bias[:, None], (LEN, PAIR))
     queries, keys, value_rows, stacked = project(
-        pairs, gather_table, panel_rows, cuts, first_mine, first_other, cosine, sine
+        (near, near_received, far, far_received), gather_table, panel_rows, cuts, first_mine, first_other, cosine, sine
     )
     stacked = stacked.reshape(8, D, width)
     attended, query_aug = attend_forward(queries, keys, value_rows, bias)
     attention_out = sum_halves(lambda rows: dot32(rows, stacked[3], NT), attended, half)
     stream_one = stream + gate_one * attention_out
 
-    normed_two, scale_norm_two = normalise(stream_one)
+    normed_two, _ = normalise(stream_one)
     second_mine = (normed_two * (1.0 + scale_two) + shift_two).astype(bf16)
     second_other = swap_core(second_mine)
-    out_grad = cot_mine.astype(f32)
     their_out, their_grad, act_other, pre_other = feed(second_other, hidden_other, stacked, bf16)
     their_out, their_grad = swap_core(their_out), swap_core(their_grad)
     my_out, my_grad, act_mine, pre_mine = feed(second_mine, hidden_mine, stacked, f32)
-    unit_out = my_out + their_out.astype(f32)
-    normed_two_grad = my_grad + their_grad.astype(f32)
-    output_mine = (stream_one + gate_two * unit_out).astype(bf16)
-    block_output = by_core(core, output_mine, swap_core(output_mine))
-    gate_two_grad = jnp.sum(out_grad * unit_out, axis=0)
-    shift_two_grad = jnp.sum(normed_two_grad, axis=0)
-    scale_two_grad = jnp.sum(normed_two_grad * normed_two, axis=0)
-    stream_one_grad = out_grad + normalise_back(
-        normed_two_grad * (1.0 + scale_two), normed_two, scale_norm_two
-    )
-
-    gate_one_grad = jnp.sum(stream_one_grad * attention_out, axis=0)
-    attention_mine = (gate_one * stream_one_grad).astype(bf16)
+    output_mine, stream_one_grad, attention_mine, settle_sums, block_output = settle(
+        core,
+        my_out,
+        their_out,
+        my_grad,
+        their_grad,
+        stream_one,
+        attention_out,
+        cot_mine,
+        gate_one,
+        scale_two,
+        gate_two,
+    )
+    gate_two_grad, shift_two_grad, scale_two_grad, gate_one_grad = (settle_sums[i] for i in range(4))
+    output_theirs = swap_core(output_mine)
+
     attention_other = swap_core(attention_mine)
-    query_grad, key_grad, value_grad = attend_backward(
-        query_aug, keys, value_rows, attended, attention_mine, attention_other, stacked, cosine, sine, bias
-    )
-    my_grad, their_grad = inputs_grad(query_grad, key_grad, value_grad, stacked)
-    their_grad, query_grad = tie(their_grad, query_grad)
+    narrow = width // 2
+
+    def back(side, queries):
+        return attend_backward(
+            side, queries, keys, value_rows, attended, attention_mine, attention_other, stacked, cosine, sine, bias
+        )
+
+    def weight_gradients(side, head_grads):
+        column = side * narrow
+        return panel_gradients(
+            [
+                first_mine, first_other, attention_mine, attention_other, second_mine, second_other,
+                hidden_mine, hidden_other, *head_grads, attended, pre_mine, pre_other, act_mine, act_other,
+            ],
+            [(0, 1), (2, 3), (4, 5), (6, 7)],
+            [
+                [(0, (8, 8)), (0, (9, 9))],
+                [(0, (10, 10))],
+                [(column, (11, 11))],
+                [(column, (12, 13)), (width + column, (12, 13))],
+                [(column, (14, 15)), (width + column, (14, 15))],
+            ],
+            ((0, 0, (0, 1)), (0, 1, (2,)), (1, 2, (3,)), (2, 3, (4, 5)), (3, 4, (6, 7))),
+            panel_table,
+            panel_rows,
+            cuts,
+            high_count,
+            narrow,
+        )
+
+    head_grads = list(back(0, query_aug))
+    keep_a, send_a = weight_gradients(0, head_grads)
+    send_a, (query_aug,) = tie_lists(send_a, (query_aug,))
+    received_a = receive(send_a, 2)
+    head_grads += list(back(1, query_aug))
+    received_a, head_grads = tie_lists(received_a, head_grads)
+    part_a = add_all(keep_a, received_a)
+    received_a = receive(seconds(part_a), 1)
+    my_grad, their_grad = inputs_grad(head_grads, stacked)
+    received_a, head_grads, (my_grad, their_grad) = tie_lists(received_a, head_grads, (my_grad, their_grad))
+    part_a = add_all(firsts(part_a), received_a)
+    received_a = receive(seconds(part_a), 0)
+    keep_b, send_b = weight_gradients(1, head_grads[3:])
     their_grad = swap_core(their_grad)
-    halves = lambda mine, other: [(0, 0, mine), (half, 0, other)]
-    whole = lambda array: [(0, 0, array)]
-    near_pairs, far_pairs = panel_gradients(
-        [
-            halves(first_mine, first_other),
-            halves(attention_mine, attention_other),
-            halves(second_mine, second_other),
-            halves(hidden_mine, hidden_other),
-        ],
-        [
-            whole(query_grad),
-            whole(key_grad),
-            whole(value_grad),
-            whole(attended),
-            halves(pre_mine, pre_other),
-            halves(act_mine, act_other),
-        ],
-        ((0, 0, 0), (0, 1, 0), (0, 2, 0), (1, 3, 0), (2, 4, 0), (2, 4, width), (3, 5, 0), (3, 5, width)),
-        panel_table,
-        panel_rows,
-        cuts,
-        high_count,
-        width,
-    )
-
-    far_keep, far_send = firsts(far_pairs), seconds(far_pairs)
-    near_keep, near_send = firsts(near_pairs), seconds(near_pairs)
-    far_received = receive(far_send, 2)
+    received_a, send_b, (their_grad,) = tie_lists(received_a, send_b, (their_grad,))
+
+    part_a = add_all(firsts(part_a), received_a)
+    received_b = receive(send_b, 2)
     mel_grad_mine, stream_low, shrink_grad, shrink_low, grn_grad, sums, out_bias_grad, mel_gradient = stream_back(
         core, my_grad, their_grad, stream, stream_one_grad, scale_one, texts, keep, expand_pre
     )
-    far_received, (sums, mel_grad_mine) = tie_lists(far_received, (sums, mel_grad_mine))
+    received_b, part_a, (sums, mel_grad_mine) = tie_lists(received_b, part_a, (sums, mel_grad_mine))
     shift_one_grad, scale_one_grad, hidden_dot, beta_grad = sums[0], sums[1], sums[2:3], sums[3]
     out_bias_grad = out_bias_grad[0]
-    far = add_all(far_keep, far_received)
-    far_received = receive(seconds(far), 1)
+    far_a = [swap_bit(part[high_count:], 3) for part in part_a]
+    part_b = add_all(keep_b, received_b)
+    received_b = receive(seconds(part_b), 1)
     hidden_dot_all = hidden_dot + swap_core(hidden_dot)
-    mixed_grad, text_sums, wide_sums, text_grads = text_back(
+    mixed_grad, text_sums, wide_sums, *text_grads = text_back(
+        core,
+        text_table,
+        text_half,
         expand_pre,
         grn_grad,
         energy_sum,
@@ -1152,27 +1310,23 @@
     mel_grad_theirs = swap_core(mel_grad_mine)
     gain_grad, norm_bias_grad, conv_bias_grad = text_sums[0], text_sums[1], text_sums[2]
     in_bias_grad, gamma_grad = wide_sums[0], wide_sums[1] * hidden_dot[0]
-    far_received, near_send, (mixed_grad, text_grads, mel_grad_theirs) = tie_lists(
-        far_received, near_send, (mixed_grad, text_grads, mel_grad_theirs)
-    )
-    far = add_all(firsts(far), far_received)
-    far_received = receive(seconds(far), 0)
-    near_received = receive(near_send, 2)
-    text_grads = text_grads.reshape(count, 2, text_half, D)
-    text_keep_half = lax.dynamic_index_in_dim(text_grads, core, 1, keepdims=False)
-    text_send_half = lax.dynamic_index_in_dim(text_grads, 1 - core, 1, keepdims=False)
+    if len(text_grads) == 1:
+        blocks = text_grads[0].reshape(count, 2, text_half, D)
+        order = lambda which: text_slots(which, jnp.arange(count), high_count) ^ me
+        text_grads = [
+            take_blocks(lax.dynamic_index_in_dim(blocks, which, 1, keepdims=False), order(which))
+            for which in (core, 1 - core)
+        ]
+    received_b, far_a, (mixed_grad, text_keep_half, text_send_half, mel_grad_theirs) = tie_lists(
+        received_b, far_a, (mixed_grad, *text_grads, mel_grad_theirs)
+    )
+    part_b = add_all(firsts(part_b), received_b)
+    received_b = receive(seconds(part_b), 0)
     text_received = swap_core(text_send_half)
-    kernel_grad = jnp.stack([jnp.sum(mixed_grad * taps[j], axis=0) for j in range(KERNEL)])
-    border = lax.dynamic_slice_in_dim(mixed_grad, (1 - core) * (half - edge), edge, 0)
-    border = swap_core(border)
-    before = jnp.where(core == 1, border, 0.0)
-    after = jnp.where(core == 0, border, 0.0)
-    wide_grad = jnp.concatenate([before, mixed_grad, after], axis=0)
-    masked_grad = shrink_grad
-    for j in range(KERNEL):
-        start = edge + margin - j
-        masked_grad = masked_grad + wide_grad[start : start + half] * kernel[j][None, :]
-    text_grad_mine = masked_grad * keep
+    border = swap_core(lax.dynamic_slice_in_dim(mixed_grad, (1 - core) * (half - edge), edge, 0))
+    text_grad_mine, kernel_grad, text_gradient = conv_back(
+        core, mixed_grad, border, window, kernel, shrink_grad, keep
+    )
 
     vector_mine = jnp.concatenate(
         [
@@ -1204,41 +1358,38 @@
     small = half_of(core)
     in_group = (jnp.arange(GROUPS) == group).astype(f32)
 
-    far_received, near_received, (text_received, small, small_send) = tie_lists(
-        far_received, near_received, (text_received, small, small_send)
-    )
-    far = add_all(firsts(far), far_received)
-    far_last = swap_bit(far[1], 3)
-    near = add_all(near_keep, near_received)
-    near_received = receive(seconds(near), 1)
-    text_part = take_blocks(
-        add_low(text_keep_half, text_received), text_slots(core, jnp.arange(count), high_count) ^ me
-    )
-    text_part = text_part.reshape(2, 2, 2, 2 * high_count, text_half, D)
+    text_grad_theirs = swap_core(text_grad_mine)
+    text_part = add_low(text_keep_half, text_received).reshape(2, 2, 2, 2 * high_count, text_half, D)
+    mel_gradient = lax.dynamic_update_slice_in_dim(mel_gradient, mel_grad_theirs, half - first, 0)
+    received_b, (text_part, small, small_send, mel_gradient) = tie_lists(
+        received_b, (text_part, small, small_send, mel_gradient)
+    )
+    part_b = add_all(firsts(part_b), received_b)
+    far_b = [swap_bit(part[high_count:], 3) for part in part_b]
     text_received = swap_bits(text_part[1], phase_bits(text_orders, 2))
     small_received = swap_core(small_send)
-    mel_gradient = lax.dynamic_update_slice_in_dim(mel_gradient, mel_grad_theirs, half - first, 0)
-    near_received, (text_received, small_received, mel_gradient, far_last) = tie_lists(
-        near_received, (text_received, small_received, mel_gradient, far_last)
-    )
-    far_first = swap_bit(far[0], 3)
-    near = add_all(firsts(near), near_received)
-    near_received = receive(seconds(near), 0)
+    block_output = lax.dynamic_update_slice_in_dim(block_output, output_theirs, half - first, 0)
+    text_gradient = lax.dynamic_update_slice_in_dim(text_gradient, text_grad_theirs, half - first, 0)
+    far_b, (text_received, small_received, text_gradient, block_output) = tie_lists(
+        far_b, (text_received, small_received, text_gradient, block_output)
+    )
     text_part = add_low(text_part[0], text_received)
-    text_part = fold(text_part, text_orders, 1)
+    text_received = swap_bits(text_part[1], phase_bits(text_orders, 1))
     small = small + small_received
     table = in_group[:, None] * small[None, vector_half:]
     small = jnp.concatenate([small[:vector_half], table.reshape(-1)]).reshape(-1, 128)
-    small = small + swap_bits(small, (2, 0))
-    text_gradient = by_core(core, text_grad_mine, swap_core(text_grad_mine))
-    near_received, (text_part, small, text_gradient, far_first, block_output) = tie_lists(
-        near_received, (text_part, small, text_gradient, far_first, block_output)
-    )
-    near = add_all(firsts(near), near_received)
-    own_panel = jnp.concatenate(
-        [keep.astype(f32) + other.astype(f32) for keep, other in zip(near, (far_first, far_last))], axis=-2
-    )
-    own_panel = fold_high(own_panel)
+    small_received = swap_bits(small, (2, 0))
+    panel_pieces = []
+    for side, (parts, others) in enumerate(((part_a, far_a), (part_b, far_b))):
+        for index, (part, other) in enumerate(zip(parts, others)):
+            if high_count == 1:
+                arrays = [part[0], other[0]]
+            else:
+                arrays = [fold_high(part[:high_count].astype(f32) + other.astype(f32))]
+            panel_pieces.append((cuts[index], side * narrow, arrays))
+    text_received, small_received = tie(text_received, small_received)
+    text_part = add_low(text_part[0], text_received)
+    small = small + small_received
     text_part = fold(text_part, text_orders, 0)
     text_received = swap_bit(text_part[high_count:], 3)
     small = small + swap_bits(small, (0, 1))
@@ -1254,27 +1405,21 @@
     tables = small[:, vector_half:].reshape(2, GROUPS, token_half)
     modulation_grad = jnp.concatenate([tables[0], tables[1]], axis=1)
     vector_gradient = jnp.concatenate([vector_sum, jnp.sum(modulation_grad, axis=0)]) / utterances
-    share_grad = (
-        lax.dot_general(
-            time_rows, modulation_grad.astype(bf16), TN, preferred_element_type=f32
-        )
-        / utterances
-    )
-
-    own_panel = own_panel / utterances
+
     own_text = own_text / utterances
-    rotated = jnp.dot(jnp.dot(left_basis.T, own_panel, precision=solver), right_basis, precision=solver)
-    soap_moment, soap_variance, soap_direction = moments(rotated, soap_first, soap_second)
-    turned_back = jnp.dot(
-        jnp.dot(left_basis, soap_direction, precision=solver), right_basis.T, precision=solver
-    )
-    soap_weights = apply_step(soap_master, turned_back, learn_rate)
+    soap_weights, soap_moment, soap_variance = rotated_step(
+        panel_pieces, utterances, left_basis, right_basis, soap_master, soap_first, soap_second
+    )
     text_moment, text_variance, text_direction = moments(own_text, text_first, text_second)
     text_weights = apply_step(text_matrices, text_direction, learn_rate)
-    modulation_moment, modulation_variance, modulation_direction = moments(
-        share_grad, modulation_first, modulation_second
-    )
-    modulation_weights = apply_step(modulation_weight, modulation_direction, learn_rate)
+    modulation_weights, modulation_moment, modulation_variance = modulation_step(
+        utterances,
+        time_rows,
+        modulation_grad.astype(bf16),
+        modulation_weight,
+        modulation_first,
+        modulation_second,
+    )
     vector_moment, vector_variance, vector_direction = moments(
         vector_gradient, vector_first, vector_second
     )

time: 394 us -> 373 us (0.947)
  waiting for transfers between devices: 116 us -> 84.4 us
  local copies, waits for them, and re-layouts: 23 us -> 43.7 us
  starting transfers between devices: 47.7 us -> 67.2 us
  matrix products: 20.8 us -> 2.99 us
  other arithmetic: 48.8 us -> 33.8 us
    ppermute x38 -> x46, waiting for transfers between devices: 102 us -> 71.6 us  [swap_bits(): return lax.ppermute(array, ('dp', 'mp'), pairs)]
    ppermute x38 -> x46, starting transfers between devices: 44.6 us -> 65.2 us  [swap_bits(): return lax.ppermute(array, ('dp', 'mp'), pairs)]
    unnamed x166 -> x184, local copies, waits for them, and re-layouts: 5.12 us -> 25.6 us
    dot_general x5 -> x0, matrix products: 13.7 us -> none  [the longest x1 6.22 us: body(): lax.dot_general(time_rows, modulation_grad.astype(bf16), TN, preferred_el...]
    pallas_call x2 -> x4, Pallas kernels: 26.5 us -> 33.8 us  [the longest x2 26 us: panel_gradients(): pl.pallas_call(lambda *refs: gradients_kernel(panel_rows, cuts, lefts, ri...]
    select_n x3 -> x1, other arithmetic: 6.85 us -> 0.33 us  [by_core(): jnp.where(core == 0, jnp.concatenate([mine, other], axis=axis), jnp.conca...]
    pallas_call x2, Pallas kernels: 15.7 us -> 9.61 us  [feed(): pl.pallas_call(feed_kernel, grid=(1,), in_specs=[whole, whole, pl.BlockSp...]
    pallas_call x3 -> x6, Pallas kernels: 29.9 us -> 35.5 us  [in_vmem(): pl.pallas_call(kernel, in_specs=specs or [whole] * len(inputs), out_specs...]
  transfers between devices with their start and end apart: 55 -> 63, of which waited for: 26 -> 27; matrix products, arithmetic and copies ran while one was open for 17% -> 12% of each run, Pallas kernels for 10% -> 19%
where the time goes in v4:
time: 373 us; the launch traced here: 366 us
  Pallas kernels  130 us (35%)
  waiting for transfers between devices  84.4 us (23%)
  starting transfers between devices  67.2 us (18%)
  local copies, waits for them, and re-layouts  43.7 us (12%)
  other arithmetic  33.8 us (9%)
    ppermute x46, waiting for transfers between devices, swap_bits(): return lax.ppermute(array, ('dp', 'mp'), pairs)  71.6 us
    ppermute x46, starting transfers between devices, swap_bits(): return lax.ppermute(array, ('dp', 'mp'), pairs)  65.2 us
    pallas_call x6, Pallas kernels, in_vmem(): pl.pallas_call(kernel, in_specs=specs or [whole] * len(inputs), out_specs...  35.5 us
    pallas_call x2, Pallas kernels, attend_backward(): pl.pallas_call(attend_back_kernel, grid=(pairs,), in_specs=[tall(2 * PAIR...  27.9 us
    pallas_call x2, Pallas kernels, panel_gradients(): pl.pallas_call(lambda *refs: gradients_kernel(panel_rows, cuts, lefts, ri...  26 us
    unnamed x184, local copies, waits for them, and re-layouts  25.6 us
    pallas_call x1, Pallas kernels, attend_forward(): pl.pallas_call(attend_kernel, grid=(pairs,), in_specs=[tall(PAIR), tall(P...  13.5 us
    ppermute x17, waiting for transfers between devices, swap_core(): return lax.ppermute(array, 'mp', [(0, 1), (1, 0)])  12.8 us
  transfers between devices with their start and end apart: 63, of which 27 were waited for; matrix products, arithmetic and copies ran while one was open for 12% of the time, Pallas kernels for 19%

profile of v4, /device:TPU:0, one launch (start us, length us, event | category | flops | bytes accessed | tf_op | source)
XLA Modules:
  0.0 365.7 jit_solution(6421162689994725714)
XLA Ops:
  1.6 4.1 %collective-permute-start = (bf16[1,48,1024]{2,1,0:T(8,128)(2,1)S(1)}, bf16[1,48,1024]{2,1,0:T(8,128)(2,1)S(1)}, u32[]{:S(2)}, u32[]{:S(2)}) collective-permute-start(bf16[1,48,1024]{2,1,0:T(8,128)(2,1)S(1)} %fusion.38), channel_id=1, source_target_pairs={{0,16},{1,17},{2,18},{3,19},{4,20},{5,21},{6,22},{7,23},{8,24},{9,... | collective-permute-start | bytes 294920 | tf_op jit(solution)/shard_map/ppermute | solution.py:38
  10.6 4.5 %collective-permute-done.1 = f32[8,3072]{1,0:T(8,128)S(1)} collective-permute-done((f32[8,3072]{1,0:T(8,128)S(1)}, f32[8,3072]{1,0:T(8,128)S(1)}, u32[]{:S(2)}, u32[]{:S(2)}) %collective-permute-start.1) | collective-permute-done | bytes 98336 | tf_op jit(solution)/shard_map/ppermute | solution.py:38
  15.8 1.7 collective-permute-start.3
  17.4 5.4 %collective-permute-done.3 = f32[8,3072]{1,0:T(8,128)S(1)} collective-permute-done((f32[8,3072]{1,0:T(8,128)S(1)}, f32[8,3072]{1,0:T(8,128)S(1)}, u32[]{:S(2)}, u32[]{:S(2)}) %collective-permute-start.3) | collective-permute-done | bytes 98336 | tf_op jit(solution)/shard_map/ppermute | solution.py:38
  25.8 1.8 collective-permute-start.5
  27.6 3.4 collective-permute-start.8
  31.6 1.6 collective-permute-start.7
  33.2 3.2 collective-permute-done.7
  36.4 1.8 collective-permute-done.8
  42.6 1.6 collective-permute-start.13
  44.3 1.6 collective-permute-start.10
  45.9 1.7 collective-permute-start.16
  48.8 2.3 fusion.60
  51.1 5.9 %collective-permute-done.16 = bf16[1,176,512]{2,1,0:T(8,128)(2,1)} collective-permute-done((bf16[1,176,512]{2,1,0:T(8,128)(2,1)}, bf16[1,176,512]{2,1,0:T(8,128)(2,1)}, u32[]{:S(2)}, u32[]{:S(2)}) %collective-permute-start.16) | collective-permute-done | bytes 180256 | tf_op jit(solution)/shard_map/ppermute | solution.py:38
  59.6 1.5 collective-permute-start.17
  64.4 2.5 collective-permute-start.18
  68.0 1.6 collective-permute-start.19
  71.2 6.9 %collective-permute-done.14 = bf16[1,336,512]{2,1,0:T(8,128)(2,1)S(1)} collective-permute-done((bf16[1,336,512]{2,1,0:T(8,128)(2,1)}, bf16[1,336,512]{2,1,0:T(8,128)(2,1)S(1)}, u32[]{:S(2)}, u32[]{:S(2)}) %collective-permute-start.14) | collective-permute-done | bytes 344096 | tf_op jit(solution)/shard_map/ppermute | solution.py:38
  85.7 7.4 %collective-permute-done.15 = bf16[2,1,336,512]{3,2,0,1:T(8,128)(2,1)S(1)} collective-permute-done((bf16[2,1,336,512]{3,2,0,1:T(8,128)(2,1)S(1)}, bf16[2,1,336,512]{3,2,0,1:T(8,128)(2,1)S(1)}, u32[]{:S(2)}, u32[]{:S(2)}) %collective-permute-start.15) | collective-permute-done | bytes 688160 | tf_op jit(solution)/shard_map/ppermute | solution.py:38
  99.1 1.9 constant_dynamic-slice_fusion.2
  102.9 11.3 %text_forward.1 = (f32[512,1024]{1,0:T(8,128)S(1)}, f32[1,1024]{1,0:T(1,128)S(1)}, bf16[512,1024]{1,0:T(8,128)(2,1)S(1)}, bf16[512,512]{1,0:T(8,128)(2,1)S(1)}, ...) custom-call(s32[1]{0:T(128)} %bitcast.core_ref, ...), custom_call_target="tpu_custom_call" | custom-call | flops 1000 | bytes 1000 | tf_op jit(solution)/shard_map/text_forward/pallas_call | solution.py:612
  121.8 9.5 %project.1 = (bf16[1024,512]{1,0:T(8,128)(2,1)S(1)}, bf16[1024,512]{1,0:T(8,128)(2,1)S(1)}, bf16[1024,512]{1,0:T(8,128)(2,1)S(1)}, bf16[8192,512]{1,0:T(8,128)(2,1)S(1)}) custom-call(s32[64]{0:T(128)S(1)} %pad_add_fusion.1.refs_0_, bf16[4,336,512]{2,1,0:T(8,128)(2,1)S(1)} %bitcast.214, bf16[4,176,512]{2,1,0:T(8,128)(2,1)S(1)} %bitcast.217, ...), custom_call_target="tpu_custom_call" | custom-call | flops 3221225472 | bytes 25165824 | tf_op jit(solution)/shard_map/project/pallas_call | solution.py:437
  131.5 13.5 %attend.1 = (bf16[1024,512]{1,0:T(8,128)(2,1)S(1)}, bf16[1024,1024]{1,0:T(8,128)(2,1)S(1)}) custom-call(bf16[1024,512]{1,0:T(8,128)(2,1)S(1)} %get-tuple-element.198.q_ref, bf16[1024,512]{1,0:T(8,128)(2,1)S(1)} %get-tuple-element.199.k_ref.kr_ref, bf16[1024,512]{1,0:T(8,128)(2,1)S(1)} %get-tuple-element.200.v_ref, ...), custom_call_target="tpu_custom_call" | custom-call | flops 17179869184 | bytes 6291456 | tf_op jit(solution)/shard_map/attend/pallas_call | solution.py:270
  145.9 2.6 collective-permute-done.24
  150.5 2.5 collective-permute-done.25.n_ref.refs_6_
  153.0 4.8 %feed.3 = (bf16[512,1024]{1,0:T(8,128)(2,1)S(1)}, bf16[512,1024]{1,0:T(8,128)(2,1)S(1)}, bf16[512,1024]{1,0:T(8,128)(2,1)S(1)}, bf16[512,1024]{1,0:T(8,128)(2,1)S(1)}) custom-call(bf16[512,1024]{1,0:T(8,128)(2,1)S(1)} %collective-permute-done.25.n_ref.refs_6_, bf16[512,1024]{1,0:T(8,128)(2,1)S(1)} %get-tuple-element.205.g_ref.refs_8_, ...), custom_call_target="tpu_custom_call" | custom-call | flops 4294967296 | bytes 8388608 | tf_op jit(solution)/shard_map/feed/pallas_call | solution.py:481
  158.4 4.8 %feed.2 = (f32[512,1024]{1,0:T(8,128)S(1)}, f32[512,1024]{1,0:T(8,128)S(1)}, bf16[512,1024]{1,0:T(8,128)(2,1)S(1)}, bf16[512,1024]{1,0:T(8,128)(2,1)S(1)}) custom-call(bf16[512,1024]{1,0:T(8,128)(2,1)S(1)} %add_convert_fusion.1.n_ref.refs_5_, bf16[512,1024]{1,0:T(8,128)(2,1)S(1)} %get-tuple-element.203.g_ref.refs_7_, bf16[8,1024,512]{2,1,0:T(8,128)(2,1)S(1)} %bitcast.208), custom_call_target="tpu_custom_call" | custom-call | flops 4294967296 | bytes 8388608 | tf_op jit(solution)/shard_map/feed/pallas_call | solution.py:481
  163.2 3.5 settle.1
  167.0 2.4 collective-permute-done.28.other_ref.refs_4_
  169.4 13.9 %attend_back.2 = (bf16[1024,256]{1,0:T(8,128)(2,1)S(1)}, bf16[1024,256]{1,0:T(8,128)(2,1)S(1)}, bf16[1024,256]{1,0:T(8,128)(2,1)S(1)}) custom-call(bf16[1024,1024]{1,0:T(8,128)(2,1)S(1)} %get-tuple-element.223.qa_ref, bf16[1024,512]{1,0:T(8,128)(2,1)S(1)} %get-tuple-element.199.k_ref.kr_ref, bf16[1024,512]{1,0:T(8,128)(2,1)S(1)} %get-tuple-element.200.v_ref, ...), custom_call_target="tpu_custom_call" | custom-call | flops 1000 | bytes 1000 | tf_op jit(solution)/shard_map/attend_back/pallas_call | solution.py:352
  183.4 13.6 %gradients.2 = (bf16[8,336,256]{2,1,0:T(8,128)(2,1)S(1)}, bf16[8,176,256]{2,1,0:T(8,128)(2,1)S(1)}, bf16[8,336,256]{2,1,0:T(8,128)(2,1)S(1)}, bf16[8,176,256]{2,1,0:T(8,128)(2,1)S(1)}) custom-call(s32[64]{0:T(128)S(1)} %pad_add_fusion.refs_0_, bf16[512,1024]{1,0:T(8,128)(2,1)S(1)} %get-tuple-element.187.refs_9_.refs_1_, ...), custom_call_target="tpu_custom_call" | custom-call | flops 1000 | bytes 1000 | tf_op jit(solution)/shard_map/gradients/pallas_call | solution.py:589
  198.8 14.0 %attend_back.3 = (bf16[1024,256]{1,0:T(8,128)(2,1)S(1)}, bf16[1024,256]{1,0:T(8,128)(2,1)S(1)}, bf16[1024,256]{1,0:T(8,128)(2,1)S(1)}) custom-call(bf16[1024,1024]{1,0:T(8,128)(2,1)S(1)} %get-tuple-element.223.qa_ref, bf16[1024,512]{1,0:T(8,128)(2,1)S(1)} %get-tuple-element.199.k_ref.kr_ref, bf16[1024,512]{1,0:T(8,128)(2,1)S(1)} %get-tuple-element.200.v_ref, ...), custom_call_target="tpu_custom_call" | custom-call | flops 1000 | bytes 1000 | tf_op jit(solution)/shard_map/attend_back/pallas_call | solution.py:352
  212.8 2.9 collective-permute-done.30
  218.6 3.4 inputs_grad.1
  222.0 4.7 %collective-permute-done.32 = bf16[2,2,176,256]{3,2,1,0:T(8,128)(2,1)S(1)} collective-permute-done((bf16[2,2,176,256]{3,2,1,0:T(8,128)(2,1)S(1)}, bf16[2,2,176,256]{3,2,1,0:T(8,128)(2,1)S(1)}, u32[]{:S(2)}, u32[]{:S(2)}) %collective-permute-start.32) | collective-permute-done | bytes 360480 | tf_op jit(solution)/shard_map/ppermute | solution.py:38
  230.2 12.4 %gradients.3 = (bf16[8,336,256]{2,1,0:T(8,128)(2,1)S(1)}, bf16[8,176,256]{2,1,0:T(8,128)(2,1)S(1)}, bf16[8,336,256]{2,1,0:T(8,128)(2,1)}, bf16[8,176,256]{2,1,0:T(8,128)(2,1)S(1)}) custom-call(s32[64]{0:T(128)S(1)} %pad_add_fusion.refs_0_, bf16[512,1024]{1,0:T(8,128)(2,1)S(1)} %get-tuple-element.187.refs_9_.refs_1_, ...), custom_call_target="tpu_custom_call" | custom-call | flops 1000 | bytes 1000 | tf_op jit(solution)/shard_map/gradients/pallas_call | solution.py:589
  250.2 2.3 constant_dynamic-update-slice_fusion.9
  252.4 1.9 copy-done.1
  254.3 1.6 copy-done.6
  255.9 1.6 copy-done.20
  257.5 1.6 copy-done.22
  260.3 3.4 stream_back.1
  263.9 3.3 collective-permute-done.37
  267.3 1.8 fusion
  271.2 4.8 %collective-permute-start.40 = (bf16[1,336,256]{2,1,0:T(8,128)(2,1)S(1)}, bf16[1,336,256]{2,1,0:T(8,128)(2,1)S(1)}, u32[]{:S(2)}, u32[]{:S(2)}) collective-permute-start(bf16[1,336,256]{2,1,0:T(8,128)(2,1)S(1)} %get-tuple-element.361), channel_id=1, source_target_pairs={{0,16},{1,17},{2,18},{3,19},{4,20},{5,21},{6,22},{7,23},{8,24},{9,... | collective-permute-start | bytes 516104 | tf_op jit(solution)/shard_map/ppermute | solution.py:38
  277.2 2.3 collective-permute-start.41
  279.6 7.9 %text_back.1 = (f32[512,512]{1,0:T(8,128)S(1)}, f32[3,512]{1,0:T(4,128)S(1)}, f32[2,1024]{1,0:T(2,128)S(1)}, bf16[16,48,1024]{2,1,0:T(8,128)(2,1)S(1)}, bf16[16,48,1024]{2,1,0:T(8,128)(2,1)}) custom-call(f32[512,1024]{1,0:T(8,128)S(1)} %copy-done.7, f32[512,1024]{1,0:T(8,128)S(1)} %get-tuple-element.263.grn_grad_ref, ...), custom_call_target="tpu_custom_call" | custom-call | flops 1000 | bytes 1000 | tf_op jit(solution)/shard_map/text_back/pallas_call | solution.py:612
  289.4 1.7 collective-permute-start.44
  292.8 1.9 collective-permute-done.47.border_ref
  294.7 4.1 %conv_back.1 = (f32[512,512]{1,0:T(8,128)S(1)}, f32[7,512]{1,0:T(8,128)S(1)}, f32[1024,512]{1,0:T(8,128)}) custom-call(s32[1]{0:T(128)} %bitcast.core_ref, f32[512,512]{1,0:T(8,128)S(1)} %get-tuple-element.278.mixed_ref, f32[8,512]{1,0:T(8,128)S(1)} %collective-permute-done.47.border_ref, f32[528,512]{1,0:T(8,128)S(1)} %get-tuple-element.340.window_ref, ...), custom_call_target="tpu_custom_call" | custom-call | flops 1000 | bytes 1000 | tf_op jit(solution)/shard_map/conv_back/pallas_call | solution.py:612
  302.2 2.1 add_convert_fusion
  306.4 1.9 collective-permute-start.48
  311.7 9.3 %collective-permute-done.49 = bf16[1,176,256]{2,1,0:T(8,128)(2,1)S(1)} collective-permute-done((bf16[1,176,256]{2,1,0:T(8,128)(2,1)S(1)}, bf16[1,176,256]{2,1,0:T(8,128)(2,1)S(1)}, u32[]{:S(2)}, u32[]{:S(2)}) %collective-permute-start.49) | collective-permute-done | bytes 90144 | tf_op jit(solution)/shard_map/ppermute | solution.py:38
  321.4 1.7 collective-permute-start.54
  323.3 4.8 %collective-permute-done.55 = f32[226,128]{1,0:T(8,128)S(1)} collective-permute-done((f32[226,128]{1,0:T(8,128)S(1)}, f32[226,128]{1,0:T(8,128)S(1)}, u32[]{:S(2)}, u32[]{:S(2)}) %collective-permute-start.55) | collective-permute-done | bytes 115744 | tf_op jit(solution)/shard_map/ppermute | solution.py:38
  328.1 1.9 collective-permute-done.54
  330.2 1.8 collective-permute-start.59
  332.1 3.0 collective-permute-done.59
  336.5 3.5 collective-permute-done.60
  340.6 2.6 collective-permute-start.57
  343.2 5.4 %rotated_step.1 = (f32[512,512]{1,0:T(8,128)}, f32[512,512]{1,0:T(8,128)}, f32[512,512]{1,0:T(8,128)}) custom-call(bf16[336,256]{1,0:T(8,128)(2,1)S(1)} %get-tuple-element.360.refs_0_, bf16[336,256]{1,0:T(8,128)(2,1)S(1)} %bitcast.220, bf16[176,256]{1,0:T(8,128)(2,1)S(1)} %get-tuple-element.368.refs_2_, bf16[176,256]{1,0:T(8,128)(2,1)S(1)} %bitcast.222, ...), custom_call_target="tpu_custom_call" | custom-call | flops 1000 | bytes 1000 | tf_op jit(solution)/shard_map/rotated_step/pallas_call | solution.py:612
  355.6 1.6 multiply_subtract_fusion.1
  358.6 4.4 %modulation_step.1 = (f32[64,6144]{1,0:T(8,128)}, f32[64,6144]{1,0:T(8,128)}, f32[64,6144]{1,0:T(8,128)}) custom-call(bf16[8,64]{1,0:T(8,128)(2,1)S(1)} %multiply_convert_fusion.2.refs_0_, bf16[8,6144]{1,0:T(8,128)(2,1)S(1)} %get-tuple-element.363.refs_1_, f32[64,6144]{1,0:T(8,128)S(1)} %copy-done.17, f32[64,6144]{1,0:T(8,128)S(1)} %copy-done.25, ...), custom_call_target="tpu_custom_call" | custom-call | flops 1000 | bytes 1000 | tf_op jit(solution)/shard_map/modulation_step/pallas_call | solution.py:957
  363.0 2.5 multiply_subtract_fusion
  (400 shorter events, 93.1 us)
Async XLA Ops:
  1.6 9.0 %collective-permute-start = (bf16[1,48,1024]{2,1,0:T(8,128)(2,1)S(1)}, bf16[1,48,1024]{2,1,0:T(8,128)(2,1)S(1)}, u32[]{:S(2)}, u32[]{:S(2)}) collective-permute-start(bf16[1,48,1024]{2,1,0:T(8,128)(2,1)S(1)} %fusion.38), channel_id=1, source_target_pairs={{0,16},{1,17},{2,18},{3,19},{4,20},{5,21},{6,22},{7,23},{8,24},{9,... | collective-permute-start | bytes 294920 | tf_op jit(solution)/shard_map/ppermute | solution.py:38
  7.8 7.3 %collective-permute-start.1 = (f32[8,3072]{1,0:T(8,128)S(1)}, f32[8,3072]{1,0:T(8,128)S(1)}, u32[]{:S(2)}, u32[]{:S(2)}) collective-permute-start(f32[8,3072]{1,0:T(8,128)S(1)} %fusion.32), channel_id=1, source_target_pairs={{0,16},{1,17},{2,18},{3,19},{4,20},{5,21},{6,22},{7,23},{8,24},{9,... | collective-permute-start | bytes 294920 | tf_op jit(solution)/shard_map/ppermute | solution.py:38
  15.2 7.7 %collective-permute-start.2 = (bf16[2,48,1024]{2,1,0:T(8,128)(2,1)S(1)}, bf16[2,48,1024]{2,1,0:T(8,128)(2,1)S(1)}, u32[]{:S(2)}, u32[]{:S(2)}) collective-permute-start(bf16[2,48,1024]{2,1,0:T(8,128)(2,1)S(1)} %get-tuple-element.365), channel_id=1, source_target_pairs={{0,8},{1,9},{2,10},{3,11},{4,12},{5,13},{6,14},{7,15},{8,0},{9,1},... | collective-permute-start | bytes 589832 | tf_op jit(solution)/shard_map/ppermute | solution.py:38
  15.8 7.1 %collective-permute-start.3 = (f32[8,3072]{1,0:T(8,128)S(1)}, f32[8,3072]{1,0:T(8,128)S(1)}, u32[]{:S(2)}, u32[]{:S(2)}) collective-permute-start(f32[8,3072]{1,0:T(8,128)S(1)} %add.503), channel_id=1, source_target_pairs={{0,8},{1,9},{2,10},{3,11},{4,12},{5,13},{6,14},{7,15},{8,0},{9,1},... | collective-permute-start | bytes 294920 | tf_op jit(solution)/shard_map/ppermute | solution.py:38
  23.6 14.5 %collective-permute-start.4 = (bf16[1,336,512]{2,1,0:T(8,128)(2,1)}, bf16[1,336,512]{2,1,0:T(8,128)(2,1)S(1)}, u32[]{:S(2)}, u32[]{:S(2)}) collective-permute-start(bf16[1,336,512]{2,1,0:T(8,128)(2,1)} %get-tuple-element.351), channel_id=1, source_target_pairs={{0,2},{1,5},{2,0},{3,7},{4,6},{5,1},{6,4},{7,3},{8,10},{9,13},{10,... | collective-permute-start | bytes 1032200 | tf_op jit(solution)/shard_map/ppermute | solution.py:38
  25.2 13.0 %collective-permute-start.6 = (bf16[2,2,48,1024]{3,2,1,0:T(8,128)(2,1)S(1)}, bf16[2,2,48,1024]{3,2,1,0:T(8,128)(2,1)S(1)}, u32[]{:S(2)}, u32[]{:S(2)}) collective-permute-start(bf16[2,2,48,1024]{3,2,1,0:T(8,128)(2,1)S(1)} %get-tuple-element.353), channel_id=1, source_target_pairs={{0,2},{1,5},{2,0},{3,7},{4,6},{5,1},{6,4},{7,3},{8,10},{9,13},{10,... | collective-permute-start | bytes 1179656 | tf_op jit(solution)/shard_map/ppermute | solution.py:38
  25.8 10.6 %collective-permute-start.5 = (bf16[1,176,512]{2,1,0:T(8,128)(2,1)S(1)}, bf16[1,176,512]{2,1,0:T(8,128)(2,1)S(1)}, u32[]{:S(2)}, u32[]{:S(2)}) collective-permute-start(bf16[1,176,512]{2,1,0:T(8,128)(2,1)S(1)} %get-tuple-element.349), channel_id=1, source_target_pairs={{0,8},{1,9},{2,10},{3,11},{4,12},{5,13},{6,14},{7,15},{8,0},{9,1},... | collective-permute-start | bytes 540680 | tf_op jit(solution)/shard_map/ppermute | solution.py:38
  27.6 10.5 %collective-permute-start.8 = (bf16[1,176,512]{2,1,0:T(8,128)(2,1)S(1)}, bf16[1,176,512]{2,1,0:T(8,128)(2,1)}, u32[]{:S(2)}, u32[]{:S(2)}) collective-permute-start(bf16[1,176,512]{2,1,0:T(8,128)(2,1)S(1)} %get-tuple-element.349), channel_id=1, source_target_pairs={{0,16},{1,17},{2,18},{3,19},{4,20},{5,21},{6,22},{7,23},{8,24},{9,... | collective-permute-start | bytes 540680 | tf_op jit(solution)/shard_map/ppermute | solution.py:38
  31.6 4.8 %collective-permute-start.7 = (f32[8,3072]{1,0:T(8,128)S(1)}, f32[8,3072]{1,0:T(8,128)S(1)}, u32[]{:S(2)}, u32[]{:S(2)}) collective-permute-start(f32[8,3072]{1,0:T(8,128)S(1)} %add.504), channel_id=1, source_target_pairs={{0,2},{1,5},{2,0},{3,7},{4,6},{5,1},{6,4},{7,3},{8,10},{9,13},{10,... | collective-permute-start | bytes 294920 | tf_op jit(solution)/shard_map/ppermute | solution.py:38
  39.2 22.5 %collective-permute-start.11 = (bf16[2,2,2,48,1024]{4,3,2,1,0:T(8,128)(2,1)}, bf16[2,2,2,48,1024]{4,3,2,1,0:T(8,128)(2,1)S(1)}, u32[]{:S(2)}, u32[]{:S(2)}) collective-permute-start(bf16[2,2,2,48,1024]{4,3,2,1,0:T(8,128)(2,1)} %get-tuple-element.343), channel_id=1, source_target_pairs={{0,4},{1,3},{2,6},{3,1},{4,0},{5,7},{6,2},{7,5},{8,12},{9,11},{10,... | collective-permute-start | bytes 2359304 | tf_op jit(solution)/shard_map/ppermute | solution.py:38
  41.6 20.0 %collective-permute-start.9 = (bf16[2,1,336,512]{3,2,0,1:T(8,128)(2,1)}, bf16[2,1,336,512]{3,2,0,1:T(8,128)(2,1)}, u32[]{:S(2)}, u32[]{:S(2)}) collective-permute-start(bf16[2,1,336,512]{3,2,0,1:T(8,128)(2,1)} %get-tuple-element.347), channel_id=1, source_target_pairs={{0,4},{1,9},{2,6},{3,11},{4,0},{5,13},{6,2},{7,15},{8,12},{9,1},{1... | collective-permute-start | bytes 2064392 | tf_op jit(solution)/shard_map/ppermute | solution.py:38
  42.6 17.0 %collective-permute-start.13 = (bf16[1,336,512]{2,1,0:T(8,128)(2,1)}, bf16[1,336,512]{2,1,0:T(8,128)(2,1)}, u32[]{:S(2)}, u32[]{:S(2)}) collective-permute-start(bf16[1,336,512]{2,1,0:T(8,128)(2,1)} %get-tuple-element.351), channel_id=1, source_target_pairs={{0,16},{1,17},{2,18},{3,19},{4,20},{5,21},{6,22},{7,23},{8,24},{9,... | collective-permute-start | bytes 1032200 | tf_op jit(solution)/shard_map/ppermute | solution.py:38
  44.3 17.3 %collective-permute-start.10 = (bf16[2,1,176,512]{3,2,0,1:T(8,128)(2,1)S(1)}, bf16[2,1,176,512]{3,2,0,1:T(8,128)(2,1)}, u32[]{:S(2)}, u32[]{:S(2)}) collective-permute-start(bf16[2,1,176,512]{3,2,0,1:T(8,128)(2,1)S(1)} %get-tuple-element.357), channel_id=1, source_target_pairs={{0,2},{1,3},{2,0},{3,1},{4,6},{5,7},{6,4},{7,5},{8,10},{9,11},{10,... | collective-permute-start | bytes 1081352 | tf_op jit(solution)/shard_map/ppermute | solution.py:38
  45.9 11.1 %collective-permute-start.16 = (bf16[1,176,512]{2,1,0:T(8,128)(2,1)}, bf16[1,176,512]{2,1,0:T(8,128)(2,1)}, u32[]{:S(2)}, u32[]{:S(2)}) collective-permute-start(bf16[1,176,512]{2,1,0:T(8,128)(2,1)} %collective-permute-done.8), channel_id=1, source_target_pairs={{0,8},{1,9},{2,10},{3,11},{4,12},{5,13},{6,14},{7,15},{8,0},{9,1},... | collective-permute-start | bytes 540680 | tf_op jit(solution)/shard_map/ppermute | solution.py:38
  57.0 4.6 %collective-permute-start.12 = (f32[8,3072]{1,0:T(8,128)S(1)}, f32[8,3072]{1,0:T(8,128)S(1)}, u32[]{:S(2)}, u32[]{:S(2)}) collective-permute-start(f32[8,3072]{1,0:T(8,128)S(1)} %add.505), channel_id=1, source_target_pairs={{0,4},{1,3},{2,6},{3,1},{4,0},{5,7},{6,2},{7,5},{8,12},{9,11},{10,... | collective-permute-start | bytes 294920 | tf_op jit(solution)/shard_map/ppermute | solution.py:38
  59.6 26.1 %collective-permute-start.17 = (bf16[2,1,176,512]{3,2,0,1:T(8,128)(2,1)S(1)}, bf16[2,1,176,512]{3,2,0,1:T(8,128)(2,1)S(1)}, u32[]{:S(2)}, u32[]{:S(2)}) collective-permute-start(bf16[2,1,176,512]{3,2,0,1:T(8,128)(2,1)S(1)} %get-tuple-element.355), channel_id=1, source_target_pairs={{0,2},{1,3},{2,0},{3,1},{4,6},{5,7},{6,4},{7,5},{8,10},{9,11},{10,... | collective-permute-start | bytes 1081352 | tf_op jit(solution)/shard_map/ppermute | solution.py:38
  61.6 16.4 %collective-permute-start.14 = (bf16[1,336,512]{2,1,0:T(8,128)(2,1)}, bf16[1,336,512]{2,1,0:T(8,128)(2,1)S(1)}, u32[]{:S(2)}, u32[]{:S(2)}) collective-permute-start(bf16[1,336,512]{2,1,0:T(8,128)(2,1)} %collective-permute-done.13), channel_id=1, source_target_pairs={{0,2},{1,5},{2,0},{3,7},{4,6},{5,1},{6,4},{7,3},{8,10},{9,13},{10,... | collective-permute-start | bytes 1032200 | tf_op jit(solution)/shard_map/ppermute | solution.py:38
  64.4 28.7 %collective-permute-start.18 = (bf16[2,2,1,336,512]{4,3,1,2,0:T(8,128)(2,1)S(1)}, bf16[2,2,1,336,512]{4,3,1,2,0:T(8,128)(2,1)S(1)}, u32[]{:S(2)}, u32[]{:S(2)}) collective-permute-start(bf16[2,2,1,336,512]{4,3,1,2,0:T(8,128)(2,1)S(1)} %pad_maximum_fusion.2), channel_id=1, source_target_pairs={{0,8},{1,3},{2,10},{3,1},{4,12},{5,7},{6,14},{7,5},{8,0},{9,11},{1... | collective-permute-start | bytes 4128776 | tf_op jit(solution)/shard_map/ppermute | solution.py:38
  68.0 17.7 %collective-permute-start.19 = (bf16[2,2,1,176,512]{4,3,1,2,0:T(8,128)(2,1)S(1)}, bf16[2,2,1,176,512]{4,3,1,2,0:T(8,128)(2,1)S(1)}, u32[]{:S(2)}, u32[]{:S(2)}) collective-permute-start(bf16[2,2,1,176,512]{4,3,1,2,0:T(8,128)(2,1)S(1)} %pad_maximum_fusion.6), channel_id=1, source_target_pairs={{0,4},{1,5},{2,6},{3,7},{4,0},{5,1},{6,2},{7,3},{8,12},{9,13},{10,... | collective-permute-start | bytes 2162696 | tf_op jit(solution)/shard_map/ppermute | solution.py:38
  69.6 1.4 collective-permute-start.21
  71.0 22.1 %collective-permute-start.20 = (bf16[16,48,1024]{2,1,0:T(8,128)(2,1)S(1)}, bf16[16,48,1024]{2,1,0:T(8,128)(2,1)S(1)}, u32[]{:S(2)}, u32[]{:S(2)}) collective-permute-start(bf16[16,48,1024]{2,1,0:T(8,128)(2,1)S(1)} %bitcast.212), channel_id=1, source_target_pairs={{0,1},{1,0},{2,3},{3,2},{4,5},{5,4},{6,7},{7,6},{8,9},{9,8},{10,11... | collective-permute-start | bytes 4718600 | tf_op jit(solution)/shard_map/ppermute | solution.py:30
  79.2 14.0 %collective-permute-start.15 = (bf16[2,1,336,512]{3,2,0,1:T(8,128)(2,1)S(1)}, bf16[2,1,336,512]{3,2,0,1:T(8,128)(2,1)S(1)}, u32[]{:S(2)}, u32[]{:S(2)}) collective-permute-start(bf16[2,1,336,512]{3,2,0,1:T(8,128)(2,1)S(1)} %get-tuple-element.345), channel_id=1, source_target_pairs={{0,4},{1,9},{2,6},{3,11},{4,0},{5,13},{6,2},{7,15},{8,12},{9,1},{1... | collective-permute-start | bytes 2064392 | tf_op jit(solution)/shard_map/ppermute | solution.py:38
  94.5 24.6 %collective-permute-start.22 = (bf16[2,2,1,336,512]{4,3,1,2,0:T(8,128)(2,1)}, bf16[2,2,1,336,512]{4,3,1,2,0:T(8,128)(2,1)}, u32[]{:S(2)}, u32[]{:S(2)}) collective-permute-start(bf16[2,2,1,336,512]{4,3,1,2,0:T(8,128)(2,1)} %pad_maximum_fusion.3), channel_id=1, source_target_pairs={{0,8},{1,3},{2,10},{3,1},{4,12},{5,7},{6,14},{7,5},{8,0},{9,11},{1... | collective-permute-start | bytes 4128776 | tf_op jit(solution)/shard_map/ppermute | solution.py:38
  96.5 22.6 %collective-permute-start.23 = (bf16[2,2,1,176,512]{4,3,1,2,0:T(8,128)(2,1)}, bf16[2,2,1,176,512]{4,3,1,2,0:T(8,128)(2,1)}, u32[]{:S(2)}, u32[]{:S(2)}) collective-permute-start(bf16[2,2,1,176,512]{4,3,1,2,0:T(8,128)(2,1)} %pad_maximum_fusion.7), channel_id=1, source_target_pairs={{0,4},{1,5},{2,6},{3,7},{4,0},{5,1},{6,2},{7,3},{8,12},{9,13},{10,... | collective-permute-start | bytes 2162696 | tf_op jit(solution)/shard_map/ppermute | solution.py:38
  117.4 31.1 %copy-start.3 = (f32[512,1024]{1,0:T(8,128)}, f32[512,1024]{1,0:T(8,128)S(1)}, u32[]{:S(2)}) copy-start(f32[512,1024]{1,0:T(8,128)S(1)} %get-tuple-element.189.stream_ref) | copy-start | bytes 6291460
  145.8 2.7 collective-permute-start.24
  150.3 2.7 collective-permute-start.25
  157.8 5.4 %collective-permute-start.26 = (bf16[512,1024]{1,0:T(8,128)(2,1)S(1)}, bf16[512,1024]{1,0:T(8,128)(2,1)S(1)}, u32[]{:S(2)}, u32[]{:S(2)}) collective-permute-start(bf16[512,1024]{1,0:T(8,128)(2,1)S(1)} %get-tuple-element.206), channel_id=1, source_target_pairs={{0,1},{1,0},{2,3},{3,2},{4,5},{5,4},{6,7},{7,6},{8,9},{9,8},{10,11... | collective-permute-start | bytes 3145736 | tf_op jit(solution)/shard_map/ppermute | solution.py:30
  158.0 5.2 %collective-permute-start.27 = (bf16[512,1024]{1,0:T(8,128)(2,1)S(1)}, bf16[512,1024]{1,0:T(8,128)(2,1)S(1)}, u32[]{:S(2)}, u32[]{:S(2)}) collective-permute-start(bf16[512,1024]{1,0:T(8,128)(2,1)S(1)} %get-tuple-element.208), channel_id=1, source_target_pairs={{0,1},{1,0},{2,3},{3,2},{4,5},{5,4},{6,7},{7,6},{8,9},{9,8},{10,11... | collective-permute-start | bytes 3145736 | tf_op jit(solution)/shard_map/ppermute | solution.py:30
  166.7 2.7 collective-permute-start.28
  196.9 18.8 %collective-permute-start.29 = (bf16[2,2,2,336,256]{4,3,2,1,0:T(8,128)(2,1)S(1)}, bf16[2,2,2,336,256]{4,3,2,1,0:T(8,128)(2,1)S(1)}, u32[]{:S(2)}, u32[]{:S(2)}) collective-permute-start(bf16[2,2,2,336,256]{4,3,2,1,0:T(8,128)(2,1)S(1)} %bitcast.234), channel_id=1, source_target_pairs={{0,8},{1,3},{2,10},{3,1},{4,12},{5,7},{6,14},{7,5},{8,0},{9,11},{1... | collective-permute-start | bytes 4128776 | tf_op jit(solution)/shard_map/ppermute | solution.py:38
  198.3 17.5 %collective-permute-start.30 = (bf16[2,2,2,176,256]{4,3,2,1,0:T(8,128)(2,1)S(1)}, bf16[2,2,2,176,256]{4,3,2,1,0:T(8,128)(2,1)S(1)}, u32[]{:S(2)}, u32[]{:S(2)}) collective-permute-start(bf16[2,2,2,176,256]{4,3,2,1,0:T(8,128)(2,1)S(1)} %bitcast.237), channel_id=1, source_target_pairs={{0,4},{1,5},{2,6},{3,7},{4,0},{5,1},{6,2},{7,3},{8,12},{9,13},{10,... | collective-permute-start | bytes 2162696 | tf_op jit(solution)/shard_map/ppermute | solution.py:38
  216.2 11.0 %collective-permute-start.31 = (bf16[2,2,336,256]{3,2,1,0:T(8,128)(2,1)S(1)}, bf16[2,2,336,256]{3,2,1,0:T(8,128)(2,1)S(1)}, u32[]{:S(2)}, u32[]{:S(2)}) collective-permute-start(bf16[2,2,336,256]{3,2,1,0:T(8,128)(2,1)S(1)} %slice_bitcast_fusion.4), channel_id=1, source_target_pairs={{0,4},{1,9},{2,6},{3,11},{4,0},{5,13},{6,2},{7,15},{8,12},{9,1},{1... | collective-permute-start | bytes 2064392 | tf_op jit(solution)/shard_map/ppermute | solution.py:38
  217.6 9.1 %collective-permute-start.32 = (bf16[2,2,176,256]{3,2,1,0:T(8,128)(2,1)S(1)}, bf16[2,2,176,256]{3,2,1,0:T(8,128)(2,1)S(1)}, u32[]{:S(2)}, u32[]{:S(2)}) collective-permute-start(bf16[2,2,176,256]{3,2,1,0:T(8,128)(2,1)S(1)} %slice_bitcast_fusion.10), channel_id=1, source_target_pairs={{0,2},{1,3},{2,0},{3,1},{4,6},{5,7},{6,4},{7,5},{8,10},{9,11},{10,... | collective-permute-start | bytes 1081352 | tf_op jit(solution)/shard_map/ppermute | solution.py:38
  218.6 31.6 %collective-permute-start.53 = (bf16[512,1024]{1,0:T(8,128)(2,1)}, bf16[512,1024]{1,0:T(8,128)(2,1)}, u32[]{:S(2)}, u32[]{:S(2)}) collective-permute-start(bf16[512,1024]{1,0:T(8,128)(2,1)} %get-tuple-element.294), channel_id=1, source_target_pairs={{0,1},{1,0},{2,3},{3,2},{4,5},{5,4},{6,7},{7,6},{8,9},{9,8},{10,11... | collective-permute-start | bytes 3145736 | tf_op jit(solution)/shard_map/ppermute | solution.py:30
  227.2 18.3 %collective-permute-start.35 = (bf16[512,1024]{1,0:T(8,128)(2,1)S(1)}, bf16[512,1024]{1,0:T(8,128)(2,1)S(1)}, u32[]{:S(2)}, u32[]{:S(2)}) collective-permute-start(bf16[512,1024]{1,0:T(8,128)(2,1)S(1)} %get-tuple-element.246), channel_id=1, source_target_pairs={{0,1},{1,0},{2,3},{3,2},{4,5},{5,4},{6,7},{7,6},{8,9},{9,8},{10,11... | collective-permute-start | bytes 3145736 | tf_op jit(solution)/shard_map/ppermute | solution.py:30
  227.4 18.0 %collective-permute-start.33 = (bf16[2,336,256]{2,1,0:T(8,128)(2,1)S(1)}, bf16[2,336,256]{2,1,0:T(8,128)(2,1)S(1)}, u32[]{:S(2)}, u32[]{:S(2)}) collective-permute-start(bf16[2,336,256]{2,1,0:T(8,128)(2,1)S(1)} %slice_bitcast_fusion.14), channel_id=1, source_target_pairs={{0,2},{1,5},{2,0},{3,7},{4,6},{5,1},{6,4},{7,3},{8,10},{9,13},{10,... | collective-permute-start | bytes 1032200 | tf_op jit(solution)/shard_map/ppermute | solution.py:38
  229.0 16.5 %collective-permute-start.34 = (bf16[2,176,256]{2,1,0:T(8,128)(2,1)S(1)}, bf16[2,176,256]{2,1,0:T(8,128)(2,1)S(1)}, u32[]{:S(2)}, u32[]{:S(2)}) collective-permute-start(bf16[2,176,256]{2,1,0:T(8,128)(2,1)S(1)} %slice_bitcast_fusion.20), channel_id=1, source_target_pairs={{0,8},{1,9},{2,10},{3,11},{4,12},{5,13},{6,14},{7,15},{8,0},{9,1},... | collective-permute-start | bytes 540680 | tf_op jit(solution)/shard_map/ppermute | solution.py:38
  246.6 20.7 %collective-permute-start.36 = (bf16[2,2,2,336,256]{4,3,2,1,0:T(8,128)(2,1)}, bf16[2,2,2,336,256]{4,3,2,1,0:T(8,128)(2,1)}, u32[]{:S(2)}, u32[]{:S(2)}) collective-permute-start(bf16[2,2,2,336,256]{4,3,2,1,0:T(8,128)(2,1)} %bitcast.63), channel_id=1, source_target_pairs={{0,8},{1,3},{2,10},{3,1},{4,12},{5,7},{6,14},{7,5},{8,0},{9,11},{1... | collective-permute-start | bytes 4128776 | tf_op jit(solution)/shard_map/ppermute | solution.py:38
  249.4 17.8 %collective-permute-start.37 = (bf16[2,2,2,176,256]{4,3,2,1,0:T(8,128)(2,1)}, bf16[2,2,2,176,256]{4,3,2,1,0:T(8,128)(2,1)S(1)}, u32[]{:S(2)}, u32[]{:S(2)}) collective-permute-start(bf16[2,2,2,176,256]{4,3,2,1,0:T(8,128)(2,1)} %bitcast.236), channel_id=1, source_target_pairs={{0,4},{1,5},{2,6},{3,7},{4,0},{5,1},{6,2},{7,3},{8,12},{9,13},{10,... | collective-permute-start | bytes 2162696 | tf_op jit(solution)/shard_map/ppermute | solution.py:38
  269.2 19.2 %collective-permute-start.38 = (bf16[2,2,336,256]{3,2,1,0:T(8,128)(2,1)S(1)}, bf16[2,2,336,256]{3,2,1,0:T(8,128)(2,1)S(1)}, u32[]{:S(2)}, u32[]{:S(2)}) collective-permute-start(bf16[2,2,336,256]{3,2,1,0:T(8,128)(2,1)S(1)} %slice_bitcast_fusion.1), channel_id=1, source_target_pairs={{0,4},{1,9},{2,6},{3,11},{4,0},{5,13},{6,2},{7,15},{8,12},{9,1},{1... | collective-permute-start | bytes 2064392 | tf_op jit(solution)/shard_map/ppermute | solution.py:38
  270.5 17.9 %collective-permute-start.43 = (f32[512,1024]{1,0:T(8,128)S(1)}, f32[512,1024]{1,0:T(8,128)S(1)}, u32[]{:S(2)}, u32[]{:S(2)}) collective-permute-start(f32[512,1024]{1,0:T(8,128)S(1)} %get-tuple-element.273), channel_id=1, source_target_pairs={{0,1},{1,0},{2,3},{3,2},{4,5},{5,4},{6,7},{7,6},{8,9},{9,8},{10,11... | collective-permute-start | bytes 6291464 | tf_op jit(solution)/shard_map/ppermute | solution.py:30
  270.7 17.7 %collective-permute-start.39 = (bf16[2,2,176,256]{3,2,1,0:T(8,128)(2,1)S(1)}, bf16[2,2,176,256]{3,2,1,0:T(8,128)(2,1)S(1)}, u32[]{:S(2)}, u32[]{:S(2)}) collective-permute-start(bf16[2,2,176,256]{3,2,1,0:T(8,128)(2,1)S(1)} %slice_bitcast_fusion.8), channel_id=1, source_target_pairs={{0,2},{1,3},{2,0},{3,1},{4,6},{5,7},{6,4},{7,5},{8,10},{9,11},{10,... | collective-permute-start | bytes 1081352 | tf_op jit(solution)/shard_map/ppermute | solution.py:38
  271.2 17.1 %collective-permute-start.40 = (bf16[1,336,256]{2,1,0:T(8,128)(2,1)S(1)}, bf16[1,336,256]{2,1,0:T(8,128)(2,1)S(1)}, u32[]{:S(2)}, u32[]{:S(2)}) collective-permute-start(bf16[1,336,256]{2,1,0:T(8,128)(2,1)S(1)} %get-tuple-element.361), channel_id=1, source_target_pairs={{0,16},{1,17},{2,18},{3,19},{4,20},{5,21},{6,22},{7,23},{8,24},{9,... | collective-permute-start | bytes 516104 | tf_op jit(solution)/shard_map/ppermute | solution.py:38
  276.0 1.2 collective-permute-start.42
  277.2 11.2 %collective-permute-start.41 = (bf16[1,176,256]{2,1,0:T(8,128)(2,1)S(1)}, bf16[1,176,256]{2,1,0:T(8,128)(2,1)S(1)}, u32[]{:S(2)}, u32[]{:S(2)}) collective-permute-start(bf16[1,176,256]{2,1,0:T(8,128)(2,1)S(1)} %get-tuple-element.369), channel_id=1, source_target_pairs={{0,16},{1,17},{2,18},{3,19},{4,20},{5,21},{6,22},{7,23},{8,24},{9,... | collective-permute-start | bytes 270344 | tf_op jit(solution)/shard_map/ppermute | solution.py:38
  289.4 15.0 %collective-permute-start.44 = (bf16[2,336,256]{2,1,0:T(8,128)(2,1)}, bf16[2,336,256]{2,1,0:T(8,128)(2,1)}, u32[]{:S(2)}, u32[]{:S(2)}) collective-permute-start(bf16[2,336,256]{2,1,0:T(8,128)(2,1)} %slice_bitcast_fusion.11), channel_id=1, source_target_pairs={{0,2},{1,5},{2,0},{3,7},{4,6},{5,1},{6,4},{7,3},{8,10},{9,13},{10,... | collective-permute-start | bytes 1032200 | tf_op jit(solution)/shard_map/ppermute | solution.py:38
  291.2 11.0 %collective-permute-start.46 = (bf16[16,48,1024]{2,1,0:T(8,128)(2,1)}, bf16[16,48,1024]{2,1,0:T(8,128)(2,1)}, u32[]{:S(2)}, u32[]{:S(2)}) collective-permute-start(bf16[16,48,1024]{2,1,0:T(8,128)(2,1)} %get-tuple-element.277), channel_id=1, source_target_pairs={{0,1},{1,0},{2,3},{3,2},{4,5},{5,4},{6,7},{7,6},{8,9},{9,8},{10,11... | collective-permute-start | bytes 4718600 | tf_op jit(solution)/shard_map/ppermute | solution.py:30
  292.0 12.4 %collective-permute-start.45 = (bf16[2,176,256]{2,1,0:T(8,128)(2,1)}, bf16[2,176,256]{2,1,0:T(8,128)(2,1)}, u32[]{:S(2)}, u32[]{:S(2)}) collective-permute-start(bf16[2,176,256]{2,1,0:T(8,128)(2,1)} %slice_bitcast_fusion.18), channel_id=1, source_target_pairs={{0,8},{1,9},{2,10},{3,11},{4,12},{5,13},{6,14},{7,15},{8,0},{9,1},... | collective-permute-start | bytes 540680 | tf_op jit(solution)/shard_map/ppermute | solution.py:38
  292.2 2.5 collective-permute-start.47
  299.8 10.7 %collective-permute-start.52 = (f32[512,512]{1,0:T(8,128)}, f32[512,512]{1,0:T(8,128)S(1)}, u32[]{:S(2)}, u32[]{:S(2)}) collective-permute-start(f32[512,512]{1,0:T(8,128)} %copy-done.48), channel_id=1, source_target_pairs={{0,1},{1,0},{2,3},{3,2},{4,5},{5,4},{6,7},{7,6},{8,9},{9,8},{10,11... | collective-permute-start | bytes 3145736 | tf_op jit(solution)/shard_map/ppermute | solution.py:30
  304.4 16.5 %collective-permute-start.50 = (bf16[2,2,2,48,1024]{4,3,2,1,0:T(8,128)(2,1)S(1)}, bf16[2,2,2,48,1024]{4,3,2,1,0:T(8,128)(2,1)S(1)}, u32[]{:S(2)}, u32[]{:S(2)}) collective-permute-start(bf16[2,2,2,48,1024]{4,3,2,1,0:T(8,128)(2,1)S(1)} %slice_bitcast_fusion), channel_id=1, source_target_pairs={{0,4},{1,3},{2,6},{3,1},{4,0},{5,7},{6,2},{7,5},{8,12},{9,11},{10,... | collective-permute-start | bytes 2359304 | tf_op jit(solution)/shard_map/ppermute | solution.py:38
  306.4 14.5 %collective-permute-start.48 = (bf16[1,336,256]{2,1,0:T(8,128)(2,1)S(1)}, bf16[1,336,256]{2,1,0:T(8,128)(2,1)S(1)}, u32[]{:S(2)}, u32[]{:S(2)}) collective-permute-start(bf16[1,336,256]{2,1,0:T(8,128)(2,1)S(1)} %get-tuple-element.359), channel_id=1, source_target_pairs={{0,16},{1,17},{2,18},{3,19},{4,20},{5,21},{6,22},{7,23},{8,24},{9,... | collective-permute-start | bytes 516104 | tf_op jit(solution)/shard_map/ppermute | solution.py:38
  309.3 11.6 %collective-permute-start.49 = (bf16[1,176,256]{2,1,0:T(8,128)(2,1)S(1)}, bf16[1,176,256]{2,1,0:T(8,128)(2,1)S(1)}, u32[]{:S(2)}, u32[]{:S(2)}) collective-permute-start(bf16[1,176,256]{2,1,0:T(8,128)(2,1)S(1)} %get-tuple-element.367), channel_id=1, source_target_pairs={{0,16},{1,17},{2,18},{3,19},{4,20},{5,21},{6,22},{7,23},{8,24},{9,... | collective-permute-start | bytes 270344 | tf_op jit(solution)/shard_map/ppermute | solution.py:38
  310.5 1.2 collective-permute-start.51
  321.4 8.6 %collective-permute-start.54 = (bf16[2,2,48,1024]{3,2,1,0:T(8,128)(2,1)S(1)}, bf16[2,2,48,1024]{3,2,1,0:T(8,128)(2,1)S(1)}, u32[]{:S(2)}, u32[]{:S(2)}) collective-permute-start(bf16[2,2,48,1024]{3,2,1,0:T(8,128)(2,1)S(1)} %slice_bitcast_fusion.5), channel_id=1, source_target_pairs={{0,2},{1,5},{2,0},{3,7},{4,6},{5,1},{6,4},{7,3},{8,10},{9,13},{10,... | collective-permute-start | bytes 1179656 | tf_op jit(solution)/shard_map/ppermute | solution.py:38
  323.2 4.9 %collective-permute-start.55 = (f32[226,128]{1,0:T(8,128)S(1)}, f32[226,128]{1,0:T(8,128)S(1)}, u32[]{:S(2)}, u32[]{:S(2)}) collective-permute-start(f32[226,128]{1,0:T(8,128)S(1)} %maximum_bitcast_fusion), channel_id=1, source_target_pairs={{0,8},{1,3},{2,10},{3,1},{4,12},{5,7},{6,14},{7,5},{8,0},{9,11},{1... | collective-permute-start | bytes 347144 | tf_op jit(solution)/shard_map/ppermute | solution.py:38
  330.2 4.9 %collective-permute-start.59 = (f32[226,128]{1,0:T(8,128)S(1)}, f32[226,128]{1,0:T(8,128)S(1)}, u32[]{:S(2)}, u32[]{:S(2)}) collective-permute-start(f32[226,128]{1,0:T(8,128)S(1)} %fusion.49), channel_id=1, source_target_pairs={{0,2},{1,5},{2,0},{3,7},{4,6},{5,1},{6,4},{7,3},{8,10},{9,13},{10,... | collective-permute-start | bytes 347144 | tf_op jit(solution)/shard_map/ppermute | solution.py:38
  332.0 8.5 %collective-permute-start.56 = (bf16[2,48,1024]{2,1,0:T(8,128)(2,1)S(1)}, bf16[2,48,1024]{2,1,0:T(8,128)(2,1)S(1)}, u32[]{:S(2)}, u32[]{:S(2)}) collective-permute-start(bf16[2,48,1024]{2,1,0:T(8,128)(2,1)S(1)} %slice_bitcast_fusion.15), channel_id=1, source_target_pairs={{0,8},{1,9},{2,10},{3,11},{4,12},{5,13},{6,14},{7,15},{8,0},{9,1},... | collective-permute-start | bytes 589832 | tf_op jit(solution)/shard_map/ppermute | solution.py:38
  335.1 4.9 %collective-permute-start.60 = (f32[226,128]{1,0:T(8,128)S(1)}, f32[226,128]{1,0:T(8,128)S(1)}, u32[]{:S(2)}, u32[]{:S(2)}) collective-permute-start(f32[226,128]{1,0:T(8,128)S(1)} %fusion.71), channel_id=1, source_target_pairs={{0,4},{1,9},{2,6},{3,11},{4,0},{5,13},{6,2},{7,15},{8,12},{9,1},{1... | collective-permute-start | bytes 347144 | tf_op jit(solution)/shard_map/ppermute | solution.py:38
  340.0 8.5 %collective-permute-start.61 = (f32[226,128]{1,0:T(8,128)S(1)}, f32[226,128]{1,0:T(8,128)S(1)}, u32[]{:S(2)}, u32[]{:S(2)}) collective-permute-start(f32[226,128]{1,0:T(8,128)S(1)} %add.585), channel_id=1, source_target_pairs={{0,16},{1,17},{2,18},{3,19},{4,20},{5,21},{6,22},{7,23},{8,24},{9,... | collective-permute-start | bytes 347144 | tf_op jit(solution)/shard_map/ppermute | solution.py:38
  340.6 9.2 %collective-permute-start.57 = (bf16[1,48,1024]{2,1,0:T(8,128)(2,1)S(1)}, bf16[1,48,1024]{2,1,0:T(8,128)(2,1)S(1)}, u32[]{:S(2)}, u32[]{:S(2)}) collective-permute-start(bf16[1,48,1024]{2,1,0:T(8,128)(2,1)S(1)} %slice.454), channel_id=1, source_target_pairs={{0,16},{1,17},{2,18},{3,19},{4,20},{5,21},{6,22},{7,23},{8,24},{9,... | collective-permute-start | bytes 294920 | tf_op jit(solution)/shard_map/ppermute | solution.py:38
  348.6 2.0 collective-permute-start.62
  350.5 12.5 %collective-permute-start.58 = (f32[48,1024]{1,0:T(8,128)}, f32[48,1024]{1,0:T(8,128)}, u32[]{:S(2)}, u32[]{:S(2)}) collective-permute-start(f32[48,1024]{1,0:T(8,128)} %add_bitcast_fusion), channel_id=1, source_target_pairs={{0,1},{1,0},{2,3},{3,2},{4,5},{5,4},{6,7},{7,6},{8,9},{9,8},{10,11... | collective-permute-start | bytes 589832 | tf_op jit(solution)/shard_map/ppermute | solution.py:30
  (84 other events, 555.7 us)

commit v5 on v4

--- a/solution.py
+++ b/solution.py
@@ -184,8 +184,9 @@
 ROWS = 256
 LONG_ROWS = 512
 PAIR = 2 * HEAD
-vmem_bytes = 12 * 1024 * 1024
-gradient_bytes = 20 * 1024 * 1024
+vmem_bytes = 16 * 1024 * 1024
+gradient_bytes = 24 * 1024 * 1024
+project_bytes = 32 * 1024 * 1024
 
 
 def dot32(left, right, dims=NN):
@@ -288,8 +289,16 @@
 
 def attend_back_kernel(
     qa_ref, kr_ref, v_ref, o_ref, mine_ref, other_ref, weight_ref, cos_ref, sin_ref, bias_ref,
-    dq_ref, dk_ref, dv_ref, doa_ref, dka_ref, dva_ref,
+    dq_ref, dk_ref, dv_ref, *rest,
 ):
+    doa_ref, dka_ref, dva_ref = rest[-3:]
+    if len(rest) > 3:
+
+        @pl.when(pl.program_id(0) == 0)
+        def _():
+            rest[0][...] = mine_ref[...].T
+            rest[1][...] = other_ref[...].T
+
     lane = lax.broadcasted_iota(jnp.int32, (LEN, PAIR), 1)
     lane_rows = lax.broadcasted_iota(jnp.int32, (ROWS, PAIR), 1)
     cosine, sine = cos_ref[...], sin_ref[...]
@@ -347,6 +356,7 @@
 def attend_backward(side, queries, keys, values, outputs, grad_mine, grad_other, stacked, cosine, sine, bias):
     width = values.shape[1] // 2
     pairs = width // PAIR
+    turned = grad_mine.shape[::-1]
     tall = lambda columns: pl.BlockSpec((LEN, columns), lambda pair: (0, pair + side * pairs))
     whole = lambda shape: pl.BlockSpec(shape, lambda pair: (0, 0))
     return pl.pallas_call(
@@ -357,8 +367,9 @@
         + [whole(grad_mine.shape)] * 2
         + [pl.BlockSpec((1, D, PAIR), lambda pair: (3, 0, pair + side * pairs))]
         + [whole((LEN, PAIR))] * 3,
-        out_specs=[pl.BlockSpec((LEN, PAIR), lambda pair: (0, pair))] * 3,
-        out_shape=[jax.ShapeDtypeStruct((LEN, width), bf16)] * 3,
+        out_specs=[pl.BlockSpec((LEN, PAIR), lambda pair: (0, pair))] * 3 + [whole(turned)] * (2 - 2 * side),
+        out_shape=[jax.ShapeDtypeStruct((LEN, width), bf16)] * 3
+        + [jax.ShapeDtypeStruct(turned, bf16)] * (2 - 2 * side),
         scratch_shapes=[
             pltpu.VMEM((LEN, 2 * PAIR), bf16),
             pltpu.VMEM((LEN, 2 * PAIR), f32),
@@ -387,31 +398,24 @@
 
 def project_kernel(panel_rows, cuts, slots_ref, *refs):
     parts, refs = refs[: 4 * PARTS], refs[4 * PARTS :]
-    mine_ref, other_ref, cos_ref, sin_ref, q_ref, k_ref, v_ref, out_ref, held, in_sems, out_sem = refs
+    mine_ref, other_ref, cos_ref, sin_ref, q_ref, k_ref, v_ref, out_ref = refs
     per_block = D // panel_rows
 
     def fetch(panel, carry):
-        group = jnp.minimum(panel // per_block, 3)
-
         def copy(number, lead, start, rows):
-            pltpu.make_async_copy(
-                parts[number].at[lead], held.at[pl.ds(start, rows)], in_sems.at[group]
-            ).start()
+            out_ref[pl.ds(start, rows), :] = parts[number][lead]
 
         part_copies(slots_ref, 8 * per_block, panel, cuts, panel * panel_rows, copy)
         return carry
 
     lax.fori_loop(0, 8 * per_block, fetch, 0)
     half = mine_ref.shape[0]
-    width = held.shape[1]
+    width = out_ref.shape[1]
     lane = lax.broadcasted_iota(jnp.int32, (half, PAIR), 1)
     for block, ref in enumerate((q_ref, k_ref, v_ref)):
-        place = pl.ds(block * D, D)
-        pltpu.make_async_copy(held.at[place], held.at[place], in_sems.at[block]).wait()
-        pltpu.make_async_copy(held.at[place], out_ref.at[place], out_sem).start()
         for part, rows_ref in enumerate((mine_ref, other_ref)):
             rows = slice(part * half, (part + 1) * half)
-            product = dot32(rows_ref[...], held[block * D : (block + 1) * D])
+            product = dot32(rows_ref[...], out_ref[block * D : (block + 1) * D, :])
             if block == 2:
                 ref[rows, :] = product.astype(bf16)
                 continue
@@ -422,29 +426,19 @@
                 if block == 0:
                     turned = (turned.astype(f32) * 0.125).astype(bf16)
                 ref[rows, columns] = turned
-    place = pl.ds(3 * D, 5 * D)
-    pltpu.make_async_copy(held.at[place], held.at[place], in_sems.at[3]).wait()
-    pltpu.make_async_copy(held.at[place], out_ref.at[place], out_sem).start()
-    pltpu.make_async_copy(held, out_ref, out_sem).wait()
 
 
 def project(groups, slots, panel_rows, cuts, mine, other, cosine, sine):
     width = groups[0][0].shape[-1]
     parts = [array.reshape((-1,) + array.shape[-2:]) for group in groups for array in group]
     whole = pl.BlockSpec(memory_space=pltpu.VMEM)
-    anywhere = pl.BlockSpec(memory_space=pl.ANY)
     tall = jax.ShapeDtypeStruct((LEN, width), bf16)
     return pl.pallas_call(
         lambda *refs: project_kernel(panel_rows, cuts, *refs),
-        in_specs=[pl.BlockSpec(memory_space=pltpu.SMEM)] + [anywhere] * (4 * PARTS) + [whole] * 4,
-        out_specs=[whole] * 3 + [anywhere],
+        in_specs=[pl.BlockSpec(memory_space=pltpu.SMEM)] + [whole] * (4 * PARTS + 4),
+        out_specs=[whole] * 4,
         out_shape=[tall] * 3 + [jax.ShapeDtypeStruct((8 * D, width), bf16)],
-        scratch_shapes=[
-            pltpu.VMEM((8 * D, width), bf16),
-            pltpu.SemaphoreType.DMA((4,)),
-            pltpu.SemaphoreType.DMA,
-        ],
-        compiler_params=pltpu.CompilerParams(vmem_limit_bytes=vmem_bytes),
+        compiler_params=pltpu.CompilerParams(vmem_limit_bytes=project_bytes),
         cost_estimate=pl.CostEstimate(
             flops=2 * LEN * 3 * D * width, bytes_accessed=48 * D * width, transcendentals=0
         ),
@@ -452,9 +446,11 @@
     )(slots, *parts, mine, other, cosine, sine)
 
 
-def feed_kernel(n_ref, g_ref, w_ref, f_ref, d_ref, a_ref, u_ref):
+def feed_kernel(n_ref, g_ref, w_ref, f_ref, d_ref, a_ref, u_ref, n_t_ref, g_t_ref):
     width = w_ref.shape[2]
     rows, grads = n_ref[...], g_ref[...]
+    n_t_ref[...] = rows.T
+    g_t_ref[...] = grads.T
     pre = [dot32(rows, w_ref[i]) for i in range(2)]
     act_grad = [dot32(grads, w_ref[2 + i]) for i in range(2)]
     acts, pre_grads = [], []
@@ -482,8 +478,8 @@
         feed_kernel,
         grid=(1,),
         in_specs=[whole, whole, pl.BlockSpec((4, D, width), lambda step: (1, 0, 0))],
-        out_specs=[whole] * 4,
-        out_shape=[sums, sums, low, low],
+        out_specs=[whole] * 4 + [pl.BlockSpec((D, half), lambda step: (0, 0))] * 2,
+        out_shape=[sums, sums, low, low] + [jax.ShapeDtypeStruct((D, half), bf16)] * 2,
         compiler_params=pltpu.CompilerParams(vmem_limit_bytes=vmem_bytes),
         cost_estimate=pl.CostEstimate(
             flops=2 * 4 * half * D * D, bytes_accessed=16 * D * width, transcendentals=half * D
@@ -527,12 +523,10 @@
 def gradients_kernel(panel_rows, cuts, lefts, rights, uses, slots_ref, *refs):
     in_count = 1 + max(max(max(pair) for pair in lefts), max(max(pair) for group in rights for _, pair in group))
     inputs, refs = refs[:in_count], refs[in_count:]
-    parts, (block_ref, out_sems) = refs[: 2 * PARTS], refs[2 * PARTS :]
-    tall, side = block_ref.shape[2:]
+    parts, (block_ref,) = refs[: 2 * PARTS], refs[2 * PARTS :]
+    tall, side = block_ref.shape[1:]
     half = LEN // 2
     pieces = tall // panel_rows
-    step = 0
-    drained = {}
 
     def rows_of(pair, part, columns):
         if pair[0] == pair[1]:
@@ -541,42 +535,28 @@
 
     for left, right, blocks in uses:
         for left_start in range(0, D, tall):
-            place = step % 2
-            for number in drained.get(place, ()):
-                pltpu.make_async_copy(
-                    block_ref.at[place, number], block_ref.at[place, number], out_sems.at[place]
-                ).wait()
             product = None
             for part in range(2):
                 columns = [rows_of(pair, part, slice(start, start + side)) for start, pair in rights[right]]
                 wide = columns[0] if len(columns) == 1 else jnp.concatenate(columns, axis=1)
-                term = dot32(rows_of(lefts[left], part, slice(left_start, left_start + tall)), wide, TN)
+                term = dot32(inputs[lefts[left][part]][left_start : left_start + tall, :], wide)
                 product = term if product is None else product + term
-            for number, block in enumerate(blocks):
-                block_ref[place, number] = product[:, number * side : (number + 1) * side].astype(bf16)
-
-            def send(piece, carry, place=place, left_start=left_start, blocks=blocks):
-                for number, block in enumerate(blocks):
+            places = [(block * D + left_start) // tall for block in blocks]
+            for number, place in enumerate(places):
+                block_ref[place] = product[:, number * side : (number + 1) * side].astype(bf16)
+
+            def send(piece, carry, places=places):
+                for place in places:
 
                     def copy(array, lead, start, rows):
-                        pltpu.make_async_copy(
-                            block_ref.at[place, number, pl.ds(start, rows)],
-                            parts[array].at[lead],
-                            out_sems.at[place],
-                        ).start()
-
-                    panel = (block * D + left_start) // panel_rows + piece
-                    part_copies(slots_ref, 8 * D // panel_rows, panel, cuts, piece * panel_rows, copy, 2)
+                        parts[array][lead] = block_ref[place, pl.ds(start, rows), :]
+
+                    part_copies(
+                        slots_ref, 8 * D // panel_rows, place * pieces + piece, cuts, piece * panel_rows, copy, 2
+                    )
                 return carry
 
             lax.fori_loop(0, pieces, send, 0)
-            drained[place] = range(len(blocks))
-            step += 1
-    for place, numbers in drained.items():
-        for number in numbers:
-            pltpu.make_async_copy(
-                block_ref.at[place, number], block_ref.at[place, number], out_sems.at[place]
-            ).wait()
 
 
 def panel_gradients(arrays, lefts, rights, uses, slots, panel_rows, cuts, high_count, width):
@@ -590,9 +570,9 @@
         lambda *refs: gradients_kernel(panel_rows, cuts, lefts, rights, uses, *refs),
         in_specs=[pl.BlockSpec(memory_space=pltpu.SMEM)]
         + [pl.BlockSpec(memory_space=pltpu.VMEM)] * len(arrays),
-        out_specs=[pl.BlockSpec(memory_space=pl.ANY)] * (2 * PARTS),
+        out_specs=[pl.BlockSpec(memory_space=pltpu.VMEM)] * (2 * PARTS),
         out_shape=outs,
-        scratch_shapes=[pltpu.VMEM((2, 2, tall, width), bf16), pltpu.SemaphoreType.DMA((2,))],
+        scratch_shapes=[pltpu.VMEM((8 * D // tall, tall, width), bf16)],
         compiler_params=pltpu.CompilerParams(vmem_limit_bytes=gradient_bytes),
         cost_estimate=beside,
         name="gradients",
@@ -624,25 +604,25 @@
 def text_forward_kernel(
     core_ref, table_ref, mine_ref, other_ref, normed_ref, masked_ref, keep_ref, mel_mine_ref, mel_other_ref,
     in_bias_ref, gamma_ref, beta_ref, bias_ref, shift_ref, scale_ref,
-    pre_ref, energy_ref, grn_ref, text_ref, stream_ref, first_ref, other_first_ref, texts_ref, hidden_held, held, sem, out_sem,
+    pre_ref, energy_ref, grn_ref, text_ref, stream_ref, first_ref, other_first_ref, first_t_ref, other_first_t_ref, texts_ref,
+    hidden_held,
 ):
     rows = mine_ref.shape[1]
     half = stream_ref.shape[0]
 
+    held = texts_ref
+
     def fetch(block, carry):
-        place = held.at[pl.ds(pl.multiple_of(block * rows, 16), rows)]
+        place = pl.ds(pl.multiple_of(block * rows, 16), rows)
         for part, ref in enumerate((mine_ref, other_ref)):
 
             @pl.when((block + core_ref[0]) % 2 == part)
             def _():
-                pltpu.make_async_copy(ref.at[table_ref[block]], place, sem).start()
+                texts_ref[place, :] = ref[table_ref[block]]
 
         return carry
 
     lax.fori_loop(0, table_ref.shape[0], fetch, 0)
-    pltpu.make_async_copy(held, held, sem).wait()
-    out = pltpu.make_async_copy(held, texts_ref, out_sem)
-    out.start()
     energy_sum = jnp.zeros((1, TXT_FF), f32)
     for part in range(2):
         frames = slice(part * half, (part + 1) * half)
@@ -669,13 +649,14 @@
             text_ref[...] = text_low
             stream_ref[...] = stream
             first_ref[...] = first
+            first_t_ref[...] = first.T
         else:
             other_first_ref[...] = first
-    out.wait()
+            other_first_t_ref[...] = first.T
 
 
 def text_forward(core, table, *inputs):
-    whole, anywhere = pl.BlockSpec(memory_space=pltpu.VMEM), pl.BlockSpec(memory_space=pl.ANY)
+    whole = pl.BlockSpec(memory_space=pltpu.VMEM)
     scalars = pl.BlockSpec(memory_space=pltpu.SMEM)
     half = LEN // 2
     return in_vmem(
@@ -690,22 +671,19 @@
             ((half, D), f32),
             ((half, D), bf16),
             ((half, D), bf16),
+            ((D, half), bf16),
+            ((D, half), bf16),
             ((3 * TEXT, D), bf16),
         ],
-        [
-            pltpu.VMEM((LEN, TXT_FF), f32),
-            pltpu.VMEM((3 * TEXT, D), bf16),
-            pltpu.SemaphoreType.DMA,
-            pltpu.SemaphoreType.DMA,
-        ],
-        [scalars, scalars, anywhere, anywhere] + [whole] * (len(inputs) - 2),
-        [whole] * 7 + [anywhere],
+        [pltpu.VMEM((LEN, TXT_FF), f32)],
+        [scalars, scalars] + [whole] * len(inputs),
+        [whole] * 10,
     )
 
 
 def stream_back_kernel(
     core_ref, my_ref, their_ref, stream_ref, later_ref, scale_ref, texts_ref, keep_ref, pre_ref,
-    mel_ref, low_ref, shrink_ref, shrink_low_ref, grn_grad_ref, sums_ref, bias_sum_ref, full_ref, sem,
+    mel_ref, low_ref, shrink_ref, shrink_low_ref, grn_grad_ref, sums_ref, bias_sum_ref, full_ref,
 ):
     half = mel_ref.shape[0]
     grad = my_ref[...] + their_ref[...].astype(f32)
@@ -715,8 +693,7 @@
     mel_grad = later_ref[...] + normalise_back(grad * (1.0 + scale_ref[...]), normed, scale)
     mel_ref[...] = mel_grad
     place = pl.ds(pl.multiple_of(core_ref[0] * half, half), half)
-    out = pltpu.make_async_copy(mel_ref, full_ref.at[place], sem)
-    out.start()
+    full_ref[place, :] = mel_ref[...]
     low = mel_grad.astype(bf16)
     low_ref[...] = low
     shrink_grad = dot32(low, texts_ref[2 * TEXT :], NT) * keep_ref[...]
@@ -730,7 +707,6 @@
     sums_ref[2:3] = jnp.sum(grn_grad * (pre * gelu_parts(pre)[0]), axis=0, keepdims=True)
     sums_ref[3:4] = jnp.sum(grn_grad, axis=0, keepdims=True)
     sums_ref[4:8] = jnp.zeros((4, D), f32)
-    out.wait()
 
 
 def stream_back(core, *inputs):
@@ -750,9 +726,9 @@
             ((1, TEXT), f32),
             ((2 * half, D), f32),
         ],
-        [pltpu.SemaphoreType.DMA],
+        [],
         [pl.BlockSpec(memory_space=pltpu.SMEM)] + [whole] * len(inputs),
-        [whole] * 7 + [pl.BlockSpec(memory_space=pl.ANY)],
+        [whole] * 8,
     )
 
 
@@ -786,26 +762,25 @@
     mixed_ref[...] = mixed_grad
     if len(rest) == 1:
         return
-    keep_ref, send_ref, _, sem = rest
+    keep_ref, send_ref, _ = rest
     rows = keep_ref.shape[1]
 
     def place(block, carry):
-        piece = grads_ref.at[pl.ds(pl.multiple_of(block * rows, 16), rows)]
+        piece = pl.ds(pl.multiple_of(block * rows, 16), rows)
         for part, ref in enumerate((keep_ref, send_ref)):
 
             @pl.when((block + core_ref[0]) % 2 == part)
             def _():
-                pltpu.make_async_copy(piece, ref.at[table_ref[block]], sem).start()
+                ref[table_ref[block]] = grads_ref[piece, :]
 
         return carry
 
     lax.fori_loop(0, table_ref.shape[0], place, 0)
-    pltpu.make_async_copy(grads_ref, grads_ref, sem).wait()
 
 
 def text_back(core, table, rows, *inputs):
     half = inputs[0].shape[0]
-    whole, anywhere = pl.BlockSpec(memory_space=pltpu.VMEM), pl.BlockSpec(memory_space=pl.ANY)
+    whole = pl.BlockSpec(memory_space=pltpu.VMEM)
     scalars = pl.BlockSpec(memory_space=pltpu.SMEM)
     outs = [((half, TEXT), f32), ((3, TEXT), f32), ((2, TXT_FF), f32)]
     apart = rows % 16 == 0
@@ -815,15 +790,15 @@
         "text_back",
         inputs + (core.reshape(1).astype(jnp.int32), table),
         outs + ([blocks] * 2 if apart else [((3 * TEXT, D), bf16)]),
-        [pltpu.VMEM((3 * TEXT, D), bf16), pltpu.SemaphoreType.DMA] if apart else [],
+        [pltpu.VMEM((3 * TEXT, D), bf16)] if apart else [],
         [whole] * len(inputs) + [scalars] * 2,
-        [whole] * 3 + ([anywhere] * 2 if apart else [whole]),
+        [whole] * (5 if apart else 4),
     )
 
 
 def conv_back_kernel(
     core_ref, mixed_ref, border_ref, window_ref, kernel_ref, shrink_ref, keep_ref,
-    mine_ref, kernel_grad_ref, full_ref, wide, sem,
+    mine_ref, kernel_grad_ref, full_ref, wide,
 ):
     half = mixed_ref.shape[0]
     edge, margin = border_ref.shape[0], KERNEL // 2
@@ -840,37 +815,34 @@
         kernel_grad_ref[j : j + 1] = jnp.sum(mixed * tap, axis=0, keepdims=True)
     mine_ref[...] = total * keep_ref[...]
     place = pl.ds(pl.multiple_of(core_ref[0] * half, half), half)
-    out = pltpu.make_async_copy(mine_ref, full_ref.at[place], sem)
-    out.start()
-    out.wait()
+    full_ref[place, :] = mine_ref[...]
 
 
 def conv_back(core, *inputs):
     half = inputs[0].shape[0]
-    whole, anywhere = pl.BlockSpec(memory_space=pltpu.VMEM), pl.BlockSpec(memory_space=pl.ANY)
+    whole = pl.BlockSpec(memory_space=pltpu.VMEM)
     return in_vmem(
         conv_back_kernel,
         "conv_back",
         (core.reshape(1).astype(jnp.int32),) + inputs,
         [((half, TEXT), f32), ((KERNEL, TEXT), f32), ((2 * half, TEXT), f32)],
-        [pltpu.VMEM((half + 2 * inputs[1].shape[0], TEXT), f32), pltpu.SemaphoreType.DMA],
+        [pltpu.VMEM((half + 2 * inputs[1].shape[0], TEXT), f32)],
         [pl.BlockSpec(memory_space=pltpu.SMEM)] + [whole] * len(inputs),
-        [whole] * 2 + [anywhere],
+        [whole] * 3,
     )
 
 
 def settle_kernel(
     core_ref, my_out_ref, their_out_ref, my_grad_ref, their_grad_ref, stream_ref, attention_ref, cot_ref,
     gate_one_ref, scale_ref, gate_two_ref,
-    output_ref, later_ref, attention_grad_ref, sums_ref, full_ref, sem,
+    output_ref, later_ref, attention_grad_ref, sums_ref, full_ref,
 ):
     half = output_ref.shape[0]
     unit_out = my_out_ref[...] + their_out_ref[...].astype(f32)
     stream = stream_ref[...]
     output_ref[...] = (stream + gate_two_ref[...] * unit_out).astype(bf16)
     place = pl.ds(pl.multiple_of(core_ref[0] * half, half), half)
-    out = pltpu.make_async_copy(output_ref, full_ref.at[place], sem)
-    out.start()
+    full_ref[place, :] = output_ref[...]
     out_grad = cot_ref[...].astype(f32)
     sums_ref[0:1] = jnp.sum(out_grad * unit_out, axis=0, keepdims=True)
     grad = my_grad_ref[...] + their_grad_ref[...].astype(f32)
@@ -881,20 +853,19 @@
     later_ref[...] = later
     sums_ref[3:4] = jnp.sum(later * attention_ref[...], axis=0, keepdims=True)
     attention_grad_ref[...] = (gate_one_ref[...] * later).astype(bf16)
-    out.wait()
 
 
 def settle(core, *inputs):
     half = inputs[0].shape[0]
-    whole, anywhere = pl.BlockSpec(memory_space=pltpu.VMEM), pl.BlockSpec(memory_space=pl.ANY)
+    whole = pl.BlockSpec(memory_space=pltpu.VMEM)
     return in_vmem(
         settle_kernel,
         "settle",
         (core.reshape(1).astype(jnp.int32),) + inputs,
         [((half, D), bf16), ((half, D), f32), ((half, D), bf16), ((4, D), f32), ((2 * half, D), bf16)],
-        [pltpu.SemaphoreType.DMA],
+        [],
         [pl.BlockSpec(memory_space=pltpu.SMEM)] + [whole] * len(inputs),
-        [whole] * 4 + [anywhere],
+        [whole] * 5,
     )
 
 
@@ -1173,7 +1144,7 @@
     shift_one, scale_one, gate_one, shift_two, scale_two, gate_two = (
         modulation_row[:, i * D : (i + 1) * D] for i in range(6)
     )
-    expand_pre, energy_sum, grn_low, text_low, stream, first_mine, first_other, texts = text_forward(
+    expand_pre, energy_sum, grn_low, text_low, stream, first_mine, first_other, first_t, first_other_t, texts = text_forward(
         core,
         text_table,
         text_mine,
@@ -1210,9 +1181,9 @@
     normed_two, _ = normalise(stream_one)
     second_mine = (normed_two * (1.0 + scale_two) + shift_two).astype(bf16)
     second_other = swap_core(second_mine)
-    their_out, their_grad, act_other, pre_other = feed(second_other, hidden_other, stacked, bf16)
+    their_out, their_grad, act_other, pre_other, second_other_t, hidden_other_t = feed(second_other, hidden_other, stacked, bf16)
     their_out, their_grad = swap_core(their_out), swap_core(their_grad)
-    my_out, my_grad, act_mine, pre_mine = feed(second_mine, hidden_mine, stacked, f32)
+    my_out, my_grad, act_mine, pre_mine, second_t, hidden_t = feed(second_mine, hidden_mine, stacked, f32)
     output_mine, stream_one_grad, attention_mine, settle_sums, block_output = settle(
         core,
         my_out,
@@ -1241,8 +1212,8 @@
         column = side * narrow
         return panel_gradients(
             [
-                first_mine, first_other, attention_mine, attention_other, second_mine, second_other,
-                hidden_mine, hidden_other, *head_grads, attended, pre_mine, pre_other, act_mine, act_other,
+                first_t, first_other_t, attention_t, attention_other_t, second_t, second_other_t,
+                hidden_t, hidden_other_t, *head_grads, attended, pre_mine, pre_other, act_mine, act_other,
             ],
             [(0, 1), (2, 3), (4, 5), (6, 7)],
             [
@@ -1260,7 +1231,7 @@
             narrow,
         )
 
-    head_grads = list(back(0, query_aug))
+    *head_grads, attention_t, attention_other_t = back(0, query_aug)
     keep_a, send_a = weight_gradients(0, head_grads)
     send_a, (query_aug,) = tie_lists(send_a, (query_aug,))
     received_a = receive(send_a, 2)
@@ -1387,7 +1358,12 @@
             else:
                 arrays = [fold_high(part[:high_count].astype(f32) + other.astype(f32))]
             panel_pieces.append((cuts[index], side * narrow, arrays))
-    text_received, small_received = tie(text_received, small_received)
+    soap_weights, soap_moment, soap_variance = rotated_step(
+        panel_pieces, utterances, left_basis, right_basis, soap_master, soap_first, soap_second
+    )
+    text_received, small_received, soap_weights, soap_moment, soap_variance = tie(
+        text_received, small_received, soap_weights, soap_moment, soap_variance
+    )
     text_part = add_low(text_part[0], text_received)
     small = small + small_received
     text_part = fold(text_part, text_orders, 0)
@@ -1407,9 +1383,6 @@
     vector_gradient = jnp.concatenate([vector_sum, jnp.sum(modulation_grad, axis=0)]) / utterances
 
     own_text = own_text / utterances
-    soap_weights, soap_moment, soap_variance = rotated_step(
-        panel_pieces, utterances, left_basis, right_basis, soap_master, soap_first, soap_second
-    )
     text_moment, text_variance, text_direction = moments(own_text, text_first, text_second)
     text_weights = apply_step(text_matrices, text_direction, learn_rate)
     modulation_weights, modulation_moment, modulation_variance = modulation_step(

time: 373 us -> 366 us (0.981)
  Pallas kernels: 130 us -> 118 us
    pallas_call x2, Pallas kernels: 26 us -> 17.4 us  [panel_gradients(): pl.pallas_call(lambda *refs: gradients_kernel(panel_rows, cuts, lefts, ri...]
    unnamed x184 -> x218, local copies, waits for them, and re-layouts: 25.6 us -> 28.3 us
  transfers between devices with their start and end apart: 63 -> 63, of which waited for: 27 -> 27; matrix products, arithmetic and copies ran while one was open for 12% -> 13% of each run, Pallas kernels for 19% -> 18%
where the time goes in v5:
time: 366 us; the launch traced here: 359 us
  Pallas kernels  118 us (32%)
  waiting for transfers between devices  83.9 us (23%)
  starting transfers between devices  66.7 us (18%)
  local copies, waits for them, and re-layouts  47.2 us (13%)
  other arithmetic  35.8 us (10%)
  between operations  3.94 us (1%)
    ppermute x46, waiting for transfers between devices, swap_bits(): return lax.ppermute(array, ('dp', 'mp'), pairs)  72 us
    ppermute x46, starting transfers between devices, swap_bits(): return lax.ppermute(array, ('dp', 'mp'), pairs)  64.9 us
    pallas_call x6, Pallas kernels, in_vmem(): pl.pallas_call(kernel, in_specs=specs or [whole] * len(inputs), out_specs...  32 us
    pallas_call x2, Pallas kernels, attend_backward(): pl.pallas_call(attend_back_kernel, grid=(pairs,), in_specs=[tall(2 * PAIR...  28.4 us
    unnamed x218, local copies, waits for them, and re-layouts  28.3 us
    pallas_call x2, Pallas kernels, panel_gradients(): pl.pallas_call(lambda *refs: gradients_kernel(panel_rows, cuts, lefts, ri...  17.4 us
    pallas_call x1, Pallas kernels, attend_forward(): pl.pallas_call(attend_kernel, grid=(pairs,), in_specs=[tall(PAIR), tall(P...  13.3 us
    ppermute x17, waiting for transfers between devices, swap_core(): return lax.ppermute(array, 'mp', [(0, 1), (1, 0)])  11.9 us
  transfers between devices with their start and end apart: 63, of which 27 were waited for; matrix products, arithmetic and copies ran while one was open for 13% of the time, Pallas kernels for 18%

profile of v5, /device:TPU:0, one launch (start us, length us, event | category | flops | bytes accessed | tf_op | source)
XLA Modules:
  0.0 359.0 jit_solution(16930900056029425303)
XLA Ops:
  1.6 4.1 %collective-permute-start = (bf16[1,48,1024]{2,1,0:T(8,128)(2,1)S(1)}, bf16[1,48,1024]{2,1,0:T(8,128)(2,1)S(1)}, u32[]{:S(2)}, u32[]{:S(2)}) collective-permute-start(bf16[1,48,1024]{2,1,0:T(8,128)(2,1)S(1)} %fusion.38), channel_id=1, source_target_pairs={{0,16},{1,17},{2,18},{3,19},{4,20},{5,21},{6,22},{7,23},{8,24},{9,... | collective-permute-start | bytes 294920 | tf_op jit(solution)/shard_map/ppermute | solution.py:38
  10.6 4.5 %collective-permute-done.1 = f32[8,3072]{1,0:T(8,128)S(1)} collective-permute-done((f32[8,3072]{1,0:T(8,128)S(1)}, f32[8,3072]{1,0:T(8,128)S(1)}, u32[]{:S(2)}, u32[]{:S(2)}) %collective-permute-start.1) | collective-permute-done | bytes 98336 | tf_op jit(solution)/shard_map/ppermute | solution.py:38
  15.8 1.7 collective-permute-start.3
  17.4 5.4 %collective-permute-done.3 = f32[8,3072]{1,0:T(8,128)S(1)} collective-permute-done((f32[8,3072]{1,0:T(8,128)S(1)}, f32[8,3072]{1,0:T(8,128)S(1)}, u32[]{:S(2)}, u32[]{:S(2)}) %collective-permute-start.3) | collective-permute-done | bytes 98336 | tf_op jit(solution)/shard_map/ppermute | solution.py:38
  25.8 1.8 collective-permute-start.5
  27.6 3.4 collective-permute-start.8
  31.6 1.6 collective-permute-start.7
  33.2 3.2 collective-permute-done.7
  36.4 1.8 collective-permute-done.8
  42.6 1.6 collective-permute-start.13
  44.3 1.6 collective-permute-start.10
  45.9 1.7 collective-permute-start.16
  48.8 2.3 fusion.60
  51.1 5.9 %collective-permute-done.16 = bf16[1,176,512]{2,1,0:T(8,128)(2,1)} collective-permute-done((bf16[1,176,512]{2,1,0:T(8,128)(2,1)}, bf16[1,176,512]{2,1,0:T(8,128)(2,1)}, u32[]{:S(2)}, u32[]{:S(2)}) %collective-permute-start.16) | collective-permute-done | bytes 180256 | tf_op jit(solution)/shard_map/ppermute | solution.py:38
  59.6 1.5 collective-permute-start.17
  64.4 2.5 collective-permute-start.18
  68.0 1.6 collective-permute-start.19
  71.2 6.9 %collective-permute-done.14 = bf16[1,336,512]{2,1,0:T(8,128)(2,1)S(1)} collective-permute-done((bf16[1,336,512]{2,1,0:T(8,128)(2,1)}, bf16[1,336,512]{2,1,0:T(8,128)(2,1)S(1)}, u32[]{:S(2)}, u32[]{:S(2)}) %collective-permute-start.14) | collective-permute-done | bytes 344096 | tf_op jit(solution)/shard_map/ppermute | solution.py:38
  85.7 7.4 %collective-permute-done.15 = bf16[2,1,336,512]{3,2,0,1:T(8,128)(2,1)S(1)} collective-permute-done((bf16[2,1,336,512]{3,2,0,1:T(8,128)(2,1)S(1)}, bf16[2,1,336,512]{3,2,0,1:T(8,128)(2,1)S(1)}, u32[]{:S(2)}, u32[]{:S(2)}) %collective-permute-start.15) | collective-permute-done | bytes 688160 | tf_op jit(solution)/shard_map/ppermute | solution.py:38
  99.1 1.9 constant_dynamic-slice_fusion.2
  102.9 7.5 %text_forward.1 = (f32[512,1024]{1,0:T(8,128)S(1)}, f32[1,1024]{1,0:T(1,128)S(1)}, bf16[512,1024]{1,0:T(8,128)(2,1)S(1)}, bf16[512,512]{1,0:T(8,128)(2,1)S(1)}, ...) custom-call(s32[1]{0:T(128)} %bitcast.core_ref, ...), custom_call_target="tpu_custom_call" | custom-call | flops 1000 | bytes 1000 | tf_op jit(solution)/shard_map/text_forward/pallas_call | solution.py:592
  113.6 2.0 multiply_convert_fusion.1
  118.6 9.8 %project.1 = (bf16[1024,512]{1,0:T(8,128)(2,1)S(1)}, bf16[1024,512]{1,0:T(8,128)(2,1)S(1)}, bf16[1024,512]{1,0:T(8,128)(2,1)S(1)}, bf16[8192,512]{1,0:T(8,128)(2,1)}) custom-call(s32[64]{0:T(128)S(1)} %pad_add_fusion.1.refs_0_, bf16[4,336,512]{2,1,0:T(8,128)(2,1)S(1)} %bitcast.214, bf16[4,176,512]{2,1,0:T(8,128)(2,1)S(1)} %bitcast.217, ...), custom_call_target="tpu_custom_call" | custom-call | flops 3221225472 | bytes 25165824 | tf_op jit(solution)/shard_map/project/pallas_call | solution.py:436
  128.6 13.3 %attend.1 = (bf16[1024,512]{1,0:T(8,128)(2,1)S(1)}, bf16[1024,1024]{1,0:T(8,128)(2,1)S(1)}) custom-call(bf16[1024,512]{1,0:T(8,128)(2,1)S(1)} %get-tuple-element.210.q_ref, bf16[1024,512]{1,0:T(8,128)(2,1)S(1)} %get-tuple-element.211.k_ref.kr_ref, bf16[1024,512]{1,0:T(8,128)(2,1)S(1)} %get-tuple-element.212.v_ref, ...), custom_call_target="tpu_custom_call" | custom-call | flops 17179869184 | bytes 6291456 | tf_op jit(solution)/shard_map/attend/pallas_call | solution.py:271
  142.8 2.6 collective-permute-done.24
  147.3 2.5 collective-permute-done.25.n_ref
  149.9 4.8 %feed.3 = (bf16[512,1024]{1,0:T(8,128)(2,1)S(1)}, bf16[512,1024]{1,0:T(8,128)(2,1)S(1)}, bf16[512,1024]{1,0:T(8,128)(2,1)S(1)}, bf16[512,1024]{1,0:T(8,128)(2,1)...) custom-call(bf16[512,1024]{1,0:T(8,128)(2,1)S(1)} %collective-permute-done.25.n_ref, ...), custom_call_target="tpu_custom_call" | custom-call | flops 4294967296 | bytes 8388608 | tf_op jit(solution)/shard_map/feed/pallas_call | solution.py:477
  155.3 4.8 %feed.2 = (f32[512,1024]{1,0:T(8,128)S(1)}, f32[512,1024]{1,0:T(8,128)S(1)}, bf16[512,1024]{1,0:T(8,128)(2,1)S(1)}, bf16[512,1024]{1,0:T(8,128)(2,1)S(1)}, bf16[...) custom-call(bf16[512,1024]{1,0:T(8,128)(2,1)S(1)} %add_convert_fusion.1.n_ref, bf16[512,1024]{1,0:T(8,128)(2,1)S(1)} %copy-done.51, ...), custom_call_target="tpu_custom_call" | custom-call | flops 4294967296 | bytes 8388608 | tf_op jit(solution)/shard_map/feed/pallas_call | solution.py:477
  162.1 3.7 %settle.1 = (bf16[512,1024]{1,0:T(8,128)(2,1)}, f32[512,1024]{1,0:T(8,128)S(1)}, bf16[512,1024]{1,0:T(8,128)(2,1)S(1)}, f32[4,1024]{1,0:T(4,128)S(1)}, bf16[1024,1024]{1,0:T(8,128)(2,1)}) custom-call(s32[1]{0:T(128)} %bitcast.core_ref, f32[512,1024]{1,0:T(8,128)S(1)} %get-tuple-element.218.my_out_ref, ...), custom_call_target="tpu_custom_call" | custom-call | flops 1000 | bytes 1000 | tf_op jit(solution)/shard_map/settle/pallas_call | solution.py:592
  167.4 2.4 collective-permute-done.28.other_ref
  169.8 14.4 %attend_back.2 = (bf16[1024,256]{1,0:T(8,128)(2,1)S(1)}, bf16[1024,256]{1,0:T(8,128)(2,1)S(1)}, bf16[1024,256]{1,0:T(8,128)(2,1)S(1)}, bf16[1024,512]{1,0:T(8,128)(2,1)S(1)}, bf16[1024,512]{1,0:T(8,128)(2,1)S(1)}) custom-call(bf16[1024,1024]{1,0:T(8,128)(2,1)S(1)} %get-tuple-element.242.qa_ref, bf16[1024,512]{1,0:T(8,128)(2,1)S(1)} %copy-done.23, ...), custom_call_target="tpu_custom_call" | custom-call | flops 1000 | bytes 1000 | tf_op jit(solution)/shard_map/attend_back/pallas_call | solution.py:362
  184.3 8.1 %gradients.2 = (bf16[8,336,256]{2,1,0:T(8,128)(2,1)S(1)}, bf16[8,176,256]{2,1,0:T(8,128)(2,1)S(1)}, bf16[8,336,256]{2,1,0:T(8,128)(2,1)S(1)}, bf16[8,176,256]{2,1,0:T(8,128)(2,1)S(1)}) custom-call(s32[64]{0:T(128)S(1)} %pad_add_fusion.refs_0_, bf16[1024,512]{1,0:T(8,128)(2,1)S(1)} %get-tuple-element.196.refs_1_, ...), custom_call_target="tpu_custom_call" | custom-call | flops 1000 | bytes 1000 | tf_op jit(solution)/shard_map/gradients/pallas_call | solution.py:569
  194.3 13.9 %attend_back.3 = (bf16[1024,256]{1,0:T(8,128)(2,1)S(1)}, bf16[1024,256]{1,0:T(8,128)(2,1)S(1)}, bf16[1024,256]{1,0:T(8,128)(2,1)S(1)}) custom-call(bf16[1024,1024]{1,0:T(8,128)(2,1)S(1)} %get-tuple-element.242.qa_ref, bf16[1024,512]{1,0:T(8,128)(2,1)S(1)} %copy-done.23, bf16[1024,512]{1,0:T(8,128)(2,1)S(1)} %copy-done.25, ...), custom_call_target="tpu_custom_call" | custom-call | flops 1000 | bytes 1000 | tf_op jit(solution)/shard_map/attend_back/pallas_call | solution.py:362
  208.2 3.0 collective-permute-done.30
  214.0 3.4 inputs_grad.1
  217.5 4.7 %collective-permute-done.32 = bf16[2,2,176,256]{3,2,1,0:T(8,128)(2,1)S(1)} collective-permute-done((bf16[2,2,176,256]{3,2,1,0:T(8,128)(2,1)S(1)}, bf16[2,2,176,256]{3,2,1,0:T(8,128)(2,1)S(1)}, u32[]{:S(2)}, u32[]{:S(2)}) %collective-permute-start.32) | collective-permute-done | bytes 360480 | tf_op jit(solution)/shard_map/ppermute | solution.py:38
  226.3 9.3 %gradients.3 = (bf16[8,336,256]{2,1,0:T(8,128)(2,1)S(1)}, bf16[8,176,256]{2,1,0:T(8,128)(2,1)S(1)}, bf16[8,336,256]{2,1,0:T(8,128)(2,1)}, bf16[8,176,256]{2,1,0:T(8,128)(2,1)S(1)}) custom-call(s32[64]{0:T(128)S(1)} %pad_add_fusion.refs_0_, bf16[1024,512]{1,0:T(8,128)(2,1)S(1)} %get-tuple-element.196.refs_1_, ...), custom_call_target="tpu_custom_call" | custom-call | flops 1000 | bytes 1000 | tf_op jit(solution)/shard_map/gradients/pallas_call | solution.py:569
  242.1 2.3 constant_dynamic-update-slice_fusion.9
  244.3 1.9 copy-done.2
  246.2 1.6 copy-done.7
  247.8 1.6 copy-done.36
  249.4 1.6 copy-done.38
  252.2 4.4 %stream_back.1 = (f32[512,1024]{1,0:T(8,128)S(1)}, bf16[512,1024]{1,0:T(8,128)(2,1)S(1)}, f32[512,512]{1,0:T(8,128)S(1)}, bf16[512,512]{1,0:T(8,128)(2,1)S(1)}, ...) custom-call(s32[1]{0:T(128)} %bitcast.core_ref, ...), custom_call_target="tpu_custom_call" | custom-call | flops 1000 | bytes 1000 | tf_op jit(solution)/shard_map/stream_back/pallas_call | solution.py:592
  256.8 2.2 collective-permute-done.37
  259.0 1.8 fusion
  263.1 5.0 %collective-permute-start.40 = (bf16[1,336,256]{2,1,0:T(8,128)(2,1)S(1)}, bf16[1,336,256]{2,1,0:T(8,128)(2,1)S(1)}, u32[]{:S(2)}, u32[]{:S(2)}) collective-permute-start(bf16[1,336,256]{2,1,0:T(8,128)(2,1)S(1)} %get-tuple-element.383), channel_id=1, source_target_pairs={{0,16},{1,17},{2,18},{3,19},{4,20},{5,21},{6,22},{7,23},{8,24},{9,... | collective-permute-start | bytes 516104 | tf_op jit(solution)/shard_map/ppermute | solution.py:38
  269.2 2.3 collective-permute-start.41
  271.6 6.7 %text_back.1 = (f32[512,512]{1,0:T(8,128)S(1)}, f32[3,512]{1,0:T(4,128)S(1)}, f32[2,1024]{1,0:T(2,128)S(1)}, bf16[16,48,1024]{2,1,0:T(8,128)(2,1)S(1)}, bf16[16,48,1024]{2,1,0:T(8,128)(2,1)}) custom-call(f32[512,1024]{1,0:T(8,128)S(1)} %copy-done.8, f32[512,1024]{1,0:T(8,128)S(1)} %get-tuple-element.282.grn_grad_ref, ...), custom_call_target="tpu_custom_call" | custom-call | flops 1000 | bytes 1000 | tf_op jit(solution)/shard_map/text_back/pallas_call | solution.py:592
  281.4 1.7 collective-permute-start.44
  284.8 1.9 collective-permute-done.47.border_ref
  286.7 4.4 %conv_back.1 = (f32[512,512]{1,0:T(8,128)S(1)}, f32[7,512]{1,0:T(8,128)S(1)}, f32[1024,512]{1,0:T(8,128)}) custom-call(s32[1]{0:T(128)} %bitcast.core_ref, f32[512,512]{1,0:T(8,128)S(1)} %get-tuple-element.297.mixed_ref, f32[8,512]{1,0:T(8,128)S(1)} %collective-permute-done.47.border_ref, f32[528,512]{1,0:T(8,128)S(1)} %get-tuple-element.362.window_ref, ...), custom_call_target="tpu_custom_call" | custom-call | flops 1000 | bytes 1000 | tf_op jit(solution)/shard_map/conv_back/pallas_call | solution.py:592
  294.5 2.1 add_convert_fusion
  298.5 1.8 collective-permute-start.48
  303.8 9.4 %collective-permute-done.49 = bf16[1,176,256]{2,1,0:T(8,128)(2,1)S(1)} collective-permute-done((bf16[1,176,256]{2,1,0:T(8,128)(2,1)S(1)}, bf16[1,176,256]{2,1,0:T(8,128)(2,1)S(1)}, u32[]{:S(2)}, u32[]{:S(2)}) %collective-permute-start.49) | collective-permute-done | bytes 90144 | tf_op jit(solution)/shard_map/ppermute | solution.py:38
  313.5 1.8 collective-permute-start.54
  315.6 5.4 %rotated_step.1 = (f32[512,512]{1,0:T(8,128)}, f32[512,512]{1,0:T(8,128)}, f32[512,512]{1,0:T(8,128)}) custom-call(bf16[336,256]{1,0:T(8,128)(2,1)S(1)} %get-tuple-element.382.refs_0_, bf16[336,256]{1,0:T(8,128)(2,1)S(1)} %bitcast.220, bf16[176,256]{1,0:T(8,128)(2,1)S(1)} %get-tuple-element.390.refs_2_, bf16[176,256]{1,0:T(8,128)(2,1)S(1)} %bitcast.222, ...), custom_call_target="tpu_custom_call" | custom-call | flops 1000 | bytes 1000 | tf_op jit(solution)/shard_map/rotated_step/pallas_call | solution.py:592
  322.3 1.8 collective-permute-start.59
  324.2 3.0 collective-permute-done.59
  328.6 3.5 collective-permute-done.60
  332.2 1.9 collective-permute-start.61
  335.3 6.4 %collective-permute-done.61 = f32[226,128]{1,0:T(8,128)S(1)} collective-permute-done((f32[226,128]{1,0:T(8,128)S(1)}, f32[226,128]{1,0:T(8,128)S(1)}, u32[]{:S(2)}, u32[]{:S(2)}) %collective-permute-start.61) | collective-permute-done | bytes 115744 | tf_op jit(solution)/shard_map/ppermute | solution.py:38
  348.6 1.6 multiply_subtract_fusion.1
  351.6 4.4 %modulation_step.1 = (f32[64,6144]{1,0:T(8,128)}, f32[64,6144]{1,0:T(8,128)}, f32[64,6144]{1,0:T(8,128)}) custom-call(bf16[8,64]{1,0:T(8,128)(2,1)S(1)} %multiply_convert_fusion.2.refs_0_, bf16[8,6144]{1,0:T(8,128)(2,1)S(1)} %get-tuple-element.385.refs_1_, f32[64,6144]{1,0:T(8,128)S(1)} %copy-done.33, f32[64,6144]{1,0:T(8,128)S(1)} %copy-done.41, ...), custom_call_target="tpu_custom_call" | custom-call | flops 1000 | bytes 1000 | tf_op jit(solution)/shard_map/modulation_step/pallas_call | solution.py:928
  356.1 2.5 multiply_subtract_fusion
  (434 shorter events, 97.4 us)
Async XLA Ops:
  1.6 9.0 %collective-permute-start = (bf16[1,48,1024]{2,1,0:T(8,128)(2,1)S(1)}, bf16[1,48,1024]{2,1,0:T(8,128)(2,1)S(1)}, u32[]{:S(2)}, u32[]{:S(2)}) collective-permute-start(bf16[1,48,1024]{2,1,0:T(8,128)(2,1)S(1)} %fusion.38), channel_id=1, source_target_pairs={{0,16},{1,17},{2,18},{3,19},{4,20},{5,21},{6,22},{7,23},{8,24},{9,... | collective-permute-start | bytes 294920 | tf_op jit(solution)/shard_map/ppermute | solution.py:38
  7.8 7.3 %collective-permute-start.1 = (f32[8,3072]{1,0:T(8,128)S(1)}, f32[8,3072]{1,0:T(8,128)S(1)}, u32[]{:S(2)}, u32[]{:S(2)}) collective-permute-start(f32[8,3072]{1,0:T(8,128)S(1)} %fusion.32), channel_id=1, source_target_pairs={{0,16},{1,17},{2,18},{3,19},{4,20},{5,21},{6,22},{7,23},{8,24},{9,... | collective-permute-start | bytes 294920 | tf_op jit(solution)/shard_map/ppermute | solution.py:38
  15.2 7.7 %collective-permute-start.2 = (bf16[2,48,1024]{2,1,0:T(8,128)(2,1)S(1)}, bf16[2,48,1024]{2,1,0:T(8,128)(2,1)S(1)}, u32[]{:S(2)}, u32[]{:S(2)}) collective-permute-start(bf16[2,48,1024]{2,1,0:T(8,128)(2,1)S(1)} %get-tuple-element.387), channel_id=1, source_target_pairs={{0,8},{1,9},{2,10},{3,11},{4,12},{5,13},{6,14},{7,15},{8,0},{9,1},... | collective-permute-start | bytes 589832 | tf_op jit(solution)/shard_map/ppermute | solution.py:38
  15.8 7.1 %collective-permute-start.3 = (f32[8,3072]{1,0:T(8,128)S(1)}, f32[8,3072]{1,0:T(8,128)S(1)}, u32[]{:S(2)}, u32[]{:S(2)}) collective-permute-start(f32[8,3072]{1,0:T(8,128)S(1)} %add.503), channel_id=1, source_target_pairs={{0,8},{1,9},{2,10},{3,11},{4,12},{5,13},{6,14},{7,15},{8,0},{9,1},... | collective-permute-start | bytes 294920 | tf_op jit(solution)/shard_map/ppermute | solution.py:38
  23.6 14.5 %collective-permute-start.4 = (bf16[1,336,512]{2,1,0:T(8,128)(2,1)}, bf16[1,336,512]{2,1,0:T(8,128)(2,1)S(1)}, u32[]{:S(2)}, u32[]{:S(2)}) collective-permute-start(bf16[1,336,512]{2,1,0:T(8,128)(2,1)} %get-tuple-element.373), channel_id=1, source_target_pairs={{0,2},{1,5},{2,0},{3,7},{4,6},{5,1},{6,4},{7,3},{8,10},{9,13},{10,... | collective-permute-start | bytes 1032200 | tf_op jit(solution)/shard_map/ppermute | solution.py:38
  25.2 13.0 %collective-permute-start.6 = (bf16[2,2,48,1024]{3,2,1,0:T(8,128)(2,1)S(1)}, bf16[2,2,48,1024]{3,2,1,0:T(8,128)(2,1)S(1)}, u32[]{:S(2)}, u32[]{:S(2)}) collective-permute-start(bf16[2,2,48,1024]{3,2,1,0:T(8,128)(2,1)S(1)} %get-tuple-element.375), channel_id=1, source_target_pairs={{0,2},{1,5},{2,0},{3,7},{4,6},{5,1},{6,4},{7,3},{8,10},{9,13},{10,... | collective-permute-start | bytes 1179656 | tf_op jit(solution)/shard_map/ppermute | solution.py:38
  25.8 10.6 %collective-permute-start.5 = (bf16[1,176,512]{2,1,0:T(8,128)(2,1)S(1)}, bf16[1,176,512]{2,1,0:T(8,128)(2,1)S(1)}, u32[]{:S(2)}, u32[]{:S(2)}) collective-permute-start(bf16[1,176,512]{2,1,0:T(8,128)(2,1)S(1)} %get-tuple-element.371), channel_id=1, source_target_pairs={{0,8},{1,9},{2,10},{3,11},{4,12},{5,13},{6,14},{7,15},{8,0},{9,1},... | collective-permute-start | bytes 540680 | tf_op jit(solution)/shard_map/ppermute | solution.py:38
  27.6 10.5 %collective-permute-start.8 = (bf16[1,176,512]{2,1,0:T(8,128)(2,1)S(1)}, bf16[1,176,512]{2,1,0:T(8,128)(2,1)}, u32[]{:S(2)}, u32[]{:S(2)}) collective-permute-start(bf16[1,176,512]{2,1,0:T(8,128)(2,1)S(1)} %get-tuple-element.371), channel_id=1, source_target_pairs={{0,16},{1,17},{2,18},{3,19},{4,20},{5,21},{6,22},{7,23},{8,24},{9,... | collective-permute-start | bytes 540680 | tf_op jit(solution)/shard_map/ppermute | solution.py:38
  31.6 4.8 %collective-permute-start.7 = (f32[8,3072]{1,0:T(8,128)S(1)}, f32[8,3072]{1,0:T(8,128)S(1)}, u32[]{:S(2)}, u32[]{:S(2)}) collective-permute-start(f32[8,3072]{1,0:T(8,128)S(1)} %add.504), channel_id=1, source_target_pairs={{0,2},{1,5},{2,0},{3,7},{4,6},{5,1},{6,4},{7,3},{8,10},{9,13},{10,... | collective-permute-start | bytes 294920 | tf_op jit(solution)/shard_map/ppermute | solution.py:38
  39.2 22.5 %collective-permute-start.11 = (bf16[2,2,2,48,1024]{4,3,2,1,0:T(8,128)(2,1)}, bf16[2,2,2,48,1024]{4,3,2,1,0:T(8,128)(2,1)S(1)}, u32[]{:S(2)}, u32[]{:S(2)}) collective-permute-start(bf16[2,2,2,48,1024]{4,3,2,1,0:T(8,128)(2,1)} %get-tuple-element.365), channel_id=1, source_target_pairs={{0,4},{1,3},{2,6},{3,1},{4,0},{5,7},{6,2},{7,5},{8,12},{9,11},{10,... | collective-permute-start | bytes 2359304 | tf_op jit(solution)/shard_map/ppermute | solution.py:38
  41.6 20.0 %collective-permute-start.9 = (bf16[2,1,336,512]{3,2,0,1:T(8,128)(2,1)}, bf16[2,1,336,512]{3,2,0,1:T(8,128)(2,1)}, u32[]{:S(2)}, u32[]{:S(2)}) collective-permute-start(bf16[2,1,336,512]{3,2,0,1:T(8,128)(2,1)} %get-tuple-element.369), channel_id=1, source_target_pairs={{0,4},{1,9},{2,6},{3,11},{4,0},{5,13},{6,2},{7,15},{8,12},{9,1},{1... | collective-permute-start | bytes 2064392 | tf_op jit(solution)/shard_map/ppermute | solution.py:38
  42.6 17.0 %collective-permute-start.13 = (bf16[1,336,512]{2,1,0:T(8,128)(2,1)}, bf16[1,336,512]{2,1,0:T(8,128)(2,1)}, u32[]{:S(2)}, u32[]{:S(2)}) collective-permute-start(bf16[1,336,512]{2,1,0:T(8,128)(2,1)} %get-tuple-element.373), channel_id=1, source_target_pairs={{0,16},{1,17},{2,18},{3,19},{4,20},{5,21},{6,22},{7,23},{8,24},{9,... | collective-permute-start | bytes 1032200 | tf_op jit(solution)/shard_map/ppermute | solution.py:38
  44.3 17.3 %collective-permute-start.10 = (bf16[2,1,176,512]{3,2,0,1:T(8,128)(2,1)S(1)}, bf16[2,1,176,512]{3,2,0,1:T(8,128)(2,1)}, u32[]{:S(2)}, u32[]{:S(2)}) collective-permute-start(bf16[2,1,176,512]{3,2,0,1:T(8,128)(2,1)S(1)} %get-tuple-element.379), channel_id=1, source_target_pairs={{0,2},{1,3},{2,0},{3,1},{4,6},{5,7},{6,4},{7,5},{8,10},{9,11},{10,... | collective-permute-start | bytes 1081352 | tf_op jit(solution)/shard_map/ppermute | solution.py:38
  45.9 11.1 %collective-permute-start.16 = (bf16[1,176,512]{2,1,0:T(8,128)(2,1)}, bf16[1,176,512]{2,1,0:T(8,128)(2,1)}, u32[]{:S(2)}, u32[]{:S(2)}) collective-permute-start(bf16[1,176,512]{2,1,0:T(8,128)(2,1)} %collective-permute-done.8), channel_id=1, source_target_pairs={{0,8},{1,9},{2,10},{3,11},{4,12},{5,13},{6,14},{7,15},{8,0},{9,1},... | collective-permute-start | bytes 540680 | tf_op jit(solution)/shard_map/ppermute | solution.py:38
  57.0 4.6 %collective-permute-start.12 = (f32[8,3072]{1,0:T(8,128)S(1)}, f32[8,3072]{1,0:T(8,128)S(1)}, u32[]{:S(2)}, u32[]{:S(2)}) collective-permute-start(f32[8,3072]{1,0:T(8,128)S(1)} %add.505), channel_id=1, source_target_pairs={{0,4},{1,3},{2,6},{3,1},{4,0},{5,7},{6,2},{7,5},{8,12},{9,11},{10,... | collective-permute-start | bytes 294920 | tf_op jit(solution)/shard_map/ppermute | solution.py:38
  59.6 26.1 %collective-permute-start.17 = (bf16[2,1,176,512]{3,2,0,1:T(8,128)(2,1)S(1)}, bf16[2,1,176,512]{3,2,0,1:T(8,128)(2,1)S(1)}, u32[]{:S(2)}, u32[]{:S(2)}) collective-permute-start(bf16[2,1,176,512]{3,2,0,1:T(8,128)(2,1)S(1)} %get-tuple-element.377), channel_id=1, source_target_pairs={{0,2},{1,3},{2,0},{3,1},{4,6},{5,7},{6,4},{7,5},{8,10},{9,11},{10,... | collective-permute-start | bytes 1081352 | tf_op jit(solution)/shard_map/ppermute | solution.py:38
  61.6 16.4 %collective-permute-start.14 = (bf16[1,336,512]{2,1,0:T(8,128)(2,1)}, bf16[1,336,512]{2,1,0:T(8,128)(2,1)S(1)}, u32[]{:S(2)}, u32[]{:S(2)}) collective-permute-start(bf16[1,336,512]{2,1,0:T(8,128)(2,1)} %collective-permute-done.13), channel_id=1, source_target_pairs={{0,2},{1,5},{2,0},{3,7},{4,6},{5,1},{6,4},{7,3},{8,10},{9,13},{10,... | collective-permute-start | bytes 1032200 | tf_op jit(solution)/shard_map/ppermute | solution.py:38
  64.4 28.7 %collective-permute-start.18 = (bf16[2,2,1,336,512]{4,3,1,2,0:T(8,128)(2,1)S(1)}, bf16[2,2,1,336,512]{4,3,1,2,0:T(8,128)(2,1)S(1)}, u32[]{:S(2)}, u32[]{:S(2)}) collective-permute-start(bf16[2,2,1,336,512]{4,3,1,2,0:T(8,128)(2,1)S(1)} %pad_maximum_fusion.2), channel_id=1, source_target_pairs={{0,8},{1,3},{2,10},{3,1},{4,12},{5,7},{6,14},{7,5},{8,0},{9,11},{1... | collective-permute-start | bytes 4128776 | tf_op jit(solution)/shard_map/ppermute | solution.py:38
  68.0 17.7 %collective-permute-start.19 = (bf16[2,2,1,176,512]{4,3,1,2,0:T(8,128)(2,1)S(1)}, bf16[2,2,1,176,512]{4,3,1,2,0:T(8,128)(2,1)S(1)}, u32[]{:S(2)}, u32[]{:S(2)}) collective-permute-start(bf16[2,2,1,176,512]{4,3,1,2,0:T(8,128)(2,1)S(1)} %pad_maximum_fusion.6), channel_id=1, source_target_pairs={{0,4},{1,5},{2,6},{3,7},{4,0},{5,1},{6,2},{7,3},{8,12},{9,13},{10,... | collective-permute-start | bytes 2162696 | tf_op jit(solution)/shard_map/ppermute | solution.py:38
  69.6 1.4 collective-permute-start.21
  71.0 22.1 %collective-permute-start.20 = (bf16[16,48,1024]{2,1,0:T(8,128)(2,1)S(1)}, bf16[16,48,1024]{2,1,0:T(8,128)(2,1)S(1)}, u32[]{:S(2)}, u32[]{:S(2)}) collective-permute-start(bf16[16,48,1024]{2,1,0:T(8,128)(2,1)S(1)} %bitcast.212), channel_id=1, source_target_pairs={{0,1},{1,0},{2,3},{3,2},{4,5},{5,4},{6,7},{7,6},{8,9},{9,8},{10,11... | collective-permute-start | bytes 4718600 | tf_op jit(solution)/shard_map/ppermute | solution.py:30
  79.2 14.0 %collective-permute-start.15 = (bf16[2,1,336,512]{3,2,0,1:T(8,128)(2,1)S(1)}, bf16[2,1,336,512]{3,2,0,1:T(8,128)(2,1)S(1)}, u32[]{:S(2)}, u32[]{:S(2)}) collective-permute-start(bf16[2,1,336,512]{3,2,0,1:T(8,128)(2,1)S(1)} %get-tuple-element.367), channel_id=1, source_target_pairs={{0,4},{1,9},{2,6},{3,11},{4,0},{5,13},{6,2},{7,15},{8,12},{9,1},{1... | collective-permute-start | bytes 2064392 | tf_op jit(solution)/shard_map/ppermute | solution.py:38
  94.5 21.6 %collective-permute-start.22 = (bf16[2,2,1,336,512]{4,3,1,2,0:T(8,128)(2,1)}, bf16[2,2,1,336,512]{4,3,1,2,0:T(8,128)(2,1)}, u32[]{:S(2)}, u32[]{:S(2)}) collective-permute-start(bf16[2,2,1,336,512]{4,3,1,2,0:T(8,128)(2,1)} %pad_maximum_fusion.3), channel_id=1, source_target_pairs={{0,8},{1,3},{2,10},{3,1},{4,12},{5,7},{6,14},{7,5},{8,0},{9,11},{1... | collective-permute-start | bytes 4128776 | tf_op jit(solution)/shard_map/ppermute | solution.py:38
  96.5 19.6 %collective-permute-start.23 = (bf16[2,2,1,176,512]{4,3,1,2,0:T(8,128)(2,1)}, bf16[2,2,1,176,512]{4,3,1,2,0:T(8,128)(2,1)}, u32[]{:S(2)}, u32[]{:S(2)}) collective-permute-start(bf16[2,2,1,176,512]{4,3,1,2,0:T(8,128)(2,1)} %pad_maximum_fusion.7), channel_id=1, source_target_pairs={{0,4},{1,5},{2,6},{3,7},{4,0},{5,1},{6,2},{7,3},{8,12},{9,13},{10,... | collective-permute-start | bytes 2162696 | tf_op jit(solution)/shard_map/ppermute | solution.py:38
  113.5 31.9 %copy-start.4 = (f32[512,1024]{1,0:T(8,128)}, f32[512,1024]{1,0:T(8,128)S(1)}, u32[]{:S(2)}) copy-start(f32[512,1024]{1,0:T(8,128)S(1)} %get-tuple-element.215.stream_ref) | copy-start | bytes 6291460
  142.7 2.7 collective-permute-start.24
  147.1 2.7 collective-permute-start.25
  154.7 7.4 %collective-permute-start.26 = (bf16[512,1024]{1,0:T(8,128)(2,1)S(1)}, bf16[512,1024]{1,0:T(8,128)(2,1)S(1)}, u32[]{:S(2)}, u32[]{:S(2)}) collective-permute-start(bf16[512,1024]{1,0:T(8,128)(2,1)S(1)} %get-tuple-element.220), channel_id=1, source_target_pairs={{0,1},{1,0},{2,3},{3,2},{4,5},{5,4},{6,7},{7,6},{8,9},{9,8},{10,11... | collective-permute-start | bytes 3145736 | tf_op jit(solution)/shard_map/ppermute | solution.py:30
  154.9 7.2 %collective-permute-start.27 = (bf16[512,1024]{1,0:T(8,128)(2,1)S(1)}, bf16[512,1024]{1,0:T(8,128)(2,1)S(1)}, u32[]{:S(2)}, u32[]{:S(2)}) collective-permute-start(bf16[512,1024]{1,0:T(8,128)(2,1)S(1)} %get-tuple-element.222), channel_id=1, source_target_pairs={{0,1},{1,0},{2,3},{3,2},{4,5},{5,4},{6,7},{7,6},{8,9},{9,8},{10,11... | collective-permute-start | bytes 3145736 | tf_op jit(solution)/shard_map/ppermute | solution.py:30
  167.2 2.7 collective-permute-start.28
  192.4 18.8 %collective-permute-start.29 = (bf16[2,2,2,336,256]{4,3,2,1,0:T(8,128)(2,1)S(1)}, bf16[2,2,2,336,256]{4,3,2,1,0:T(8,128)(2,1)S(1)}, u32[]{:S(2)}, u32[]{:S(2)}) collective-permute-start(bf16[2,2,2,336,256]{4,3,2,1,0:T(8,128)(2,1)S(1)} %bitcast.234), channel_id=1, source_target_pairs={{0,8},{1,3},{2,10},{3,1},{4,12},{5,7},{6,14},{7,5},{8,0},{9,11},{1... | collective-permute-start | bytes 4128776 | tf_op jit(solution)/shard_map/ppermute | solution.py:38
  193.7 17.5 %collective-permute-start.30 = (bf16[2,2,2,176,256]{4,3,2,1,0:T(8,128)(2,1)S(1)}, bf16[2,2,2,176,256]{4,3,2,1,0:T(8,128)(2,1)S(1)}, u32[]{:S(2)}, u32[]{:S(2)}) collective-permute-start(bf16[2,2,2,176,256]{4,3,2,1,0:T(8,128)(2,1)S(1)} %bitcast.237), channel_id=1, source_target_pairs={{0,4},{1,5},{2,6},{3,7},{4,0},{5,1},{6,2},{7,3},{8,12},{9,13},{10,... | collective-permute-start | bytes 2162696 | tf_op jit(solution)/shard_map/ppermute | solution.py:38
  211.7 11.0 %collective-permute-start.31 = (bf16[2,2,336,256]{3,2,1,0:T(8,128)(2,1)S(1)}, bf16[2,2,336,256]{3,2,1,0:T(8,128)(2,1)S(1)}, u32[]{:S(2)}, u32[]{:S(2)}) collective-permute-start(bf16[2,2,336,256]{3,2,1,0:T(8,128)(2,1)S(1)} %slice_bitcast_fusion.4), channel_id=1, source_target_pairs={{0,4},{1,9},{2,6},{3,11},{4,0},{5,13},{6,2},{7,15},{8,12},{9,1},{1... | collective-permute-start | bytes 2064392 | tf_op jit(solution)/shard_map/ppermute | solution.py:38
  213.1 9.1 %collective-permute-start.32 = (bf16[2,2,176,256]{3,2,1,0:T(8,128)(2,1)S(1)}, bf16[2,2,176,256]{3,2,1,0:T(8,128)(2,1)S(1)}, u32[]{:S(2)}, u32[]{:S(2)}) collective-permute-start(bf16[2,2,176,256]{3,2,1,0:T(8,128)(2,1)S(1)} %slice_bitcast_fusion.10), channel_id=1, source_target_pairs={{0,2},{1,3},{2,0},{3,1},{4,6},{5,7},{6,4},{7,5},{8,10},{9,11},{10,... | collective-permute-start | bytes 1081352 | tf_op jit(solution)/shard_map/ppermute | solution.py:38
  214.0 28.0 %collective-permute-start.53 = (bf16[512,1024]{1,0:T(8,128)(2,1)}, bf16[512,1024]{1,0:T(8,128)(2,1)}, u32[]{:S(2)}, u32[]{:S(2)}) collective-permute-start(bf16[512,1024]{1,0:T(8,128)(2,1)} %get-tuple-element.313), channel_id=1, source_target_pairs={{0,1},{1,0},{2,3},{3,2},{4,5},{5,4},{6,7},{7,6},{8,9},{9,8},{10,11... | collective-permute-start | bytes 3145736 | tf_op jit(solution)/shard_map/ppermute | solution.py:30
  222.7 14.9 %collective-permute-start.35 = (bf16[512,1024]{1,0:T(8,128)(2,1)S(1)}, bf16[512,1024]{1,0:T(8,128)(2,1)S(1)}, u32[]{:S(2)}, u32[]{:S(2)}) collective-permute-start(bf16[512,1024]{1,0:T(8,128)(2,1)S(1)} %get-tuple-element.265), channel_id=1, source_target_pairs={{0,1},{1,0},{2,3},{3,2},{4,5},{5,4},{6,7},{7,6},{8,9},{9,8},{10,11... | collective-permute-start | bytes 3145736 | tf_op jit(solution)/shard_map/ppermute | solution.py:30
  222.9 14.6 %collective-permute-start.33 = (bf16[2,336,256]{2,1,0:T(8,128)(2,1)S(1)}, bf16[2,336,256]{2,1,0:T(8,128)(2,1)S(1)}, u32[]{:S(2)}, u32[]{:S(2)}) collective-permute-start(bf16[2,336,256]{2,1,0:T(8,128)(2,1)S(1)} %slice_bitcast_fusion.14), channel_id=1, source_target_pairs={{0,2},{1,5},{2,0},{3,7},{4,6},{5,1},{6,4},{7,3},{8,10},{9,13},{10,... | collective-permute-start | bytes 1032200 | tf_op jit(solution)/shard_map/ppermute | solution.py:38
  225.2 12.4 %collective-permute-start.34 = (bf16[2,176,256]{2,1,0:T(8,128)(2,1)S(1)}, bf16[2,176,256]{2,1,0:T(8,128)(2,1)S(1)}, u32[]{:S(2)}, u32[]{:S(2)}) collective-permute-start(bf16[2,176,256]{2,1,0:T(8,128)(2,1)S(1)} %slice_bitcast_fusion.20), channel_id=1, source_target_pairs={{0,8},{1,9},{2,10},{3,11},{4,12},{5,13},{6,14},{7,15},{8,0},{9,1},... | collective-permute-start | bytes 540680 | tf_op jit(solution)/shard_map/ppermute | solution.py:38
  238.9 20.1 %collective-permute-start.36 = (bf16[2,2,2,336,256]{4,3,2,1,0:T(8,128)(2,1)}, bf16[2,2,2,336,256]{4,3,2,1,0:T(8,128)(2,1)}, u32[]{:S(2)}, u32[]{:S(2)}) collective-permute-start(bf16[2,2,2,336,256]{4,3,2,1,0:T(8,128)(2,1)} %bitcast.63), channel_id=1, source_target_pairs={{0,8},{1,3},{2,10},{3,1},{4,12},{5,7},{6,14},{7,5},{8,0},{9,11},{1... | collective-permute-start | bytes 4128776 | tf_op jit(solution)/shard_map/ppermute | solution.py:38
  241.4 17.6 %collective-permute-start.37 = (bf16[2,2,2,176,256]{4,3,2,1,0:T(8,128)(2,1)}, bf16[2,2,2,176,256]{4,3,2,1,0:T(8,128)(2,1)S(1)}, u32[]{:S(2)}, u32[]{:S(2)}) collective-permute-start(bf16[2,2,2,176,256]{4,3,2,1,0:T(8,128)(2,1)} %bitcast.236), channel_id=1, source_target_pairs={{0,4},{1,5},{2,6},{3,7},{4,0},{5,1},{6,2},{7,3},{8,12},{9,13},{10,... | collective-permute-start | bytes 2162696 | tf_op jit(solution)/shard_map/ppermute | solution.py:38
  260.9 19.5 %collective-permute-start.38 = (bf16[2,2,336,256]{3,2,1,0:T(8,128)(2,1)S(1)}, bf16[2,2,336,256]{3,2,1,0:T(8,128)(2,1)S(1)}, u32[]{:S(2)}, u32[]{:S(2)}) collective-permute-start(bf16[2,2,336,256]{3,2,1,0:T(8,128)(2,1)S(1)} %slice_bitcast_fusion.1), channel_id=1, source_target_pairs={{0,4},{1,9},{2,6},{3,11},{4,0},{5,13},{6,2},{7,15},{8,12},{9,1},{1... | collective-permute-start | bytes 2064392 | tf_op jit(solution)/shard_map/ppermute | solution.py:38
  262.4 18.0 %collective-permute-start.43 = (f32[512,1024]{1,0:T(8,128)S(1)}, f32[512,1024]{1,0:T(8,128)S(1)}, u32[]{:S(2)}, u32[]{:S(2)}) collective-permute-start(f32[512,1024]{1,0:T(8,128)S(1)} %get-tuple-element.292), channel_id=1, source_target_pairs={{0,1},{1,0},{2,3},{3,2},{4,5},{5,4},{6,7},{7,6},{8,9},{9,8},{10,11... | collective-permute-start | bytes 6291464 | tf_op jit(solution)/shard_map/ppermute | solution.py:30
  262.6 17.8 %collective-permute-start.39 = (bf16[2,2,176,256]{3,2,1,0:T(8,128)(2,1)S(1)}, bf16[2,2,176,256]{3,2,1,0:T(8,128)(2,1)S(1)}, u32[]{:S(2)}, u32[]{:S(2)}) collective-permute-start(bf16[2,2,176,256]{3,2,1,0:T(8,128)(2,1)S(1)} %slice_bitcast_fusion.8), channel_id=1, source_target_pairs={{0,2},{1,3},{2,0},{3,1},{4,6},{5,7},{6,4},{7,5},{8,10},{9,11},{10,... | collective-permute-start | bytes 1081352 | tf_op jit(solution)/shard_map/ppermute | solution.py:38
  263.1 17.3 %collective-permute-start.40 = (bf16[1,336,256]{2,1,0:T(8,128)(2,1)S(1)}, bf16[1,336,256]{2,1,0:T(8,128)(2,1)S(1)}, u32[]{:S(2)}, u32[]{:S(2)}) collective-permute-start(bf16[1,336,256]{2,1,0:T(8,128)(2,1)S(1)} %get-tuple-element.383), channel_id=1, source_target_pairs={{0,16},{1,17},{2,18},{3,19},{4,20},{5,21},{6,22},{7,23},{8,24},{9,... | collective-permute-start | bytes 516104 | tf_op jit(solution)/shard_map/ppermute | solution.py:38
  268.1 1.2 collective-permute-start.42
  269.2 11.2 %collective-permute-start.41 = (bf16[1,176,256]{2,1,0:T(8,128)(2,1)S(1)}, bf16[1,176,256]{2,1,0:T(8,128)(2,1)S(1)}, u32[]{:S(2)}, u32[]{:S(2)}) collective-permute-start(bf16[1,176,256]{2,1,0:T(8,128)(2,1)S(1)} %get-tuple-element.391), channel_id=1, source_target_pairs={{0,16},{1,17},{2,18},{3,19},{4,20},{5,21},{6,22},{7,23},{8,24},{9,... | collective-permute-start | bytes 270344 | tf_op jit(solution)/shard_map/ppermute | solution.py:38
  281.4 15.3 %collective-permute-start.44 = (bf16[2,336,256]{2,1,0:T(8,128)(2,1)}, bf16[2,336,256]{2,1,0:T(8,128)(2,1)}, u32[]{:S(2)}, u32[]{:S(2)}) collective-permute-start(bf16[2,336,256]{2,1,0:T(8,128)(2,1)} %slice_bitcast_fusion.11), channel_id=1, source_target_pairs={{0,2},{1,5},{2,0},{3,7},{4,6},{5,1},{6,4},{7,3},{8,10},{9,13},{10,... | collective-permute-start | bytes 1032200 | tf_op jit(solution)/shard_map/ppermute | solution.py:38
  283.2 11.3 %collective-permute-start.46 = (bf16[16,48,1024]{2,1,0:T(8,128)(2,1)}, bf16[16,48,1024]{2,1,0:T(8,128)(2,1)}, u32[]{:S(2)}, u32[]{:S(2)}) collective-permute-start(bf16[16,48,1024]{2,1,0:T(8,128)(2,1)} %get-tuple-element.296), channel_id=1, source_target_pairs={{0,1},{1,0},{2,3},{3,2},{4,5},{5,4},{6,7},{7,6},{8,9},{9,8},{10,11... | collective-permute-start | bytes 4718600 | tf_op jit(solution)/shard_map/ppermute | solution.py:30
  284.0 12.7 %collective-permute-start.45 = (bf16[2,176,256]{2,1,0:T(8,128)(2,1)}, bf16[2,176,256]{2,1,0:T(8,128)(2,1)}, u32[]{:S(2)}, u32[]{:S(2)}) collective-permute-start(bf16[2,176,256]{2,1,0:T(8,128)(2,1)} %slice_bitcast_fusion.18), channel_id=1, source_target_pairs={{0,8},{1,9},{2,10},{3,11},{4,12},{5,13},{6,14},{7,15},{8,0},{9,1},... | collective-permute-start | bytes 540680 | tf_op jit(solution)/shard_map/ppermute | solution.py:38
  284.3 2.4 collective-permute-start.47
  292.1 10.4 %collective-permute-start.52 = (f32[512,512]{1,0:T(8,128)}, f32[512,512]{1,0:T(8,128)S(1)}, u32[]{:S(2)}, u32[]{:S(2)}) collective-permute-start(f32[512,512]{1,0:T(8,128)} %copy-done.65), channel_id=1, source_target_pairs={{0,1},{1,0},{2,3},{3,2},{4,5},{5,4},{6,7},{7,6},{8,9},{9,8},{10,11... | collective-permute-start | bytes 3145736 | tf_op jit(solution)/shard_map/ppermute | solution.py:30
  296.8 16.4 %collective-permute-start.50 = (bf16[2,2,2,48,1024]{4,3,2,1,0:T(8,128)(2,1)S(1)}, bf16[2,2,2,48,1024]{4,3,2,1,0:T(8,128)(2,1)S(1)}, u32[]{:S(2)}, u32[]{:S(2)}) collective-permute-start(bf16[2,2,2,48,1024]{4,3,2,1,0:T(8,128)(2,1)S(1)} %slice_bitcast_fusion), channel_id=1, source_target_pairs={{0,4},{1,3},{2,6},{3,1},{4,0},{5,7},{6,2},{7,5},{8,12},{9,11},{10,... | collective-permute-start | bytes 2359304 | tf_op jit(solution)/shard_map/ppermute | solution.py:38
  298.5 14.6 %collective-permute-start.48 = (bf16[1,336,256]{2,1,0:T(8,128)(2,1)S(1)}, bf16[1,336,256]{2,1,0:T(8,128)(2,1)S(1)}, u32[]{:S(2)}, u32[]{:S(2)}) collective-permute-start(bf16[1,336,256]{2,1,0:T(8,128)(2,1)S(1)} %get-tuple-element.381), channel_id=1, source_target_pairs={{0,16},{1,17},{2,18},{3,19},{4,20},{5,21},{6,22},{7,23},{8,24},{9,... | collective-permute-start | bytes 516104 | tf_op jit(solution)/shard_map/ppermute | solution.py:38
  301.3 11.8 %collective-permute-start.49 = (bf16[1,176,256]{2,1,0:T(8,128)(2,1)S(1)}, bf16[1,176,256]{2,1,0:T(8,128)(2,1)S(1)}, u32[]{:S(2)}, u32[]{:S(2)}) collective-permute-start(bf16[1,176,256]{2,1,0:T(8,128)(2,1)S(1)} %get-tuple-element.389), channel_id=1, source_target_pairs={{0,16},{1,17},{2,18},{3,19},{4,20},{5,21},{6,22},{7,23},{8,24},{9,... | collective-permute-start | bytes 270344 | tf_op jit(solution)/shard_map/ppermute | solution.py:38
  302.6 1.2 collective-permute-start.51
  313.5 8.6 %collective-permute-start.54 = (bf16[2,2,48,1024]{3,2,1,0:T(8,128)(2,1)S(1)}, bf16[2,2,48,1024]{3,2,1,0:T(8,128)(2,1)S(1)}, u32[]{:S(2)}, u32[]{:S(2)}) collective-permute-start(bf16[2,2,48,1024]{3,2,1,0:T(8,128)(2,1)S(1)} %slice_bitcast_fusion.6), channel_id=1, source_target_pairs={{0,2},{1,5},{2,0},{3,7},{4,6},{5,1},{6,4},{7,3},{8,10},{9,13},{10,... | collective-permute-start | bytes 1179656 | tf_op jit(solution)/shard_map/ppermute | solution.py:38
  315.5 5.5 %collective-permute-start.55 = (f32[226,128]{1,0:T(8,128)S(1)}, f32[226,128]{1,0:T(8,128)S(1)}, u32[]{:S(2)}, u32[]{:S(2)}) collective-permute-start(f32[226,128]{1,0:T(8,128)S(1)} %maximum_bitcast_fusion), channel_id=1, source_target_pairs={{0,8},{1,3},{2,10},{3,1},{4,12},{5,7},{6,14},{7,5},{8,0},{9,11},{1... | collective-permute-start | bytes 347144 | tf_op jit(solution)/shard_map/ppermute | solution.py:38
  322.3 4.9 %collective-permute-start.59 = (f32[226,128]{1,0:T(8,128)S(1)}, f32[226,128]{1,0:T(8,128)S(1)}, u32[]{:S(2)}, u32[]{:S(2)}) collective-permute-start(f32[226,128]{1,0:T(8,128)S(1)} %fusion.49), channel_id=1, source_target_pairs={{0,2},{1,5},{2,0},{3,7},{4,6},{5,1},{6,4},{7,3},{8,10},{9,13},{10,... | collective-permute-start | bytes 347144 | tf_op jit(solution)/shard_map/ppermute | solution.py:38
  324.1 9.9 %collective-permute-start.56 = (bf16[2,48,1024]{2,1,0:T(8,128)(2,1)S(1)}, bf16[2,48,1024]{2,1,0:T(8,128)(2,1)S(1)}, u32[]{:S(2)}, u32[]{:S(2)}) collective-permute-start(bf16[2,48,1024]{2,1,0:T(8,128)(2,1)S(1)} %slice_bitcast_fusion.15), channel_id=1, source_target_pairs={{0,8},{1,9},{2,10},{3,11},{4,12},{5,13},{6,14},{7,15},{8,0},{9,1},... | collective-permute-start | bytes 589832 | tf_op jit(solution)/shard_map/ppermute | solution.py:38
  327.2 4.9 %collective-permute-start.60 = (f32[226,128]{1,0:T(8,128)S(1)}, f32[226,128]{1,0:T(8,128)S(1)}, u32[]{:S(2)}, u32[]{:S(2)}) collective-permute-start(f32[226,128]{1,0:T(8,128)S(1)} %fusion.71), channel_id=1, source_target_pairs={{0,4},{1,9},{2,6},{3,11},{4,0},{5,13},{6,2},{7,15},{8,12},{9,1},{1... | collective-permute-start | bytes 347144 | tf_op jit(solution)/shard_map/ppermute | solution.py:38
  332.2 9.6 %collective-permute-start.61 = (f32[226,128]{1,0:T(8,128)S(1)}, f32[226,128]{1,0:T(8,128)S(1)}, u32[]{:S(2)}, u32[]{:S(2)}) collective-permute-start(f32[226,128]{1,0:T(8,128)S(1)} %add.585), channel_id=1, source_target_pairs={{0,16},{1,17},{2,18},{3,19},{4,20},{5,21},{6,22},{7,23},{8,24},{9,... | collective-permute-start | bytes 347144 | tf_op jit(solution)/shard_map/ppermute | solution.py:38
  334.2 8.6 %collective-permute-start.57 = (bf16[1,48,1024]{2,1,0:T(8,128)(2,1)S(1)}, bf16[1,48,1024]{2,1,0:T(8,128)(2,1)S(1)}, u32[]{:S(2)}, u32[]{:S(2)}) collective-permute-start(bf16[1,48,1024]{2,1,0:T(8,128)(2,1)S(1)} %slice.454), channel_id=1, source_target_pairs={{0,16},{1,17},{2,18},{3,19},{4,20},{5,21},{6,22},{7,23},{8,24},{9,... | collective-permute-start | bytes 294920 | tf_op jit(solution)/shard_map/ppermute | solution.py:38
  341.8 1.9 collective-permute-start.62
  343.5 12.5 %collective-permute-start.58 = (f32[48,1024]{1,0:T(8,128)}, f32[48,1024]{1,0:T(8,128)}, u32[]{:S(2)}, u32[]{:S(2)}) collective-permute-start(f32[48,1024]{1,0:T(8,128)} %add_bitcast_fusion), channel_id=1, source_target_pairs={{0,1},{1,0},{2,3},{3,2},{4,5},{5,4},{6,7},{7,6},{8,9},{9,8},{10,11... | collective-permute-start | bytes 589832 | tf_op jit(solution)/shard_map/ppermute | solution.py:30
  (101 other events, 649.0 us)

commit v6 on v5

--- a/solution.py
+++ b/solution.py
@@ -184,9 +184,14 @@
 ROWS = 256
 LONG_ROWS = 512
 PAIR = 2 * HEAD
-vmem_bytes = 16 * 1024 * 1024
-gradient_bytes = 24 * 1024 * 1024
-project_bytes = 32 * 1024 * 1024
+mebibyte = 1024 * 1024
+vmem_bytes = 12 * mebibyte
+feed_bytes = 16 * mebibyte
+attend_back_bytes = 16 * mebibyte
+text_forward_bytes = 20 * mebibyte
+text_back_bytes = 16 * mebibyte
+gradient_bytes = 20 * mebibyte
+project_bytes = 24 * mebibyte
 
 
 def dot32(left, right, dims=NN):
@@ -375,7 +380,7 @@
             pltpu.VMEM((LEN, 2 * PAIR), f32),
             pltpu.VMEM((LEN, 2 * PAIR), f32),
         ],
-        compiler_params=pltpu.CompilerParams(vmem_limit_bytes=vmem_bytes),
+        compiler_params=pltpu.CompilerParams(vmem_limit_bytes=attend_back_bytes),
         cost_estimate=beside,
         name="attend_back",
     )(queries, keys, values, outputs, grad_mine, grad_other, stacked, cosine, sine, bias)
@@ -480,7 +485,7 @@
         in_specs=[whole, whole, pl.BlockSpec((4, D, width), lambda step: (1, 0, 0))],
         out_specs=[whole] * 4 + [pl.BlockSpec((D, half), lambda step: (0, 0))] * 2,
         out_shape=[sums, sums, low, low] + [jax.ShapeDtypeStruct((D, half), bf16)] * 2,
-        compiler_params=pltpu.CompilerParams(vmem_limit_bytes=vmem_bytes),
+        compiler_params=pltpu.CompilerParams(vmem_limit_bytes=feed_bytes),
         cost_estimate=pl.CostEstimate(
             flops=2 * 4 * half * D * D, bytes_accessed=16 * D * width, transcendentals=half * D
         ),
@@ -587,7 +592,7 @@
     return share, density
 
 
-def in_vmem(kernel, name, inputs, outs, scratch=(), specs=None, out_specs=None):
+def in_vmem(kernel, name, inputs, outs, scratch=(), specs=None, out_specs=None, limit=vmem_bytes):
     whole = pl.BlockSpec(memory_space=pltpu.VMEM)
     return pl.pallas_call(
         kernel,
@@ -595,7 +600,7 @@
         out_specs=out_specs or [whole] * len(outs),
         out_shape=[jax.ShapeDtypeStruct(shape, kind) for shape, kind in outs],
         scratch_shapes=list(scratch),
-        compiler_params=pltpu.CompilerParams(vmem_limit_bytes=vmem_bytes),
+        compiler_params=pltpu.CompilerParams(vmem_limit_bytes=limit),
         cost_estimate=beside,
         name=name,
     )(*inputs)
@@ -678,6 +683,7 @@
         [pltpu.VMEM((LEN, TXT_FF), f32)],
         [scalars, scalars] + [whole] * len(inputs),
         [whole] * 10,
+        text_forward_bytes,
     )
 
 
@@ -793,6 +799,7 @@
         [pltpu.VMEM((3 * TEXT, D), bf16)] if apart else [],
         [whole] * len(inputs) + [scalars] * 2,
         [whole] * (5 if apart else 4),
+        text_back_bytes,
     )
 
 
@@ -1239,16 +1246,16 @@
     received_a, head_grads = tie_lists(received_a, head_grads)
     part_a = add_all(keep_a, received_a)
     received_a = receive(seconds(part_a), 1)
-    my_grad, their_grad = inputs_grad(head_grads, stacked)
-    received_a, head_grads, (my_grad, their_grad) = tie_lists(received_a, head_grads, (my_grad, their_grad))
+    keep_b, send_b = weight_gradients(1, head_grads[3:])
+    received_a, send_b, head_grads = tie_lists(received_a, send_b, head_grads)
     part_a = add_all(firsts(part_a), received_a)
     received_a = receive(seconds(part_a), 0)
-    keep_b, send_b = weight_gradients(1, head_grads[3:])
-    their_grad = swap_core(their_grad)
-    received_a, send_b, (their_grad,) = tie_lists(received_a, send_b, (their_grad,))
+    my_grad, their_grad = inputs_grad(head_grads, stacked)
+    received_a, send_b, (my_grad, their_grad) = tie_lists(received_a, send_b, (my_grad, their_grad))
 
     part_a = add_all(firsts(part_a), received_a)
     received_b = receive(send_b, 2)
+    their_grad = swap_core(their_grad)
     mel_grad_mine, stream_low, shrink_grad, shrink_low, grn_grad, sums, out_bias_grad, mel_gradient = stream_back(
         core, my_grad, their_grad, stream, stream_one_grad, scale_one, texts, keep, expand_pre
     )
@@ -1318,27 +1325,29 @@
     token_half = 3 * D
 
     def half_of(which):
+        half_vector = lax.dynamic_slice_in_dim(vector_mine, which * vector_half, vector_half, 0)
         return jnp.concatenate(
             [
-                lax.dynamic_slice_in_dim(vector_mine, which * vector_half, vector_half, 0),
-                lax.dynamic_slice_in_dim(token, which * token_half, token_half, 0),
+                jnp.pad(half_vector, (0, 2 * token_half - vector_half)).reshape(2, token_half),
+                lax.dynamic_slice_in_dim(token, which * token_half, token_half, 0)[None],
             ]
         )
 
-    small_send = half_of(1 - core)
     small = half_of(core)
+    small_received = swap_core(half_of(1 - core))
     in_group = (jnp.arange(GROUPS) == group).astype(f32)
-
     text_grad_theirs = swap_core(text_grad_mine)
     text_part = add_low(text_keep_half, text_received).reshape(2, 2, 2, 2 * high_count, text_half, D)
     mel_gradient = lax.dynamic_update_slice_in_dim(mel_gradient, mel_grad_theirs, half - first, 0)
-    received_b, (text_part, small, small_send, mel_gradient) = tie_lists(
-        received_b, (text_part, small, small_send, mel_gradient)
-    )
+    received_b, (text_part, small, small_received, mel_gradient) = tie_lists(
+        received_b, (text_part, small, small_received, mel_gradient)
+    )
+    small = small + small_received
+    small = jnp.concatenate([in_group[:, None] * small[2:], small[:2]])
     part_b = add_all(firsts(part_b), received_b)
     far_b = [swap_bit(part[high_count:], 3) for part in part_b]
     text_received = swap_bits(text_part[1], phase_bits(text_orders, 2))
-    small_received = swap_core(small_send)
+    small_received = swap_bits(small, (2, 0))
     block_output = lax.dynamic_update_slice_in_dim(block_output, output_theirs, half - first, 0)
     text_gradient = lax.dynamic_update_slice_in_dim(text_gradient, text_grad_theirs, half - first, 0)
     far_b, (text_received, small_received, text_gradient, block_output) = tie_lists(
@@ -1347,9 +1356,7 @@
     text_part = add_low(text_part[0], text_received)
     text_received = swap_bits(text_part[1], phase_bits(text_orders, 1))
     small = small + small_received
-    table = in_group[:, None] * small[None, vector_half:]
-    small = jnp.concatenate([small[:vector_half], table.reshape(-1)]).reshape(-1, 128)
-    small_received = swap_bits(small, (2, 0))
+    small_received = swap_bits(small, (0, 1))
     panel_pieces = []
     for side, (parts, others) in enumerate(((part_a, far_a), (part_b, far_b))):
         for index, (part, other) in enumerate(zip(parts, others)):
@@ -1368,7 +1375,6 @@
     small = small + small_received
     text_part = fold(text_part, text_orders, 0)
     text_received = swap_bit(text_part[high_count:], 3)
-    small = small + swap_bits(small, (0, 1))
     small = small + swap_bits(small, (1, 2))
     small = small + swap_bit(small, 3)
     own_text = text_part[:high_count].astype(f32) + text_received.astype(f32)
@@ -1376,10 +1382,15 @@
         small = small + swap_bit(small, bit)
     own_text = fold_high(own_text)
     own_text = by_core(core, own_text, swap_core(own_text))
-    small = by_core(core, small[None], swap_core(small)[None]).reshape(2, -1)
-    vector_sum = small[:, :vector_half].reshape(-1)
-    tables = small[:, vector_half:].reshape(2, GROUPS, token_half)
-    modulation_grad = jnp.concatenate([tables[0], tables[1]], axis=1)
+    small = by_core(core, small, swap_core(small), axis=1)
+    modulation_grad = small[:GROUPS]
+    vector_sum = jnp.concatenate(
+        [
+            small[GROUPS + row, which * token_half : which * token_half + min(token_half, vector_half - row * token_half)]
+            for which in range(2)
+            for row in range(2)
+        ]
+    )
     vector_gradient = jnp.concatenate([vector_sum, jnp.sum(modulation_grad, axis=0)]) / utterances
 
     own_text = own_text / utterances

time: 366 us -> 355 us (0.970)
  local copies, waits for them, and re-layouts: 47.2 us -> 36.4 us
  starting transfers between devices: 66.7 us -> 72.2 us
    unnamed x218 -> x182, local copies, waits for them, and re-layouts: 28.3 us -> 22.6 us
  transfers between devices with their start and end apart: 63 -> 63, of which waited for: 27 -> 24; matrix products, arithmetic and copies ran while one was open for 13% -> 12% of each run, Pallas kernels for 18% -> 19%
where the time goes in v6:
time: 355 us; the launch traced here: 349 us
  Pallas kernels  118 us (33%)
  waiting for transfers between devices  81.9 us (23%)
  starting transfers between devices  72.2 us (20%)
  local copies, waits for them, and re-layouts  36.4 us (10%)
  other arithmetic  33.6 us (9%)
  between operations  3.95 us (1%)
    ppermute x46, waiting for transfers between devices, swap_bits(): return lax.ppermute(array, ('dp', 'mp'), pairs)  69.9 us
    ppermute x46, starting transfers between devices, swap_bits(): return lax.ppermute(array, ('dp', 'mp'), pairs)  67.7 us
    pallas_call x6, Pallas kernels, in_vmem(): pl.pallas_call(kernel, in_specs=specs or [whole] * len(inputs), out_specs...  33.5 us
    pallas_call x2, Pallas kernels, attend_backward(): pl.pallas_call(attend_back_kernel, grid=(pairs,), in_specs=[tall(2 * PAIR...  28.4 us
    unnamed x182, local copies, waits for them, and re-layouts  22.6 us
    pallas_call x2, Pallas kernels, panel_gradients(): pl.pallas_call(lambda *refs: gradients_kernel(panel_rows, cuts, lefts, ri...  17.3 us
    pallas_call x1, Pallas kernels, attend_forward(): pl.pallas_call(attend_kernel, grid=(pairs,), in_specs=[tall(PAIR), tall(P...  13.3 us
    ppermute x17, waiting for transfers between devices, swap_core(): return lax.ppermute(array, 'mp', [(0, 1), (1, 0)])  12.1 us
  transfers between devices with their start and end apart: 63, of which 24 were waited for; matrix products, arithmetic and copies ran while one was open for 12% of the time, Pallas kernels for 19%

profile of v6, /device:TPU:0, one launch (start us, length us, event | category | flops | bytes accessed | tf_op | source)
XLA Modules:
  0.0 348.6 jit_solution(2036154612255811465)
XLA Ops:
  1.6 4.1 %collective-permute-start = (bf16[1,48,1024]{2,1,0:T(8,128)(2,1)S(1)}, bf16[1,48,1024]{2,1,0:T(8,128)(2,1)S(1)}, u32[]{:S(2)}, u32[]{:S(2)}) collective-permute-start(bf16[1,48,1024]{2,1,0:T(8,128)(2,1)S(1)} %fusion.38), channel_id=1, source_target_pairs={{0,16},{1,17},{2,18},{3,19},{4,20},{5,21},{6,22},{7,23},{8,24},{9,... | collective-permute-start | bytes 294920 | tf_op jit(solution)/shard_map/ppermute | solution.py:38
  10.6 4.5 %collective-permute-done.1 = f32[8,3072]{1,0:T(8,128)S(1)} collective-permute-done((f32[8,3072]{1,0:T(8,128)S(1)}, f32[8,3072]{1,0:T(8,128)S(1)}, u32[]{:S(2)}, u32[]{:S(2)}) %collective-permute-start.1) | collective-permute-done | bytes 98336 | tf_op jit(solution)/shard_map/ppermute | solution.py:38
  15.8 1.7 collective-permute-start.3
  17.4 5.4 %collective-permute-done.3 = f32[8,3072]{1,0:T(8,128)S(1)} collective-permute-done((f32[8,3072]{1,0:T(8,128)S(1)}, f32[8,3072]{1,0:T(8,128)S(1)}, u32[]{:S(2)}, u32[]{:S(2)}) %collective-permute-start.3) | collective-permute-done | bytes 98336 | tf_op jit(solution)/shard_map/ppermute | solution.py:38
  25.8 1.8 collective-permute-start.5
  27.6 3.4 collective-permute-start.8
  31.6 1.6 collective-permute-start.7
  33.2 3.2 collective-permute-done.7
  36.4 1.8 collective-permute-done.8
  39.2 1.5 collective-permute-start.11
  42.6 1.6 collective-permute-start.13
  44.3 1.6 collective-permute-start.10
  45.9 1.7 collective-permute-start.16
  48.8 2.2 fusion.60
  51.1 5.9 %collective-permute-done.16 = bf16[1,176,512]{2,1,0:T(8,128)(2,1)} collective-permute-done((bf16[1,176,512]{2,1,0:T(8,128)(2,1)}, bf16[1,176,512]{2,1,0:T(8,128)(2,1)}, u32[]{:S(2)}, u32[]{:S(2)}) %collective-permute-start.16) | collective-permute-done | bytes 180256 | tf_op jit(solution)/shard_map/ppermute | solution.py:38
  57.0 1.5 collective-permute-start.12
  59.6 1.5 collective-permute-start.17
  61.6 1.5 collective-permute-start.14
  64.4 2.5 collective-permute-start.18
  68.0 1.6 collective-permute-start.19
  71.2 6.9 %collective-permute-done.14 = bf16[1,336,512]{2,1,0:T(8,128)(2,1)S(1)} collective-permute-done((bf16[1,336,512]{2,1,0:T(8,128)(2,1)}, bf16[1,336,512]{2,1,0:T(8,128)(2,1)S(1)}, u32[]{:S(2)}, u32[]{:S(2)}) %collective-permute-start.14) | collective-permute-done | bytes 344096 | tf_op jit(solution)/shard_map/ppermute | solution.py:38
  85.7 7.4 %collective-permute-done.15 = bf16[2,1,336,512]{3,2,0,1:T(8,128)(2,1)S(1)} collective-permute-done((bf16[2,1,336,512]{3,2,0,1:T(8,128)(2,1)S(1)}, bf16[2,1,336,512]{3,2,0,1:T(8,128)(2,1)S(1)}, u32[]{:S(2)}, u32[]{:S(2)}) %collective-permute-start.15) | collective-permute-done | bytes 688160 | tf_op jit(solution)/shard_map/ppermute | solution.py:38
  99.0 1.9 constant_dynamic-slice_fusion.2
  102.9 7.5 %text_forward.1 = (f32[512,1024]{1,0:T(8,128)S(1)}, f32[1,1024]{1,0:T(1,128)S(1)}, bf16[512,1024]{1,0:T(8,128)(2,1)S(1)}, bf16[512,512]{1,0:T(8,128)(2,1)S(1)}, ...) custom-call(s32[1]{0:T(128)} %bitcast.core_ref, ...), custom_call_target="tpu_custom_call" | custom-call | flops 1000 | bytes 1000 | tf_op jit(solution)/shard_map/text_forward/pallas_call | solution.py:597
  115.5 1.5 copy-done.29
  117.9 7.0 %project.1 = (bf16[1024,512]{1,0:T(8,128)(2,1)S(1)}, bf16[1024,512]{1,0:T(8,128)(2,1)S(1)}, bf16[1024,512]{1,0:T(8,128)(2,1)S(1)}, bf16[8192,512]{1,0:T(8,128)(2,1)S(1)}) custom-call(s32[64]{0:T(128)S(1)} %pad_add_fusion.1.refs_0_, bf16[4,336,512]{2,1,0:T(8,128)(2,1)S(1)} %bitcast.200, bf16[4,176,512]{2,1,0:T(8,128)(2,1)S(1)} %bitcast.203, ...), custom_call_target="tpu_custom_call" | custom-call | flops 3221225472 | bytes 25165824 | tf_op jit(solution)/shard_map/project/pallas_call | solution.py:441
  125.1 13.3 %attend.1 = (bf16[1024,512]{1,0:T(8,128)(2,1)S(1)}, bf16[1024,1024]{1,0:T(8,128)(2,1)S(1)}) custom-call(bf16[1024,512]{1,0:T(8,128)(2,1)S(1)} %get-tuple-element.214.q_ref, bf16[1024,512]{1,0:T(8,128)(2,1)S(1)} %get-tuple-element.215.k_ref.kr_ref, bf16[1024,512]{1,0:T(8,128)(2,1)S(1)} %get-tuple-element.216.v_ref, ...), custom_call_target="tpu_custom_call" | custom-call | flops 17179869184 | bytes 6291456 | tf_op jit(solution)/shard_map/attend/pallas_call | solution.py:276
  139.3 2.6 collective-permute-done.24
  143.9 2.5 collective-permute-done.25.n_ref
  146.4 4.8 %feed.3 = (bf16[512,1024]{1,0:T(8,128)(2,1)S(1)}, bf16[512,1024]{1,0:T(8,128)(2,1)S(1)}, bf16[512,1024]{1,0:T(8,128)(2,1)S(1)}, bf16[512,1024]{1,0:T(8,128)(2,1)...) custom-call(bf16[512,1024]{1,0:T(8,128)(2,1)S(1)} %collective-permute-done.25.n_ref, ...), custom_call_target="tpu_custom_call" | custom-call | flops 4294967296 | bytes 8388608 | tf_op jit(solution)/shard_map/feed/pallas_call | solution.py:482
  151.8 4.8 %feed.2 = (f32[512,1024]{1,0:T(8,128)S(1)}, f32[512,1024]{1,0:T(8,128)S(1)}, bf16[512,1024]{1,0:T(8,128)(2,1)S(1)}, bf16[512,1024]{1,0:T(8,128)(2,1)S(1)}, bf16[...) custom-call(bf16[512,1024]{1,0:T(8,128)(2,1)S(1)} %add_convert_fusion.1.n_ref, ...), custom_call_target="tpu_custom_call" | custom-call | flops 4294967296 | bytes 8388608 | tf_op jit(solution)/shard_map/feed/pallas_call | solution.py:482
  158.0 1.6 copy-done.23
  159.6 3.6 %settle.1 = (bf16[512,1024]{1,0:T(8,128)(2,1)}, f32[512,1024]{1,0:T(8,128)S(1)}, bf16[512,1024]{1,0:T(8,128)(2,1)S(1)}, f32[4,1024]{1,0:T(4,128)S(1)}, bf16[1024,1024]{1,0:T(8,128)(2,1)}) custom-call(s32[1]{0:T(128)} %bitcast.core_ref, f32[512,1024]{1,0:T(8,128)S(1)} %get-tuple-element.222.my_out_ref, ...), custom_call_target="tpu_custom_call" | custom-call | flops 1000 | bytes 1000 | tf_op jit(solution)/shard_map/settle/pallas_call | solution.py:597
  164.7 2.4 collective-permute-done.28.other_ref
  167.2 14.4 %attend_back.2 = (bf16[1024,256]{1,0:T(8,128)(2,1)S(1)}, bf16[1024,256]{1,0:T(8,128)(2,1)S(1)}, bf16[1024,256]{1,0:T(8,128)(2,1)S(1)}, bf16[1024,512]{1,0:T(8,128)(2,1)S(1)}, bf16[1024,512]{1,0:T(8,128)(2,1)S(1)}) custom-call(bf16[1024,1024]{1,0:T(8,128)(2,1)S(1)} %get-tuple-element.245.qa_ref, bf16[1024,512]{1,0:T(8,128)(2,1)S(1)} %get-tuple-element.215.k_ref.kr_ref, ...), custom_call_target="tpu_custom_call" | custom-call | flops 1000 | bytes 1000 | tf_op jit(solution)/shard_map/attend_back/pallas_call | solution.py:367
  181.6 8.0 %gradients.2 = (bf16[8,336,256]{2,1,0:T(8,128)(2,1)S(1)}, bf16[8,176,256]{2,1,0:T(8,128)(2,1)S(1)}, bf16[8,336,256]{2,1,0:T(8,128)(2,1)S(1)}, bf16[8,176,256]{2,1,0:T(8,128)(2,1)S(1)}) custom-call(s32[64]{0:T(128)S(1)} %pad_add_fusion.refs_0_, bf16[1024,512]{1,0:T(8,128)(2,1)S(1)} %get-tuple-element.200.refs_1_, ...), custom_call_target="tpu_custom_call" | custom-call | flops 1000 | bytes 1000 | tf_op jit(solution)/shard_map/gradients/pallas_call | solution.py:574
  191.6 13.9 %attend_back.3 = (bf16[1024,256]{1,0:T(8,128)(2,1)S(1)}, bf16[1024,256]{1,0:T(8,128)(2,1)S(1)}, bf16[1024,256]{1,0:T(8,128)(2,1)S(1)}) custom-call(bf16[1024,1024]{1,0:T(8,128)(2,1)S(1)} %get-tuple-element.245.qa_ref, bf16[1024,512]{1,0:T(8,128)(2,1)S(1)} %get-tuple-element.215.k_ref.kr_ref, bf16[1024,512]{1,0:T(8,128)(2,1)S(1)} %get-tuple-element.216.v_ref, ...), custom_call_target="tpu_custom_call" | custom-call | flops 1000 | bytes 1000 | tf_op jit(solution)/shard_map/attend_back/pallas_call | solution.py:367
  205.5 2.9 collective-permute-done.30
  211.3 9.3 %gradients.3 = (bf16[8,336,256]{2,1,0:T(8,128)(2,1)S(1)}, bf16[8,176,256]{2,1,0:T(8,128)(2,1)S(1)}, bf16[8,336,256]{2,1,0:T(8,128)(2,1)}, bf16[8,176,256]{2,1,0:T(8,128)(2,1)S(1)}) custom-call(s32[64]{0:T(128)S(1)} %pad_add_fusion.refs_0_, bf16[1024,512]{1,0:T(8,128)(2,1)S(1)} %get-tuple-element.200.refs_1_, ...), custom_call_target="tpu_custom_call" | custom-call | flops 1000 | bytes 1000 | tf_op jit(solution)/shard_map/gradients/pallas_call | solution.py:574
  223.7 3.8 %inputs_grad.1 = (f32[512,1024]{1,0:T(8,128)S(1)}, bf16[512,1024]{1,0:T(8,128)(2,1)}) custom-call(bf16[1024,256]{1,0:T(8,128)(2,1)S(1)} %get-tuple-element.266.refs_9_.refs_0_, bf16[1024,256]{1,0:T(8,128)(2,1)S(1)} %get-tuple-element.267.refs_10_.refs_1_, bf16[1024,256]{1,0:T(8,128)(2,1)S(1)} %get-tuple-element.268.refs_11_.refs_2_, ...), custom_call_target="tpu_custom_call" | custom-call | flops 1000 | bytes 1000 | tf_op jit(solution)/shard_map/inputs_grad/pallas_call | solution.py:515
  233.2 2.3 constant_dynamic-update-slice_fusion.9
  237.7 1.6 copy-done.5
  239.3 1.6 copy-done.19
  240.9 1.6 copy-done.21
  242.5 5.7 %stream_back.1 = (f32[512,1024]{1,0:T(8,128)S(1)}, bf16[512,1024]{1,0:T(8,128)(2,1)S(1)}, f32[512,512]{1,0:T(8,128)S(1)}, bf16[512,512]{1,0:T(8,128)(2,1)S(1)}, ...) custom-call(s32[1]{0:T(128)} %bitcast.core_ref, ...), custom_call_target="tpu_custom_call" | custom-call | flops 1000 | bytes 1000 | tf_op jit(solution)/shard_map/stream_back/pallas_call | solution.py:597
  248.2 2.7 collective-permute-done.36
  250.9 1.8 fusion.1
  255.2 4.1 %collective-permute-start.40 = (bf16[1,336,256]{2,1,0:T(8,128)(2,1)S(1)}, bf16[1,336,256]{2,1,0:T(8,128)(2,1)S(1)}, u32[]{:S(2)}, u32[]{:S(2)}) collective-permute-start(bf16[1,336,256]{2,1,0:T(8,128)(2,1)S(1)} %get-tuple-element.393), channel_id=1, source_target_pairs={{0,16},{1,17},{2,18},{3,19},{4,20},{5,21},{6,22},{7,23},{8,24},{9,... | collective-permute-start | bytes 516104 | tf_op jit(solution)/shard_map/ppermute | solution.py:38
  260.5 1.9 collective-permute-start.41
  262.4 6.9 %text_back.1 = (f32[512,512]{1,0:T(8,128)S(1)}, f32[3,512]{1,0:T(4,128)S(1)}, f32[2,1024]{1,0:T(2,128)S(1)}, bf16[16,48,1024]{2,1,0:T(8,128)(2,1)S(1)}, bf16[16,48,1024]{2,1,0:T(8,128)(2,1)}) custom-call(f32[512,1024]{1,0:T(8,128)S(1)} %copy-done.6, f32[512,1024]{1,0:T(8,128)S(1)} %get-tuple-element.290.grn_grad_ref, ...), custom_call_target="tpu_custom_call" | custom-call | flops 1000 | bytes 1000 | tf_op jit(solution)/shard_map/text_back/pallas_call | solution.py:597
  271.5 2.4 collective-permute-start.44
  276.1 2.2 collective-permute-done.47.border_ref
  278.3 4.5 %conv_back.1 = (f32[512,512]{1,0:T(8,128)S(1)}, f32[7,512]{1,0:T(8,128)S(1)}, f32[1024,512]{1,0:T(8,128)}) custom-call(s32[1]{0:T(128)} %bitcast.core_ref, f32[512,512]{1,0:T(8,128)S(1)} %get-tuple-element.305.mixed_ref, f32[8,512]{1,0:T(8,128)S(1)} %collective-permute-done.47.border_ref, f32[528,512]{1,0:T(8,128)S(1)} %get-tuple-element.370.window_ref, ...), custom_call_target="tpu_custom_call" | custom-call | flops 1000 | bytes 1000 | tf_op jit(solution)/shard_map/conv_back/pallas_call | solution.py:597
  286.7 2.2 add_convert_fusion
  290.3 3.5 collective-permute-start.49
  297.3 9.0 %collective-permute-done.50 = bf16[1,176,256]{2,1,0:T(8,128)(2,1)S(1)} collective-permute-done((bf16[1,176,256]{2,1,0:T(8,128)(2,1)S(1)}, bf16[1,176,256]{2,1,0:T(8,128)(2,1)S(1)}, u32[]{:S(2)}, u32[]{:S(2)}) %collective-permute-start.50) | collective-permute-done | bytes 90144 | tf_op jit(solution)/shard_map/ppermute | solution.py:38
  309.6 5.3 %rotated_step.1 = (f32[512,512]{1,0:T(8,128)}, f32[512,512]{1,0:T(8,128)}, f32[512,512]{1,0:T(8,128)}) custom-call(bf16[336,256]{1,0:T(8,128)(2,1)S(1)} %get-tuple-element.392.refs_0_, bf16[336,256]{1,0:T(8,128)(2,1)S(1)} %bitcast.206, bf16[176,256]{1,0:T(8,128)(2,1)S(1)} %get-tuple-element.398.refs_2_, bf16[176,256]{1,0:T(8,128)(2,1)S(1)} %bitcast.208, ...), custom_call_target="tpu_custom_call" | custom-call | flops 1000 | bytes 1000 | tf_op jit(solution)/shard_map/rotated_step/pallas_call | solution.py:597
  315.0 2.4 collective-permute-done.56
  319.7 4.6 %collective-permute-done.60 = f32[10,3072]{1,0:T(8,128)S(1)} collective-permute-done((f32[10,3072]{1,0:T(8,128)S(1)}, f32[10,3072]{1,0:T(8,128)S(1)}, u32[]{:S(2)}, u32[]{:S(2)}) %collective-permute-start.60) | collective-permute-done | bytes 122912 | tf_op jit(solution)/shard_map/ppermute | solution.py:38
  324.3 2.0 collective-permute-start.61
  326.4 1.9 collective-permute-start.58
  328.3 10.4 %collective-permute-done.61 = f32[10,3072]{1,0:T(8,128)S(1)} collective-permute-done((f32[10,3072]{1,0:T(8,128)S(1)}, f32[10,3072]{1,0:T(8,128)S(1)}, u32[]{:S(2)}, u32[]{:S(2)}) %collective-permute-start.61) | collective-permute-done | bytes 122912 | tf_op jit(solution)/shard_map/ppermute | solution.py:38
  338.7 1.6 collective-permute-start.62
  342.4 4.4 %modulation_step.1 = (f32[64,6144]{1,0:T(8,128)}, f32[64,6144]{1,0:T(8,128)}, f32[64,6144]{1,0:T(8,128)}) custom-call(bf16[8,64]{1,0:T(8,128)(2,1)S(1)} %multiply_convert_fusion.2.refs_0_, bf16[8,6144]{1,0:T(8,128)(2,1)S(1)} %slice.590.refs_1_, f32[64,6144]{1,0:T(8,128)S(1)} %copy-done.16, f32[64,6144]{1,0:T(8,128)S(1)} %copy-done.26, f32[64,6144]{1,0:T(8,128)S(1)} %copy-done.27), custom_call_target="tpu_custom_call" | custom-call | flops 1000 | bytes 1000 | tf_op jit(solution)/shard_map/modulation_step/pallas_call | solution.py:935
  (400 shorter events, 87.1 us)
Async XLA Ops:
  1.6 9.0 %collective-permute-start = (bf16[1,48,1024]{2,1,0:T(8,128)(2,1)S(1)}, bf16[1,48,1024]{2,1,0:T(8,128)(2,1)S(1)}, u32[]{:S(2)}, u32[]{:S(2)}) collective-permute-start(bf16[1,48,1024]{2,1,0:T(8,128)(2,1)S(1)} %fusion.38), channel_id=1, source_target_pairs={{0,16},{1,17},{2,18},{3,19},{4,20},{5,21},{6,22},{7,23},{8,24},{9,... | collective-permute-start | bytes 294920 | tf_op jit(solution)/shard_map/ppermute | solution.py:38
  7.8 7.3 %collective-permute-start.1 = (f32[8,3072]{1,0:T(8,128)S(1)}, f32[8,3072]{1,0:T(8,128)S(1)}, u32[]{:S(2)}, u32[]{:S(2)}) collective-permute-start(f32[8,3072]{1,0:T(8,128)S(1)} %fusion.32), channel_id=1, source_target_pairs={{0,16},{1,17},{2,18},{3,19},{4,20},{5,21},{6,22},{7,23},{8,24},{9,... | collective-permute-start | bytes 294920 | tf_op jit(solution)/shard_map/ppermute | solution.py:38
  15.2 7.7 %collective-permute-start.2 = (bf16[2,48,1024]{2,1,0:T(8,128)(2,1)S(1)}, bf16[2,48,1024]{2,1,0:T(8,128)(2,1)S(1)}, u32[]{:S(2)}, u32[]{:S(2)}) collective-permute-start(bf16[2,48,1024]{2,1,0:T(8,128)(2,1)S(1)} %get-tuple-element.395), channel_id=1, source_target_pairs={{0,8},{1,9},{2,10},{3,11},{4,12},{5,13},{6,14},{7,15},{8,0},{9,1},... | collective-permute-start | bytes 589832 | tf_op jit(solution)/shard_map/ppermute | solution.py:38
  15.8 7.1 %collective-permute-start.3 = (f32[8,3072]{1,0:T(8,128)S(1)}, f32[8,3072]{1,0:T(8,128)S(1)}, u32[]{:S(2)}, u32[]{:S(2)}) collective-permute-start(f32[8,3072]{1,0:T(8,128)S(1)} %add.507), channel_id=1, source_target_pairs={{0,8},{1,9},{2,10},{3,11},{4,12},{5,13},{6,14},{7,15},{8,0},{9,1},... | collective-permute-start | bytes 294920 | tf_op jit(solution)/shard_map/ppermute | solution.py:38
  23.6 14.5 %collective-permute-start.4 = (bf16[1,336,512]{2,1,0:T(8,128)(2,1)}, bf16[1,336,512]{2,1,0:T(8,128)(2,1)S(1)}, u32[]{:S(2)}, u32[]{:S(2)}) collective-permute-start(bf16[1,336,512]{2,1,0:T(8,128)(2,1)} %get-tuple-element.381), channel_id=1, source_target_pairs={{0,2},{1,5},{2,0},{3,7},{4,6},{5,1},{6,4},{7,3},{8,10},{9,13},{10,... | collective-permute-start | bytes 1032200 | tf_op jit(solution)/shard_map/ppermute | solution.py:38
  25.2 13.0 %collective-permute-start.6 = (bf16[2,2,48,1024]{3,2,1,0:T(8,128)(2,1)S(1)}, bf16[2,2,48,1024]{3,2,1,0:T(8,128)(2,1)S(1)}, u32[]{:S(2)}, u32[]{:S(2)}) collective-permute-start(bf16[2,2,48,1024]{3,2,1,0:T(8,128)(2,1)S(1)} %get-tuple-element.385), channel_id=1, source_target_pairs={{0,2},{1,5},{2,0},{3,7},{4,6},{5,1},{6,4},{7,3},{8,10},{9,13},{10,... | collective-permute-start | bytes 1179656 | tf_op jit(solution)/shard_map/ppermute | solution.py:38
  25.8 10.6 %collective-permute-start.5 = (bf16[1,176,512]{2,1,0:T(8,128)(2,1)S(1)}, bf16[1,176,512]{2,1,0:T(8,128)(2,1)S(1)}, u32[]{:S(2)}, u32[]{:S(2)}) collective-permute-start(bf16[1,176,512]{2,1,0:T(8,128)(2,1)S(1)} %get-tuple-element.379), channel_id=1, source_target_pairs={{0,8},{1,9},{2,10},{3,11},{4,12},{5,13},{6,14},{7,15},{8,0},{9,1},... | collective-permute-start | bytes 540680 | tf_op jit(solution)/shard_map/ppermute | solution.py:38
  27.6 10.5 %collective-permute-start.8 = (bf16[1,176,512]{2,1,0:T(8,128)(2,1)S(1)}, bf16[1,176,512]{2,1,0:T(8,128)(2,1)}, u32[]{:S(2)}, u32[]{:S(2)}) collective-permute-start(bf16[1,176,512]{2,1,0:T(8,128)(2,1)S(1)} %get-tuple-element.379), channel_id=1, source_target_pairs={{0,16},{1,17},{2,18},{3,19},{4,20},{5,21},{6,22},{7,23},{8,24},{9,... | collective-permute-start | bytes 540680 | tf_op jit(solution)/shard_map/ppermute | solution.py:38
  31.6 4.8 %collective-permute-start.7 = (f32[8,3072]{1,0:T(8,128)S(1)}, f32[8,3072]{1,0:T(8,128)S(1)}, u32[]{:S(2)}, u32[]{:S(2)}) collective-permute-start(f32[8,3072]{1,0:T(8,128)S(1)} %add.508), channel_id=1, source_target_pairs={{0,2},{1,5},{2,0},{3,7},{4,6},{5,1},{6,4},{7,3},{8,10},{9,13},{10,... | collective-permute-start | bytes 294920 | tf_op jit(solution)/shard_map/ppermute | solution.py:38
  39.2 22.5 %collective-permute-start.11 = (bf16[2,2,2,48,1024]{4,3,2,1,0:T(8,128)(2,1)}, bf16[2,2,2,48,1024]{4,3,2,1,0:T(8,128)(2,1)S(1)}, u32[]{:S(2)}, u32[]{:S(2)}) collective-permute-start(bf16[2,2,2,48,1024]{4,3,2,1,0:T(8,128)(2,1)} %get-tuple-element.373), channel_id=1, source_target_pairs={{0,4},{1,3},{2,6},{3,1},{4,0},{5,7},{6,2},{7,5},{8,12},{9,11},{10,... | collective-permute-start | bytes 2359304 | tf_op jit(solution)/shard_map/ppermute | solution.py:38
  41.6 20.0 %collective-permute-start.9 = (bf16[2,1,336,512]{3,2,0,1:T(8,128)(2,1)}, bf16[2,1,336,512]{3,2,0,1:T(8,128)(2,1)}, u32[]{:S(2)}, u32[]{:S(2)}) collective-permute-start(bf16[2,1,336,512]{3,2,0,1:T(8,128)(2,1)} %get-tuple-element.377), channel_id=1, source_target_pairs={{0,4},{1,9},{2,6},{3,11},{4,0},{5,13},{6,2},{7,15},{8,12},{9,1},{1... | collective-permute-start | bytes 2064392 | tf_op jit(solution)/shard_map/ppermute | solution.py:38
  42.6 17.0 %collective-permute-start.13 = (bf16[1,336,512]{2,1,0:T(8,128)(2,1)}, bf16[1,336,512]{2,1,0:T(8,128)(2,1)}, u32[]{:S(2)}, u32[]{:S(2)}) collective-permute-start(bf16[1,336,512]{2,1,0:T(8,128)(2,1)} %get-tuple-element.381), channel_id=1, source_target_pairs={{0,16},{1,17},{2,18},{3,19},{4,20},{5,21},{6,22},{7,23},{8,24},{9,... | collective-permute-start | bytes 1032200 | tf_op jit(solution)/shard_map/ppermute | solution.py:38
  44.3 17.3 %collective-permute-start.10 = (bf16[2,1,176,512]{3,2,0,1:T(8,128)(2,1)S(1)}, bf16[2,1,176,512]{3,2,0,1:T(8,128)(2,1)}, u32[]{:S(2)}, u32[]{:S(2)}) collective-permute-start(bf16[2,1,176,512]{3,2,0,1:T(8,128)(2,1)S(1)} %get-tuple-element.389), channel_id=1, source_target_pairs={{0,2},{1,3},{2,0},{3,1},{4,6},{5,7},{6,4},{7,5},{8,10},{9,11},{10,... | collective-permute-start | bytes 1081352 | tf_op jit(solution)/shard_map/ppermute | solution.py:38
  45.9 11.1 %collective-permute-start.16 = (bf16[1,176,512]{2,1,0:T(8,128)(2,1)}, bf16[1,176,512]{2,1,0:T(8,128)(2,1)}, u32[]{:S(2)}, u32[]{:S(2)}) collective-permute-start(bf16[1,176,512]{2,1,0:T(8,128)(2,1)} %collective-permute-done.8), channel_id=1, source_target_pairs={{0,8},{1,9},{2,10},{3,11},{4,12},{5,13},{6,14},{7,15},{8,0},{9,1},... | collective-permute-start | bytes 540680 | tf_op jit(solution)/shard_map/ppermute | solution.py:38
  57.0 4.6 %collective-permute-start.12 = (f32[8,3072]{1,0:T(8,128)S(1)}, f32[8,3072]{1,0:T(8,128)S(1)}, u32[]{:S(2)}, u32[]{:S(2)}) collective-permute-start(f32[8,3072]{1,0:T(8,128)S(1)} %add.509), channel_id=1, source_target_pairs={{0,4},{1,3},{2,6},{3,1},{4,0},{5,7},{6,2},{7,5},{8,12},{9,11},{10,... | collective-permute-start | bytes 294920 | tf_op jit(solution)/shard_map/ppermute | solution.py:38
  59.6 26.1 %collective-permute-start.17 = (bf16[2,1,176,512]{3,2,0,1:T(8,128)(2,1)S(1)}, bf16[2,1,176,512]{3,2,0,1:T(8,128)(2,1)S(1)}, u32[]{:S(2)}, u32[]{:S(2)}) collective-permute-start(bf16[2,1,176,512]{3,2,0,1:T(8,128)(2,1)S(1)} %get-tuple-element.387), channel_id=1, source_target_pairs={{0,2},{1,3},{2,0},{3,1},{4,6},{5,7},{6,4},{7,5},{8,10},{9,11},{10,... | collective-permute-start | bytes 1081352 | tf_op jit(solution)/shard_map/ppermute | solution.py:38
  61.6 16.4 %collective-permute-start.14 = (bf16[1,336,512]{2,1,0:T(8,128)(2,1)}, bf16[1,336,512]{2,1,0:T(8,128)(2,1)S(1)}, u32[]{:S(2)}, u32[]{:S(2)}) collective-permute-start(bf16[1,336,512]{2,1,0:T(8,128)(2,1)} %collective-permute-done.13), channel_id=1, source_target_pairs={{0,2},{1,5},{2,0},{3,7},{4,6},{5,1},{6,4},{7,3},{8,10},{9,13},{10,... | collective-permute-start | bytes 1032200 | tf_op jit(solution)/shard_map/ppermute | solution.py:38
  64.4 28.7 %collective-permute-start.18 = (bf16[2,2,1,336,512]{4,3,1,2,0:T(8,128)(2,1)S(1)}, bf16[2,2,1,336,512]{4,3,1,2,0:T(8,128)(2,1)S(1)}, u32[]{:S(2)}, u32[]{:S(2)}) collective-permute-start(bf16[2,2,1,336,512]{4,3,1,2,0:T(8,128)(2,1)S(1)} %pad_maximum_fusion.2), channel_id=1, source_target_pairs={{0,8},{1,3},{2,10},{3,1},{4,12},{5,7},{6,14},{7,5},{8,0},{9,11},{1... | collective-permute-start | bytes 4128776 | tf_op jit(solution)/shard_map/ppermute | solution.py:38
  68.0 17.7 %collective-permute-start.19 = (bf16[2,2,1,176,512]{4,3,1,2,0:T(8,128)(2,1)S(1)}, bf16[2,2,1,176,512]{4,3,1,2,0:T(8,128)(2,1)S(1)}, u32[]{:S(2)}, u32[]{:S(2)}) collective-permute-start(bf16[2,2,1,176,512]{4,3,1,2,0:T(8,128)(2,1)S(1)} %pad_maximum_fusion.6), channel_id=1, source_target_pairs={{0,4},{1,5},{2,6},{3,7},{4,0},{5,1},{6,2},{7,3},{8,12},{9,13},{10,... | collective-permute-start | bytes 2162696 | tf_op jit(solution)/shard_map/ppermute | solution.py:38
  69.6 1.4 collective-permute-start.21
  71.0 22.1 %collective-permute-start.20 = (bf16[16,48,1024]{2,1,0:T(8,128)(2,1)S(1)}, bf16[16,48,1024]{2,1,0:T(8,128)(2,1)S(1)}, u32[]{:S(2)}, u32[]{:S(2)}) collective-permute-start(bf16[16,48,1024]{2,1,0:T(8,128)(2,1)S(1)} %bitcast.198), channel_id=1, source_target_pairs={{0,1},{1,0},{2,3},{3,2},{4,5},{5,4},{6,7},{7,6},{8,9},{9,8},{10,11... | collective-permute-start | bytes 4718600 | tf_op jit(solution)/shard_map/ppermute | solution.py:30
  79.2 14.0 %collective-permute-start.15 = (bf16[2,1,336,512]{3,2,0,1:T(8,128)(2,1)S(1)}, bf16[2,1,336,512]{3,2,0,1:T(8,128)(2,1)S(1)}, u32[]{:S(2)}, u32[]{:S(2)}) collective-permute-start(bf16[2,1,336,512]{3,2,0,1:T(8,128)(2,1)S(1)} %get-tuple-element.375), channel_id=1, source_target_pairs={{0,4},{1,9},{2,6},{3,11},{4,0},{5,13},{6,2},{7,15},{8,12},{9,1},{1... | collective-permute-start | bytes 2064392 | tf_op jit(solution)/shard_map/ppermute | solution.py:38
  94.5 20.7 %collective-permute-start.22 = (bf16[2,2,1,336,512]{4,3,1,2,0:T(8,128)(2,1)}, bf16[2,2,1,336,512]{4,3,1,2,0:T(8,128)(2,1)}, u32[]{:S(2)}, u32[]{:S(2)}) collective-permute-start(bf16[2,2,1,336,512]{4,3,1,2,0:T(8,128)(2,1)} %pad_maximum_fusion.3), channel_id=1, source_target_pairs={{0,8},{1,3},{2,10},{3,1},{4,12},{5,7},{6,14},{7,5},{8,0},{9,11},{1... | collective-permute-start | bytes 4128776 | tf_op jit(solution)/shard_map/ppermute | solution.py:38
  96.5 18.7 %collective-permute-start.23 = (bf16[2,2,1,176,512]{4,3,1,2,0:T(8,128)(2,1)}, bf16[2,2,1,176,512]{4,3,1,2,0:T(8,128)(2,1)}, u32[]{:S(2)}, u32[]{:S(2)}) collective-permute-start(bf16[2,2,1,176,512]{4,3,1,2,0:T(8,128)(2,1)} %pad_maximum_fusion.7), channel_id=1, source_target_pairs={{0,4},{1,5},{2,6},{3,7},{4,0},{5,1},{6,2},{7,3},{8,12},{9,13},{10,... | collective-permute-start | bytes 2162696 | tf_op jit(solution)/shard_map/ppermute | solution.py:38
  113.5 28.4 %copy-start.2 = (f32[512,1024]{1,0:T(8,128)}, f32[512,1024]{1,0:T(8,128)S(1)}, u32[]{:S(2)}) copy-start(f32[512,1024]{1,0:T(8,128)S(1)} %get-tuple-element.219.stream_ref) | copy-start | bytes 6291460
  139.2 2.7 collective-permute-start.24
  143.7 2.7 collective-permute-start.25
  151.2 6.7 %collective-permute-start.26 = (bf16[512,1024]{1,0:T(8,128)(2,1)S(1)}, bf16[512,1024]{1,0:T(8,128)(2,1)S(1)}, u32[]{:S(2)}, u32[]{:S(2)}) collective-permute-start(bf16[512,1024]{1,0:T(8,128)(2,1)S(1)} %get-tuple-element.224), channel_id=1, source_target_pairs={{0,1},{1,0},{2,3},{3,2},{4,5},{5,4},{6,7},{7,6},{8,9},{9,8},{10,11... | collective-permute-start | bytes 3145736 | tf_op jit(solution)/shard_map/ppermute | solution.py:30
  151.4 6.5 %collective-permute-start.27 = (bf16[512,1024]{1,0:T(8,128)(2,1)S(1)}, bf16[512,1024]{1,0:T(8,128)(2,1)S(1)}, u32[]{:S(2)}, u32[]{:S(2)}) collective-permute-start(bf16[512,1024]{1,0:T(8,128)(2,1)S(1)} %get-tuple-element.226), channel_id=1, source_target_pairs={{0,1},{1,0},{2,3},{3,2},{4,5},{5,4},{6,7},{7,6},{8,9},{9,8},{10,11... | collective-permute-start | bytes 3145736 | tf_op jit(solution)/shard_map/ppermute | solution.py:30
  164.5 2.7 collective-permute-start.28
  189.7 18.8 %collective-permute-start.29 = (bf16[2,2,2,336,256]{4,3,2,1,0:T(8,128)(2,1)S(1)}, bf16[2,2,2,336,256]{4,3,2,1,0:T(8,128)(2,1)S(1)}, u32[]{:S(2)}, u32[]{:S(2)}) collective-permute-start(bf16[2,2,2,336,256]{4,3,2,1,0:T(8,128)(2,1)S(1)} %bitcast.220), channel_id=1, source_target_pairs={{0,8},{1,3},{2,10},{3,1},{4,12},{5,7},{6,14},{7,5},{8,0},{9,11},{1... | collective-permute-start | bytes 4128776 | tf_op jit(solution)/shard_map/ppermute | solution.py:38
  191.0 17.5 %collective-permute-start.30 = (bf16[2,2,2,176,256]{4,3,2,1,0:T(8,128)(2,1)S(1)}, bf16[2,2,2,176,256]{4,3,2,1,0:T(8,128)(2,1)S(1)}, u32[]{:S(2)}, u32[]{:S(2)}) collective-permute-start(bf16[2,2,2,176,256]{4,3,2,1,0:T(8,128)(2,1)S(1)} %bitcast.223), channel_id=1, source_target_pairs={{0,4},{1,5},{2,6},{3,7},{4,0},{5,1},{6,2},{7,3},{8,12},{9,13},{10,... | collective-permute-start | bytes 2162696 | tf_op jit(solution)/shard_map/ppermute | solution.py:38
  208.9 11.8 %collective-permute-start.31 = (bf16[2,2,336,256]{3,2,1,0:T(8,128)(2,1)S(1)}, bf16[2,2,336,256]{3,2,1,0:T(8,128)(2,1)S(1)}, u32[]{:S(2)}, u32[]{:S(2)}) collective-permute-start(bf16[2,2,336,256]{3,2,1,0:T(8,128)(2,1)S(1)} %slice_bitcast_fusion.3), channel_id=1, source_target_pairs={{0,4},{1,9},{2,6},{3,11},{4,0},{5,13},{6,2},{7,15},{8,12},{9,1},{1... | collective-permute-start | bytes 2064392 | tf_op jit(solution)/shard_map/ppermute | solution.py:38
  210.4 10.3 %collective-permute-start.32 = (bf16[2,2,176,256]{3,2,1,0:T(8,128)(2,1)S(1)}, bf16[2,2,176,256]{3,2,1,0:T(8,128)(2,1)S(1)}, u32[]{:S(2)}, u32[]{:S(2)}) collective-permute-start(bf16[2,2,176,256]{3,2,1,0:T(8,128)(2,1)S(1)} %slice_bitcast_fusion.10), channel_id=1, source_target_pairs={{0,2},{1,3},{2,0},{3,1},{4,6},{5,7},{6,4},{7,5},{8,10},{9,11},{10,... | collective-permute-start | bytes 1081352 | tf_op jit(solution)/shard_map/ppermute | solution.py:38
  211.3 21.8 %collective-permute-start.54 = (bf16[512,1024]{1,0:T(8,128)(2,1)}, bf16[512,1024]{1,0:T(8,128)(2,1)}, u32[]{:S(2)}, u32[]{:S(2)}) collective-permute-start(bf16[512,1024]{1,0:T(8,128)(2,1)} %get-tuple-element.322), channel_id=1, source_target_pairs={{0,1},{1,0},{2,3},{3,2},{4,5},{5,4},{6,7},{7,6},{8,9},{9,8},{10,11... | collective-permute-start | bytes 3145736 | tf_op jit(solution)/shard_map/ppermute | solution.py:30
  220.9 8.2 %collective-permute-start.33 = (bf16[2,336,256]{2,1,0:T(8,128)(2,1)S(1)}, bf16[2,336,256]{2,1,0:T(8,128)(2,1)S(1)}, u32[]{:S(2)}, u32[]{:S(2)}) collective-permute-start(bf16[2,336,256]{2,1,0:T(8,128)(2,1)S(1)} %slice_bitcast_fusion.14), channel_id=1, source_target_pairs={{0,2},{1,5},{2,0},{3,7},{4,6},{5,1},{6,4},{7,3},{8,10},{9,13},{10,... | collective-permute-start | bytes 1032200 | tf_op jit(solution)/shard_map/ppermute | solution.py:38
  222.3 6.8 %collective-permute-start.34 = (bf16[2,176,256]{2,1,0:T(8,128)(2,1)S(1)}, bf16[2,176,256]{2,1,0:T(8,128)(2,1)S(1)}, u32[]{:S(2)}, u32[]{:S(2)}) collective-permute-start(bf16[2,176,256]{2,1,0:T(8,128)(2,1)S(1)} %slice_bitcast_fusion.20), channel_id=1, source_target_pairs={{0,8},{1,9},{2,10},{3,11},{4,12},{5,13},{6,14},{7,15},{8,0},{9,1},... | collective-permute-start | bytes 540680 | tf_op jit(solution)/shard_map/ppermute | solution.py:38
  229.1 21.8 %collective-permute-start.35 = (bf16[2,2,2,336,256]{4,3,2,1,0:T(8,128)(2,1)}, bf16[2,2,2,336,256]{4,3,2,1,0:T(8,128)(2,1)}, u32[]{:S(2)}, u32[]{:S(2)}) collective-permute-start(bf16[2,2,2,336,256]{4,3,2,1,0:T(8,128)(2,1)} %bitcast.60), channel_id=1, source_target_pairs={{0,8},{1,3},{2,10},{3,1},{4,12},{5,7},{6,14},{7,5},{8,0},{9,11},{1... | collective-permute-start | bytes 4128776 | tf_op jit(solution)/shard_map/ppermute | solution.py:38
  230.4 7.3 %collective-permute-start.37 = (bf16[512,1024]{1,0:T(8,128)(2,1)}, bf16[512,1024]{1,0:T(8,128)(2,1)}, u32[]{:S(2)}, u32[]{:S(2)}) collective-permute-start(bf16[512,1024]{1,0:T(8,128)(2,1)} %get-tuple-element.279), channel_id=1, source_target_pairs={{0,1},{1,0},{2,3},{3,2},{4,5},{5,4},{6,7},{7,6},{8,9},{9,8},{10,11... | collective-permute-start | bytes 3145736 | tf_op jit(solution)/shard_map/ppermute | solution.py:30
  232.1 18.7 %collective-permute-start.36 = (bf16[2,2,2,176,256]{4,3,2,1,0:T(8,128)(2,1)}, bf16[2,2,2,176,256]{4,3,2,1,0:T(8,128)(2,1)S(1)}, u32[]{:S(2)}, u32[]{:S(2)}) collective-permute-start(bf16[2,2,2,176,256]{4,3,2,1,0:T(8,128)(2,1)} %bitcast.222), channel_id=1, source_target_pairs={{0,4},{1,5},{2,6},{3,7},{4,0},{5,1},{6,2},{7,3},{8,12},{9,13},{10,... | collective-permute-start | bytes 2162696 | tf_op jit(solution)/shard_map/ppermute | solution.py:38
  252.8 17.8 %collective-permute-start.38 = (bf16[2,2,336,256]{3,2,1,0:T(8,128)(2,1)S(1)}, bf16[2,2,336,256]{3,2,1,0:T(8,128)(2,1)S(1)}, u32[]{:S(2)}, u32[]{:S(2)}) collective-permute-start(bf16[2,2,336,256]{3,2,1,0:T(8,128)(2,1)S(1)} %slice_bitcast_fusion.1), channel_id=1, source_target_pairs={{0,4},{1,9},{2,6},{3,11},{4,0},{5,13},{6,2},{7,15},{8,12},{9,1},{1... | collective-permute-start | bytes 2064392 | tf_op jit(solution)/shard_map/ppermute | solution.py:38
  253.9 16.7 %collective-permute-start.43 = (f32[512,1024]{1,0:T(8,128)S(1)}, f32[512,1024]{1,0:T(8,128)S(1)}, u32[]{:S(2)}, u32[]{:S(2)}) collective-permute-start(f32[512,1024]{1,0:T(8,128)S(1)} %get-tuple-element.300), channel_id=1, source_target_pairs={{0,1},{1,0},{2,3},{3,2},{4,5},{5,4},{6,7},{7,6},{8,9},{9,8},{10,11... | collective-permute-start | bytes 6291464 | tf_op jit(solution)/shard_map/ppermute | solution.py:30
  254.1 16.4 %collective-permute-start.39 = (bf16[2,2,176,256]{3,2,1,0:T(8,128)(2,1)S(1)}, bf16[2,2,176,256]{3,2,1,0:T(8,128)(2,1)S(1)}, u32[]{:S(2)}, u32[]{:S(2)}) collective-permute-start(bf16[2,2,176,256]{3,2,1,0:T(8,128)(2,1)S(1)} %slice_bitcast_fusion.8), channel_id=1, source_target_pairs={{0,2},{1,3},{2,0},{3,1},{4,6},{5,7},{6,4},{7,5},{8,10},{9,11},{10,... | collective-permute-start | bytes 1081352 | tf_op jit(solution)/shard_map/ppermute | solution.py:38
  255.2 15.4 %collective-permute-start.40 = (bf16[1,336,256]{2,1,0:T(8,128)(2,1)S(1)}, bf16[1,336,256]{2,1,0:T(8,128)(2,1)S(1)}, u32[]{:S(2)}, u32[]{:S(2)}) collective-permute-start(bf16[1,336,256]{2,1,0:T(8,128)(2,1)S(1)} %get-tuple-element.393), channel_id=1, source_target_pairs={{0,16},{1,17},{2,18},{3,19},{4,20},{5,21},{6,22},{7,23},{8,24},{9,... | collective-permute-start | bytes 516104 | tf_op jit(solution)/shard_map/ppermute | solution.py:38
  259.3 1.2 collective-permute-start.42
  260.5 10.1 %collective-permute-start.41 = (bf16[1,176,256]{2,1,0:T(8,128)(2,1)S(1)}, bf16[1,176,256]{2,1,0:T(8,128)(2,1)S(1)}, u32[]{:S(2)}, u32[]{:S(2)}) collective-permute-start(bf16[1,176,256]{2,1,0:T(8,128)(2,1)S(1)} %get-tuple-element.399), channel_id=1, source_target_pairs={{0,16},{1,17},{2,18},{3,19},{4,20},{5,21},{6,22},{7,23},{8,24},{9,... | collective-permute-start | bytes 270344 | tf_op jit(solution)/shard_map/ppermute | solution.py:38
  271.5 17.4 %collective-permute-start.44 = (bf16[2,336,256]{2,1,0:T(8,128)(2,1)}, bf16[2,336,256]{2,1,0:T(8,128)(2,1)}, u32[]{:S(2)}, u32[]{:S(2)}) collective-permute-start(bf16[2,336,256]{2,1,0:T(8,128)(2,1)} %slice_bitcast_fusion.11), channel_id=1, source_target_pairs={{0,2},{1,5},{2,0},{3,7},{4,6},{5,1},{6,4},{7,3},{8,10},{9,13},{10,... | collective-permute-start | bytes 1032200 | tf_op jit(solution)/shard_map/ppermute | solution.py:38
  274.7 14.2 %collective-permute-start.45 = (bf16[2,176,256]{2,1,0:T(8,128)(2,1)}, bf16[2,176,256]{2,1,0:T(8,128)(2,1)}, u32[]{:S(2)}, u32[]{:S(2)}) collective-permute-start(bf16[2,176,256]{2,1,0:T(8,128)(2,1)} %slice_bitcast_fusion.18), channel_id=1, source_target_pairs={{0,8},{1,9},{2,10},{3,11},{4,12},{5,13},{6,14},{7,15},{8,0},{9,1},... | collective-permute-start | bytes 540680 | tf_op jit(solution)/shard_map/ppermute | solution.py:38
  275.3 11.5 %collective-permute-start.46 = (bf16[16,48,1024]{2,1,0:T(8,128)(2,1)}, bf16[16,48,1024]{2,1,0:T(8,128)(2,1)}, u32[]{:S(2)}, u32[]{:S(2)}) collective-permute-start(bf16[16,48,1024]{2,1,0:T(8,128)(2,1)} %get-tuple-element.304), channel_id=1, source_target_pairs={{0,1},{1,0},{2,3},{3,2},{4,5},{5,4},{6,7},{7,6},{8,9},{9,8},{10,11... | collective-permute-start | bytes 4718600 | tf_op jit(solution)/shard_map/ppermute | solution.py:30
  275.3 3.1 collective-permute-start.47
  286.1 2.8 collective-permute-start.48
  286.5 10.6 %collective-permute-start.53 = (f32[512,512]{1,0:T(8,128)}, f32[512,512]{1,0:T(8,128)S(1)}, u32[]{:S(2)}, u32[]{:S(2)}) collective-permute-start(f32[512,512]{1,0:T(8,128)} %copy-done.47), channel_id=1, source_target_pairs={{0,1},{1,0},{2,3},{3,2},{4,5},{5,4},{6,7},{7,6},{8,9},{9,8},{10,11... | collective-permute-start | bytes 3145736 | tf_op jit(solution)/shard_map/ppermute | solution.py:30
  290.3 16.8 %collective-permute-start.49 = (bf16[1,336,256]{2,1,0:T(8,128)(2,1)S(1)}, bf16[1,336,256]{2,1,0:T(8,128)(2,1)S(1)}, u32[]{:S(2)}, u32[]{:S(2)}) collective-permute-start(bf16[1,336,256]{2,1,0:T(8,128)(2,1)S(1)} %get-tuple-element.391), channel_id=1, source_target_pairs={{0,16},{1,17},{2,18},{3,19},{4,20},{5,21},{6,22},{7,23},{8,24},{9,... | collective-permute-start | bytes 516104 | tf_op jit(solution)/shard_map/ppermute | solution.py:38
  294.7 11.6 %collective-permute-start.50 = (bf16[1,176,256]{2,1,0:T(8,128)(2,1)S(1)}, bf16[1,176,256]{2,1,0:T(8,128)(2,1)S(1)}, u32[]{:S(2)}, u32[]{:S(2)}) collective-permute-start(bf16[1,176,256]{2,1,0:T(8,128)(2,1)S(1)} %get-tuple-element.397), channel_id=1, source_target_pairs={{0,16},{1,17},{2,18},{3,19},{4,20},{5,21},{6,22},{7,23},{8,24},{9,... | collective-permute-start | bytes 270344 | tf_op jit(solution)/shard_map/ppermute | solution.py:38
  294.9 12.2 %collective-permute-start.51 = (bf16[2,2,2,48,1024]{4,3,2,1,0:T(8,128)(2,1)S(1)}, bf16[2,2,2,48,1024]{4,3,2,1,0:T(8,128)(2,1)S(1)}, u32[]{:S(2)}, u32[]{:S(2)}) collective-permute-start(bf16[2,2,2,48,1024]{4,3,2,1,0:T(8,128)(2,1)S(1)} %slice_bitcast_fusion), channel_id=1, source_target_pairs={{0,4},{1,3},{2,6},{3,1},{4,0},{5,7},{6,2},{7,5},{8,12},{9,11},{10,... | collective-permute-start | bytes 2359304 | tf_op jit(solution)/shard_map/ppermute | solution.py:38
  296.0 11.1 %collective-permute-start.52 = (f32[10,3072]{1,0:T(8,128)S(1)}, f32[10,3072]{1,0:T(8,128)S(1)}, u32[]{:S(2)}, u32[]{:S(2)}) collective-permute-start(f32[10,3072]{1,0:T(8,128)S(1)} %pad_maximum_fusion.14), channel_id=1, source_target_pairs={{0,8},{1,3},{2,10},{3,1},{4,12},{5,7},{6,14},{7,5},{8,0},{9,11},{1... | collective-permute-start | bytes 368648 | tf_op jit(solution)/shard_map/ppermute | solution.py:38
  307.4 10.0 %collective-permute-start.55 = (bf16[2,2,48,1024]{3,2,1,0:T(8,128)(2,1)S(1)}, bf16[2,2,48,1024]{3,2,1,0:T(8,128)(2,1)S(1)}, u32[]{:S(2)}, u32[]{:S(2)}) collective-permute-start(bf16[2,2,48,1024]{3,2,1,0:T(8,128)(2,1)S(1)} %slice_bitcast_fusion.6), channel_id=1, source_target_pairs={{0,2},{1,5},{2,0},{3,7},{4,6},{5,1},{6,4},{7,3},{8,10},{9,13},{10,... | collective-permute-start | bytes 1179656 | tf_op jit(solution)/shard_map/ppermute | solution.py:38
  308.2 9.1 %collective-permute-start.56 = (f32[10,3072]{1,0:T(8,128)S(1)}, f32[10,3072]{1,0:T(8,128)S(1)}, u32[]{:S(2)}, u32[]{:S(2)}) collective-permute-start(f32[10,3072]{1,0:T(8,128)S(1)} %fusion.48), channel_id=1, source_target_pairs={{0,2},{1,5},{2,0},{3,7},{4,6},{5,1},{6,4},{7,3},{8,10},{9,13},{10,... | collective-permute-start | bytes 368648 | tf_op jit(solution)/shard_map/ppermute | solution.py:38
  317.6 8.7 %collective-permute-start.57 = (bf16[2,48,1024]{2,1,0:T(8,128)(2,1)S(1)}, bf16[2,48,1024]{2,1,0:T(8,128)(2,1)S(1)}, u32[]{:S(2)}, u32[]{:S(2)}) collective-permute-start(bf16[2,48,1024]{2,1,0:T(8,128)(2,1)S(1)} %slice_bitcast_fusion.15), channel_id=1, source_target_pairs={{0,8},{1,9},{2,10},{3,11},{4,12},{5,13},{6,14},{7,15},{8,0},{9,1},... | collective-permute-start | bytes 589832 | tf_op jit(solution)/shard_map/ppermute | solution.py:38
  318.6 5.7 %collective-permute-start.60 = (f32[10,3072]{1,0:T(8,128)S(1)}, f32[10,3072]{1,0:T(8,128)S(1)}, u32[]{:S(2)}, u32[]{:S(2)}) collective-permute-start(f32[10,3072]{1,0:T(8,128)S(1)} %add.588), channel_id=1, source_target_pairs={{0,4},{1,9},{2,6},{3,11},{4,0},{5,13},{6,2},{7,15},{8,12},{9,1},{1... | collective-permute-start | bytes 368648 | tf_op jit(solution)/shard_map/ppermute | solution.py:38
  324.3 14.4 %collective-permute-start.61 = (f32[10,3072]{1,0:T(8,128)S(1)}, f32[10,3072]{1,0:T(8,128)S(1)}, u32[]{:S(2)}, u32[]{:S(2)}) collective-permute-start(f32[10,3072]{1,0:T(8,128)S(1)} %add.589), channel_id=1, source_target_pairs={{0,16},{1,17},{2,18},{3,19},{4,20},{5,21},{6,22},{7,23},{8,24},{9,... | collective-permute-start | bytes 368648 | tf_op jit(solution)/shard_map/ppermute | solution.py:38
  326.4 14.4 %collective-permute-start.58 = (bf16[1,48,1024]{2,1,0:T(8,128)(2,1)S(1)}, bf16[1,48,1024]{2,1,0:T(8,128)(2,1)S(1)}, u32[]{:S(2)}, u32[]{:S(2)}) collective-permute-start(bf16[1,48,1024]{2,1,0:T(8,128)(2,1)S(1)} %slice.457), channel_id=1, source_target_pairs={{0,16},{1,17},{2,18},{3,19},{4,20},{5,21},{6,22},{7,23},{8,24},{9,... | collective-permute-start | bytes 294920 | tf_op jit(solution)/shard_map/ppermute | solution.py:38
  338.7 2.7 collective-permute-start.62
  340.8 6.1 %collective-permute-start.59 = (f32[48,1024]{1,0:T(8,128)S(1)}, f32[48,1024]{1,0:T(8,128)S(1)}, u32[]{:S(2)}, u32[]{:S(2)}) collective-permute-start(f32[48,1024]{1,0:T(8,128)S(1)} %add_bitcast_fusion), channel_id=1, source_target_pairs={{0,1},{1,0},{2,3},{3,2},{4,5},{5,4},{6,7},{7,6},{8,9},{9,8},{10,11... | collective-permute-start | bytes 589832 | tf_op jit(solution)/shard_map/ppermute | solution.py:30
  (83 other events, 589.7 us)

commit v7 on v6

--- a/solution.py
+++ b/solution.py
@@ -186,12 +186,12 @@
 PAIR = 2 * HEAD
 mebibyte = 1024 * 1024
 vmem_bytes = 12 * mebibyte
-feed_bytes = 16 * mebibyte
-attend_back_bytes = 16 * mebibyte
-text_forward_bytes = 20 * mebibyte
-text_back_bytes = 16 * mebibyte
-gradient_bytes = 20 * mebibyte
-project_bytes = 24 * mebibyte
+feed_bytes = 12 * mebibyte
+attend_back_bytes = 14 * mebibyte
+text_forward_bytes = 16 * mebibyte
+text_back_bytes = 12 * mebibyte
+gradient_bytes = 18 * mebibyte
+project_bytes = 22 * mebibyte
 
 
 def dot32(left, right, dims=NN):
@@ -920,32 +920,41 @@
     )
 
 
-def modulation_kernel(utterances, time_ref, table_ref, old_ref, first_ref, second_ref, weights_ref, moment_ref, variance_ref):
-    grad = dot32(time_ref[...], table_ref[...], TN) / utterances
+def modulation_kernel(
+    utterances, core_ref, time_ref, mine_ref, other_ref, old_ref, first_ref, second_ref,
+    weights_ref, moment_ref, variance_ref, sums_ref,
+):
+    mine = pl.program_id(0) // 3 == core_ref[0]
+    table = jnp.where(mine, mine_ref[...], other_ref[...])
+    sums_ref[...] = jnp.sum(table, axis=0, keepdims=True)
+    grad = dot32(time_ref[...], table.astype(bf16), TN) / utterances
     moment, variance, direction = moments(grad, first_ref[...], second_ref[...])
     moment_ref[...] = moment
     variance_ref[...] = variance
     weights_ref[...] = apply_step(old_ref[...], direction, learn_rate)
 
 
-def modulation_step(utterances, time_rows, table, old, first, second):
+def modulation_step(utterances, core, time_rows, mine, other, old, first, second):
     rows, columns = old.shape
     step = columns // 6
     tall = pl.BlockSpec((rows, step), lambda i: (0, i))
+    part = pl.BlockSpec((GROUPS, step), lambda i: (0, i % 3))
     return pl.pallas_call(
         lambda *refs: modulation_kernel(utterances, *refs),
         grid=(6,),
         in_specs=[
+            pl.BlockSpec(memory_space=pltpu.SMEM),
             pl.BlockSpec((GROUPS, rows), lambda i: (0, 0)),
-            pl.BlockSpec((GROUPS, step), lambda i: (0, i)),
+            part,
+            part,
         ]
         + [tall] * 3,
-        out_specs=[tall] * 3,
-        out_shape=[jax.ShapeDtypeStruct(old.shape, f32)] * 3,
+        out_specs=[tall] * 3 + [pl.BlockSpec((1, step), lambda i: (0, i))],
+        out_shape=[jax.ShapeDtypeStruct(old.shape, f32)] * 3 + [jax.ShapeDtypeStruct((1, columns), f32)],
         compiler_params=pltpu.CompilerParams(vmem_limit_bytes=vmem_bytes),
         cost_estimate=beside,
         name="modulation_step",
-    )(time_rows, table, old, first, second)
+    )(core.reshape(1).astype(jnp.int32), time_rows, mine, other, old, first, second)
 
 
 def vector_parts(vectors):
@@ -1323,18 +1332,16 @@
     )
     vector_half = vector_mine.shape[0] // 2
     token_half = 3 * D
-
-    def half_of(which):
-        half_vector = lax.dynamic_slice_in_dim(vector_mine, which * vector_half, vector_half, 0)
-        return jnp.concatenate(
-            [
-                jnp.pad(half_vector, (0, 2 * token_half - vector_half)).reshape(2, token_half),
-                lax.dynamic_slice_in_dim(token, which * token_half, token_half, 0)[None],
-            ]
-        )
-
-    small = half_of(core)
-    small_received = swap_core(half_of(1 - core))
+    vector_columns = vector_half // GROUPS
+
+    def half_of(values, which, size):
+        return lax.dynamic_slice_in_dim(values, which * size, size, 0)
+
+    def both_of(which):
+        return jnp.concatenate([half_of(token, which, token_half), half_of(vector_mine, which, vector_half)])
+
+    small = both_of(core)
+    small_received = swap_core(both_of(1 - core))
     in_group = (jnp.arange(GROUPS) == group).astype(f32)
     text_grad_theirs = swap_core(text_grad_mine)
     text_part = add_low(text_keep_half, text_received).reshape(2, 2, 2, 2 * high_count, text_half, D)
@@ -1343,7 +1350,9 @@
         received_b, (text_part, small, small_received, mel_gradient)
     )
     small = small + small_received
-    small = jnp.concatenate([in_group[:, None] * small[2:], small[:2]])
+    small = jnp.concatenate(
+        [in_group[:, None] * small[None, :token_half], small[token_half:].reshape(GROUPS, vector_columns)], axis=1
+    )
     part_b = add_all(firsts(part_b), received_b)
     far_b = [swap_bit(part[high_count:], 3) for part in part_b]
     text_received = swap_bits(text_part[1], phase_bits(text_orders, 2))
@@ -1382,28 +1391,16 @@
         small = small + swap_bit(small, bit)
     own_text = fold_high(own_text)
     own_text = by_core(core, own_text, swap_core(own_text))
-    small = by_core(core, small, swap_core(small), axis=1)
-    modulation_grad = small[:GROUPS]
-    vector_sum = jnp.concatenate(
-        [
-            small[GROUPS + row, which * token_half : which * token_half + min(token_half, vector_half - row * token_half)]
-            for which in range(2)
-            for row in range(2)
-        ]
-    )
-    vector_gradient = jnp.concatenate([vector_sum, jnp.sum(modulation_grad, axis=0)]) / utterances
+    other = swap_core(small)
+    vector_sum = by_core(core, small[:, token_half:].reshape(-1), other[:, token_half:].reshape(-1))
 
     own_text = own_text / utterances
     text_moment, text_variance, text_direction = moments(own_text, text_first, text_second)
     text_weights = apply_step(text_matrices, text_direction, learn_rate)
-    modulation_weights, modulation_moment, modulation_variance = modulation_step(
-        utterances,
-        time_rows,
-        modulation_grad.astype(bf16),
-        modulation_weight,
-        modulation_first,
-        modulation_second,
-    )
+    modulation_weights, modulation_moment, modulation_variance, group_sums = modulation_step(
+        utterances, core, time_rows, small, other, modulation_weight, modulation_first, modulation_second
+    )
+    vector_gradient = jnp.concatenate([vector_sum, group_sums[0]]) / utterances
     vector_moment, vector_variance, vector_direction = moments(
         vector_gradient, vector_first, vector_second
     )

time: 355 us -> 351 us (0.989)
  waiting for transfers between devices: 81.9 us -> 75.6 us
  other arithmetic: 33.6 us -> 37.5 us
    ppermute x46, waiting for transfers between devices: 69.9 us -> 64 us  [swap_bits(): return lax.ppermute(array, ('dp', 'mp'), pairs)]
    unnamed x182 -> x174, local copies, waits for them, and re-layouts: 22.6 us -> 21 us
  transfers between devices with their start and end apart: 63 -> 63, of which waited for: 24 -> 25; matrix products, arithmetic and copies ran while one was open for 12% -> 13% of each run, Pallas kernels for 19% -> 19%
where the time goes in v7:
time: 351 us; the launch traced here: 344 us
  Pallas kernels  118 us (34%)
  waiting for transfers between devices  75.6 us (22%)
  starting transfers between devices  69.2 us (20%)
  local copies, waits for them, and re-layouts  37.8 us (11%)
  other arithmetic  37.5 us (11%)
  between operations  3.76 us (1%)
    ppermute x46, starting transfers between devices, swap_bits(): return lax.ppermute(array, ('dp', 'mp'), pairs)  67.1 us
    ppermute x46, waiting for transfers between devices, swap_bits(): return lax.ppermute(array, ('dp', 'mp'), pairs)  64 us
    pallas_call x6, Pallas kernels, in_vmem(): pl.pallas_call(kernel, in_specs=specs or [whole] * len(inputs), out_specs...  33.6 us
    pallas_call x2, Pallas kernels, attend_backward(): pl.pallas_call(attend_back_kernel, grid=(pairs,), in_specs=[tall(2 * PAIR...  28.4 us
    unnamed x174, local copies, waits for them, and re-layouts  21 us
    pallas_call x2, Pallas kernels, panel_gradients(): pl.pallas_call(lambda *refs: gradients_kernel(panel_rows, cuts, lefts, ri...  17.3 us
    pallas_call x1, Pallas kernels, attend_forward(): pl.pallas_call(attend_kernel, grid=(pairs,), in_specs=[tall(PAIR), tall(P...  13.3 us
    ppermute x17, waiting for transfers between devices, swap_core(): return lax.ppermute(array, 'mp', [(0, 1), (1, 0)])  11.6 us
  transfers between devices with their start and end apart: 63, of which 25 were waited for; matrix products, arithmetic and copies ran while one was open for 13% of the time, Pallas kernels for 19%

profile of v7, /device:TPU:0, one launch (start us, length us, event | category | flops | bytes accessed | tf_op | source)
XLA Modules:
  0.0 344.4 jit_solution(1192303616498770018)
XLA Ops:
  1.6 4.1 %collective-permute-start = (bf16[1,48,1024]{2,1,0:T(8,128)(2,1)S(1)}, bf16[1,48,1024]{2,1,0:T(8,128)(2,1)S(1)}, u32[]{:S(2)}, u32[]{:S(2)}) collective-permute-start(bf16[1,48,1024]{2,1,0:T(8,128)(2,1)S(1)} %fusion.38), channel_id=1, source_target_pairs={{0,16},{1,17},{2,18},{3,19},{4,20},{5,21},{6,22},{7,23},{8,24},{9,... | collective-permute-start | bytes 294920 | tf_op jit(solution)/shard_map/ppermute | solution.py:38
  10.6 4.5 %collective-permute-done.1 = f32[8,3072]{1,0:T(8,128)S(1)} collective-permute-done((f32[8,3072]{1,0:T(8,128)S(1)}, f32[8,3072]{1,0:T(8,128)S(1)}, u32[]{:S(2)}, u32[]{:S(2)}) %collective-permute-start.1) | collective-permute-done | bytes 98336 | tf_op jit(solution)/shard_map/ppermute | solution.py:38
  15.8 1.7 collective-permute-start.3
  17.4 5.4 %collective-permute-done.3 = f32[8,3072]{1,0:T(8,128)S(1)} collective-permute-done((f32[8,3072]{1,0:T(8,128)S(1)}, f32[8,3072]{1,0:T(8,128)S(1)}, u32[]{:S(2)}, u32[]{:S(2)}) %collective-permute-start.3) | collective-permute-done | bytes 98336 | tf_op jit(solution)/shard_map/ppermute | solution.py:38
  25.8 1.8 collective-permute-start.5
  27.6 3.4 collective-permute-start.8
  31.6 1.6 collective-permute-start.7
  33.2 3.2 collective-permute-done.7
  36.4 1.8 collective-permute-done.8
  39.2 1.5 collective-permute-start.11
  42.6 1.6 collective-permute-start.13
  44.3 1.6 collective-permute-start.10
  45.9 1.7 collective-permute-start.16
  48.8 2.3 fusion.60
  51.1 5.9 %collective-permute-done.16 = bf16[1,176,512]{2,1,0:T(8,128)(2,1)} collective-permute-done((bf16[1,176,512]{2,1,0:T(8,128)(2,1)}, bf16[1,176,512]{2,1,0:T(8,128)(2,1)}, u32[]{:S(2)}, u32[]{:S(2)}) %collective-permute-start.16) | collective-permute-done | bytes 180256 | tf_op jit(solution)/shard_map/ppermute | solution.py:38
  59.6 1.5 collective-permute-start.17
  61.6 1.5 collective-permute-start.14
  64.4 2.5 collective-permute-start.18
  68.0 1.6 collective-permute-start.19
  71.2 6.9 %collective-permute-done.14 = bf16[1,336,512]{2,1,0:T(8,128)(2,1)S(1)} collective-permute-done((bf16[1,336,512]{2,1,0:T(8,128)(2,1)}, bf16[1,336,512]{2,1,0:T(8,128)(2,1)S(1)}, u32[]{:S(2)}, u32[]{:S(2)}) %collective-permute-start.14) | collective-permute-done | bytes 344096 | tf_op jit(solution)/shard_map/ppermute | solution.py:38
  85.7 7.4 %collective-permute-done.15 = bf16[2,1,336,512]{3,2,0,1:T(8,128)(2,1)S(1)} collective-permute-done((bf16[2,1,336,512]{3,2,0,1:T(8,128)(2,1)S(1)}, bf16[2,1,336,512]{3,2,0,1:T(8,128)(2,1)S(1)}, u32[]{:S(2)}, u32[]{:S(2)}) %collective-permute-start.15) | collective-permute-done | bytes 688160 | tf_op jit(solution)/shard_map/ppermute | solution.py:38
  99.0 1.9 constant_dynamic-slice_fusion.2
  102.9 7.5 %text_forward.1 = (f32[512,1024]{1,0:T(8,128)S(1)}, f32[1,1024]{1,0:T(1,128)S(1)}, bf16[512,1024]{1,0:T(8,128)(2,1)S(1)}, bf16[512,512]{1,0:T(8,128)(2,1)S(1)}, ...) custom-call(s32[1]{0:T(128)} %bitcast.core_ref.refs_0_, ...), custom_call_target="tpu_custom_call" | custom-call | flops 1000 | bytes 1000 | tf_op jit(solution)/shard_map/text_forward/pallas_call | solution.py:597
  117.9 7.0 %project.1 = (bf16[1024,512]{1,0:T(8,128)(2,1)S(1)}, bf16[1024,512]{1,0:T(8,128)(2,1)S(1)}, bf16[1024,512]{1,0:T(8,128)(2,1)S(1)}, bf16[8192,512]{1,0:T(8,128)(2,1)S(1)}) custom-call(s32[64]{0:T(128)S(1)} %pad_add_fusion.1.refs_0_, bf16[4,336,512]{2,1,0:T(8,128)(2,1)S(1)} %bitcast.196, bf16[4,176,512]{2,1,0:T(8,128)(2,1)S(1)} %bitcast.199, ...), custom_call_target="tpu_custom_call" | custom-call | flops 3221225472 | bytes 25165824 | tf_op jit(solution)/shard_map/project/pallas_call | solution.py:441
  125.2 13.3 %attend.1 = (bf16[1024,512]{1,0:T(8,128)(2,1)S(1)}, bf16[1024,1024]{1,0:T(8,128)(2,1)S(1)}) custom-call(bf16[1024,512]{1,0:T(8,128)(2,1)S(1)} %get-tuple-element.215.q_ref, bf16[1024,512]{1,0:T(8,128)(2,1)S(1)} %get-tuple-element.216.k_ref.kr_ref, bf16[1024,512]{1,0:T(8,128)(2,1)S(1)} %get-tuple-element.217.v_ref, ...), custom_call_target="tpu_custom_call" | custom-call | flops 17179869184 | bytes 6291456 | tf_op jit(solution)/shard_map/attend/pallas_call | solution.py:276
  139.3 2.6 collective-permute-done.24
  143.9 2.5 collective-permute-done.25.n_ref
  146.4 4.8 %feed.3 = (bf16[512,1024]{1,0:T(8,128)(2,1)S(1)}, bf16[512,1024]{1,0:T(8,128)(2,1)S(1)}, bf16[512,1024]{1,0:T(8,128)(2,1)S(1)}, bf16[512,1024]{1,0:T(8,128)(2,1)...) custom-call(bf16[512,1024]{1,0:T(8,128)(2,1)S(1)} %collective-permute-done.25.n_ref, ...), custom_call_target="tpu_custom_call" | custom-call | flops 4294967296 | bytes 8388608 | tf_op jit(solution)/shard_map/feed/pallas_call | solution.py:482
  151.9 4.8 %feed.2 = (f32[512,1024]{1,0:T(8,128)S(1)}, f32[512,1024]{1,0:T(8,128)S(1)}, bf16[512,1024]{1,0:T(8,128)(2,1)S(1)}, bf16[512,1024]{1,0:T(8,128)(2,1)S(1)}, bf16[...) custom-call(bf16[512,1024]{1,0:T(8,128)(2,1)S(1)} %add_convert_fusion.1.n_ref, ...), custom_call_target="tpu_custom_call" | custom-call | flops 4294967296 | bytes 8388608 | tf_op jit(solution)/shard_map/feed/pallas_call | solution.py:482
  156.7 3.7 %settle.1 = (bf16[512,1024]{1,0:T(8,128)(2,1)}, f32[512,1024]{1,0:T(8,128)S(1)}, bf16[512,1024]{1,0:T(8,128)(2,1)S(1)}, f32[4,1024]{1,0:T(4,128)S(1)}, bf16[1024,1024]{1,0:T(8,128)(2,1)}) custom-call(s32[1]{0:T(128)} %bitcast.core_ref.refs_0_, f32[512,1024]{1,0:T(8,128)S(1)} %get-tuple-element.223.my_out_ref, ...), custom_call_target="tpu_custom_call" | custom-call | flops 1000 | bytes 1000 | tf_op jit(solution)/shard_map/settle/pallas_call | solution.py:597
  162.0 2.5 collective-permute-done.28.other_ref
  164.5 14.4 %attend_back.2 = (bf16[1024,256]{1,0:T(8,128)(2,1)S(1)}, bf16[1024,256]{1,0:T(8,128)(2,1)S(1)}, bf16[1024,256]{1,0:T(8,128)(2,1)S(1)}, bf16[1024,512]{1,0:T(8,128)(2,1)S(1)}, bf16[1024,512]{1,0:T(8,128)(2,1)S(1)}) custom-call(bf16[1024,1024]{1,0:T(8,128)(2,1)S(1)} %get-tuple-element.246.qa_ref, bf16[1024,512]{1,0:T(8,128)(2,1)S(1)} %get-tuple-element.216.k_ref.kr_ref, ...), custom_call_target="tpu_custom_call" | custom-call | flops 1000 | bytes 1000 | tf_op jit(solution)/shard_map/attend_back/pallas_call | solution.py:367
  178.9 8.0 %gradients.2 = (bf16[8,336,256]{2,1,0:T(8,128)(2,1)S(1)}, bf16[8,176,256]{2,1,0:T(8,128)(2,1)S(1)}, bf16[8,336,256]{2,1,0:T(8,128)(2,1)S(1)}, bf16[8,176,256]{2,1,0:T(8,128)(2,1)S(1)}) custom-call(s32[64]{0:T(128)S(1)} %pad_add_fusion.refs_0_, bf16[1024,512]{1,0:T(8,128)(2,1)S(1)} %get-tuple-element.201.refs_1_, ...), custom_call_target="tpu_custom_call" | custom-call | flops 1000 | bytes 1000 | tf_op jit(solution)/shard_map/gradients/pallas_call | solution.py:574
  188.8 13.9 %attend_back.3 = (bf16[1024,256]{1,0:T(8,128)(2,1)S(1)}, bf16[1024,256]{1,0:T(8,128)(2,1)S(1)}, bf16[1024,256]{1,0:T(8,128)(2,1)S(1)}) custom-call(bf16[1024,1024]{1,0:T(8,128)(2,1)S(1)} %get-tuple-element.246.qa_ref, bf16[1024,512]{1,0:T(8,128)(2,1)S(1)} %get-tuple-element.216.k_ref.kr_ref, bf16[1024,512]{1,0:T(8,128)(2,1)S(1)} %get-tuple-element.217.v_ref, ...), custom_call_target="tpu_custom_call" | custom-call | flops 1000 | bytes 1000 | tf_op jit(solution)/shard_map/attend_back/pallas_call | solution.py:367
  202.8 3.0 collective-permute-done.30
  208.5 9.3 %gradients.3 = (bf16[8,336,256]{2,1,0:T(8,128)(2,1)S(1)}, bf16[8,176,256]{2,1,0:T(8,128)(2,1)S(1)}, bf16[8,336,256]{2,1,0:T(8,128)(2,1)}, bf16[8,176,256]{2,1,0:T(8,128)(2,1)S(1)}) custom-call(s32[64]{0:T(128)S(1)} %pad_add_fusion.refs_0_, bf16[1024,512]{1,0:T(8,128)(2,1)S(1)} %get-tuple-element.201.refs_1_, ...), custom_call_target="tpu_custom_call" | custom-call | flops 1000 | bytes 1000 | tf_op jit(solution)/shard_map/gradients/pallas_call | solution.py:574
  220.9 3.8 %inputs_grad.1 = (f32[512,1024]{1,0:T(8,128)S(1)}, bf16[512,1024]{1,0:T(8,128)(2,1)}) custom-call(bf16[1024,256]{1,0:T(8,128)(2,1)S(1)} %get-tuple-element.267.refs_9_.refs_0_, bf16[1024,256]{1,0:T(8,128)(2,1)S(1)} %get-tuple-element.268.refs_10_.refs_1_, bf16[1024,256]{1,0:T(8,128)(2,1)S(1)} %get-tuple-element.269.refs_11_.refs_2_, ...), custom_call_target="tpu_custom_call" | custom-call | flops 1000 | bytes 1000 | tf_op jit(solution)/shard_map/inputs_grad/pallas_call | solution.py:515
  230.2 2.3 constant_dynamic-update-slice_fusion.6
  234.7 1.6 copy-done.5
  236.3 1.6 copy-done.19
  237.9 1.6 copy-done.21
  239.5 5.7 %stream_back.1 = (f32[512,1024]{1,0:T(8,128)S(1)}, bf16[512,1024]{1,0:T(8,128)(2,1)S(1)}, f32[512,512]{1,0:T(8,128)S(1)}, bf16[512,512]{1,0:T(8,128)(2,1)S(1)}, ...) custom-call(s32[1]{0:T(128)} %bitcast.core_ref.refs_0_, ...), custom_call_target="tpu_custom_call" | custom-call | flops 1000 | bytes 1000 | tf_op jit(solution)/shard_map/stream_back/pallas_call | solution.py:597
  245.2 2.7 collective-permute-done.36
  247.9 1.8 fusion.1
  252.2 4.1 %collective-permute-start.40 = (bf16[1,336,256]{2,1,0:T(8,128)(2,1)S(1)}, bf16[1,336,256]{2,1,0:T(8,128)(2,1)S(1)}, u32[]{:S(2)}, u32[]{:S(2)}) collective-permute-start(bf16[1,336,256]{2,1,0:T(8,128)(2,1)S(1)} %get-tuple-element.391), channel_id=1, source_target_pairs={{0,16},{1,17},{2,18},{3,19},{4,20},{5,21},{6,22},{7,23},{8,24},{9,... | collective-permute-start | bytes 516104 | tf_op jit(solution)/shard_map/ppermute | solution.py:38
  257.5 1.8 collective-permute-start.41
  259.4 6.9 %text_back.1 = (f32[512,512]{1,0:T(8,128)S(1)}, f32[3,512]{1,0:T(4,128)S(1)}, f32[2,1024]{1,0:T(2,128)S(1)}, bf16[16,48,1024]{2,1,0:T(8,128)(2,1)S(1)}, bf16[16,48,1024]{2,1,0:T(8,128)(2,1)}) custom-call(f32[512,1024]{1,0:T(8,128)S(1)} %copy-done.6, f32[512,1024]{1,0:T(8,128)S(1)} %get-tuple-element.291.grn_grad_ref, ...), custom_call_target="tpu_custom_call" | custom-call | flops 1000 | bytes 1000 | tf_op jit(solution)/shard_map/text_back/pallas_call | solution.py:597
  268.5 2.4 collective-permute-start.44
  272.8 1.7 collective-permute-done.47.border_ref
  274.5 4.4 %conv_back.1 = (f32[512,512]{1,0:T(8,128)S(1)}, f32[7,512]{1,0:T(8,128)S(1)}, f32[1024,512]{1,0:T(8,128)}) custom-call(s32[1]{0:T(128)} %bitcast.core_ref.refs_0_, f32[512,512]{1,0:T(8,128)S(1)} %get-tuple-element.307.mixed_ref, f32[8,512]{1,0:T(8,128)S(1)} %collective-permute-done.47.border_ref, f32[528,512]{1,0:T(8,128)S(1)} %get-tuple-element.370.window_ref, ...), custom_call_target="tpu_custom_call" | custom-call | flops 1000 | bytes 1000 | tf_op jit(solution)/shard_map/conv_back/pallas_call | solution.py:597
  282.8 2.2 add_convert_fusion
  286.4 2.4 collective-permute-start.49
  292.8 2.4 constant_dynamic-update-slice_fusion.7
  295.2 6.1 %collective-permute-done.50 = bf16[1,176,256]{2,1,0:T(8,128)(2,1)S(1)} collective-permute-done((bf16[1,176,256]{2,1,0:T(8,128)(2,1)S(1)}, bf16[1,176,256]{2,1,0:T(8,128)(2,1)S(1)}, u32[]{:S(2)}, u32[]{:S(2)}) %collective-permute-start.50) | collective-permute-done | bytes 90144 | tf_op jit(solution)/shard_map/ppermute | solution.py:38
  304.2 2.0 collective-permute-start.56
  306.2 5.4 %rotated_step.1 = (f32[512,512]{1,0:T(8,128)}, f32[512,512]{1,0:T(8,128)}, f32[512,512]{1,0:T(8,128)}) custom-call(bf16[336,256]{1,0:T(8,128)(2,1)S(1)} %get-tuple-element.390.refs_0_, bf16[336,256]{1,0:T(8,128)(2,1)S(1)} %bitcast.202, bf16[176,256]{1,0:T(8,128)(2,1)S(1)} %get-tuple-element.396.refs_2_, bf16[176,256]{1,0:T(8,128)(2,1)S(1)} %bitcast.204, ...), custom_call_target="tpu_custom_call" | custom-call | flops 1000 | bytes 1000 | tf_op jit(solution)/shard_map/rotated_step/pallas_call | solution.py:597
  311.6 1.6 collective-permute-done.56
  315.5 3.8 %collective-permute-done.60 = f32[8,3616]{1,0:T(8,128)S(1)} collective-permute-done((f32[8,3616]{1,0:T(8,128)S(1)}, f32[8,3616]{1,0:T(8,128)S(1)}, u32[]{:S(2)}, u32[]{:S(2)}) %collective-permute-start.60) | collective-permute-done | bytes 115744 | tf_op jit(solution)/shard_map/ppermute | solution.py:38
  319.3 3.0 collective-permute-start.61
  323.8 7.3 %collective-permute-done.61 = f32[8,3616]{1,0:T(8,128)S(1)} collective-permute-done((f32[8,3616]{1,0:T(8,128)S(1)}, f32[8,3616]{1,0:T(8,128)S(1)}, u32[]{:S(2)}, u32[]{:S(2)}) %collective-permute-start.61) | collective-permute-done | bytes 115744 | tf_op jit(solution)/shard_map/ppermute | solution.py:38
  331.2 1.8 collective-permute-done.58
  333.1 1.7 add_bitcast_fusion
  336.3 4.5 %modulation_step.1 = (f32[64,6144]{1,0:T(8,128)}, f32[64,6144]{1,0:T(8,128)}, f32[64,6144]{1,0:T(8,128)}, f32[1,6144]{1,0:T(1,128)S(1)}) custom-call(s32[1]{0:T(128)} %bitcast.core_ref.refs_0_, bf16[8,64]{1,0:T(8,128)(2,1)S(1)} %multiply_convert_fusion.2.refs_1_, f32[8,3616]{1,0:T(8,128)S(1)} %add.586.refs_2_, ...), custom_call_target="tpu_custom_call" | custom-call | flops 1000 | bytes 1000 | tf_op jit(solution)/shard_map/modulation_step/pallas_call | solution.py:942
  341.5 2.5 multiply_subtract_fusion
  (388 shorter events, 88.9 us)
Async XLA Ops:
  1.6 9.0 %collective-permute-start = (bf16[1,48,1024]{2,1,0:T(8,128)(2,1)S(1)}, bf16[1,48,1024]{2,1,0:T(8,128)(2,1)S(1)}, u32[]{:S(2)}, u32[]{:S(2)}) collective-permute-start(bf16[1,48,1024]{2,1,0:T(8,128)(2,1)S(1)} %fusion.38), channel_id=1, source_target_pairs={{0,16},{1,17},{2,18},{3,19},{4,20},{5,21},{6,22},{7,23},{8,24},{9,... | collective-permute-start | bytes 294920 | tf_op jit(solution)/shard_map/ppermute | solution.py:38
  7.8 7.3 %collective-permute-start.1 = (f32[8,3072]{1,0:T(8,128)S(1)}, f32[8,3072]{1,0:T(8,128)S(1)}, u32[]{:S(2)}, u32[]{:S(2)}) collective-permute-start(f32[8,3072]{1,0:T(8,128)S(1)} %fusion.32), channel_id=1, source_target_pairs={{0,16},{1,17},{2,18},{3,19},{4,20},{5,21},{6,22},{7,23},{8,24},{9,... | collective-permute-start | bytes 294920 | tf_op jit(solution)/shard_map/ppermute | solution.py:38
  15.2 7.7 %collective-permute-start.2 = (bf16[2,48,1024]{2,1,0:T(8,128)(2,1)S(1)}, bf16[2,48,1024]{2,1,0:T(8,128)(2,1)S(1)}, u32[]{:S(2)}, u32[]{:S(2)}) collective-permute-start(bf16[2,48,1024]{2,1,0:T(8,128)(2,1)S(1)} %get-tuple-element.393), channel_id=1, source_target_pairs={{0,8},{1,9},{2,10},{3,11},{4,12},{5,13},{6,14},{7,15},{8,0},{9,1},... | collective-permute-start | bytes 589832 | tf_op jit(solution)/shard_map/ppermute | solution.py:38
  15.8 7.1 %collective-permute-start.3 = (f32[8,3072]{1,0:T(8,128)S(1)}, f32[8,3072]{1,0:T(8,128)S(1)}, u32[]{:S(2)}, u32[]{:S(2)}) collective-permute-start(f32[8,3072]{1,0:T(8,128)S(1)} %add.503), channel_id=1, source_target_pairs={{0,8},{1,9},{2,10},{3,11},{4,12},{5,13},{6,14},{7,15},{8,0},{9,1},... | collective-permute-start | bytes 294920 | tf_op jit(solution)/shard_map/ppermute | solution.py:38
  23.6 14.5 %collective-permute-start.4 = (bf16[1,336,512]{2,1,0:T(8,128)(2,1)}, bf16[1,336,512]{2,1,0:T(8,128)(2,1)S(1)}, u32[]{:S(2)}, u32[]{:S(2)}) collective-permute-start(bf16[1,336,512]{2,1,0:T(8,128)(2,1)} %get-tuple-element.381), channel_id=1, source_target_pairs={{0,2},{1,5},{2,0},{3,7},{4,6},{5,1},{6,4},{7,3},{8,10},{9,13},{10,... | collective-permute-start | bytes 1032200 | tf_op jit(solution)/shard_map/ppermute | solution.py:38
  25.2 13.0 %collective-permute-start.6 = (bf16[2,2,48,1024]{3,2,1,0:T(8,128)(2,1)S(1)}, bf16[2,2,48,1024]{3,2,1,0:T(8,128)(2,1)S(1)}, u32[]{:S(2)}, u32[]{:S(2)}) collective-permute-start(bf16[2,2,48,1024]{3,2,1,0:T(8,128)(2,1)S(1)} %get-tuple-element.383), channel_id=1, source_target_pairs={{0,2},{1,5},{2,0},{3,7},{4,6},{5,1},{6,4},{7,3},{8,10},{9,13},{10,... | collective-permute-start | bytes 1179656 | tf_op jit(solution)/shard_map/ppermute | solution.py:38
  25.8 10.6 %collective-permute-start.5 = (bf16[1,176,512]{2,1,0:T(8,128)(2,1)S(1)}, bf16[1,176,512]{2,1,0:T(8,128)(2,1)S(1)}, u32[]{:S(2)}, u32[]{:S(2)}) collective-permute-start(bf16[1,176,512]{2,1,0:T(8,128)(2,1)S(1)} %get-tuple-element.379), channel_id=1, source_target_pairs={{0,8},{1,9},{2,10},{3,11},{4,12},{5,13},{6,14},{7,15},{8,0},{9,1},... | collective-permute-start | bytes 540680 | tf_op jit(solution)/shard_map/ppermute | solution.py:38
  27.6 10.5 %collective-permute-start.8 = (bf16[1,176,512]{2,1,0:T(8,128)(2,1)S(1)}, bf16[1,176,512]{2,1,0:T(8,128)(2,1)}, u32[]{:S(2)}, u32[]{:S(2)}) collective-permute-start(bf16[1,176,512]{2,1,0:T(8,128)(2,1)S(1)} %get-tuple-element.379), channel_id=1, source_target_pairs={{0,16},{1,17},{2,18},{3,19},{4,20},{5,21},{6,22},{7,23},{8,24},{9,... | collective-permute-start | bytes 540680 | tf_op jit(solution)/shard_map/ppermute | solution.py:38
  31.6 4.8 %collective-permute-start.7 = (f32[8,3072]{1,0:T(8,128)S(1)}, f32[8,3072]{1,0:T(8,128)S(1)}, u32[]{:S(2)}, u32[]{:S(2)}) collective-permute-start(f32[8,3072]{1,0:T(8,128)S(1)} %add.504), channel_id=1, source_target_pairs={{0,2},{1,5},{2,0},{3,7},{4,6},{5,1},{6,4},{7,3},{8,10},{9,13},{10,... | collective-permute-start | bytes 294920 | tf_op jit(solution)/shard_map/ppermute | solution.py:38
  39.2 22.5 %collective-permute-start.11 = (bf16[2,2,2,48,1024]{4,3,2,1,0:T(8,128)(2,1)}, bf16[2,2,2,48,1024]{4,3,2,1,0:T(8,128)(2,1)S(1)}, u32[]{:S(2)}, u32[]{:S(2)}) collective-permute-start(bf16[2,2,2,48,1024]{4,3,2,1,0:T(8,128)(2,1)} %get-tuple-element.373), channel_id=1, source_target_pairs={{0,4},{1,3},{2,6},{3,1},{4,0},{5,7},{6,2},{7,5},{8,12},{9,11},{10,... | collective-permute-start | bytes 2359304 | tf_op jit(solution)/shard_map/ppermute | solution.py:38
  41.6 20.0 %collective-permute-start.9 = (bf16[2,1,336,512]{3,2,0,1:T(8,128)(2,1)}, bf16[2,1,336,512]{3,2,0,1:T(8,128)(2,1)}, u32[]{:S(2)}, u32[]{:S(2)}) collective-permute-start(bf16[2,1,336,512]{3,2,0,1:T(8,128)(2,1)} %get-tuple-element.377), channel_id=1, source_target_pairs={{0,4},{1,9},{2,6},{3,11},{4,0},{5,13},{6,2},{7,15},{8,12},{9,1},{1... | collective-permute-start | bytes 2064392 | tf_op jit(solution)/shard_map/ppermute | solution.py:38
  42.6 17.0 %collective-permute-start.13 = (bf16[1,336,512]{2,1,0:T(8,128)(2,1)}, bf16[1,336,512]{2,1,0:T(8,128)(2,1)}, u32[]{:S(2)}, u32[]{:S(2)}) collective-permute-start(bf16[1,336,512]{2,1,0:T(8,128)(2,1)} %get-tuple-element.381), channel_id=1, source_target_pairs={{0,16},{1,17},{2,18},{3,19},{4,20},{5,21},{6,22},{7,23},{8,24},{9,... | collective-permute-start | bytes 1032200 | tf_op jit(solution)/shard_map/ppermute | solution.py:38
  44.3 17.3 %collective-permute-start.10 = (bf16[2,1,176,512]{3,2,0,1:T(8,128)(2,1)S(1)}, bf16[2,1,176,512]{3,2,0,1:T(8,128)(2,1)}, u32[]{:S(2)}, u32[]{:S(2)}) collective-permute-start(bf16[2,1,176,512]{3,2,0,1:T(8,128)(2,1)S(1)} %get-tuple-element.387), channel_id=1, source_target_pairs={{0,2},{1,3},{2,0},{3,1},{4,6},{5,7},{6,4},{7,5},{8,10},{9,11},{10,... | collective-permute-start | bytes 1081352 | tf_op jit(solution)/shard_map/ppermute | solution.py:38
  45.9 11.1 %collective-permute-start.16 = (bf16[1,176,512]{2,1,0:T(8,128)(2,1)}, bf16[1,176,512]{2,1,0:T(8,128)(2,1)}, u32[]{:S(2)}, u32[]{:S(2)}) collective-permute-start(bf16[1,176,512]{2,1,0:T(8,128)(2,1)} %collective-permute-done.8), channel_id=1, source_target_pairs={{0,8},{1,9},{2,10},{3,11},{4,12},{5,13},{6,14},{7,15},{8,0},{9,1},... | collective-permute-start | bytes 540680 | tf_op jit(solution)/shard_map/ppermute | solution.py:38
  57.0 4.6 %collective-permute-start.12 = (f32[8,3072]{1,0:T(8,128)S(1)}, f32[8,3072]{1,0:T(8,128)S(1)}, u32[]{:S(2)}, u32[]{:S(2)}) collective-permute-start(f32[8,3072]{1,0:T(8,128)S(1)} %add.505), channel_id=1, source_target_pairs={{0,4},{1,3},{2,6},{3,1},{4,0},{5,7},{6,2},{7,5},{8,12},{9,11},{10,... | collective-permute-start | bytes 294920 | tf_op jit(solution)/shard_map/ppermute | solution.py:38
  59.6 26.1 %collective-permute-start.17 = (bf16[2,1,176,512]{3,2,0,1:T(8,128)(2,1)S(1)}, bf16[2,1,176,512]{3,2,0,1:T(8,128)(2,1)S(1)}, u32[]{:S(2)}, u32[]{:S(2)}) collective-permute-start(bf16[2,1,176,512]{3,2,0,1:T(8,128)(2,1)S(1)} %get-tuple-element.385), channel_id=1, source_target_pairs={{0,2},{1,3},{2,0},{3,1},{4,6},{5,7},{6,4},{7,5},{8,10},{9,11},{10,... | collective-permute-start | bytes 1081352 | tf_op jit(solution)/shard_map/ppermute | solution.py:38
  61.6 16.4 %collective-permute-start.14 = (bf16[1,336,512]{2,1,0:T(8,128)(2,1)}, bf16[1,336,512]{2,1,0:T(8,128)(2,1)S(1)}, u32[]{:S(2)}, u32[]{:S(2)}) collective-permute-start(bf16[1,336,512]{2,1,0:T(8,128)(2,1)} %collective-permute-done.13), channel_id=1, source_target_pairs={{0,2},{1,5},{2,0},{3,7},{4,6},{5,1},{6,4},{7,3},{8,10},{9,13},{10,... | collective-permute-start | bytes 1032200 | tf_op jit(solution)/shard_map/ppermute | solution.py:38
  64.4 28.7 %collective-permute-start.18 = (bf16[2,2,1,336,512]{4,3,1,2,0:T(8,128)(2,1)S(1)}, bf16[2,2,1,336,512]{4,3,1,2,0:T(8,128)(2,1)S(1)}, u32[]{:S(2)}, u32[]{:S(2)}) collective-permute-start(bf16[2,2,1,336,512]{4,3,1,2,0:T(8,128)(2,1)S(1)} %pad_maximum_fusion.2), channel_id=1, source_target_pairs={{0,8},{1,3},{2,10},{3,1},{4,12},{5,7},{6,14},{7,5},{8,0},{9,11},{1... | collective-permute-start | bytes 4128776 | tf_op jit(solution)/shard_map/ppermute | solution.py:38
  68.0 17.7 %collective-permute-start.19 = (bf16[2,2,1,176,512]{4,3,1,2,0:T(8,128)(2,1)S(1)}, bf16[2,2,1,176,512]{4,3,1,2,0:T(8,128)(2,1)S(1)}, u32[]{:S(2)}, u32[]{:S(2)}) collective-permute-start(bf16[2,2,1,176,512]{4,3,1,2,0:T(8,128)(2,1)S(1)} %pad_maximum_fusion.6), channel_id=1, source_target_pairs={{0,4},{1,5},{2,6},{3,7},{4,0},{5,1},{6,2},{7,3},{8,12},{9,13},{10,... | collective-permute-start | bytes 2162696 | tf_op jit(solution)/shard_map/ppermute | solution.py:38
  69.6 1.4 collective-permute-start.21
  71.0 22.1 %collective-permute-start.20 = (bf16[16,48,1024]{2,1,0:T(8,128)(2,1)S(1)}, bf16[16,48,1024]{2,1,0:T(8,128)(2,1)S(1)}, u32[]{:S(2)}, u32[]{:S(2)}) collective-permute-start(bf16[16,48,1024]{2,1,0:T(8,128)(2,1)S(1)} %bitcast.194), channel_id=1, source_target_pairs={{0,1},{1,0},{2,3},{3,2},{4,5},{5,4},{6,7},{7,6},{8,9},{9,8},{10,11... | collective-permute-start | bytes 4718600 | tf_op jit(solution)/shard_map/ppermute | solution.py:30
  79.2 14.0 %collective-permute-start.15 = (bf16[2,1,336,512]{3,2,0,1:T(8,128)(2,1)S(1)}, bf16[2,1,336,512]{3,2,0,1:T(8,128)(2,1)S(1)}, u32[]{:S(2)}, u32[]{:S(2)}) collective-permute-start(bf16[2,1,336,512]{3,2,0,1:T(8,128)(2,1)S(1)} %get-tuple-element.375), channel_id=1, source_target_pairs={{0,4},{1,9},{2,6},{3,11},{4,0},{5,13},{6,2},{7,15},{8,12},{9,1},{1... | collective-permute-start | bytes 2064392 | tf_op jit(solution)/shard_map/ppermute | solution.py:38
  94.5 20.8 %collective-permute-start.22 = (bf16[2,2,1,336,512]{4,3,1,2,0:T(8,128)(2,1)}, bf16[2,2,1,336,512]{4,3,1,2,0:T(8,128)(2,1)}, u32[]{:S(2)}, u32[]{:S(2)}) collective-permute-start(bf16[2,2,1,336,512]{4,3,1,2,0:T(8,128)(2,1)} %pad_maximum_fusion.3), channel_id=1, source_target_pairs={{0,8},{1,3},{2,10},{3,1},{4,12},{5,7},{6,14},{7,5},{8,0},{9,11},{1... | collective-permute-start | bytes 4128776 | tf_op jit(solution)/shard_map/ppermute | solution.py:38
  96.5 18.8 %collective-permute-start.23 = (bf16[2,2,1,176,512]{4,3,1,2,0:T(8,128)(2,1)}, bf16[2,2,1,176,512]{4,3,1,2,0:T(8,128)(2,1)}, u32[]{:S(2)}, u32[]{:S(2)}) collective-permute-start(bf16[2,2,1,176,512]{4,3,1,2,0:T(8,128)(2,1)} %pad_maximum_fusion.7), channel_id=1, source_target_pairs={{0,4},{1,5},{2,6},{3,7},{4,0},{5,1},{6,2},{7,3},{8,12},{9,13},{10,... | collective-permute-start | bytes 2162696 | tf_op jit(solution)/shard_map/ppermute | solution.py:38
  113.6 28.4 %copy-start.2 = (f32[512,1024]{1,0:T(8,128)}, f32[512,1024]{1,0:T(8,128)S(1)}, u32[]{:S(2)}) copy-start(f32[512,1024]{1,0:T(8,128)S(1)} %get-tuple-element.220.stream_ref) | copy-start | bytes 6291460
  139.3 2.7 collective-permute-start.24
  143.7 2.7 collective-permute-start.25
  151.3 5.4 %collective-permute-start.26 = (bf16[512,1024]{1,0:T(8,128)(2,1)S(1)}, bf16[512,1024]{1,0:T(8,128)(2,1)S(1)}, u32[]{:S(2)}, u32[]{:S(2)}) collective-permute-start(bf16[512,1024]{1,0:T(8,128)(2,1)S(1)} %get-tuple-element.225), channel_id=1, source_target_pairs={{0,1},{1,0},{2,3},{3,2},{4,5},{5,4},{6,7},{7,6},{8,9},{9,8},{10,11... | collective-permute-start | bytes 3145736 | tf_op jit(solution)/shard_map/ppermute | solution.py:30
  151.5 5.2 %collective-permute-start.27 = (bf16[512,1024]{1,0:T(8,128)(2,1)S(1)}, bf16[512,1024]{1,0:T(8,128)(2,1)S(1)}, u32[]{:S(2)}, u32[]{:S(2)}) collective-permute-start(bf16[512,1024]{1,0:T(8,128)(2,1)S(1)} %get-tuple-element.227), channel_id=1, source_target_pairs={{0,1},{1,0},{2,3},{3,2},{4,5},{5,4},{6,7},{7,6},{8,9},{9,8},{10,11... | collective-permute-start | bytes 3145736 | tf_op jit(solution)/shard_map/ppermute | solution.py:30
  161.8 2.7 collective-permute-start.28
  186.9 18.8 %collective-permute-start.29 = (bf16[2,2,2,336,256]{4,3,2,1,0:T(8,128)(2,1)S(1)}, bf16[2,2,2,336,256]{4,3,2,1,0:T(8,128)(2,1)S(1)}, u32[]{:S(2)}, u32[]{:S(2)}) collective-permute-start(bf16[2,2,2,336,256]{4,3,2,1,0:T(8,128)(2,1)S(1)} %bitcast.217), channel_id=1, source_target_pairs={{0,8},{1,3},{2,10},{3,1},{4,12},{5,7},{6,14},{7,5},{8,0},{9,11},{1... | collective-permute-start | bytes 4128776 | tf_op jit(solution)/shard_map/ppermute | solution.py:38
  188.2 17.5 %collective-permute-start.30 = (bf16[2,2,2,176,256]{4,3,2,1,0:T(8,128)(2,1)S(1)}, bf16[2,2,2,176,256]{4,3,2,1,0:T(8,128)(2,1)S(1)}, u32[]{:S(2)}, u32[]{:S(2)}) collective-permute-start(bf16[2,2,2,176,256]{4,3,2,1,0:T(8,128)(2,1)S(1)} %bitcast.220), channel_id=1, source_target_pairs={{0,4},{1,5},{2,6},{3,7},{4,0},{5,1},{6,2},{7,3},{8,12},{9,13},{10,... | collective-permute-start | bytes 2162696 | tf_op jit(solution)/shard_map/ppermute | solution.py:38
  206.2 11.7 %collective-permute-start.31 = (bf16[2,2,336,256]{3,2,1,0:T(8,128)(2,1)S(1)}, bf16[2,2,336,256]{3,2,1,0:T(8,128)(2,1)S(1)}, u32[]{:S(2)}, u32[]{:S(2)}) collective-permute-start(bf16[2,2,336,256]{3,2,1,0:T(8,128)(2,1)S(1)} %slice_bitcast_fusion.3), channel_id=1, source_target_pairs={{0,4},{1,9},{2,6},{3,11},{4,0},{5,13},{6,2},{7,15},{8,12},{9,1},{1... | collective-permute-start | bytes 2064392 | tf_op jit(solution)/shard_map/ppermute | solution.py:38
  207.6 10.2 %collective-permute-start.32 = (bf16[2,2,176,256]{3,2,1,0:T(8,128)(2,1)S(1)}, bf16[2,2,176,256]{3,2,1,0:T(8,128)(2,1)S(1)}, u32[]{:S(2)}, u32[]{:S(2)}) collective-permute-start(bf16[2,2,176,256]{3,2,1,0:T(8,128)(2,1)S(1)} %slice_bitcast_fusion.10), channel_id=1, source_target_pairs={{0,2},{1,3},{2,0},{3,1},{4,6},{5,7},{6,4},{7,5},{8,10},{9,11},{10,... | collective-permute-start | bytes 1081352 | tf_op jit(solution)/shard_map/ppermute | solution.py:38
  208.5 21.6 %collective-permute-start.54 = (bf16[512,1024]{1,0:T(8,128)(2,1)}, bf16[512,1024]{1,0:T(8,128)(2,1)}, u32[]{:S(2)}, u32[]{:S(2)}) collective-permute-start(bf16[512,1024]{1,0:T(8,128)(2,1)} %get-tuple-element.323), channel_id=1, source_target_pairs={{0,1},{1,0},{2,3},{3,2},{4,5},{5,4},{6,7},{7,6},{8,9},{9,8},{10,11... | collective-permute-start | bytes 3145736 | tf_op jit(solution)/shard_map/ppermute | solution.py:30
  218.1 8.2 %collective-permute-start.33 = (bf16[2,336,256]{2,1,0:T(8,128)(2,1)S(1)}, bf16[2,336,256]{2,1,0:T(8,128)(2,1)S(1)}, u32[]{:S(2)}, u32[]{:S(2)}) collective-permute-start(bf16[2,336,256]{2,1,0:T(8,128)(2,1)S(1)} %slice_bitcast_fusion.14), channel_id=1, source_target_pairs={{0,2},{1,5},{2,0},{3,7},{4,6},{5,1},{6,4},{7,3},{8,10},{9,13},{10,... | collective-permute-start | bytes 1032200 | tf_op jit(solution)/shard_map/ppermute | solution.py:38
  219.5 6.8 %collective-permute-start.34 = (bf16[2,176,256]{2,1,0:T(8,128)(2,1)S(1)}, bf16[2,176,256]{2,1,0:T(8,128)(2,1)S(1)}, u32[]{:S(2)}, u32[]{:S(2)}) collective-permute-start(bf16[2,176,256]{2,1,0:T(8,128)(2,1)S(1)} %slice_bitcast_fusion.20), channel_id=1, source_target_pairs={{0,8},{1,9},{2,10},{3,11},{4,12},{5,13},{6,14},{7,15},{8,0},{9,1},... | collective-permute-start | bytes 540680 | tf_op jit(solution)/shard_map/ppermute | solution.py:38
  226.3 21.6 %collective-permute-start.35 = (bf16[2,2,2,336,256]{4,3,2,1,0:T(8,128)(2,1)}, bf16[2,2,2,336,256]{4,3,2,1,0:T(8,128)(2,1)}, u32[]{:S(2)}, u32[]{:S(2)}) collective-permute-start(bf16[2,2,2,336,256]{4,3,2,1,0:T(8,128)(2,1)} %bitcast.60), channel_id=1, source_target_pairs={{0,8},{1,3},{2,10},{3,1},{4,12},{5,7},{6,14},{7,5},{8,0},{9,11},{1... | collective-permute-start | bytes 4128776 | tf_op jit(solution)/shard_map/ppermute | solution.py:38
  227.6 7.1 %collective-permute-start.37 = (bf16[512,1024]{1,0:T(8,128)(2,1)}, bf16[512,1024]{1,0:T(8,128)(2,1)}, u32[]{:S(2)}, u32[]{:S(2)}) collective-permute-start(bf16[512,1024]{1,0:T(8,128)(2,1)} %get-tuple-element.280), channel_id=1, source_target_pairs={{0,1},{1,0},{2,3},{3,2},{4,5},{5,4},{6,7},{7,6},{8,9},{9,8},{10,11... | collective-permute-start | bytes 3145736 | tf_op jit(solution)/shard_map/ppermute | solution.py:30
  229.1 18.8 %collective-permute-start.36 = (bf16[2,2,2,176,256]{4,3,2,1,0:T(8,128)(2,1)}, bf16[2,2,2,176,256]{4,3,2,1,0:T(8,128)(2,1)S(1)}, u32[]{:S(2)}, u32[]{:S(2)}) collective-permute-start(bf16[2,2,2,176,256]{4,3,2,1,0:T(8,128)(2,1)} %bitcast.219), channel_id=1, source_target_pairs={{0,4},{1,5},{2,6},{3,7},{4,0},{5,1},{6,2},{7,3},{8,12},{9,13},{10,... | collective-permute-start | bytes 2162696 | tf_op jit(solution)/shard_map/ppermute | solution.py:38
  249.8 17.7 %collective-permute-start.38 = (bf16[2,2,336,256]{3,2,1,0:T(8,128)(2,1)S(1)}, bf16[2,2,336,256]{3,2,1,0:T(8,128)(2,1)S(1)}, u32[]{:S(2)}, u32[]{:S(2)}) collective-permute-start(bf16[2,2,336,256]{3,2,1,0:T(8,128)(2,1)S(1)} %slice_bitcast_fusion.1), channel_id=1, source_target_pairs={{0,4},{1,9},{2,6},{3,11},{4,0},{5,13},{6,2},{7,15},{8,12},{9,1},{1... | collective-permute-start | bytes 2064392 | tf_op jit(solution)/shard_map/ppermute | solution.py:38
  250.9 16.7 %collective-permute-start.43 = (f32[512,1024]{1,0:T(8,128)S(1)}, f32[512,1024]{1,0:T(8,128)S(1)}, u32[]{:S(2)}, u32[]{:S(2)}) collective-permute-start(f32[512,1024]{1,0:T(8,128)S(1)} %get-tuple-element.301), channel_id=1, source_target_pairs={{0,1},{1,0},{2,3},{3,2},{4,5},{5,4},{6,7},{7,6},{8,9},{9,8},{10,11... | collective-permute-start | bytes 6291464 | tf_op jit(solution)/shard_map/ppermute | solution.py:30
  251.1 16.4 %collective-permute-start.39 = (bf16[2,2,176,256]{3,2,1,0:T(8,128)(2,1)S(1)}, bf16[2,2,176,256]{3,2,1,0:T(8,128)(2,1)S(1)}, u32[]{:S(2)}, u32[]{:S(2)}) collective-permute-start(bf16[2,2,176,256]{3,2,1,0:T(8,128)(2,1)S(1)} %slice_bitcast_fusion.8), channel_id=1, source_target_pairs={{0,2},{1,3},{2,0},{3,1},{4,6},{5,7},{6,4},{7,5},{8,10},{9,11},{10,... | collective-permute-start | bytes 1081352 | tf_op jit(solution)/shard_map/ppermute | solution.py:38
  252.2 15.3 %collective-permute-start.40 = (bf16[1,336,256]{2,1,0:T(8,128)(2,1)S(1)}, bf16[1,336,256]{2,1,0:T(8,128)(2,1)S(1)}, u32[]{:S(2)}, u32[]{:S(2)}) collective-permute-start(bf16[1,336,256]{2,1,0:T(8,128)(2,1)S(1)} %get-tuple-element.391), channel_id=1, source_target_pairs={{0,16},{1,17},{2,18},{3,19},{4,20},{5,21},{6,22},{7,23},{8,24},{9,... | collective-permute-start | bytes 516104 | tf_op jit(solution)/shard_map/ppermute | solution.py:38
  256.3 1.2 collective-permute-start.42
  257.5 10.0 %collective-permute-start.41 = (bf16[1,176,256]{2,1,0:T(8,128)(2,1)S(1)}, bf16[1,176,256]{2,1,0:T(8,128)(2,1)S(1)}, u32[]{:S(2)}, u32[]{:S(2)}) collective-permute-start(bf16[1,176,256]{2,1,0:T(8,128)(2,1)S(1)} %get-tuple-element.397), channel_id=1, source_target_pairs={{0,16},{1,17},{2,18},{3,19},{4,20},{5,21},{6,22},{7,23},{8,24},{9,... | collective-permute-start | bytes 270344 | tf_op jit(solution)/shard_map/ppermute | solution.py:38
  268.5 16.5 %collective-permute-start.44 = (bf16[2,336,256]{2,1,0:T(8,128)(2,1)}, bf16[2,336,256]{2,1,0:T(8,128)(2,1)}, u32[]{:S(2)}, u32[]{:S(2)}) collective-permute-start(bf16[2,336,256]{2,1,0:T(8,128)(2,1)} %slice_bitcast_fusion.11), channel_id=1, source_target_pairs={{0,2},{1,5},{2,0},{3,7},{4,6},{5,1},{6,4},{7,3},{8,10},{9,13},{10,... | collective-permute-start | bytes 1032200 | tf_op jit(solution)/shard_map/ppermute | solution.py:38
  271.0 11.7 %collective-permute-start.46 = (bf16[16,48,1024]{2,1,0:T(8,128)(2,1)}, bf16[16,48,1024]{2,1,0:T(8,128)(2,1)}, u32[]{:S(2)}, u32[]{:S(2)}) collective-permute-start(bf16[16,48,1024]{2,1,0:T(8,128)(2,1)} %get-tuple-element.305), channel_id=1, source_target_pairs={{0,1},{1,0},{2,3},{3,2},{4,5},{5,4},{6,7},{7,6},{8,9},{9,8},{10,11... | collective-permute-start | bytes 4718600 | tf_op jit(solution)/shard_map/ppermute | solution.py:30
  271.8 13.2 %collective-permute-start.45 = (bf16[2,176,256]{2,1,0:T(8,128)(2,1)}, bf16[2,176,256]{2,1,0:T(8,128)(2,1)}, u32[]{:S(2)}, u32[]{:S(2)}) collective-permute-start(bf16[2,176,256]{2,1,0:T(8,128)(2,1)} %slice_bitcast_fusion.18), channel_id=1, source_target_pairs={{0,8},{1,9},{2,10},{3,11},{4,12},{5,13},{6,14},{7,15},{8,0},{9,1},... | collective-permute-start | bytes 540680 | tf_op jit(solution)/shard_map/ppermute | solution.py:38
  272.3 2.2 collective-permute-start.47
  282.2 2.8 collective-permute-start.48
  282.4 10.5 %collective-permute-start.53 = (f32[512,512]{1,0:T(8,128)}, f32[512,512]{1,0:T(8,128)}, u32[]{:S(2)}, u32[]{:S(2)}) collective-permute-start(f32[512,512]{1,0:T(8,128)} %copy-done.45), channel_id=1, source_target_pairs={{0,1},{1,0},{2,3},{3,2},{4,5},{5,4},{6,7},{7,6},{8,9},{9,8},{10,11... | collective-permute-start | bytes 3145736 | tf_op jit(solution)/shard_map/ppermute | solution.py:30
  286.4 15.1 %collective-permute-start.49 = (bf16[1,336,256]{2,1,0:T(8,128)(2,1)S(1)}, bf16[1,336,256]{2,1,0:T(8,128)(2,1)S(1)}, u32[]{:S(2)}, u32[]{:S(2)}) collective-permute-start(bf16[1,336,256]{2,1,0:T(8,128)(2,1)S(1)} %get-tuple-element.389), channel_id=1, source_target_pairs={{0,16},{1,17},{2,18},{3,19},{4,20},{5,21},{6,22},{7,23},{8,24},{9,... | collective-permute-start | bytes 516104 | tf_op jit(solution)/shard_map/ppermute | solution.py:38
  289.8 11.6 %collective-permute-start.50 = (bf16[1,176,256]{2,1,0:T(8,128)(2,1)S(1)}, bf16[1,176,256]{2,1,0:T(8,128)(2,1)S(1)}, u32[]{:S(2)}, u32[]{:S(2)}) collective-permute-start(bf16[1,176,256]{2,1,0:T(8,128)(2,1)S(1)} %get-tuple-element.395), channel_id=1, source_target_pairs={{0,16},{1,17},{2,18},{3,19},{4,20},{5,21},{6,22},{7,23},{8,24},{9,... | collective-permute-start | bytes 270344 | tf_op jit(solution)/shard_map/ppermute | solution.py:38
  290.5 12.1 %collective-permute-start.51 = (bf16[2,2,2,48,1024]{4,3,2,1,0:T(8,128)(2,1)S(1)}, bf16[2,2,2,48,1024]{4,3,2,1,0:T(8,128)(2,1)S(1)}, u32[]{:S(2)}, u32[]{:S(2)}) collective-permute-start(bf16[2,2,2,48,1024]{4,3,2,1,0:T(8,128)(2,1)S(1)} %slice_bitcast_fusion), channel_id=1, source_target_pairs={{0,4},{1,3},{2,6},{3,1},{4,0},{5,7},{6,2},{7,5},{8,12},{9,11},{10,... | collective-permute-start | bytes 2359304 | tf_op jit(solution)/shard_map/ppermute | solution.py:38
  291.7 9.7 %collective-permute-start.52 = (f32[8,3616]{1,0:T(8,128)S(1)}, f32[8,3616]{1,0:T(8,128)S(1)}, u32[]{:S(2)}, u32[]{:S(2)}) collective-permute-start(f32[8,3616]{1,0:T(8,128)S(1)} %pad_maximum_fusion.14), channel_id=1, source_target_pairs={{0,8},{1,3},{2,10},{3,1},{4,12},{5,7},{6,14},{7,5},{8,0},{9,11},{1... | collective-permute-start | bytes 347144 | tf_op jit(solution)/shard_map/ppermute | solution.py:38
  304.0 9.1 %collective-permute-start.55 = (bf16[2,2,48,1024]{3,2,1,0:T(8,128)(2,1)S(1)}, bf16[2,2,48,1024]{3,2,1,0:T(8,128)(2,1)S(1)}, u32[]{:S(2)}, u32[]{:S(2)}) collective-permute-start(bf16[2,2,48,1024]{3,2,1,0:T(8,128)(2,1)S(1)} %slice_bitcast_fusion.6), channel_id=1, source_target_pairs={{0,2},{1,5},{2,0},{3,7},{4,6},{5,1},{6,4},{7,3},{8,10},{9,13},{10,... | collective-permute-start | bytes 1179656 | tf_op jit(solution)/shard_map/ppermute | solution.py:38
  304.2 9.0 %collective-permute-start.56 = (f32[8,3616]{1,0:T(8,128)S(1)}, f32[8,3616]{1,0:T(8,128)S(1)}, u32[]{:S(2)}, u32[]{:S(2)}) collective-permute-start(f32[8,3616]{1,0:T(8,128)S(1)} %fusion.49), channel_id=1, source_target_pairs={{0,2},{1,5},{2,0},{3,7},{4,6},{5,1},{6,4},{7,3},{8,10},{9,13},{10,... | collective-permute-start | bytes 347144 | tf_op jit(solution)/shard_map/ppermute | solution.py:38
  313.3 9.0 %collective-permute-start.57 = (bf16[2,48,1024]{2,1,0:T(8,128)(2,1)S(1)}, bf16[2,48,1024]{2,1,0:T(8,128)(2,1)S(1)}, u32[]{:S(2)}, u32[]{:S(2)}) collective-permute-start(bf16[2,48,1024]{2,1,0:T(8,128)(2,1)S(1)} %slice_bitcast_fusion.15), channel_id=1, source_target_pairs={{0,8},{1,9},{2,10},{3,11},{4,12},{5,13},{6,14},{7,15},{8,0},{9,1},... | collective-permute-start | bytes 589832 | tf_op jit(solution)/shard_map/ppermute | solution.py:38
  314.4 4.9 %collective-permute-start.60 = (f32[8,3616]{1,0:T(8,128)S(1)}, f32[8,3616]{1,0:T(8,128)S(1)}, u32[]{:S(2)}, u32[]{:S(2)}) collective-permute-start(f32[8,3616]{1,0:T(8,128)S(1)} %add.584), channel_id=1, source_target_pairs={{0,4},{1,9},{2,6},{3,11},{4,0},{5,13},{6,2},{7,15},{8,12},{9,1},{1... | collective-permute-start | bytes 347144 | tf_op jit(solution)/shard_map/ppermute | solution.py:38
  319.3 11.7 %collective-permute-start.61 = (f32[8,3616]{1,0:T(8,128)S(1)}, f32[8,3616]{1,0:T(8,128)S(1)}, u32[]{:S(2)}, u32[]{:S(2)}) collective-permute-start(f32[8,3616]{1,0:T(8,128)S(1)} %add.585), channel_id=1, source_target_pairs={{0,16},{1,17},{2,18},{3,19},{4,20},{5,21},{6,22},{7,23},{8,24},{9,... | collective-permute-start | bytes 347144 | tf_op jit(solution)/shard_map/ppermute | solution.py:38
  323.0 10.0 %collective-permute-start.58 = (bf16[1,48,1024]{2,1,0:T(8,128)(2,1)}, bf16[1,48,1024]{2,1,0:T(8,128)(2,1)}, u32[]{:S(2)}, u32[]{:S(2)}) collective-permute-start(bf16[1,48,1024]{2,1,0:T(8,128)(2,1)} %slice.445), channel_id=1, source_target_pairs={{0,16},{1,17},{2,18},{3,19},{4,20},{5,21},{6,22},{7,23},{8,24},{9,... | collective-permute-start | bytes 294920 | tf_op jit(solution)/shard_map/ppermute | solution.py:38
  331.1 3.7 %collective-permute-start.62 = (f32[8,3616]{1,0:T(8,128)S(1)}, f32[8,3616]{1,0:T(8,128)S(1)}, u32[]{:S(2)}, u32[]{:S(2)}) collective-permute-start(f32[8,3616]{1,0:T(8,128)S(1)} %add.586.refs_2_), channel_id=1, source_target_pairs={{0,1},{1,0},{2,3},{3,2},{4,5},{5,4},{6,7},{7,6},{8,9},{9,8},{10,11... | collective-permute-start | bytes 347144 | tf_op jit(solution)/shard_map/ppermute | solution.py:30
  334.7 6.7 %collective-permute-start.59 = (f32[48,1024]{1,0:T(8,128)}, f32[48,1024]{1,0:T(8,128)}, u32[]{:S(2)}, u32[]{:S(2)}) collective-permute-start(f32[48,1024]{1,0:T(8,128)} %add_bitcast_fusion), channel_id=1, source_target_pairs={{0,1},{1,0},{2,3},{3,2},{4,5},{5,4},{6,7},{7,6},{8,9},{9,8},{10,11... | collective-permute-start | bytes 589832 | tf_op jit(solution)/shard_map/ppermute | solution.py:30
  (81 other events, 482.5 us)
